TPU v7x, 128 devices: a whole 4x4x4 slice. The times are simulated.
128 devices in a mesh: tm: 32 (over x, y, core), rows: 4 (over z).
Axes of the slice: x: 4, y: 4, z: 4, core: 2. Of those that a mesh axis runs over, the one named last changes fastest.
Arguments:
- latents: bfloat16 [32, 64, 128, 512], P('tm', 'rows'), may hold values from -36 to 36
- conv_weight: bfloat16 [3, 3, 3, 512, 512], replicated, may hold values from -0.0546875 to 0.0546875
- w_query: bfloat16 [512, 512], replicated, may hold values from -4 to 4
- w_key: bfloat16 [512, 512], replicated, may hold values from -4 to 4
- w_value: bfloat16 [512, 512], replicated, may hold values from -0.25 to 0.25
- w_out: bfloat16 [512, 512], replicated, may hold values from -0.25 to 0.25
Outputs:
- block_out: bfloat16 [32, 64, 128, 512], P('tm', 'rows')
All inputs are finite; a program needn't handle non-finite values.
Results may differ from a plain program's by a relative error of at most 0.0055.
Values may be sent and summed in bfloat16 or wider, within the bound.
No kernel may reach another device: no remote copies, remote signals or barrier semaphores. Data moves between devices by JAX's collectives and lax.ppermute only.
A program may use at most 192 MiB of HBM per device.

v0:
```python
import jax
import jax.numpy as jnp
from jax import lax
from jax.sharding import PartitionSpec as P

GROUPS = 32


def shifted_2(array, axis, by):
    devices = lax.axis_size(axis)
    pairs = [(i, i + by) for i in range(devices) if 0 <= i + by < devices]
    return lax.ppermute(array, axis, pairs)


def with_halo(array, sides, width):
    for axis, dim in sides:
        devices, length = (lax.axis_size(axis), array.shape[dim])
        up = [(i, (i + 1) % devices) for i in range(devices - 1)]
        down = [(j, i) for i, j in up]
        last = lax.slice_in_dim(array, length - width, length, axis=dim)
        initial = lax.slice_in_dim(array, 0, width, axis=dim)
        before = lax.ppermute(last, axis, up)
        after = lax.ppermute(initial, axis, down)
        array = jnp.concatenate([before, array, after], axis=dim)
    return array


def group_norm(values):
    frames, height, width, chans = values.shape
    count = height * lax.axis_size("rows") * width * (chans // GROUPS)
    grouped = values.reshape(frames, height, width, GROUPS, chans // GROUPS)
    center = lax.psum(jnp.sum(grouped, axis=(1, 2, 4)), "rows") / count
    shifted = grouped - center[:, None, None, :, None]
    spread = lax.psum(jnp.sum(shifted * shifted, axis=(1, 2, 4)), "rows") / count
    return (shifted * lax.rsqrt(spread + 1e-06)[:, None, None, :, None]).reshape(values.shape)


def attend(query, keys, values):
    frames = query.shape[0]
    chans = query.shape[-1]
    scores = jnp.einsum(
        "tapc,sapc->apts", query, keys, preferred_element_type=jnp.float32
    ) / jnp.sqrt(jnp.float32(chans))
    causal = jnp.arange(frames)[:, None] >= jnp.arange(frames)[None, :]
    scores = jnp.where(causal[None, None], scores, jnp.float32(-1e30))
    weights = jax.nn.softmax(scores, axis=-1).astype(jnp.bfloat16)
    return jnp.einsum(
        "apts,sapc->tapc", weights, values, preferred_element_type=jnp.float32
    ).astype(jnp.bfloat16)


def local(latents, conv_weight, w_query, w_key, w_value, w_out):
    frames, height, width, chans = latents.shape
    acted = jax.nn.silu(group_norm(latents.astype(jnp.float32))).astype(jnp.bfloat16)
    earlier = [shifted_2(acted, "tm", offset) for offset in (2, 1)]
    stacked = jnp.concatenate(earlier + [acted], axis=0)
    padded = with_halo(stacked, (("rows", 1),), 1)
    padded = jnp.pad(padded, ((0, 0), (0, 0), (1, 1), (0, 0)))
    folded = conv_weight.reshape(3, 3, 3 * chans, chans)
    total = jnp.zeros((height * width, chans), jnp.float32)
    for time_tap in range(3):
        for row_tap in range(3):
            window = jnp.concatenate(
                [
                    padded[time_tap, row_tap : row_tap + height, col_tap : col_tap + width]
                    for col_tap in range(3)
                ],
                axis=-1,
            )
            total = total + jnp.dot(
                window.reshape(height * width, 3 * chans),
                folded[time_tap, row_tap],
                preferred_element_type=jnp.float32,
            )
    mid = (latents.astype(jnp.float32) + total.reshape(1, height, width, chans)).astype(
        jnp.bfloat16
    )
    normed = group_norm(mid.astype(jnp.float32)).astype(jnp.bfloat16)
    groups_tm = lax.axis_size("tm")
    pixels = height * width
    flat = normed.reshape(pixels, chans)
    query = (
        jnp.dot(flat, w_query, preferred_element_type=jnp.float32)
        .astype(jnp.bfloat16)
        .reshape(1, groups_tm, pixels // groups_tm, chans)
    )
    keys = (
        jnp.dot(flat, w_key, preferred_element_type=jnp.float32)
        .astype(jnp.bfloat16)
        .reshape(1, groups_tm, pixels // groups_tm, chans)
    )
    values = (
        jnp.dot(flat, w_value, preferred_element_type=jnp.float32)
        .astype(jnp.bfloat16)
        .reshape(1, groups_tm, pixels // groups_tm, chans)
    )
    attended = attend(
        lax.all_to_all(query, "tm", split_axis=1, concat_axis=0, tiled=True),
        lax.all_to_all(keys, "tm", split_axis=1, concat_axis=0, tiled=True),
        lax.all_to_all(values, "tm", split_axis=1, concat_axis=0, tiled=True),
    )
    returned = lax.all_to_all(attended, "tm", split_axis=0, concat_axis=1, tiled=True)
    update = jnp.dot(returned.reshape(pixels, chans), w_out, preferred_element_type=jnp.float32)
    return (mid.astype(jnp.float32) + update.reshape(1, height, width, chans)).astype(jnp.bfloat16)


def solution(mesh):
    in_specs = (P("tm", "rows", None, None), P(), P(), P(), P(), P())
    out_specs = P("tm", "rows", None, None)
    return jax.shard_map(local, mesh=mesh, in_specs=in_specs, out_specs=out_specs, check_vma=False)
```

profile of v0, /device:TPU:1, one launch (start us, length us, event | category | flops | bytes accessed | tf_op | source)
XLA Modules:
  0.0 368.6 jit_solution(10549507808836984160)
XLA Ops:
  0.0 2.1 convert_reduce_fusion.1
  2.2 0.1 reduce_sum.63
  2.3 10.6 %psum.28 = f32[1,32]{1,0:T(1,128)S(1)} all-reduce(f32[1,32]{1,0:T(1,128)S(1)} %bitcast.167), channel_id=1, replica_groups=mesh['tm'=32,'rows'=4] {'rows'}, use_global_device_ids=true, to_apply=%region_2.0 | all-reduce | flops 32 | bytes 256 | tf_op jit(solution)/shard_map/psum | solution.py:32
  13.0 0.6 fusion.73
  13.9 6.0 %psum.29 = f32[1,32]{1,0:T(1,128)S(1)} all-reduce(f32[1,32]{1,0:T(1,128)S(1)} %bitcast.168), channel_id=1, replica_groups=mesh['tm'=32,'rows'=4] {'rows'}, use_global_device_ids=true, to_apply=%region_5.6 | all-reduce | flops 32 | bytes 256 | tf_op jit(solution)/shard_map/psum | solution.py:34
  20.0 1.2 fusion.70
  21.2 3.3 collective-permute-start
  24.6 7.7 %collective-permute-start.1 = (bf16[1,16,128,512]{3,2,1,0:T(8,128)(2,1)S(1)}, bf16[1,16,128,512]{3,2,1,0:T(8,128)(2,1)S(1)}, u32[]{:S(2)}, u32[]{:S(2)}) collective-permute-start(bf16[1,16,128,512]{3,2,1,0:T(8,128)(2,1)S(1)} %fusion.70), channel_id=1, source_target_pairs={{0,4},{4,8},{8,12},{12,16},{16,20},{20,24},{24,28},{28,32},{32,36}... | collective-permute-start | bytes 6291464 | tf_op jit(solution)/shard_map/ppermute | solution.py:12
  32.2 32.7 %collective-permute-done = bf16[1,16,128,512]{3,2,1,0:T(8,128)(2,1)S(1)} collective-permute-done((bf16[1,16,128,512]{3,2,1,0:T(8,128)(2,1)S(1)}, bf16[1,16,128,512]{3,2,1,0:T(8,128)(2,1)S(1)}, u32[]{:S(2)}, u32[]{:S(2)}) %collective-permute-start) | collective-permute-done | bytes 2097184 | tf_op jit(solution)/shard_map/ppermute | solution.py:12
  64.9 27.4 %collective-permute-done.1 = bf16[1,16,128,512]{3,2,1,0:T(8,128)(2,1)S(1)} collective-permute-done((bf16[1,16,128,512]{3,2,1,0:T(8,128)(2,1)S(1)}, bf16[1,16,128,512]{3,2,1,0:T(8,128)(2,1)S(1)}, u32[]{:S(2)}, u32[]{:S(2)}) %collective-permute-start.1) | collective-permute-done | bytes 2097184 | tf_op jit(solution)/shard_map/ppermute | solution.py:12
  92.4 3.4 collective-permute-start.2
  95.8 1.5 collective-permute-start.3
  97.3 3.2 collective-permute-done.2
  100.5 3.8 %collective-permute-done.3 = bf16[3,1,128,512]{3,2,1,0:T(8,128)(2,1)S(1)} collective-permute-done((bf16[3,1,128,512]{3,2,1,0:T(8,128)(2,1)S(1)}, bf16[3,1,128,512]{3,2,1,0:T(8,128)(2,1)S(1)}, u32[]{:S(2)}, u32[]{:S(2)}) %collective-permute-start.3) | collective-permute-done | bytes 393248 | tf_op jit(solution)/shard_map/ppermute | solution.py:23
  104.3 6.1 %select_maximum_fusion = bf16[3,18,130,512]{3,2,1,0:T(8,128)(2,1)S(1)} fusion(bf16[3,1,128,512]{3,2,1,0:T(8,128)(2,1)S(1)} %collective-permute-done.3, bf16[3,1,128,512]{3,2,1,0:T(8,128)(2,1)S(1)} %collective-permute-done.2, bf16[1,16,128,512]{3,2,1,0:T(8,128)(2,1)S(1)} %fusion.70, bf16[1,16,128,512]{3,2,1,0:T(8,128)(2,1)S(1)} %collective-permute-done.1, ...), kind=kLoop, calls=%fused_computation.4 | loop fusion | flops 64696320 | bytes 14266368 | tf_op jit(solution)/shard_map/concatenate | solution.py:24
  110.4 12.4 %fusion.112 = (bf16[1,16,128,512]{3,2,1,0:T(8,128)(2,1)}, bf16[1,16,128,512]{3,2,1,0:T(8,128)(2,1)}, bf16[1,16,128,512]{3,2,1,0:T(8,128)(2,1)}, bf16[1,16,128,51...) fusion(bf16[3,18,130,512]{3,2,1,0:T(8,128)(2,1)S(1)} %select_ma, ...), kind=kLoop, calls=%fused_computation.142 | loop fusion | bytes 75497472 | tf_op jit(solution)/shard_map/slice | solution.py:65
  122.8 8.1 %fusion.13 = f32[2048,512]{1,0:T(8,128)} fusion(bf16[2048,512]{1,0:T(8,128)(2,1)} %bitcast.144, bf16[2048,512]{1,0:T(8,128)(2,1)S(1)} %bitcast.125, bf16[2048,512]{1,0:T(8,128)(2,1)} %bitcast.145, bf16[3,3,1536,512]{3,2,1,0:T(8,128)(2,1)} %bitcast.157), kind=kOutput, calls=%fused_computation.17 | convolution fusion | flops 3240099840 | bytes 12058624 | tf_op jit(solution)/shard_map/dot_general | solution.py:70
  130.9 0.9 pad_maximum_fusion.9
  131.8 0.7 copy-done.15
  132.5 0.6 copy-done.16
  133.1 6.3 %fusion.7 = f32[2048,512]{1,0:T(8,128)} fusion(bf16[2048,512]{1,0:T(8,128)(2,1)S(1)} %bitcast.142, bf16[2048,512]{1,0:T(8,128)(2,1)S(1)} %bitcast.149, bf16[2048,512]{1,0:T(8,128)(2,1)S(1)} %bitcast.143, bf16[3,3,1536,512]{3,2,1,0:T(8,128)(2,1)} %bitcast.158), kind=kOutput, calls=%fused_computation.11 | convolution fusion | flops 3240099840 | bytes 12058624 | tf_op jit(solution)/shard_map/dot_general | solution.py:70
  139.5 2.3 pad_maximum_fusion
  141.7 0.7 copy-done.14
  142.4 6.5 %fusion.19 = f32[2048,512]{1,0:T(8,128)} fusion(bf16[2048,512]{1,0:T(8,128)(2,1)S(1)} %bitcast.139, bf16[2048,512]{1,0:T(8,128)(2,1)S(1)} %bitcast.148, bf16[2048,512]{1,0:T(8,128)(2,1)S(1)} %bitcast.140, bf16[3,3,1536,512]{3,2,1,0:T(8,128)(2,1)} %bitcast.159), kind=kOutput, calls=%fused_computation.23 | convolution fusion | flops 3240099840 | bytes 12058624 | tf_op jit(solution)/shard_map/dot_general | solution.py:70
  148.9 6.5 %fusion.25 = f32[2048,512]{1,0:T(8,128)} fusion(bf16[2048,512]{1,0:T(8,128)(2,1)S(1)} %bitcast.137, bf16[2048,512]{1,0:T(8,128)(2,1)S(1)} %bitcast.146, bf16[2048,512]{1,0:T(8,128)(2,1)S(1)} %bitcast.138, bf16[3,3,1536,512]{3,2,1,0:T(8,128)(2,1)} %bitcast.160), kind=kOutput, calls=%fused_computation.29 | convolution fusion | flops 3240099840 | bytes 12058624 | tf_op jit(solution)/shard_map/dot_general | solution.py:70
  155.4 6.5 %fusion.31 = f32[2048,512]{1,0:T(8,128)} fusion(bf16[2048,512]{1,0:T(8,128)(2,1)S(1)} %bitcast.135, bf16[2048,512]{1,0:T(8,128)(2,1)S(1)} %bitcast.124, bf16[2048,512]{1,0:T(8,128)(2,1)S(1)} %bitcast.136, bf16[3,3,1536,512]{3,2,1,0:T(8,128)(2,1)} %bitcast.161), kind=kOutput, calls=%fused_computation.35 | convolution fusion | flops 3240099840 | bytes 12058624 | tf_op jit(solution)/shard_map/dot_general | solution.py:70
  161.9 6.5 %fusion.37 = f32[2048,512]{1,0:T(8,128)} fusion(bf16[2048,512]{1,0:T(8,128)(2,1)S(1)} %bitcast.133, bf16[2048,512]{1,0:T(8,128)(2,1)S(1)} %bitcast.147, bf16[2048,512]{1,0:T(8,128)(2,1)S(1)} %bitcast.134, bf16[3,3,1536,512]{3,2,1,0:T(8,128)(2,1)} %bitcast.162), kind=kOutput, calls=%fused_computation.41 | convolution fusion | flops 3240099840 | bytes 12058624 | tf_op jit(solution)/shard_map/dot_general | solution.py:70
  168.5 6.5 %fusion.43 = f32[2048,512]{1,0:T(8,128)} fusion(bf16[2048,512]{1,0:T(8,128)(2,1)S(1)} %bitcast.131, bf16[2048,512]{1,0:T(8,128)(2,1)S(1)} %bitcast.141, bf16[2048,512]{1,0:T(8,128)(2,1)S(1)} %bitcast.132, bf16[3,3,1536,512]{3,2,1,0:T(8,128)(2,1)} %bitcast.163), kind=kOutput, calls=%fused_computation.47 | convolution fusion | flops 3240099840 | bytes 12058624 | tf_op jit(solution)/shard_map/dot_general | solution.py:70
  174.9 6.6 %fusion.49 = f32[2048,512]{1,0:T(8,128)} fusion(bf16[2048,512]{1,0:T(8,128)(2,1)S(1)} %bitcast.129, bf16[2048,512]{1,0:T(8,128)(2,1)S(1)} %bitcast.123, bf16[2048,512]{1,0:T(8,128)(2,1)S(1)} %bitcast.130, bf16[3,3,1536,512]{3,2,1,0:T(8,128)(2,1)} %bitcast.164), kind=kOutput, calls=%fused_computation.53 | convolution fusion | flops 3240099840 | bytes 12058624 | tf_op jit(solution)/shard_map/dot_general | solution.py:70
  181.5 16.5 %convert_reduce_fusion = (f32[512]{0:T(512)S(1)}, bf16[1,16,128,512]{3,2,1,0:T(8,128)(2,1)}) fusion(bf16[1,16,128,512]{3,2,1,0:T(8,128)(2,1)S(1)} %copy-done.1, bf16[3,3,1536,512]{3,2,1,0:T(8,128)(2,1)} %bitcast.165, bf16[2048,512]{1,0:T(8,128)(2,1)} %bitcast.127, bf16[2048,512]{1,0:T(8,128)(2,1)} %bitcast.128, bf16[2048,512]{1,0:T(8,128)(2,1)} %bitcast.126, ...), kind=kOutput, calls=%fused_computation.67 | convolution fusion | flops 3253730816 | bytes 45615104 | tf_op jit(solution)/shard_map/dot_general | solution.py:70
  198.2 6.1 %psum.30 = f32[1,32]{1,0:T(1,128)S(1)} all-reduce(f32[1,32]{1,0:T(1,128)S(1)} %bitcast.169), channel_id=1, replica_groups=mesh['tm'=32,'rows'=4] {'rows'}, use_global_device_ids=true, to_apply=%region_8.9 | all-reduce | flops 32 | bytes 256 | tf_op jit(solution)/shard_map/psum | solution.py:32
  204.5 2.2 fusion.71
  206.9 7.4 %psum.31 = f32[1,32]{1,0:T(1,128)S(1)} all-reduce(f32[1,32]{1,0:T(1,128)S(1)} %bitcast.166), channel_id=1, replica_groups=mesh['tm'=32,'rows'=4] {'rows'}, use_global_device_ids=true, to_apply=%region_11.12 | all-reduce | flops 32 | bytes 256 | tf_op jit(solution)/shard_map/psum | solution.py:34
  214.6 0.5 fusion.72
  215.1 2.5 convolution_convert_fusion.1
  217.7 15.9 %all-to-all-start.1 = ((bf16[1,32,64,512]{3,2,0,1:T(8,128)(2,1)}), bf16[1,32,64,512]{3,2,0,1:T(8,128)(2,1)}, u32[]{:S(2)}, u32[]{:S(2)}) async-start(bf16[1,32,64,512]{3,2,0,1:T(8,128)(2,1)} %bitcast.155), calls=%async_computation.1 | async-start | bytes 4194304 | tf_op jit(solution)/shard_map/all_to_all | solution.py:98
  233.6 4.2 %convolution_convert_fusion = bf16[2048,512]{1,0:T(8,128)(2,1)} fusion(bf16[2048,512]{1,0:T(8,128)(2,1)} %bitcast.151, bf16[512,512]{1,0:T(8,128)(2,1)S(1)} %copy-done.18), kind=kOutput, calls=%fused_computation.87 | convolution fusion | flops 1074790400 | bytes 4718592 | tf_op jit(solution)/shard_map/dot_general | solution.py:88
  237.8 24.2 %all-to-all-done.1 = bf16[1,32,64,512]{3,2,0,1:T(8,128)(2,1)} async-done(((bf16[1,32,64,512]{3,2,0,1:T(8,128)(2,1)}), bf16[1,32,64,512]{3,2,0,1:T(8,128)(2,1)}, u32[]{:S(2)}, u32[]{:S(2)}) %all-to-all-start.1) | async-done | bytes 2097184 | tf_op jit(solution)/shard_map/all_to_all | solution.py:98
  261.9 5.3 %all-to-all-start.2 = ((bf16[1,32,64,512]{3,2,0,1:T(8,128)(2,1)}), bf16[1,32,64,512]{3,2,0,1:T(8,128)(2,1)}, u32[]{:S(2)}, u32[]{:S(2)}) async-start(bf16[1,32,64,512]{3,2,0,1:T(8,128)(2,1)} %bitcast.154), calls=%async_computation.2 | async-start | bytes 4194304 | tf_op jit(solution)/shard_map/all_to_all | solution.py:99
  267.3 4.2 %convolution_convert_fusion.2 = bf16[2048,512]{1,0:T(8,128)(2,1)} fusion(bf16[2048,512]{1,0:T(8,128)(2,1)} %bitcast.152, bf16[512,512]{1,0:T(8,128)(2,1)S(1)} %copy-done.19), kind=kOutput, calls=%fused_computation.89 | convolution fusion | flops 1074790400 | bytes 4718592 | tf_op jit(solution)/shard_map/dot_general | solution.py:93
  271.5 24.2 %all-to-all-done.2 = bf16[1,32,64,512]{3,2,0,1:T(8,128)(2,1)} async-done(((bf16[1,32,64,512]{3,2,0,1:T(8,128)(2,1)}), bf16[1,32,64,512]{3,2,0,1:T(8,128)(2,1)}, u32[]{:S(2)}, u32[]{:S(2)}) %all-to-all-start.2) | async-done | bytes 2097184 | tf_op jit(solution)/shard_map/all_to_all | solution.py:99
  295.7 5.2 %all-to-all-start = ((bf16[1,32,64,512]{3,2,0,1:T(8,128)(2,1)}), bf16[1,32,64,512]{3,2,0,1:T(8,128)(2,1)}, u32[]{:S(2)}, u32[]{:S(2)}) async-start(bf16[1,32,64,512]{3,2,0,1:T(8,128)(2,1)} %bitcast.153), calls=%async_computation | async-start | bytes 4194304 | tf_op jit(solution)/shard_map/all_to_all | solution.py:100
  301.0 5.8 %fusion.113 = (f32[64,32]{1,0:T(8,128)S(1)}, f32[64,32,32]{1,2,0:T(8,128)}) fusion(bf16[1,32,64,512]{3,2,0,1:T(8,128)(2,1)} %all-to-all-done.2, bf16[1,32,64,512]{3,2,0,1:T(8,128)(2,1)} %all-to-all-done.1, pred[32,32]{0,1:T(8,128)(4,1)S(1)} %iota_compare_fusion.2), kind=kOutput, calls=%fused_computation.143 | convolution fusion | flops 67371040 | bytes 4465664 | tf_op jit(solution)/shard_map/sub | solution.py:46
  306.7 22.6 %all-to-all-done = bf16[1,32,64,512]{3,2,0,1:T(8,128)(2,1)} async-done(((bf16[1,32,64,512]{3,2,0,1:T(8,128)(2,1)}), bf16[1,32,64,512]{3,2,0,1:T(8,128)(2,1)}, u32[]{:S(2)}, u32[]{:S(2)}) %all-to-all-start) | async-done | bytes 2097184 | tf_op jit(solution)/shard_map/all_to_all | solution.py:100
  329.4 3.6 convert_bitcast_fusion
  332.9 1.2 copy.23
  334.1 31.9 %all_to_all.16 = bf16[32,1,64,512]{3,2,1,0:T(8,128)(2,1)S(1)} all-to-all(bf16[32,1,64,512]{3,2,1,0:T(8,128)(2,1)S(1)} %copy.23), channel_id=1, replica_groups=mesh['tm'=32,'rows'=4] {'tm'}, dimensions={0} | all-to-all | bytes 4194304 | tf_op jit(solution)/shard_map/all_to_all | solution.py:102
  366.0 2.6 fusion.75
  (60 shorter events, 1.5 us)
Async XLA Ops:
  0.0 215.1 %copy-start = (bf16[512,512]{1,0:T(8,128)(2,1)S(1)}, bf16[512,512]{1,0:T(8,128)(2,1)}, u32[]{:S(2)}) copy-start(bf16[512,512]{1,0:T(8,128)(2,1)} %param.8) | copy-start | bytes 1572868
  0.0 13.0 %copy-start.1 = (bf16[1,16,128,512]{3,2,1,0:T(8,128)(2,1)S(1)}, bf16[1,16,128,512]{3,2,1,0:T(8,128)(2,1)}, u32[]{:S(2)}) copy-start(bf16[1,16,128,512]{3,2,1,0:T(8,128)(2,1)} %param.6) | copy-start | bytes 6291460
  21.2 43.7 %collective-permute-start = (bf16[1,16,128,512]{3,2,1,0:T(8,128)(2,1)S(1)}, bf16[1,16,128,512]{3,2,1,0:T(8,128)(2,1)S(1)}, u32[]{:S(2)}, u32[]{:S(2)}) collective-permute-start(bf16[1,16,128,512]{3,2,1,0:T(8,128)(2,1)S(1)} %fusion.70), channel_id=1, source_target_pairs={{0,8},{4,12},{8,16},{12,20},{16,24},{20,28},{24,32},{28,36},{32,40... | collective-permute-start | bytes 6291464 | tf_op jit(solution)/shard_map/ppermute | solution.py:12
  24.6 67.8 %collective-permute-start.1 = (bf16[1,16,128,512]{3,2,1,0:T(8,128)(2,1)S(1)}, bf16[1,16,128,512]{3,2,1,0:T(8,128)(2,1)S(1)}, u32[]{:S(2)}, u32[]{:S(2)}) collective-permute-start(bf16[1,16,128,512]{3,2,1,0:T(8,128)(2,1)S(1)} %fusion.70), channel_id=1, source_target_pairs={{0,4},{4,8},{8,12},{12,16},{16,20},{20,24},{24,28},{28,32},{32,36}... | collective-permute-start | bytes 6291464 | tf_op jit(solution)/shard_map/ppermute | solution.py:12
  92.4 8.1 %collective-permute-start.2 = (bf16[3,1,128,512]{3,2,1,0:T(8,128)(2,1)S(1)}, bf16[3,1,128,512]{3,2,1,0:T(8,128)(2,1)S(1)}, u32[]{:S(2)}, u32[]{:S(2)}) collective-permute-start(bf16[3,1,128,512]{3,2,1,0:T(8,128)(2,1)S(1)} %get-tuple-element.31), channel_id=1, source_target_pairs={{0,1},{1,2},{2,3},{4,5},{5,6},{6,7},{8,9},{9,10},{10,11},{12,13},{... | collective-permute-start | bytes 1179656 | tf_op jit(solution)/shard_map/ppermute | solution.py:22
  95.8 8.5 %collective-permute-start.3 = (bf16[3,1,128,512]{3,2,1,0:T(8,128)(2,1)S(1)}, bf16[3,1,128,512]{3,2,1,0:T(8,128)(2,1)S(1)}, u32[]{:S(2)}, u32[]{:S(2)}) collective-permute-start(bf16[3,1,128,512]{3,2,1,0:T(8,128)(2,1)S(1)} %get-tuple-element.32), channel_id=1, source_target_pairs={{1,0},{2,1},{3,2},{5,4},{6,5},{7,6},{9,8},{10,9},{11,10},{13,12},{... | collective-permute-start | bytes 1179656 | tf_op jit(solution)/shard_map/ppermute | solution.py:23
  130.9 1.6 copy-start.15
  130.9 2.2 copy-start.16
  139.5 2.3 copy-start.13
  139.5 3.0 copy-start.14
  142.4 6.5 %copy-start.11 = (bf16[1,16,128,512]{3,2,1,0:T(8,128)(2,1)S(1)}, bf16[1,16,128,512]{3,2,1,0:T(8,128)(2,1)}, u32[]{:S(2)}) copy-start(bf16[1,16,128,512]{3,2,1,0:T(8,128)(2,1)} %get-tuple-element.16) | copy-start | bytes 6291460
  142.4 6.5 %copy-start.12 = (bf16[1,16,128,512]{3,2,1,0:T(8,128)(2,1)S(1)}, bf16[1,16,128,512]{3,2,1,0:T(8,128)(2,1)}, u32[]{:S(2)}) copy-start(bf16[1,16,128,512]{3,2,1,0:T(8,128)(2,1)} %get-tuple-element.17) | copy-start | bytes 6291460
  148.9 6.5 %copy-start.9 = (bf16[1,16,128,512]{3,2,1,0:T(8,128)(2,1)S(1)}, bf16[1,16,128,512]{3,2,1,0:T(8,128)(2,1)}, u32[]{:S(2)}) copy-start(bf16[1,16,128,512]{3,2,1,0:T(8,128)(2,1)} %get-tuple-element.14) | copy-start | bytes 6291460
  148.9 6.5 %copy-start.10 = (bf16[1,16,128,512]{3,2,1,0:T(8,128)(2,1)S(1)}, bf16[1,16,128,512]{3,2,1,0:T(8,128)(2,1)}, u32[]{:S(2)}) copy-start(bf16[1,16,128,512]{3,2,1,0:T(8,128)(2,1)} %get-tuple-element.15) | copy-start | bytes 6291460
  155.4 6.5 %copy-start.7 = (bf16[1,16,128,512]{3,2,1,0:T(8,128)(2,1)S(1)}, bf16[1,16,128,512]{3,2,1,0:T(8,128)(2,1)}, u32[]{:S(2)}) copy-start(bf16[1,16,128,512]{3,2,1,0:T(8,128)(2,1)} %get-tuple-element.12) | copy-start | bytes 6291460
  155.4 6.5 %copy-start.8 = (bf16[1,16,128,512]{3,2,1,0:T(8,128)(2,1)S(1)}, bf16[1,16,128,512]{3,2,1,0:T(8,128)(2,1)}, u32[]{:S(2)}) copy-start(bf16[1,16,128,512]{3,2,1,0:T(8,128)(2,1)} %get-tuple-element.13) | copy-start | bytes 6291460
  161.9 6.5 %copy-start.5 = (bf16[1,16,128,512]{3,2,1,0:T(8,128)(2,1)S(1)}, bf16[1,16,128,512]{3,2,1,0:T(8,128)(2,1)}, u32[]{:S(2)}) copy-start(bf16[1,16,128,512]{3,2,1,0:T(8,128)(2,1)} %get-tuple-element.10) | copy-start | bytes 6291460
  161.9 6.5 %copy-start.6 = (bf16[1,16,128,512]{3,2,1,0:T(8,128)(2,1)S(1)}, bf16[1,16,128,512]{3,2,1,0:T(8,128)(2,1)}, u32[]{:S(2)}) copy-start(bf16[1,16,128,512]{3,2,1,0:T(8,128)(2,1)} %get-tuple-element.11) | copy-start | bytes 6291460
  168.4 6.5 %copy-start.3 = (bf16[1,16,128,512]{3,2,1,0:T(8,128)(2,1)S(1)}, bf16[1,16,128,512]{3,2,1,0:T(8,128)(2,1)}, u32[]{:S(2)}) copy-start(bf16[1,16,128,512]{3,2,1,0:T(8,128)(2,1)} %get-tuple-element.8) | copy-start | bytes 6291460
  168.5 6.5 %copy-start.4 = (bf16[1,16,128,512]{3,2,1,0:T(8,128)(2,1)S(1)}, bf16[1,16,128,512]{3,2,1,0:T(8,128)(2,1)}, u32[]{:S(2)}) copy-start(bf16[1,16,128,512]{3,2,1,0:T(8,128)(2,1)} %get-tuple-element.9) | copy-start | bytes 6291460
  198.0 16.5 %copy-start.2 = (bf16[1,16,128,512]{3,2,1,0:T(8,128)(2,1)S(1)}, bf16[1,16,128,512]{3,2,1,0:T(8,128)(2,1)}, u32[]{:S(2)}) copy-start(bf16[1,16,128,512]{3,2,1,0:T(8,128)(2,1)} %get-tuple-element.6) | copy-start | bytes 6291460
  215.1 2.6 copy-start.17
  217.7 15.9 %copy-start.18 = (bf16[512,512]{1,0:T(8,128)(2,1)S(1)}, bf16[512,512]{1,0:T(8,128)(2,1)}, u32[]{:S(2)}) copy-start(bf16[512,512]{1,0:T(8,128)(2,1)} %param.9) | copy-start | bytes 1572868
  217.7 44.3 %all-to-all-start.1 = ((bf16[1,32,64,512]{3,2,0,1:T(8,128)(2,1)}), bf16[1,32,64,512]{3,2,0,1:T(8,128)(2,1)}, u32[]{:S(2)}, u32[]{:S(2)}) async-start(bf16[1,32,64,512]{3,2,0,1:T(8,128)(2,1)} %bitcast.155), calls=%async_computation.1 | async-start | bytes 4194304 | tf_op jit(solution)/shard_map/all_to_all | solution.py:98
  261.9 5.3 %copy-start.19 = (bf16[512,512]{1,0:T(8,128)(2,1)S(1)}, bf16[512,512]{1,0:T(8,128)(2,1)}, u32[]{:S(2)}) copy-start(bf16[512,512]{1,0:T(8,128)(2,1)} %param.10) | copy-start | bytes 1572868
  261.9 33.8 %all-to-all-start.2 = ((bf16[1,32,64,512]{3,2,0,1:T(8,128)(2,1)}), bf16[1,32,64,512]{3,2,0,1:T(8,128)(2,1)}, u32[]{:S(2)}, u32[]{:S(2)}) async-start(bf16[1,32,64,512]{3,2,0,1:T(8,128)(2,1)} %bitcast.154), calls=%async_computation.2 | async-start | bytes 4194304 | tf_op jit(solution)/shard_map/all_to_all | solution.py:99
  295.7 33.6 %all-to-all-start = ((bf16[1,32,64,512]{3,2,0,1:T(8,128)(2,1)}), bf16[1,32,64,512]{3,2,0,1:T(8,128)(2,1)}, u32[]{:S(2)}, u32[]{:S(2)}) async-start(bf16[1,32,64,512]{3,2,0,1:T(8,128)(2,1)} %bitcast.153), calls=%async_computation | async-start | bytes 4194304 | tf_op jit(solution)/shard_map/all_to_all | solution.py:100
  334.1 31.9 %copy-start.20 = (bf16[512,512]{1,0:T(8,128)(2,1)S(1)}, bf16[512,512]{1,0:T(8,128)(2,1)}, u32[]{:S(2)}) copy-start(bf16[512,512]{1,0:T(8,128)(2,1)} %param.11) | copy-start | bytes 1572868
where the time goes:
time: 369 us
  waiting for transfers between devices  138 us (37%)
  matrix products  92.7 us (25%)
  blocking collectives  62.1 us (17%)
  starting transfers between devices  42.3 us (11%)
  local copies, waits for them, and re-layouts  16.5 us (4%)
  other arithmetic  16.5 us (4%)
    dot_general x9, matrix products, local(): jnp.dot(window.reshape(height * width, 3 * chans), folded[time_tap, row_t...  69.9 us
    ppermute x2, waiting for transfers between devices, shifted_2(): return lax.ppermute(array, axis, pairs)  60.1 us
    all_to_all x1, blocking collectives, local(): lax.all_to_all(attended, 'tm', split_axis=0, concat_axis=1, tiled=True)  31.9 us
    all_to_all x1, waiting for transfers between devices, local(): lax.all_to_all(keys, 'tm', split_axis=1, concat_axis=0, tiled=True)  24.2 us
    all_to_all x1, waiting for transfers between devices, local(): lax.all_to_all(query, 'tm', split_axis=1, concat_axis=0, tiled=True)  24.2 us
    all_to_all x1, waiting for transfers between devices, local(): lax.all_to_all(values, 'tm', split_axis=1, concat_axis=0, tiled=True)  22.6 us
    psum x2, blocking collectives, group_norm(): center = lax.psum(jnp.sum(grouped, axis=(1, 2, 4)), 'rows') / count  16.7 us
    all_to_all x1, starting transfers between devices, local(): lax.all_to_all(query, 'tm', split_axis=1, concat_axis=0, tiled=True)  15.9 us
  transfers between devices with their start and end apart: 7, of which 7 were waited for; matrix products, arithmetic and copies ran while one was open for 4% of the time, Pallas kernels for 0%

commit v1 on v0

v1 whole, which is shorter than its diff:
```python
import functools

import jax
import jax.numpy as jnp
from jax import lax
from jax.experimental import pallas as pl
from jax.experimental.pallas import tpu as pltpu
from jax.sharding import PartitionSpec as P

GROUPS = 32
T = 32
C = 512
S = 8
W = S + 2
MSG = 104
EPS = 1e-6
BF, F32 = jnp.bfloat16, jnp.float32
HI = lax.Precision.HIGHEST


def iota(shape, dim):
    return lax.broadcasted_iota(jnp.int32, shape, dim)


def dot(a, b, precision=None):
    return jnp.dot(a, b, preferred_element_type=F32, precision=precision)


def params():
    return pltpu.CompilerParams(vmem_limit_bytes=56 * 2**20)


def cost(flops, nbytes):
    return pl.CostEstimate(flops=flops, bytes_accessed=nbytes, transcendentals=0)


def to_groups(lane):
    return (iota((C, 128), 0) // 16 + lane == iota((C, 128), 1)).astype(F32)


def from_groups(lane, dtype=F32):
    return (iota((128, C), 1) // 16 + lane == iota((128, C), 0)).astype(dtype)


def group_stats(mean, m2, count, lane):
    group_mean = dot(mean, to_groups(lane), HI) * (1.0 / 16.0)
    off = mean - dot(group_mean, from_groups(lane), HI)
    return group_mean + dot(m2 + count * (off * off), to_groups(lane + 32), HI)


def merge(parts, count):
    n = parts.shape[0]
    total = jnp.sum(parts, axis=0)
    mean = total * (1.0 / n)
    off = parts - mean[None]
    between = pltpu.roll(jnp.sum(off * off, axis=0), 32, 1)
    is_mean = (iota(total.shape, 1) // 32) % 2 == 0
    return jnp.where(is_mean, mean, total + count * between)


def latent_stats_kernel(x_ref, out_ref):
    n = x_ref.shape[0]
    step = 256

    def add(i, total):
        rows = x_ref[pl.ds(pl.multiple_of(i * step, step), step), :].astype(F32)
        return total + jnp.sum(rows.reshape(step // 8, 8, C), axis=0)

    total = lax.fori_loop(0, n // step, add, jnp.zeros((8, C), F32))
    mean = jnp.sum(total, axis=0, keepdims=True) * (1.0 / n)

    def add_square(i, total):
        rows = x_ref[pl.ds(pl.multiple_of(i * step, step), step), :].astype(F32) - mean
        return total + jnp.sum((rows * rows).reshape(step // 8, 8, C), axis=0)

    total = lax.fori_loop(0, n // step, add_square, jnp.zeros((8, C), F32))
    m2 = jnp.sum(total, axis=0, keepdims=True)
    wide = lambda v: jnp.broadcast_to(v, (8, C))
    out_ref[...] = group_stats(wide(mean), wide(m2), float(n), 0)


def message_kernel(top_ref, x_ref, bottom_ref, s0, s1, s2, s3, out_ref):
    pair = pl.program_id(0)
    parts = jnp.stack([s0[...], s1[...], s2[...], s3[...]])
    n = 2048.0 * 16.0
    whole = merge(parts, n)
    is_mean = iota(whole.shape, 1) < 32
    stats = jnp.where(is_mean, whole, lax.rsqrt(whole * (1.0 / (4.0 * n)) + EPS))
    stats = jnp.where(iota(whole.shape, 1) < 64, stats, 0.0)
    high = stats.astype(BF).astype(F32)
    middle = (stats - high).astype(BF).astype(F32)
    low = stats - high - middle
    row = jnp.concatenate([high, middle, low, jnp.zeros_like(low)], axis=1)[:1]
    for odd in range(2):
        start = 16 * pair if odd else 16 * pair - 16
        start = jnp.clip(start, 0, 96)
        first = 16 * pair + 8 * odd - 1 - start
        start = pl.multiple_of(start, 16)
        out_row, source = iota((MSG, W * 32), 0), iota((MSG, W * 32), 1)
        column = first + out_row % W
        pick = (source == (out_row // W) * 32 + column) & (column >= 0) & (column < 32)
        pick = (pick & (out_row < W * W)).astype(BF)
        for half in range(2):
            cols = pl.ds(start, 32)
            if half == 0:
                block = jnp.concatenate([top_ref[:, cols, :], x_ref[0:9, cols, :]], axis=0)
            else:
                block = jnp.concatenate([x_ref[7:16, cols, :], bottom_ref[:, cols, :]], axis=0)
            message = dot(pick, block.reshape(W * 32, C))
            message = jnp.where(iota((MSG, C), 0) == W * W, row, message)
            out_ref[2 * odd + half] = message.astype(BF)


def conv_kernel(place_ref, in_ref, w_ref, mid_ref, stats_ref, acted, latent, acc):
    step = pl.program_id(0)
    b, e = step // 3, step % 3

    @pl.when(step == 0)
    def _():
        block, z = place_ref[0], place_ref[1]
        half, column = block % 2, block // 2
        tail = in_ref[:, 96:MSG, :].reshape(T * 8, C)
        pick = (iota((T, T * 8), 1) == iota((T, T * 8), 0) * 8 + 4).astype(BF)
        pieces = dot(pick, tail).astype(BF)
        mean, scale = (
            sum(dot(pieces[:, 128 * i : 128 * i + 128], from_groups(lane, BF)) for i in range(3))
            for lane in (0, 32)
        )

        def activate(first, pixels):
            rows = pixels * T
            values = in_ref[:, first : first + pixels, :].reshape(rows, C)
            turn = iota((rows, rows), 0)
            turn = (iota((rows, rows), 1) == (turn % T) * pixels + turn // T).astype(BF)
            turned = dot(turn, values).reshape(pixels, T, C)
            u = (turned - mean[None]) * scale[None]
            act = u / (1.0 + jnp.exp(-u))
            p = iota((pixels, T, C), 0) + first
            r, c = p // W, p % W
            out = (c == 0) & (column == 0) | (c == W - 1) & (column == 15)
            out = out | (r == 0) & (half == 0) & (z == 0) | (r == W - 1) & (half == 1) & (z == 3)
            act = jnp.where(out, 0.0, act)
            flat = act.reshape(rows, C)
            frame = iota((rows, C), 0) % T
            for i in range(pixels):
                where = first + i
                if where >= W * W:
                    break
                r, c = where // W, where % W
                if 1 <= r <= S and 1 <= c <= S:
                    latent[(r - 1) * S + c - 1] = turned[i].astype(BF)
            count = min(pixels, W * W - first)
            for tap in range(3):
                by = 2 - tap
                moved = flat if by == 0 else jnp.where(frame < by, 0.0, pltpu.roll(flat, by, 0))
                moved = moved.astype(BF).reshape(pixels, T, C)
                for i in range(count):
                    acted[(first + i) // W, (first + i) % W, :, C * tap : C * tap + C] = moved[i]

        for k in range(6):
            activate(16 * k, 16)
        activate(96, 8)
        acc[...] = jnp.zeros_like(acc)

    weight = w_ref[...].reshape(3 * C, C)

    def row(r, _):
        left = acted[pl.ds(2 * r + b, 2), pl.ds(e, S)].reshape(2 * S * T, 3 * C)
        at = pl.ds(pl.multiple_of(r * 2 * S * T, 2 * S * T), 2 * S * T)
        acc[at, :] += dot(left, weight)
        return 0

    lax.fori_loop(0, S // 2, row, 0)

    @pl.when(step == 8)
    def _():
        mid = (latent[...].astype(F32) + acc[...].reshape(S * S, T, C)).astype(BF)
        mid_ref[...] = mid
        values = mid_ref[...].astype(F32)
        mean = jnp.sum(values, axis=0) * (1.0 / (S * S))
        off = mid_ref[...].astype(F32) - mean[None]
        m2 = jnp.sum(off * off, axis=0)
        half = T // 2
        stats_ref[...] = group_stats(mean[:half], m2[:half], float(S * S), 0) + group_stats(
            mean[half:], m2[half:], float(S * S), 64
        )


def merge_kernel(s0, s1, s2, s3, out_ref):
    parts = jnp.stack([s0[...], s1[...], s2[...], s3[...]])
    whole = merge(parts, float(S * S * 16))
    out_ref[...] = jnp.broadcast_to(whole[None], out_ref.shape)


def attend_kernel(mid_ref, parts_ref, wq_ref, wk_ref, wv_ref, wo_ref, out_ref, norm):
    @pl.when(pl.program_id(0) == 0)
    def _():
        count = float(S * S * 16 * 4)
        whole = merge(parts_ref[...], count)
        is_mean = (iota(whole.shape, 1) // 32) % 2 == 0
        whole = jnp.where(is_mean, whole, lax.rsqrt(whole * (1.0 / (32.0 * count)) + EPS))
        for i in range(2):
            for j in range(2):
                norm[i, 16 * j : 16 * j + 16] = dot(whole, from_groups(64 * j + 32 * i), HI)

    pixels = mid_ref.shape[0]
    rows = pixels * T
    mid = mid_ref[...].astype(F32)
    flat = ((mid - norm[0][None]) * norm[1][None]).astype(BF).reshape(rows, C)
    query = dot(flat, wq_ref[...]).astype(BF)
    keys = dot(flat, wk_ref[...]).astype(BF)
    values = dot(flat, wv_ref[...]).astype(BF)
    n = 256
    t, s = iota((n, n), 0), iota((n, n), 1)
    seen = (t // T == s // T) & (t >= s)
    parts = []
    for i in range(rows // n):
        at = slice(i * n, i * n + n)
        scores = lax.dot_general(
            query[at], keys[at], (((1,), (1,)), ((), ())), preferred_element_type=F32
        ) * (1.0 / (C**0.5))
        scores = jnp.where(seen, scores, -1e30)
        weights = jnp.exp(scores - jnp.max(scores, axis=1, keepdims=True))
        weights = (weights / jnp.sum(weights, axis=1, keepdims=True)).astype(BF)
        parts.append(dot(weights, values[at]).astype(BF))
    update = dot(jnp.concatenate(parts, axis=0), wo_ref[...])
    out = (mid.reshape(rows, C) + update).astype(BF)
    turn = iota((rows, rows), 0)
    turn = (iota((rows, rows), 1) == (turn % pixels) * T + turn // pixels).astype(BF)
    out_ref[...] = dot(turn, out).astype(BF).reshape(T, pixels, C)


def neighbours(array, axis):
    n = lax.axis_size(axis)
    return [array] + [lax.ppermute(array, axis, [(i, (i + by) % n) for i in range(n)]) for by in range(1, n)]


def local(latents, conv_weight, w_query, w_key, w_value, w_out):
    bands = lax.axis_size("rows")
    x = latents.reshape(16, 128, C)
    down = [(i, i + 1) for i in range(bands - 1)]
    top = lax.ppermute(x[15:16], "rows", down)
    bottom = lax.ppermute(x[0:1], "rows", [(j, i) for i, j in down])
    vmem = pl.BlockSpec(memory_space=pltpu.VMEM)
    stats = pl.pallas_call(
        latent_stats_kernel,
        out_shape=jax.ShapeDtypeStruct((8, 128), F32),
        in_specs=[vmem],
        out_specs=vmem,
        compiler_params=params(),
        cost_estimate=cost(2048 * C * 4, 2048 * C * 2),
        name="latent_stats",
    )(x.reshape(2048, C))
    whole = lambda *shape: pl.BlockSpec(shape, lambda i: (0,) * len(shape))
    messages = pl.pallas_call(
        message_kernel,
        grid=(8,),
        out_shape=jax.ShapeDtypeStruct((32, MSG, C), BF),
        in_specs=[whole(1, 128, C), whole(16, 128, C), whole(1, 128, C)] + [whole(8, 128)] * 4,
        out_specs=pl.BlockSpec((4, MSG, C), lambda i: (i, 0, 0)),
        compiler_params=params(),
        cost_estimate=cost(32 * MSG * 320 * C * 2, 6 * 2**20),
        name="messages",
    )(top, x, bottom, *neighbours(stats, "rows"))
    patch = lax.all_to_all(messages.reshape(1, 32, MSG, C), "tm", split_axis=1, concat_axis=0, tiled=True)
    place = jnp.stack([lax.axis_index("tm"), lax.axis_index("rows")]).astype(jnp.int32)
    mid, stats = pl.pallas_call(
        conv_kernel,
        grid=(9,),
        out_shape=(jax.ShapeDtypeStruct((S * S, T, C), BF), jax.ShapeDtypeStruct((T // 2, 128), F32)),
        in_specs=[
            pl.BlockSpec(memory_space=pltpu.SMEM),
            whole(T, MSG, C),
            pl.BlockSpec((3, 1, 1, C, C), lambda i: (0, i // 3, i % 3, 0, 0)),
        ],
        out_specs=(whole(S * S, T, C), whole(T // 2, 128)),
        scratch_shapes=[
            pltpu.VMEM((W, W, T, 3 * C), BF),
            pltpu.VMEM((S * S, T, C), BF),
            pltpu.VMEM((S * S * T, C), F32),
        ],
        compiler_params=params(),
        cost_estimate=cost(2048 * 27 * C * C * 2, 20 * 2**20),
        name="conv",
    )(place, patch.reshape(T, MSG, C), conv_weight)
    parts = pl.pallas_call(
        merge_kernel,
        out_shape=jax.ShapeDtypeStruct((32, T // 2, 128), F32),
        in_specs=[vmem] * 4,
        out_specs=vmem,
        compiler_params=params(),
        name="merge",
    )(*neighbours(stats, "rows"))
    parts = lax.all_to_all(parts[None], "tm", split_axis=1, concat_axis=0, tiled=True)
    pixels = 16
    out = pl.pallas_call(
        attend_kernel,
        grid=(S * S // pixels,),
        out_shape=jax.ShapeDtypeStruct((T, S * S, C), BF),
        in_specs=[pl.BlockSpec((pixels, T, C), lambda i: (i, 0, 0)), whole(32, T // 2, 128)] + [whole(C, C)] * 4,
        out_specs=pl.BlockSpec((T, pixels, C), lambda i: (0, i, 0)),
        scratch_shapes=[pltpu.VMEM((2, T, C), F32)],
        compiler_params=params(),
        cost_estimate=cost(2048 * C * C * 2 * 6, 8 * 2**20),
        name="attend",
    )(mid, parts.reshape(32, T // 2, 128), w_query, w_key, w_value, w_out)
    back = lax.all_to_all(out[:, None], "tm", split_axis=0, concat_axis=1, tiled=True)
    back = back.reshape(16, 2, S, S, C).transpose(1, 2, 0, 3, 4)
    return back.reshape(1, 16, 128, C)


def solution(mesh):
    in_specs = (P("tm", "rows", None, None), P(), P(), P(), P(), P())
    out_specs = P("tm", "rows", None, None)
    return jax.shard_map(local, mesh=mesh, in_specs=in_specs, out_specs=out_specs, check_vma=False)
```

time: 369 us -> 201 us (0.54)
  matrix products: 92.7 us -> 0 us
  waiting for transfers between devices: 138 us -> 47.1 us
  Pallas kernels: 0 us -> 72.9 us
  starting transfers between devices: 42.3 us -> 24.8 us
  other arithmetic: 16.5 us -> 0.55 us
  blocking collectives: 62.1 us -> 49.1 us
  local copies, waits for them, and re-layouts: 16.5 us -> 5.52 us
    dot_general x14 -> x0, matrix products: 87 us -> none  [the longest x9 69.9 us: local(): jnp.dot(window.reshape(height * width, 3 * chans), folded[time_tap, row_t...]
    pallas_call x0 -> x5, Pallas kernels: none -> 72.9 us  [the longest x1 48 us: local(): pl.pallas_call(conv_kernel, grid=(9,), out_shape=(jax.ShapeDtypeStruct((S...]
    ppermute x4 -> x8, waiting for transfers between devices: 67.1 us -> 5 us  [the longest x6 4.99 us: neighbours(): lax.ppermute(array, axis, [(i, (i + by) % n) for i in range(n)])]
    psum x4 -> x0, blocking collectives: 30.2 us -> none  [the longest x2 16.7 us: group_norm(): center = lax.psum(jnp.sum(grouped, axis=(1, 2, 4)), 'rows') / count]
    all_to_all x3 -> x1, waiting for transfers between devices: 71 us -> 42.1 us  [local(): lax.all_to_all(messages.reshape(1, 32, MSG, C), 'tm', split_axis=1, conca...]
    all_to_all x1 -> x2, blocking collectives: 31.9 us -> 49.1 us  [the longest x1 32.1 us: local(): lax.all_to_all(out[:, None], 'tm', split_axis=0, concat_axis=1, tiled=True)]
    all_to_all x3 -> x1, starting transfers between devices: 26.5 us -> 9.74 us  [local(): lax.all_to_all(messages.reshape(1, 32, MSG, C), 'tm', split_axis=1, conca...]
    slice x1, local copies, waits for them, and re-layouts: 12.4 us -> 0.98 us  [local(): bottom = lax.ppermute(x[0:1], 'rows', [(j, i) for i, j in down])]
  transfers between devices with their start and end apart: 7 -> 9, of which waited for: 7 -> 6; matrix products, arithmetic and copies ran while one was open for 4% -> 0% of each run, Pallas kernels for 0% -> 2%
where the time goes in v1:
time: 201 us; the launch traced here: 200 us
  Pallas kernels  72.9 us (36%)
  blocking collectives  49.1 us (24%)
  waiting for transfers between devices  47.1 us (23%)
  starting transfers between devices  24.8 us (12%)
  local copies, waits for them, and re-layouts  5.52 us (3%)
    pallas_call x1, Pallas kernels, local(): pl.pallas_call(conv_kernel, grid=(9,), out_shape=(jax.ShapeDtypeStruct((S...  48 us
    all_to_all x1, waiting for transfers between devices, local(): lax.all_to_all(messages.reshape(1, 32, MSG, C), 'tm', split_axis=1, conca...  42.1 us
    all_to_all x1, blocking collectives, local(): lax.all_to_all(out[:, None], 'tm', split_axis=0, concat_axis=1, tiled=True)  32.1 us
    all_to_all x1, blocking collectives, local(): lax.all_to_all(parts[None], 'tm', split_axis=1, concat_axis=0, tiled=True)  17 us
    pallas_call x1, Pallas kernels, local(): pl.pallas_call(attend_kernel, grid=(S * S // pixels,), out_shape=jax.Shap...  12.6 us
    all_to_all x1, starting transfers between devices, local(): lax.all_to_all(messages.reshape(1, 32, MSG, C), 'tm', split_axis=1, conca...  9.74 us
    ppermute x6, starting transfers between devices, neighbours(): lax.ppermute(array, axis, [(i, (i + by) % n) for i in range(n)])  9.41 us
    pallas_call x1, Pallas kernels, local(): pl.pallas_call(message_kernel, grid=(8,), out_shape=jax.ShapeDtypeStruct(...  6.86 us
  transfers between devices with their start and end apart: 9, of which 6 were waited for; matrix products, arithmetic and copies ran while one was open for 0% of the time, Pallas kernels for 2%

profile of v1, /device:TPU:1, one launch (start us, length us, event | category | flops | bytes accessed | tf_op | source)
XLA Modules:
  0.0 200.1 jit_solution(915037430014845634)
XLA Ops:
  0.0 1.0 slice_bitcast_fusion
  1.0 4.4 %collective-permute-start = (bf16[1,128,512]{2,1,0:T(8,128)(2,1)S(1)}, bf16[1,128,512]{2,1,0:T(8,128)(2,1)S(1)}, u32[]{:S(2)}, u32[]{:S(2)}) collective-permute-start(bf16[1,128,512]{2,1,0:T(8,128)(2,1)S(1)} %get-tuple-element.10), channel_id=1, source_target_pairs={{0,1},{1,2},{2,3},{4,5},{5,6},{6,7},{8,9},{9,10},{10,11},{12,13},{... | collective-permute-start | bytes 393224 | tf_op jit(solution)/shard_map/ppermute | solution.py:242
  5.4 1.3 collective-permute-start.1
  6.7 4.0 %latent_stats.1.s0 = f32[8,128]{1,0:T(8,128)} custom-call(bf16[2048,512]{1,0:T(8,128)(2,1)} %bitcast.24), custom_call_target="tpu_custom_call" | custom-call | flops 4194304 | bytes 2097152 | tf_op jit(solution)/shard_map/latent_stats/pallas_call | solution.py:245
  10.7 2.3 %collective-permute-start.2 = (f32[8,128]{1,0:T(8,128)}, f32[8,128]{1,0:T(8,128)S(1)}, u32[]{:S(2)}, u32[]{:S(2)}) collective-permute-start(f32[8,128]{1,0:T(8,128)} %latent_stats.1.s0), channel_id=1, source_target_pairs={{0,1},{1,2},{2,3},{3,0},{4,5},{5,6},{6,7},{7,4},{8,9},{9,10},{10,1... | collective-permute-start | bytes 12296 | tf_op jit(solution)/shard_map/ppermute | solution.py:235
  12.9 3.1 %collective-permute-start.3 = (f32[8,128]{1,0:T(8,128)}, f32[8,128]{1,0:T(8,128)S(1)}, u32[]{:S(2)}, u32[]{:S(2)}) collective-permute-start(f32[8,128]{1,0:T(8,128)} %latent_stats.1.s0), channel_id=1, source_target_pairs={{0,2},{1,3},{2,0},{3,1},{4,6},{5,7},{6,4},{7,5},{8,10},{9,11},{10,... | collective-permute-start | bytes 12296 | tf_op jit(solution)/shard_map/ppermute | solution.py:235
  16.0 0.7 collective-permute-start.4
  16.8 0.0 collective-permute-done.2.s1
  16.8 0.0 copy-start.6
  16.8 0.5 collective-permute-done.3.s2
  17.3 0.0 copy-start.7
  17.3 1.7 collective-permute-done.4.s3
  19.0 0.0 copy-start.8
  19.0 0.0 collective-permute-done.top_ref
  19.0 0.0 copy-start.1
  19.0 0.0 collective-permute-done.1.bottom_ref
  19.0 0.0 copy-start.2
  19.0 0.0 copy-done.6
  19.0 0.0 copy-done.7
  19.0 0.5 copy-done.8
  19.6 0.1 copy-done.1
  19.7 0.0 copy-done.2
  19.7 6.9 %messages.1 = bf16[32,104,512]{2,1,0:T(8,128)(2,1)} custom-call(bf16[1,128,512]{2,1,0:T(8,128)(2,1)} %copy-done.1, bf16[16,128,512]{2,1,0:T(8,128)(2,1)} %bitcast.25, bf16[1,128,512]{2,1,0:T(8,128)(2,1)} %copy-done.2, f32[8,128]{1,0:T(8,128)} %latent_stats.1.s0, f32[8,128]{1,0:T(8,128)} %copy-done.6, f32[8,128]{1,0:T(8,128)} %copy-done.7, f32[8,128]{1,0:T(8,128)} %copy-done.8), custom_call_target="tpu_custom_call" | custom-call | flops 1090519040 | bytes 6291456 | tf_op jit(solution)/shard_map/messages/pallas_call | solution.py:255
  26.6 9.7 %all-to-all-start = ((bf16[1,32,104,512]{3,2,0,1:T(8,128)(2,1)}), bf16[1,32,104,512]{3,2,0,1:T(8,128)(2,1)S(1)}, u32[]{:S(2)}, u32[]{:S(2)}) async-start(bf16[1,32,104,512]{3,2,0,1:T(8,128)(2,1)} %bitcast.23), calls=%async_computation | async-start | bytes 6815744 | tf_op jit(solution)/shard_map/all_to_all | solution.py:265
  36.3 0.6 pad_add_fusion.place_ref
  36.9 42.1 %all-to-all-done = bf16[1,32,104,512]{3,2,0,1:T(8,128)(2,1)S(1)} async-done(((bf16[1,32,104,512]{3,2,0,1:T(8,128)(2,1)}), bf16[1,32,104,512]{3,2,0,1:T(8,128)(2,1)S(1)}, u32[]{:S(2)}, u32[]{:S(2)}) %all-to-all-start) | async-done | bytes 3407904 | tf_op jit(solution)/shard_map/all_to_all | solution.py:265
  79.0 0.0 copy-start
  79.0 1.7 copy-done
  80.7 48.0 %conv.1 = (bf16[64,32,512]{2,1,0:T(8,128)(2,1)}, f32[16,128]{1,0:T(8,128)}) custom-call(s32[2]{0:T(128)} %pad_add_fusion.place_ref, bf16[32,104,512]{2,1,0:T(8,128)(2,1)} %bitcast.27, bf16[3,3,3,512,512]{4,3,2,1,0:T(8,128)(2,1)} %w_ref.1), custom_call_target="tpu_custom_call" | custom-call | flops 28991029248 | bytes 20971520 | tf_op jit(solution)/shard_map/conv/pallas_call | solution.py:267
  128.6 0.0 collective-permute-start.5
  128.6 3.1 %collective-permute-start.6 = (f32[16,128]{1,0:T(8,128)}, f32[16,128]{1,0:T(8,128)S(1)}, u32[]{:S(2)}, u32[]{:S(2)}) collective-permute-start(f32[16,128]{1,0:T(8,128)} %get-tuple-element.8.s0), channel_id=1, source_target_pairs={{0,2},{1,3},{2,0},{3,1},{4,6},{5,7},{6,4},{7,5},{8,10},{9,11},{10,... | collective-permute-start | bytes 24584 | tf_op jit(solution)/shard_map/ppermute | solution.py:235
  131.7 0.2 collective-permute-start.7
  131.9 0.6 collective-permute-done.5.s1
  132.6 0.0 copy-start.3
  132.6 0.5 collective-permute-done.6.s2
  133.1 0.0 copy-start.4
  133.1 1.6 collective-permute-done.7.s3
  134.7 0.0 copy-done.3
  134.7 0.0 copy-done.4
  134.7 0.0 copy-start.5
  134.7 0.6 copy-done.5
  135.3 1.5 merge.1
  136.9 17.0 %all_to_all.12 = f32[1,32,16,128]{3,2,0,1:T(8,128)} all-to-all(f32[1,32,16,128]{3,2,0,1:T(8,128)} %bitcast.29), channel_id=1, replica_groups=mesh['tm'=32,'rows'=4] {'tm'}, dimensions={1} | all-to-all | bytes 524288 | tf_op jit(solution)/shard_map/all_to_all | solution.py:294
  153.9 12.6 %attend.1 = bf16[32,64,512]{2,1,0:T(8,128)(2,1)} custom-call(bf16[64,32,512]{2,1,0:T(8,128)(2,1)} %get-tuple-element.7.mid_ref, f32[32,16,128]{2,1,0:T(8,128)} %bitcast.30, bf16[512,512]{1,0:T(8,128)(2,1)} %wq_ref.1, bf16[512,512]{1,0:T(8,128)(2,1)} %wk_ref.1, bf16[512,512]{1,0:T(8,128)(2,1)} %wv_ref.1, bf16[512,512]{1,0:T(8,128)(2,1)} %wo_ref.1), custom_call_target="tpu_custom_call" | custom-call | flops 6442450944 | bytes 8388608 | tf_op jit(solution)/shard_map/attend/pallas_call | solution.py:296
  166.5 32.1 %all_to_all.13 = bf16[32,1,64,512]{3,2,1,0:T(8,128)(2,1)S(1)} all-to-all(bf16[32,1,64,512]{3,2,1,0:T(8,128)(2,1)} %bitcast.28), channel_id=1, replica_groups=mesh['tm'=32,'rows'=4] {'tm'}, dimensions={0} | all-to-all | bytes 4194304 | tf_op jit(solution)/shard_map/all_to_all | solution.py:307
  198.5 1.5 copy.11
Async XLA Ops:
  1.0 18.0 %collective-permute-start = (bf16[1,128,512]{2,1,0:T(8,128)(2,1)S(1)}, bf16[1,128,512]{2,1,0:T(8,128)(2,1)S(1)}, u32[]{:S(2)}, u32[]{:S(2)}) collective-permute-start(bf16[1,128,512]{2,1,0:T(8,128)(2,1)S(1)} %get-tuple-element.10), channel_id=1, source_target_pairs={{0,1},{1,2},{2,3},{4,5},{5,6},{6,7},{8,9},{9,10},{10,11},{12,13},{... | collective-permute-start | bytes 393224 | tf_op jit(solution)/shard_map/ppermute | solution.py:242
  5.4 13.6 %collective-permute-start.1 = (bf16[1,128,512]{2,1,0:T(8,128)(2,1)S(1)}, bf16[1,128,512]{2,1,0:T(8,128)(2,1)S(1)}, u32[]{:S(2)}, u32[]{:S(2)}) collective-permute-start(bf16[1,128,512]{2,1,0:T(8,128)(2,1)S(1)} %get-tuple-element.9), channel_id=1, source_target_pairs={{1,0},{2,1},{3,2},{5,4},{6,5},{7,6},{9,8},{10,9},{11,10},{13,12},{... | collective-permute-start | bytes 393224 | tf_op jit(solution)/shard_map/ppermute | solution.py:243
  10.7 6.1 %collective-permute-start.2 = (f32[8,128]{1,0:T(8,128)}, f32[8,128]{1,0:T(8,128)S(1)}, u32[]{:S(2)}, u32[]{:S(2)}) collective-permute-start(f32[8,128]{1,0:T(8,128)} %latent_stats.1.s0), channel_id=1, source_target_pairs={{0,1},{1,2},{2,3},{3,0},{4,5},{5,6},{6,7},{7,4},{8,9},{9,10},{10,1... | collective-permute-start | bytes 12296 | tf_op jit(solution)/shard_map/ppermute | solution.py:235
  12.9 4.4 %collective-permute-start.3 = (f32[8,128]{1,0:T(8,128)}, f32[8,128]{1,0:T(8,128)S(1)}, u32[]{:S(2)}, u32[]{:S(2)}) collective-permute-start(f32[8,128]{1,0:T(8,128)} %latent_stats.1.s0), channel_id=1, source_target_pairs={{0,2},{1,3},{2,0},{3,1},{4,6},{5,7},{6,4},{7,5},{8,10},{9,11},{10,... | collective-permute-start | bytes 12296 | tf_op jit(solution)/shard_map/ppermute | solution.py:235
  16.0 3.0 %collective-permute-start.4 = (f32[8,128]{1,0:T(8,128)}, f32[8,128]{1,0:T(8,128)S(1)}, u32[]{:S(2)}, u32[]{:S(2)}) collective-permute-start(f32[8,128]{1,0:T(8,128)} %latent_stats.1.s0), channel_id=1, source_target_pairs={{0,3},{1,0},{2,1},{3,2},{4,7},{5,4},{6,5},{7,6},{8,11},{9,8},{10,9... | collective-permute-start | bytes 12296 | tf_op jit(solution)/shard_map/ppermute | solution.py:235
  16.8 2.3 %copy-start.6 = (f32[8,128]{1,0:T(8,128)}, f32[8,128]{1,0:T(8,128)S(1)}, u32[]{:S(2)}) copy-start(f32[8,128]{1,0:T(8,128)S(1)} %collective-permute-done.2.s1) | copy-start | bytes 12292
  17.3 1.8 copy-start.7
  19.0 0.6 copy-start.8
  19.0 0.7 copy-start.1
  19.0 0.7 copy-start.2
  26.6 52.4 %all-to-all-start = ((bf16[1,32,104,512]{3,2,0,1:T(8,128)(2,1)}), bf16[1,32,104,512]{3,2,0,1:T(8,128)(2,1)S(1)}, u32[]{:S(2)}, u32[]{:S(2)}) async-start(bf16[1,32,104,512]{3,2,0,1:T(8,128)(2,1)} %bitcast.23), calls=%async_computation | async-start | bytes 6815744 | tf_op jit(solution)/shard_map/all_to_all | solution.py:265
  79.0 1.7 copy-start
  128.6 3.9 %collective-permute-start.5 = (f32[16,128]{1,0:T(8,128)}, f32[16,128]{1,0:T(8,128)S(1)}, u32[]{:S(2)}, u32[]{:S(2)}) collective-permute-start(f32[16,128]{1,0:T(8,128)} %get-tuple-element.8.s0), channel_id=1, source_target_pairs={{0,1},{1,2},{2,3},{3,0},{4,5},{5,6},{6,7},{7,4},{8,9},{9,10},{10,1... | collective-permute-start | bytes 24584 | tf_op jit(solution)/shard_map/ppermute | solution.py:235
  128.6 4.4 %collective-permute-start.6 = (f32[16,128]{1,0:T(8,128)}, f32[16,128]{1,0:T(8,128)S(1)}, u32[]{:S(2)}, u32[]{:S(2)}) collective-permute-start(f32[16,128]{1,0:T(8,128)} %get-tuple-element.8.s0), channel_id=1, source_target_pairs={{0,2},{1,3},{2,0},{3,1},{4,6},{5,7},{6,4},{7,5},{8,10},{9,11},{10,... | collective-permute-start | bytes 24584 | tf_op jit(solution)/shard_map/ppermute | solution.py:235
  131.7 3.0 %collective-permute-start.7 = (f32[16,128]{1,0:T(8,128)}, f32[16,128]{1,0:T(8,128)S(1)}, u32[]{:S(2)}, u32[]{:S(2)}) collective-permute-start(f32[16,128]{1,0:T(8,128)} %get-tuple-element.8.s0), channel_id=1, source_target_pairs={{0,3},{1,0},{2,1},{3,2},{4,7},{5,4},{6,5},{7,6},{8,11},{9,8},{10,9... | collective-permute-start | bytes 24584 | tf_op jit(solution)/shard_map/ppermute | solution.py:235
  132.6 2.1 %copy-start.3 = (f32[16,128]{1,0:T(8,128)}, f32[16,128]{1,0:T(8,128)S(1)}, u32[]{:S(2)}) copy-start(f32[16,128]{1,0:T(8,128)S(1)} %collective-permute-done.5.s1) | copy-start | bytes 24580
  133.1 1.6 copy-start.4
  134.7 0.6 copy-start.5

commit v2 on v1

v2 whole, which is shorter than its diff:
```python
import functools

import jax
import jax.numpy as jnp
from jax import lax
from jax.experimental import pallas as pl
from jax.experimental.pallas import tpu as pltpu
from jax.sharding import PartitionSpec as P

GROUPS = 32
T = 32
C = 512
S = 8
W = S + 2
P2 = T // 2
RIM = 40
EPS = 1e-6
BF, F32 = jnp.bfloat16, jnp.float32
HI = lax.Precision.HIGHEST


def iota(shape, dim):
    return lax.broadcasted_iota(jnp.int32, shape, dim)


def dot(a, b, precision=None):
    return jnp.dot(a, b, preferred_element_type=F32, precision=precision)


def params():
    return pltpu.CompilerParams(vmem_limit_bytes=56 * 2**20)


def cost(flops, nbytes):
    return pl.CostEstimate(flops=flops, bytes_accessed=nbytes, transcendentals=0)


def to_groups(lane):
    return (iota((C, 128), 0) // 16 + lane == iota((C, 128), 1)).astype(F32)


def from_groups(lane, dtype=F32):
    return (iota((128, C), 1) // 16 + lane == iota((128, C), 0)).astype(dtype)


def group_stats(mean, m2, count, lane):
    group_mean = dot(mean, to_groups(lane), HI) * (1.0 / 16.0)
    off = mean - dot(group_mean, from_groups(lane), HI)
    return group_mean + dot(m2 + count * (off * off), to_groups(lane + 32), HI)


def merge(parts, count):
    n = parts.shape[0]
    total = jnp.sum(parts, axis=0)
    mean = total * (1.0 / n)
    off = parts - mean[None]
    between = pltpu.roll(jnp.sum(off * off, axis=0), 32, 1)
    is_mean = (iota(total.shape, 1) // 32) % 2 == 0
    return jnp.where(is_mean, mean, total + count * between)


def latent_stats_kernel(x_ref, out_ref):
    n = x_ref.shape[0]
    step = 256

    def add(i, total):
        rows = x_ref[pl.ds(pl.multiple_of(i * step, step), step), :].astype(F32)
        return total + jnp.sum(rows.reshape(step // 8, 8, C), axis=0)

    total = lax.fori_loop(0, n // step, add, jnp.zeros((8, C), F32))
    mean = jnp.sum(total, axis=0, keepdims=True) * (1.0 / n)

    def add_square(i, total):
        rows = x_ref[pl.ds(pl.multiple_of(i * step, step), step), :].astype(F32) - mean
        return total + jnp.sum((rows * rows).reshape(step // 8, 8, C), axis=0)

    total = lax.fori_loop(0, n // step, add_square, jnp.zeros((8, C), F32))
    m2 = jnp.sum(total, axis=0, keepdims=True)
    wide = lambda v: jnp.broadcast_to(v, (8, C))
    out_ref[...] = group_stats(wide(mean), wide(m2), float(n), 0)


def finish(whole, count):
    is_mean = (iota(whole.shape, 1) // 32) % 2 == 0
    return jnp.where(is_mean, whole, lax.rsqrt(whole * (1.0 / count) + EPS))


def place_kernel(place_ref, s0, s1, s2, s3, out_ref):
    n = 2048.0 * 16.0
    whole = finish(merge(jnp.stack([s0[...], s1[...], s2[...], s3[...]]), n), 4.0 * n)[:1]
    frame = place_ref[0]
    row = (frame % 2) * P2 + frame // 2
    here = (iota((T, 128), 0) == row) & (iota((T, 128), 1) < 64)
    out_ref[...] = jnp.where(here, whole, 0.0)


def rim_kernel(top_ref, x_ref, bottom_ref, out_ref):
    pair = pl.program_id(0)
    for odd in range(2):
        start = 16 * pair if odd else 16 * pair - 16
        start = jnp.clip(start, 0, 96)
        first = 16 * pair + 8 * odd - 1 - start
        start = pl.multiple_of(start, 16)
        p, source = iota((RIM, W * 32), 0), iota((RIM, W * 32), 1)
        r = jnp.where(p < 10, 0, jnp.where(p < 20, 9, jnp.where(p < 28, p - 19, p - 27)))
        c = jnp.where(p < 10, p, jnp.where(p < 20, p - 10, jnp.where(p < 28, 0, 9)))
        column = first + c
        pick = (source == r * 32 + column) & (column >= 0) & (column < 32) & (p < 36)
        pick = pick.astype(BF)
        for half in range(2):
            cols = pl.ds(start, 32)
            if half == 0:
                block = jnp.concatenate([top_ref[:, cols, :], x_ref[0:9, cols, :]], axis=0)
            else:
                block = jnp.concatenate([x_ref[7:16, cols, :], bottom_ref[:, cols, :]], axis=0)
            out_ref[2 * odd + half] = dot(pick, block.reshape(W * 32, C)).astype(BF)


def weights_kernel(w_ref, out_ref):
    g = [w_ref[i, 0, 0].astype(F32) for i in range(3)]
    ends = (g[0] + g[2]) * 0.5
    out_ref[0, 0, 0] = w_ref[0, 0, 0]
    out_ref[1, 0, 0] = (ends + g[1] * 0.5).astype(BF)
    out_ref[2, 0, 0] = (ends - g[1] * 0.5).astype(BF)
    out_ref[3, 0, 0] = w_ref[2, 0, 0]


def expand(stats_ref, norm):
    for i in range(2):
        norm[i] = dot(stats_ref[...], from_groups(32 * i), HI).reshape(2, P2, C)


def turned(in_ref, first, pixels):
    rows = pixels * T
    to, at = iota((rows, rows), 0), iota((rows, rows), 1)
    frame = 2 * (to % P2) + (to // P2) % 2
    turn = (at == frame * pixels + to // T).astype(BF)
    values = in_ref[:, first : first + pixels, :].reshape(rows, C)
    return dot(turn, values).reshape(pixels, 2, P2, C)


def activate(values, norm):
    u = (values - norm[0][None]) * norm[1][None]
    return (u / (1.0 + jnp.exp(-u))).astype(BF).astype(F32)


def time_terms(act):
    pixels = act.shape[0]
    even, odd = act[:, 0], act[:, 1]
    start = iota((pixels * P2, C), 0) % P2 == 0

    def before(v):
        v = pltpu.roll(v.reshape(pixels * P2, C), 1, 0)
        return jnp.where(start, 0.0, v).reshape(pixels, P2, C)

    even1, odd1 = before(even), before(odd)
    return [v.astype(BF) for v in (even1 - even, odd1 + even, even - odd1, odd1 - odd)]


def signs(j):
    return jnp.where(j == 3, 0.0, 1.0), jnp.where(j == 0, 0.0, jnp.where(j == 1, 1.0, -1.0))


def conv_kernel(in_ref, stats_ref, w_ref, y_ref, latent_ref, terms, norm):
    j = pl.program_id(0)

    @pl.when(j == 0)
    def _():
        expand(stats_ref, norm)
        for i in range(4):
            terms[i, 0] = jnp.zeros((S, P2, 3 * C), BF)
            terms[i, W - 1] = jnp.zeros((S, P2, 3 * C), BF)
            terms[i, 1 : S + 1, 0, :, 0:C] = jnp.zeros((S, P2, C), BF)
            terms[i, 1 : S + 1, S - 1, :, 2 * C :] = jnp.zeros((S, P2, C), BF)
        for k in range(S // 2):
            values = turned(in_ref, 16 * k, 16)
            latent_ref[16 * k : 16 * k + 16] = values.astype(BF)
            at = slice(2 * k + 1, 2 * k + 3)
            for i, v in enumerate(time_terms(activate(values, norm))):
                v = v.reshape(2, S, P2, C)
                terms[i, at, 1:S, :, 0:C] = v[:, : S - 1]
                terms[i, at, :, :, C : 2 * C] = v
                terms[i, at, 0 : S - 1, :, 2 * C :] = v[:, 1:]
        y_ref[...] = jnp.zeros_like(y_ref)

    even, odd = signs(j)
    for q in range(S // 2):
        m = sum(
            dot(terms[j, 2 * q + b : 2 * q + b + 2].reshape(2 * S * P2, 3 * C), w_ref[0, b].reshape(3 * C, C))
            for b in range(3)
        ).reshape(2 * S, P2, C)
        at = slice(16 * q, 16 * q + 16)
        y_ref[at, 0] += even * m
        y_ref[at, 1] += odd * m


def border_kernel(place_ref, in_ref, stats_ref, y_ref, latent_ref, w_ref, mid_ref, out_ref, terms, side, norm):
    j = pl.program_id(0)

    @pl.when(j == 0)
    def _():
        expand(stats_ref, norm)
        block, z = place_ref[0], place_ref[1]
        half, column = block % 2, block // 2
        above = (half == 0) & (z == 0)
        below = (half == 1) & (z == 3)
        left, right = column == 0, column == 15
        for first, pixels in ((0, 16), (16, 16), (32, 8)):
            act = activate(turned(in_ref, first, pixels), norm)
            p = iota((pixels, 2, P2, C), 0) + first
            out = above & (p < 10) | below & (p >= 10) & (p < 20)
            out = out | left & ((p == 0) | (p == 10) | (p >= 20) & (p < 28))
            out = out | right & ((p == 9) | (p == 19) | (p >= 28))
            for i, v in enumerate(time_terms(jnp.where(out, 0.0, act))):
                terms[i, first : first + pixels] = v
        side[...] = jnp.zeros_like(side)

    even, odd = signs(j)
    zero = jnp.zeros((1, P2, C), BF)

    def add(k, parts, weight):
        m = dot(jnp.concatenate(parts, axis=2).reshape(S * P2, 3 * C), weight.reshape(3 * C, C))
        m = m.reshape(S, P2, C)
        side[k, 0] += even * m
        side[k, 1] += odd * m

    for k, b in ((0, 0), (1, 2)):
        add(k, [terms[j, 10 * k + e : 10 * k + e + S] for e in range(3)], w_ref[0, b])
    for k, e in ((2, 0), (3, 2)):
        line = terms[j, 20 + 8 * (k - 2) : 28 + 8 * (k - 2)]
        parts = [jnp.concatenate([zero, line[:-1]], axis=0), line, jnp.concatenate([line[1:], zero], axis=0)]
        add(k, parts, w_ref[0, :, e])

    @pl.when(j == 3)
    def _():
        total = jnp.zeros((2, P2, C), F32)
        for p in range(S * S):
            r, c = p // S, p % S
            v = y_ref[p]
            for k, is_side, at in ((0, r == 0, c), (1, r == S - 1, c), (2, c == 0, r), (3, c == S - 1, r)):
                if is_side:
                    v = v + side[k, :, at]
            v = (latent_ref[p].astype(F32) + v).astype(BF)
            mid_ref[p] = v
            total = total + v.astype(F32)
        mean = total * (1.0 / (S * S))
        total = jnp.zeros((2, P2, C), F32)
        for p in range(S * S):
            off = mid_ref[p].astype(F32) - mean
            total = total + off * off
        out_ref[...] = sum(group_stats(mean[i], total[i], float(S * S), 64 * i) for i in range(2))


def merge_kernel(s0, s1, s2, s3, out_ref):
    parts = jnp.stack([s0[...], s1[...], s2[...], s3[...]])
    whole = merge(parts, float(S * S * 16))
    out_ref[...] = jnp.broadcast_to(whole[None], out_ref.shape)


def attend_kernel(mid_ref, parts_ref, wq_ref, wk_ref, wv_ref, wo_ref, out_ref, norm):
    @pl.when(pl.program_id(0) == 0)
    def _():
        count = float(S * S * 16 * 4)
        whole = finish(merge(parts_ref[...], count), 32.0 * count)
        for i in range(2):
            for j in range(2):
                norm[i, j] = dot(whole, from_groups(64 * j + 32 * i), HI)

    pixels = mid_ref.shape[0]
    rows = pixels * T
    mid = mid_ref[...].astype(F32)
    flat = ((mid - norm[0][None]) * norm[1][None]).astype(BF).reshape(rows, C)
    query = dot(flat, wq_ref[...]).astype(BF)
    keys = dot(flat, wk_ref[...]).astype(BF)
    values = dot(flat, wv_ref[...]).astype(BF)
    n = 256
    row, column = iota((n, n), 0), iota((n, n), 1)
    frame = lambda v: 2 * (v % P2) + (v // P2) % 2
    seen = (row // T == column // T) & (frame(row) >= frame(column))
    parts = []
    for i in range(rows // n):
        at = slice(i * n, i * n + n)
        scores = lax.dot_general(
            query[at], keys[at], (((1,), (1,)), ((), ())), preferred_element_type=F32
        ) * (1.0 / (C**0.5))
        scores = jnp.where(seen, scores, -1e30)
        weights = jnp.exp(scores - jnp.max(scores, axis=1, keepdims=True))
        weights = (weights / jnp.sum(weights, axis=1, keepdims=True)).astype(BF)
        parts.append(dot(weights, values[at]).astype(BF))
    update = dot(jnp.concatenate(parts, axis=0), wo_ref[...])
    out = (mid.reshape(rows, C) + update).astype(BF)
    to = iota((rows, rows), 0)
    frame = to // pixels
    turn = (iota((rows, rows), 1) == (to % pixels) * T + (frame % 2) * P2 + frame // 2).astype(BF)
    out_ref[...] = dot(turn, out).astype(BF).reshape(T, pixels, C)


def neighbours(array, axis):
    n = lax.axis_size(axis)
    return [array] + [lax.ppermute(array, axis, [(i, (i + by) % n) for i in range(n)]) for by in range(1, n)]


def sum_over(array, size, stride):
    span = size * stride
    total = array
    for by in range(1, size):
        pairs = [(i, i - i % span + (i + by * stride) % span) for i in range(32)]
        total = total + lax.ppermute(array, "tm", pairs)
    return total


def local(latents, conv_weight, w_query, w_key, w_value, w_out):
    bands = lax.axis_size("rows")
    x = latents.reshape(16, 128, C)
    vmem = pl.BlockSpec(memory_space=pltpu.VMEM)
    smem = pl.BlockSpec(memory_space=pltpu.SMEM)
    whole = lambda *shape: pl.BlockSpec(shape, lambda i: (0,) * len(shape))
    exchange = functools.partial(lax.all_to_all, axis_name="tm", split_axis=1, concat_axis=0, tiled=True)
    place = jnp.stack([lax.axis_index("tm"), lax.axis_index("rows")]).astype(jnp.int32)

    messages = x.reshape(2, S, 16, S, C).transpose(2, 0, 1, 3, 4)
    patch = exchange(messages.reshape(1, 32, S * S, C)).reshape(T, S * S, C)

    stats = pl.pallas_call(
        latent_stats_kernel,
        out_shape=jax.ShapeDtypeStruct((8, 128), F32),
        in_specs=[vmem],
        out_specs=vmem,
        compiler_params=params(),
        cost_estimate=cost(2048 * C * 4, 2048 * C * 2),
        name="latent_stats",
    )(x.reshape(2048, C))
    stats = pl.pallas_call(
        place_kernel,
        out_shape=jax.ShapeDtypeStruct((T, 128), F32),
        in_specs=[smem] + [vmem] * 4,
        out_specs=vmem,
        compiler_params=params(),
        cost_estimate=cost(2**20, 2**16),
        name="place_stats",
    )(place, *neighbours(stats, "rows"))
    for size, stride in ((4, 2), (4, 8), (2, 1)):
        stats = sum_over(stats, size, stride)

    weights = pl.pallas_call(
        weights_kernel,
        grid=(3, 3),
        out_shape=jax.ShapeDtypeStruct((4, 3, 3, C, C), BF),
        in_specs=[pl.BlockSpec((3, 1, 1, C, C), lambda b, e: (0, b, e, 0, 0))],
        out_specs=pl.BlockSpec((4, 1, 1, C, C), lambda b, e: (0, b, e, 0, 0)),
        compiler_params=params(),
        cost_estimate=cost(9 * 4 * C * C, 9 * 7 * C * C * 2),
        name="weights",
    )(conv_weight)

    down = [(i, i + 1) for i in range(bands - 1)]
    top = lax.ppermute(x[15:16], "rows", down)
    bottom = lax.ppermute(x[0:1], "rows", [(j, i) for i, j in down])
    rim = pl.pallas_call(
        rim_kernel,
        grid=(8,),
        out_shape=jax.ShapeDtypeStruct((32, RIM, C), BF),
        in_specs=[whole(1, 128, C), whole(16, 128, C), whole(1, 128, C)],
        out_specs=pl.BlockSpec((4, RIM, C), lambda i: (i, 0, 0)),
        compiler_params=params(),
        cost_estimate=cost(32 * RIM * 320 * C * 2, 4 * 2**20),
        name="rim",
    )(top, x, bottom)
    rim, patch = lax.optimization_barrier((rim, patch))
    rim = exchange(rim[None]).reshape(T, RIM, C)

    frames = jax.ShapeDtypeStruct((S * S, 2, P2, C), BF)
    y, turned_latents = pl.pallas_call(
        conv_kernel,
        grid=(4,),
        out_shape=(jax.ShapeDtypeStruct((S * S, 2, P2, C), F32), frames),
        in_specs=[
            whole(T, S * S, C),
            whole(T, 128),
            pl.BlockSpec((1, 3, 3, C, C), lambda i: (i, 0, 0, 0, 0)),
        ],
        out_specs=(whole(S * S, 2, P2, C), whole(S * S, 2, P2, C)),
        scratch_shapes=[pltpu.VMEM((4, W, S, P2, 3 * C), BF), pltpu.VMEM((2, 2, P2, C), F32)],
        compiler_params=params(),
        cost_estimate=cost(1024 * 36 * C * C * 2, 28 * 2**20),
        name="conv",
    )(patch, stats, weights)
    mid, stats = pl.pallas_call(
        border_kernel,
        grid=(4,),
        out_shape=(frames, jax.ShapeDtypeStruct((P2, 128), F32)),
        in_specs=[
            smem,
            whole(T, RIM, C),
            whole(T, 128),
            whole(S * S, 2, P2, C),
            whole(S * S, 2, P2, C),
            pl.BlockSpec((1, 3, 3, C, C), lambda i: (i, 0, 0, 0, 0)),
        ],
        out_specs=(whole(S * S, 2, P2, C), whole(P2, 128)),
        scratch_shapes=[
            pltpu.VMEM((4, RIM, P2, C), BF),
            pltpu.VMEM((4, 2, S, P2, C), F32),
            pltpu.VMEM((2, 2, P2, C), F32),
        ],
        compiler_params=params(),
        cost_estimate=cost(16 * 128 * 3 * C * C * 2, 28 * 2**20),
        name="border",
    )(place, rim, stats, y, turned_latents, weights)
    parts = pl.pallas_call(
        merge_kernel,
        out_shape=jax.ShapeDtypeStruct((32, P2, 128), F32),
        in_specs=[vmem] * 4,
        out_specs=vmem,
        compiler_params=params(),
        name="merge",
    )(*neighbours(stats, "rows"))
    parts = exchange(parts[None]).reshape(32, P2, 128)
    pixels = 16
    out = pl.pallas_call(
        attend_kernel,
        grid=(S * S // pixels,),
        out_shape=jax.ShapeDtypeStruct((T, S * S, C), BF),
        in_specs=[pl.BlockSpec((pixels, 2, P2, C), lambda i: (i, 0, 0, 0)), whole(32, P2, 128)] + [whole(C, C)] * 4,
        out_specs=pl.BlockSpec((T, pixels, C), lambda i: (0, i, 0)),
        scratch_shapes=[pltpu.VMEM((2, 2, P2, C), F32)],
        compiler_params=params(),
        cost_estimate=cost(2048 * C * C * 2 * 6, 8 * 2**20),
        name="attend",
    )(mid, parts, w_query, w_key, w_value, w_out)
    back = lax.all_to_all(out[:, None], "tm", split_axis=0, concat_axis=1, tiled=True)
    back = back.reshape(16, 2, S, S, C).transpose(1, 2, 0, 3, 4)
    return back.reshape(1, 16, 128, C)


def solution(mesh):
    in_specs = (P("tm", "rows", None, None), P(), P(), P(), P(), P())
    out_specs = P("tm", "rows", None, None)
    return jax.shard_map(local, mesh=mesh, in_specs=in_specs, out_specs=out_specs, check_vma=False)
```

time: 201 us -> 201 us (level)
  waiting for transfers between devices: 47.1 us -> 11.7 us
  starting transfers between devices: 24.8 us -> 40.1 us
  Pallas kernels: 72.9 us -> 87.2 us
  local copies, waits for them, and re-layouts: 5.52 us -> 9.28 us
    all_to_all x1 -> x2, waiting for transfers between devices: 42.1 us -> 0.01 us  [the longest x1 0.01 us: local(): rim = exchange(rim[None]).reshape(T, RIM, C)]
    pallas_call x3 -> x6, Pallas kernels: 56.4 us -> 70.6 us  [the longest x1 29 us: local(): pl.pallas_call(conv_kernel, grid=(4,), out_shape=(jax.ShapeDtypeStruct((S...]
    ppermute x0 -> x7, starting transfers between devices: none -> 12.2 us  [sum_over(): total = total + lax.ppermute(array, 'tm', pairs)]
    ppermute x0 -> x7, waiting for transfers between devices: none -> 5.39 us  [sum_over(): total = total + lax.ppermute(array, 'tm', pairs)]
    all_to_all x1 -> x2, starting transfers between devices: 9.74 us -> 13.7 us  [the longest x1 8.59 us: local(): patch = exchange(messages.reshape(1, 32, S * S, C)).reshape(T, S * S, C)]
    another operation x0 -> x1, local copies, waits for them, and re-layouts: none -> 3.19 us  [local(): messages = x.reshape(2, S, 16, S, C).transpose(2, 0, 1, 3, 4)]
  transfers between devices with their start and end apart: 9 -> 17, of which waited for: 6 -> 5; matrix products, arithmetic and copies ran while one was open for 0% -> 1% of each run, Pallas kernels for 2% -> 28%
where the time goes in v2:
time: 201 us; the launch traced here: 200 us
  Pallas kernels  87.2 us (43%)
  blocking collectives  50 us (25%)
  starting transfers between devices  40.1 us (20%)
  waiting for transfers between devices  11.7 us (6%)
  local copies, waits for them, and re-layouts  9.28 us (5%)
    all_to_all x1, blocking collectives, local(): lax.all_to_all(out[:, None], 'tm', split_axis=0, concat_axis=1, tiled=True)  32.1 us
    pallas_call x1, Pallas kernels, local(): pl.pallas_call(conv_kernel, grid=(4,), out_shape=(jax.ShapeDtypeStruct((S...  29 us
    all_to_all x1, blocking collectives, local(): parts = exchange(parts[None]).reshape(32, P2, 128)  17.9 us
    pallas_call x1, Pallas kernels, local(): pl.pallas_call(border_kernel, grid=(4,), out_shape=(frames, jax.ShapeDtyp...  17.2 us
    pallas_call x1, Pallas kernels, local(): pl.pallas_call(weights_kernel, grid=(3, 3), out_shape=jax.ShapeDtypeStruc...  15.4 us
    pallas_call x1, Pallas kernels, local(): pl.pallas_call(attend_kernel, grid=(S * S // pixels,), out_shape=jax.Shap...  12.6 us
    ppermute x7, starting transfers between devices, sum_over(): total = total + lax.ppermute(array, 'tm', pairs)  12.2 us
    ppermute x6, starting transfers between devices, neighbours(): lax.ppermute(array, axis, [(i, (i + by) % n) for i in range(n)])  8.83 us
  transfers between devices with their start and end apart: 17, of which 5 were waited for; matrix products, arithmetic and copies ran while one was open for 1% of the time, Pallas kernels for 28%

profile of v2, /device:TPU:1, one launch (start us, length us, event | category | flops | bytes accessed | tf_op | source)
XLA Modules:
  0.0 200.4 jit_solution(17226043043786387885)
XLA Ops:
  0.0 3.2 %copy.9 = bf16[2,8,16,8,512]{4,3,1,0,2:T(8,128)(2,1)} copy(bf16[2,8,16,8,512]{4,3,2,1,0:T(8,128)(2,1)} %bitcast.28) | data formatting | bytes 4194304 | tf_op jit(solution)/shard_map/reshape;reshape | solution.py:321
  3.2 8.6 %all-to-all-start = ((bf16[1,32,64,512]{3,2,0,1:T(8,128)(2,1)}), bf16[1,32,64,512]{3,2,0,1:T(8,128)(2,1)S(1)}, u32[]{:S(2)}, u32[]{:S(2)}) async-start(bf16[1,32,64,512]{3,2,0,1:T(8,128)(2,1)} %bitcast.7), calls=%async_computation | async-start | bytes 4194304 | tf_op jit(solution)/shard_map/all_to_all | solution.py:322
  11.8 4.0 %latent_stats.1.s0 = f32[8,128]{1,0:T(8,128)} custom-call(bf16[2048,512]{1,0:T(8,128)(2,1)} %bitcast.29), custom_call_target="tpu_custom_call" | custom-call | flops 4194304 | bytes 2097152 | tf_op jit(solution)/shard_map/latent_stats/pallas_call | solution.py:324
  15.8 3.8 %collective-permute-start.4 = (f32[8,128]{1,0:T(8,128)}, f32[8,128]{1,0:T(8,128)S(1)}, u32[]{:S(2)}, u32[]{:S(2)}) collective-permute-start(f32[8,128]{1,0:T(8,128)} %latent_stats.1.s0), channel_id=1, source_target_pairs={{0,3},{1,0},{2,1},{3,2},{4,7},{5,4},{6,5},{7,6},{8,11},{9,8},{10,9... | collective-permute-start | bytes 12296 | tf_op jit(solution)/shard_map/ppermute | solution.py:300
  19.5 0.0 collective-permute-start.3
  19.5 0.7 collective-permute-start.2
  20.2 0.6 pad_add_fusion.place_ref
  20.8 0.0 collective-permute-done.4.s3
  20.8 3.2 %collective-permute-done.3.s2 = f32[8,128]{1,0:T(8,128)S(1)} collective-permute-done((f32[8,128]{1,0:T(8,128)}, f32[8,128]{1,0:T(8,128)S(1)}, u32[]{:S(2)}, u32[]{:S(2)}) %collective-permute-start.3) | collective-permute-done | bytes 4128 | tf_op jit(solution)/shard_map/ppermute | solution.py:300
  24.0 0.0 collective-permute-done.2.s1
  24.0 0.6 copy-done.8
  24.6 0.6 copy-done.9
  25.2 1.5 place_stats.1
  26.7 2.6 %collective-permute-start.7 = (f32[32,128]{1,0:T(8,128)}, f32[32,128]{1,0:T(8,128)S(1)}, u32[]{:S(2)}, u32[]{:S(2)}) collective-permute-start(f32[32,128]{1,0:T(8,128)} %place_stats.1), channel_id=1, source_target_pairs={{0,24},{4,28},{8,0},{12,4},{16,8},{20,12},{24,16},{28,20},{32,56},... | collective-permute-start | bytes 49160 | tf_op jit(solution)/shard_map/ppermute | solution.py:308
  29.3 0.6 collective-permute-start.6
  29.8 0.6 collective-permute-start.5
  30.4 4.2 %collective-permute-done.7 = f32[32,128]{1,0:T(8,128)S(1)} collective-permute-done((f32[32,128]{1,0:T(8,128)}, f32[32,128]{1,0:T(8,128)S(1)}, u32[]{:S(2)}, u32[]{:S(2)}) %collective-permute-start.7) | collective-permute-done | bytes 16416 | tf_op jit(solution)/shard_map/ppermute | solution.py:308
  34.7 1.1 collective-permute-done.5
  35.8 0.7 add_add_fusion.1
  36.5 5.0 %collective-permute-start.10 = (f32[32,128]{1,0:T(8,128)S(1)}, f32[32,128]{1,0:T(8,128)S(1)}, u32[]{:S(2)}, u32[]{:S(2)}) collective-permute-start(f32[32,128]{1,0:T(8,128)S(1)} %add_add_fusion.1), channel_id=1, source_target_pairs={{0,96},{4,100},{8,104},{12,108},{16,112},{20,116},{24,120},{28,124... | collective-permute-start | bytes 49160 | tf_op jit(solution)/shard_map/ppermute | solution.py:308
  41.6 1.1 collective-permute-start.9
  42.6 0.5 collective-permute-start.8
  43.2 1.0 slice_bitcast_fusion
  44.1 1.3 collective-permute-start.1
  45.4 4.2 %collective-permute-start = (bf16[1,128,512]{2,1,0:T(8,128)(2,1)S(1)}, bf16[1,128,512]{2,1,0:T(8,128)(2,1)S(1)}, u32[]{:S(2)}, u32[]{:S(2)}) collective-permute-start(bf16[1,128,512]{2,1,0:T(8,128)(2,1)S(1)} %get-tuple-element.18), channel_id=1, source_target_pairs={{0,1},{1,2},{2,3},{4,5},{5,6},{6,7},{8,9},{9,10},{10,11},{12,13},{... | collective-permute-start | bytes 393224 | tf_op jit(solution)/shard_map/ppermute | solution.py:357
  49.6 0.0 collective-permute-done.10
  49.7 0.0 collective-permute-done.8
  49.7 1.8 collective-permute-start.11
  51.5 15.4 %weights.1.w_ref = bf16[4,3,3,512,512]{4,3,2,1,0:T(8,128)(2,1)} custom-call(bf16[3,3,3,512,512]{4,3,2,1,0:T(8,128)(2,1)} %w_ref.1), custom_call_target="tpu_custom_call" | custom-call | flops 9437184 | bytes 33030144 | tf_op jit(solution)/shard_map/weights/pallas_call | solution.py:345
  66.8 0.6 add.27.stats_ref
  67.5 0.6 copy-done.2
  68.1 0.0 copy-done.3
  68.1 6.1 %rim.1 = bf16[32,40,512]{2,1,0:T(8,128)(2,1)} custom-call(bf16[1,128,512]{2,1,0:T(8,128)(2,1)} %copy-done.3, bf16[16,128,512]{2,1,0:T(8,128)(2,1)} %bitcast.30, bf16[1,128,512]{2,1,0:T(8,128)(2,1)} %copy-done.2), custom_call_target="tpu_custom_call" | custom-call | flops 419430400 | bytes 4194304 | tf_op jit(solution)/shard_map/rim/pallas_call | solution.py:359
  74.2 5.1 %all-to-all-start.1 = ((bf16[1,32,40,512]{3,2,0,1:T(8,128)(2,1)}), bf16[1,32,40,512]{3,2,0,1:T(8,128)(2,1)S(1)}, u32[]{:S(2)}, u32[]{:S(2)}) async-start(bf16[1,32,40,512]{3,2,0,1:T(8,128)(2,1)} %bitcast.33), calls=%async_computation.1 | async-start | bytes 2621440 | tf_op jit(solution)/shard_map/all_to_all | solution.py:370
  79.3 29.0 %conv.1 = (f32[64,2,16,512]{3,2,1,0:T(8,128)}, bf16[64,2,16,512]{3,2,1,0:T(8,128)(2,1)}) custom-call(bf16[32,64,512]{2,1,0:T(8,128)(2,1)} %bitcast.34, f32[32,128]{1,0:T(8,128)} %add.27.stats_ref, bf16[4,3,3,512,512]{4,3,2,1,0:T(8,128)(2,1)} %weights.1.w_ref), custom_call_target="tpu_custom_call" | custom-call | flops 19327352832 | bytes 29360128 | tf_op jit(solution)/shard_map/conv/pallas_call | solution.py:373
  108.3 1.1 copy-done
  109.4 17.2 %border.1 = (bf16[64,2,16,512]{3,2,1,0:T(8,128)(2,1)}, f32[16,128]{1,0:T(8,128)}) custom-call(s32[2]{0:T(128)} %pad_add_fusion.place_ref, bf16[32,40,512]{2,1,0:T(8,128)(2,1)} %bitcast.32, f32[32,128]{1,0:T(8,128)} %add.27.stats_ref, f32[64,2,16,512]{3,2,1,0:T(8,128)} %get-tuple-element.13.y_ref, bf16[64,2,16,512]{3,2,1,0:T(8,128)(2,1)} %get-tuple-element.14.latent_ref, ...), custom_call_target="tpu_custom_call" | custom-call | flops 3221225472 | bytes 29360128 | tf_op jit(solution)/shard_map/border/pallas_call | solution.py:388
  126.6 1.4 collective-permute-start.14
  128.0 2.1 %collective-permute-start.13 = (f32[16,128]{1,0:T(8,128)}, f32[16,128]{1,0:T(8,128)S(1)}, u32[]{:S(2)}, u32[]{:S(2)}) collective-permute-start(f32[16,128]{1,0:T(8,128)} %get-tuple-element.16.s0), channel_id=1, source_target_pairs={{0,2},{1,3},{2,0},{3,1},{4,6},{5,7},{6,4},{7,5},{8,10},{9,11},{10,... | collective-permute-start | bytes 24584 | tf_op jit(solution)/shard_map/ppermute | solution.py:300
  130.2 0.8 collective-permute-start.12
  131.0 1.3 collective-permute-done.13.s2
  132.2 1.8 collective-permute-done.12.s1
  134.1 0.6 copy-done.6
  134.7 1.5 merge.1
  136.2 17.9 %all_to_all.16 = f32[1,32,16,128]{3,2,0,1:T(8,128)} all-to-all(f32[1,32,16,128]{3,2,0,1:T(8,128)} %bitcast.36), channel_id=1, replica_groups=mesh['tm'=32,'rows'=4] {'tm'}, dimensions={1} | all-to-all | bytes 524288 | tf_op jit(solution)/shard_map/all_to_all | solution.py:418
  154.2 12.6 %attend.1 = bf16[32,64,512]{2,1,0:T(8,128)(2,1)} custom-call(bf16[64,2,16,512]{3,2,1,0:T(8,128)(2,1)} %get-tuple-element.15.mid_ref, f32[32,16,128]{2,1,0:T(8,128)} %bitcast.37, bf16[512,512]{1,0:T(8,128)(2,1)} %wq_ref.1, bf16[512,512]{1,0:T(8,128)(2,1)} %wk_ref.1, bf16[512,512]{1,0:T(8,128)(2,1)} %wv_ref.1, bf16[512,512]{1,0:T(8,128)(2,1)} %wo_ref.1), custom_call_target="tpu_custom_call" | custom-call | flops 6442450944 | bytes 8388608 | tf_op jit(solution)/shard_map/attend/pallas_call | solution.py:420
  166.8 32.1 %all_to_all.17 = bf16[32,1,64,512]{3,2,1,0:T(8,128)(2,1)S(1)} all-to-all(bf16[32,1,64,512]{3,2,1,0:T(8,128)(2,1)} %bitcast.35), channel_id=1, replica_groups=mesh['tm'=32,'rows'=4] {'tm'}, dimensions={0} | all-to-all | bytes 4194304 | tf_op jit(solution)/shard_map/all_to_all | solution.py:431
  198.9 1.5 copy.13
  (23 shorter events, 0.1 us)
Async XLA Ops:
  3.2 71.0 %all-to-all-start = ((bf16[1,32,64,512]{3,2,0,1:T(8,128)(2,1)}), bf16[1,32,64,512]{3,2,0,1:T(8,128)(2,1)S(1)}, u32[]{:S(2)}, u32[]{:S(2)}) async-start(bf16[1,32,64,512]{3,2,0,1:T(8,128)(2,1)} %bitcast.7), calls=%async_computation | async-start | bytes 4194304 | tf_op jit(solution)/shard_map/all_to_all | solution.py:322
  15.8 5.0 %collective-permute-start.4 = (f32[8,128]{1,0:T(8,128)}, f32[8,128]{1,0:T(8,128)S(1)}, u32[]{:S(2)}, u32[]{:S(2)}) collective-permute-start(f32[8,128]{1,0:T(8,128)} %latent_stats.1.s0), channel_id=1, source_target_pairs={{0,3},{1,0},{2,1},{3,2},{4,7},{5,4},{6,5},{7,6},{8,11},{9,8},{10,9... | collective-permute-start | bytes 12296 | tf_op jit(solution)/shard_map/ppermute | solution.py:300
  19.5 4.5 %collective-permute-start.3 = (f32[8,128]{1,0:T(8,128)}, f32[8,128]{1,0:T(8,128)S(1)}, u32[]{:S(2)}, u32[]{:S(2)}) collective-permute-start(f32[8,128]{1,0:T(8,128)} %latent_stats.1.s0), channel_id=1, source_target_pairs={{0,2},{1,3},{2,0},{3,1},{4,6},{5,7},{6,4},{7,5},{8,10},{9,11},{10,... | collective-permute-start | bytes 12296 | tf_op jit(solution)/shard_map/ppermute | solution.py:300
  19.5 4.5 %collective-permute-start.2 = (f32[8,128]{1,0:T(8,128)}, f32[8,128]{1,0:T(8,128)S(1)}, u32[]{:S(2)}, u32[]{:S(2)}) collective-permute-start(f32[8,128]{1,0:T(8,128)} %latent_stats.1.s0), channel_id=1, source_target_pairs={{0,1},{1,2},{2,3},{3,0},{4,5},{5,6},{6,7},{7,4},{8,9},{9,10},{10,1... | collective-permute-start | bytes 12296 | tf_op jit(solution)/shard_map/ppermute | solution.py:300
  20.8 3.2 %copy-start.7 = (f32[8,128]{1,0:T(8,128)}, f32[8,128]{1,0:T(8,128)S(1)}, u32[]{:S(2)}) copy-start(f32[8,128]{1,0:T(8,128)S(1)} %collective-permute-done.4.s3) | copy-start | bytes 12292
  24.0 0.6 copy-start.8
  24.6 0.6 copy-start.9
  26.7 8.0 %collective-permute-start.7 = (f32[32,128]{1,0:T(8,128)}, f32[32,128]{1,0:T(8,128)S(1)}, u32[]{:S(2)}, u32[]{:S(2)}) collective-permute-start(f32[32,128]{1,0:T(8,128)} %place_stats.1), channel_id=1, source_target_pairs={{0,24},{4,28},{8,0},{12,4},{16,8},{20,12},{24,16},{28,20},{32,56},... | collective-permute-start | bytes 49160 | tf_op jit(solution)/shard_map/ppermute | solution.py:308
  29.3 5.4 %collective-permute-start.6 = (f32[32,128]{1,0:T(8,128)}, f32[32,128]{1,0:T(8,128)S(1)}, u32[]{:S(2)}, u32[]{:S(2)}) collective-permute-start(f32[32,128]{1,0:T(8,128)} %place_stats.1), channel_id=1, source_target_pairs={{0,16},{4,20},{8,24},{12,28},{16,0},{20,4},{24,8},{28,12},{32,48},... | collective-permute-start | bytes 49160 | tf_op jit(solution)/shard_map/ppermute | solution.py:308
  29.8 6.0 %collective-permute-start.5 = (f32[32,128]{1,0:T(8,128)}, f32[32,128]{1,0:T(8,128)S(1)}, u32[]{:S(2)}, u32[]{:S(2)}) collective-permute-start(f32[32,128]{1,0:T(8,128)} %place_stats.1), channel_id=1, source_target_pairs={{0,8},{4,12},{8,16},{12,20},{16,24},{20,28},{24,0},{28,4},{32,40},... | collective-permute-start | bytes 49160 | tf_op jit(solution)/shard_map/ppermute | solution.py:308
  36.5 13.1 %collective-permute-start.10 = (f32[32,128]{1,0:T(8,128)S(1)}, f32[32,128]{1,0:T(8,128)S(1)}, u32[]{:S(2)}, u32[]{:S(2)}) collective-permute-start(f32[32,128]{1,0:T(8,128)S(1)} %add_add_fusion.1), channel_id=1, source_target_pairs={{0,96},{4,100},{8,104},{12,108},{16,112},{20,116},{24,120},{28,124... | collective-permute-start | bytes 49160 | tf_op jit(solution)/shard_map/ppermute | solution.py:308
  41.6 8.1 %collective-permute-start.9 = (f32[32,128]{1,0:T(8,128)S(1)}, f32[32,128]{1,0:T(8,128)S(1)}, u32[]{:S(2)}, u32[]{:S(2)}) collective-permute-start(f32[32,128]{1,0:T(8,128)S(1)} %add_add_fusion.1), channel_id=1, source_target_pairs={{0,64},{4,68},{8,72},{12,76},{16,80},{20,84},{24,88},{28,92},{32,9... | collective-permute-start | bytes 49160 | tf_op jit(solution)/shard_map/ppermute | solution.py:308
  42.6 7.0 %collective-permute-start.8 = (f32[32,128]{1,0:T(8,128)S(1)}, f32[32,128]{1,0:T(8,128)S(1)}, u32[]{:S(2)}, u32[]{:S(2)}) collective-permute-start(f32[32,128]{1,0:T(8,128)S(1)} %add_add_fusion.1), channel_id=1, source_target_pairs={{0,32},{4,36},{8,40},{12,44},{16,48},{20,52},{24,56},{28,60},{32,6... | collective-permute-start | bytes 49160 | tf_op jit(solution)/shard_map/ppermute | solution.py:308
  44.1 23.3 %collective-permute-start.1 = (bf16[1,128,512]{2,1,0:T(8,128)(2,1)S(1)}, bf16[1,128,512]{2,1,0:T(8,128)(2,1)S(1)}, u32[]{:S(2)}, u32[]{:S(2)}) collective-permute-start(bf16[1,128,512]{2,1,0:T(8,128)(2,1)S(1)} %get-tuple-element.17), channel_id=1, source_target_pairs={{1,0},{2,1},{3,2},{5,4},{6,5},{7,6},{9,8},{10,9},{11,10},{13,12},{... | collective-permute-start | bytes 393224 | tf_op jit(solution)/shard_map/ppermute | solution.py:358
  45.4 22.0 %collective-permute-start = (bf16[1,128,512]{2,1,0:T(8,128)(2,1)S(1)}, bf16[1,128,512]{2,1,0:T(8,128)(2,1)S(1)}, u32[]{:S(2)}, u32[]{:S(2)}) collective-permute-start(bf16[1,128,512]{2,1,0:T(8,128)(2,1)S(1)} %get-tuple-element.18), channel_id=1, source_target_pairs={{0,1},{1,2},{2,3},{4,5},{5,6},{6,7},{8,9},{9,10},{10,11},{12,13},{... | collective-permute-start | bytes 393224 | tf_op jit(solution)/shard_map/ppermute | solution.py:357
  49.7 17.2 %collective-permute-start.11 = (f32[32,128]{1,0:T(8,128)S(1)}, f32[32,128]{1,0:T(8,128)S(1)}, u32[]{:S(2)}, u32[]{:S(2)}) collective-permute-start(f32[32,128]{1,0:T(8,128)S(1)} %add_add_fusion), channel_id=1, source_target_pairs={{0,4},{4,0},{8,12},{12,8},{16,20},{20,16},{24,28},{28,24},{32,36},... | collective-permute-start | bytes 49160 | tf_op jit(solution)/shard_map/ppermute | solution.py:308
  67.5 0.7 copy-start.2
  67.5 0.7 copy-start.3
  74.2 5.1 %copy-start.1 = (bf16[1,32,64,512]{3,2,0,1:T(8,128)(2,1)}, bf16[1,32,64,512]{3,2,0,1:T(8,128)(2,1)S(1)}, u32[]{:S(2)}) copy-start(bf16[1,32,64,512]{3,2,0,1:T(8,128)(2,1)S(1)} %all-to-all-done) | copy-start | bytes 6291460
  74.2 34.1 %all-to-all-start.1 = ((bf16[1,32,40,512]{3,2,0,1:T(8,128)(2,1)}), bf16[1,32,40,512]{3,2,0,1:T(8,128)(2,1)S(1)}, u32[]{:S(2)}, u32[]{:S(2)}) async-start(bf16[1,32,40,512]{3,2,0,1:T(8,128)(2,1)} %bitcast.33), calls=%async_computation.1 | async-start | bytes 2621440 | tf_op jit(solution)/shard_map/all_to_all | solution.py:370
  108.3 1.1 copy-start
  126.6 4.4 %collective-permute-start.14 = (f32[16,128]{1,0:T(8,128)}, f32[16,128]{1,0:T(8,128)S(1)}, u32[]{:S(2)}, u32[]{:S(2)}) collective-permute-start(f32[16,128]{1,0:T(8,128)} %get-tuple-element.16.s0), channel_id=1, source_target_pairs={{0,3},{1,0},{2,1},{3,2},{4,7},{5,4},{6,5},{7,6},{8,11},{9,8},{10,9... | collective-permute-start | bytes 24584 | tf_op jit(solution)/shard_map/ppermute | solution.py:300
  128.0 4.2 %collective-permute-start.13 = (f32[16,128]{1,0:T(8,128)}, f32[16,128]{1,0:T(8,128)S(1)}, u32[]{:S(2)}, u32[]{:S(2)}) collective-permute-start(f32[16,128]{1,0:T(8,128)} %get-tuple-element.16.s0), channel_id=1, source_target_pairs={{0,2},{1,3},{2,0},{3,1},{4,6},{5,7},{6,4},{7,5},{8,10},{9,11},{10,... | collective-permute-start | bytes 24584 | tf_op jit(solution)/shard_map/ppermute | solution.py:300
  130.2 3.9 %collective-permute-start.12 = (f32[16,128]{1,0:T(8,128)}, f32[16,128]{1,0:T(8,128)S(1)}, u32[]{:S(2)}, u32[]{:S(2)}) collective-permute-start(f32[16,128]{1,0:T(8,128)} %get-tuple-element.16.s0), channel_id=1, source_target_pairs={{0,1},{1,2},{2,3},{3,0},{4,5},{5,6},{6,7},{7,4},{8,9},{9,10},{10,1... | collective-permute-start | bytes 24584 | tf_op jit(solution)/shard_map/ppermute | solution.py:300
  131.0 3.1 %copy-start.4 = (f32[16,128]{1,0:T(8,128)}, f32[16,128]{1,0:T(8,128)S(1)}, u32[]{:S(2)}) copy-start(f32[16,128]{1,0:T(8,128)S(1)} %collective-permute-done.14.s3) | copy-start | bytes 24580
  132.2 1.9 copy-start.5
  134.1 0.6 copy-start.6

commit v3 on v2

v3 whole, which is shorter than its diff:
```python
import jax
import jax.numpy as jnp
from jax import lax
from jax.experimental import pallas as pl
from jax.experimental.pallas import tpu as pltpu
from jax.sharding import Mesh
from jax.sharding import PartitionSpec as P

GROUPS = 32
T = 32
C = 512
S = 8
W = S + 2
P2 = T // 2
MSG = 104
TM = ("x", "y", "core")
EPS = 1e-6
BF, F32 = jnp.bfloat16, jnp.float32
HI = lax.Precision.HIGHEST


def iota(shape, dim):
    return lax.broadcasted_iota(jnp.int32, shape, dim)


def dot(a, b, precision=None):
    return jnp.dot(a, b, preferred_element_type=F32, precision=precision)


def params():
    return pltpu.CompilerParams(vmem_limit_bytes=56 * 2**20)


def cost(flops, nbytes):
    return pl.CostEstimate(flops=flops, bytes_accessed=nbytes, transcendentals=0)


def to_groups(lane):
    return (iota((C, 128), 0) // 16 + lane == iota((C, 128), 1)).astype(F32)


def from_groups(lane, dtype=F32):
    return (iota((128, C), 1) // 16 + lane == iota((128, C), 0)).astype(dtype)


def group_stats(mean, m2, count, lane):
    group_mean = dot(mean, to_groups(lane), HI) * (1.0 / 16.0)
    off = mean - dot(group_mean, from_groups(lane), HI)
    return group_mean + dot(m2 + count * (off * off), to_groups(lane + 32), HI)


def merge(parts, count):
    n = parts.shape[0]
    total = jnp.sum(parts, axis=0)
    mean = total * (1.0 / n)
    off = parts - mean[None]
    between = pltpu.roll(jnp.sum(off * off, axis=0), 32, 1)
    is_mean = (iota(total.shape, 1) // 32) % 2 == 0
    return jnp.where(is_mean, mean, total + count * between)


def split_terms(v):
    high = v.astype(BF).astype(F32)
    middle = (v - high).astype(BF).astype(F32)
    return jnp.concatenate([high, middle, v - high - middle, jnp.zeros_like(v)], axis=1)


def join_terms(v):
    return sum(v[:, 128 * i : 128 * i + 128].astype(F32) for i in range(3))


def latent_stats_kernel(x_ref, up_ref, down_ref, out_ref):
    n = x_ref.shape[0]
    step = 256

    def add(i, total):
        rows = x_ref[pl.ds(pl.multiple_of(i * step, step), step), :].astype(F32)
        return total + jnp.sum(rows.reshape(step // 8, 8, C), axis=0)

    total = lax.fori_loop(0, n // step, add, jnp.zeros((8, C), F32))
    mean = jnp.sum(total, axis=0, keepdims=True) * (1.0 / n)

    def add_square(i, total):
        rows = x_ref[pl.ds(pl.multiple_of(i * step, step), step), :].astype(F32) - mean
        return total + jnp.sum((rows * rows).reshape(step // 8, 8, C), axis=0)

    total = lax.fori_loop(0, n // step, add_square, jnp.zeros((8, C), F32))
    m2 = jnp.sum(total, axis=0, keepdims=True)
    wide = lambda v: jnp.broadcast_to(v, (8, C))
    row = split_terms(group_stats(wide(mean), wide(m2), float(n), 0))
    row = jnp.concatenate([row, jnp.zeros_like(row)], axis=0).astype(BF)
    out_ref[...] = row
    up_ref[:128, :] = x_ref[n - 128 :, :]
    down_ref[:128, :] = x_ref[:128, :]
    up_ref[128:, :] = row
    down_ref[128:, :] = row


def finish(whole, count):
    is_mean = (iota(whole.shape, 1) // 32) % 2 == 0
    return jnp.where(is_mean, whole, lax.rsqrt(whole * (1.0 / count) + EPS))


def message_kernel(x_ref, up_ref, down_ref, own_ref, far_ref, out_ref, wide, sides):
    step = pl.program_id(0)

    @pl.when(step == 0)
    def _():
        n = 2048.0 * 16.0
        parts = [own_ref[...], far_ref[...], up_ref[128:, :], down_ref[128:, :]]
        whole = merge(jnp.stack([join_terms(v)[:8] for v in parts]), n)
        row = split_terms(jnp.where(iota(whole.shape, 1) < 64, finish(whole, 4.0 * n), 0.0))
        for q in range(4):
            lanes = slice(128 * q, 128 * q + 128)
            wide[q, 0] = up_ref[:128, lanes].astype(F32)
            wide[q, 17] = down_ref[:128, lanes].astype(F32)
            wide[q, 1:17] = x_ref[:, :, lanes].astype(F32)
            for half in range(2):
                sides[q, half] = jnp.zeros((16 * 24, 128), F32)
                sides[q, half, pl.ds(20, 16, stride=24), :] = jnp.broadcast_to(row[:1, lanes], (16, 128))
                for r in range(W):
                    left = wide[q, S * half + r, pl.ds(7, 15, stride=8), :]
                    right = wide[q, S * half + r, pl.ds(8, 15, stride=8), :]
                    sides[q, half, pl.ds(24 + r, 15, stride=24), :] = left
                    sides[q, half, pl.ds(W + r, 15, stride=24), :] = right

    for k in range(4):
        for half in range(2):
            cb = 4 * step + k
            cols = pl.ds(pl.multiple_of(8 * cb, 8), 8)
            rows = pl.ds(pl.multiple_of(24 * cb, 8), 24)
            for q in range(4):
                main = wide[q, S * half : S * half + W, cols, :].reshape(W * S, 128)
                side = sides[q, half, rows, :]
                message = jnp.concatenate([main, side], axis=0).astype(BF)
                out_ref[2 * k + half, :, 128 * q : 128 * q + 128] = message


def weights_kernel(w_ref, out_ref):
    g = [w_ref[i, 0, 0].astype(F32) for i in range(3)]
    ends = (g[0] + g[2]) * 0.5
    out_ref[0, 0, 0] = w_ref[0, 0, 0]
    out_ref[1, 0, 0] = (ends + g[1] * 0.5).astype(BF)
    out_ref[2, 0, 0] = (ends - g[1] * 0.5).astype(BF)
    out_ref[3, 0, 0] = w_ref[2, 0, 0]


def turned(in_ref, first, pixels):
    rows = pixels * T
    to, at = iota((rows, rows), 0), iota((rows, rows), 1)
    frame = 2 * (to % P2) + (to // P2) % 2
    turn = (at == frame * pixels + to // T).astype(BF)
    values = in_ref[:, first : first + pixels, :].reshape(rows, C)
    return dot(turn, values).reshape(pixels, 2, P2, C)


def activate(values, norm):
    u = (values - norm[0][None]) * norm[1][None]
    return (u / (1.0 + jnp.exp(-u))).astype(BF).astype(F32)


def time_terms(act):
    pixels = act.shape[0]
    even, odd = act[:, 0], act[:, 1]
    start = iota((pixels * P2, C), 0) % P2 == 0

    def before(v):
        v = pltpu.roll(v.reshape(pixels * P2, C), 1, 0)
        return jnp.where(start, 0.0, v).reshape(pixels, P2, C)

    even1, odd1 = before(even), before(odd)
    return [v.astype(BF) for v in (even1 - even, odd1 + even, even - odd1, odd1 - odd)]


def signs(j):
    return jnp.where(j == 3, 0.0, 1.0), jnp.where(j == 0, 0.0, jnp.where(j == 1, 1.0, -1.0))


def conv_kernel(place_ref, in_ref, w_ref, mid_ref, stats_ref, terms, latent, y_ref, norm):
    j = pl.program_id(0)

    @pl.when(j == 0)
    def _():
        block, z = place_ref[0], place_ref[1]
        half, column = block % 2, block // 2
        above = (half == 0) & (z == 0)
        below = (half == 1) & (z == 3)
        tail = in_ref[:, 96:MSG, :].reshape(T * 8, C)
        row = iota((T, T * 8), 0)
        row = 2 * (row % P2) + row // P2
        pieces = dot((iota((T, T * 8), 1) == row * 8 + 4).astype(BF), tail).astype(BF)
        for i in range(2):
            norm[i] = sum(
                dot(pieces[:, 128 * k : 128 * k + 128], from_groups(32 * i, BF)) for k in range(3)
            ).reshape(2, P2, C)

        for k in range(W // 2):
            values = turned(in_ref, 16 * k, 16)
            act = activate(values, norm)
            if k == 0:
                act = jnp.where(above & (iota(act.shape, 0) < S), 0.0, act)
            if k == W // 2 - 1:
                act = jnp.where(below & (iota(act.shape, 0) >= S), 0.0, act)
            for i in range(2):
                r = 2 * k + i - 1
                if 0 <= r < S:
                    latent[S * r : S * r + S] = values[S * i : S * i + S].astype(BF)
            at = slice(2 * k, 2 * k + 2)
            for i, v in enumerate(time_terms(act)):
                v = v.reshape(2, S, P2, C)
                terms[i, at, 1:S, :, 0:C] = v[:, : S - 1]
                terms[i, at, :, :, C : 2 * C] = v
                terms[i, at, 0 : S - 1, :, 2 * C :] = v[:, 1:]
        for first, pixels in ((80, 16), (96, 8)):
            act = activate(turned(in_ref, first, pixels), norm)
            p = iota(act.shape, 0) + first
            out = (column == 0) & (p < 90) | (column == 15) & (p >= 90)
            out = out | above & ((p == 80) | (p == 90)) | below & ((p == 89) | (p == 99))
            for i, v in enumerate(time_terms(jnp.where(out, 0.0, act))):
                for q in range(pixels):
                    if first + q < 90:
                        terms[i, first + q - 80, 0, :, 0:C] = v[q]
                    elif first + q < 100:
                        terms[i, first + q - 90, S - 1, :, 2 * C :] = v[q]
        y_ref[...] = jnp.zeros_like(y_ref)

    even, odd = signs(j)
    for q in range(S // 2):
        m = sum(
            dot(terms[j, 2 * q + b : 2 * q + b + 2].reshape(2 * S * P2, 3 * C), w_ref[0, b].reshape(3 * C, C))
            for b in range(3)
        ).reshape(2 * S, P2, C)
        at = slice(16 * q, 16 * q + 16)
        y_ref[at, 0] += even * m
        y_ref[at, 1] += odd * m

    @pl.when(j == 3)
    def _():
        total = jnp.zeros((2, P2, C), F32)
        for p in range(S * S):
            v = (latent[p].astype(F32) + y_ref[p]).astype(BF)
            mid_ref[p] = v
            total = total + v.astype(F32)
        mean = total * (1.0 / (S * S))
        total = jnp.zeros((2, P2, C), F32)
        for p in range(S * S):
            off = mid_ref[p].astype(F32) - mean
            total = total + off * off
        stats = sum(group_stats(mean[i], total[i], float(S * S), 64 * i) for i in range(2))
        stats_ref[...] = jnp.broadcast_to(stats[None], stats_ref.shape)


def merge_kernel(parts_ref, out_ref):
    whole = merge(parts_ref[...], float(S * S * 16))
    out_ref[...] = jnp.broadcast_to(whole[None], out_ref.shape)


def attend_kernel(mid_ref, parts_ref, wq_ref, wk_ref, wv_ref, wo_ref, out_ref, norm):
    @pl.when(pl.program_id(0) == 0)
    def _():
        count = float(S * S * 16 * 8)
        whole = finish(merge(parts_ref[...], count), 16.0 * count)
        for i in range(2):
            for j in range(2):
                norm[i, j] = dot(whole, from_groups(64 * j + 32 * i), HI)

    pixels = mid_ref.shape[0]
    rows = pixels * T
    mid = mid_ref[...].astype(F32)
    flat = ((mid - norm[0][None]) * norm[1][None]).astype(BF).reshape(rows, C)
    query = dot(flat, wq_ref[...]).astype(BF)
    keys = dot(flat, wk_ref[...]).astype(BF)
    values = dot(flat, wv_ref[...]).astype(BF)
    n = 256
    row, column = iota((n, n), 0), iota((n, n), 1)
    frame = lambda v: 2 * (v % P2) + (v // P2) % 2
    seen = (row // T == column // T) & (frame(row) >= frame(column))
    parts = []
    for i in range(rows // n):
        at = slice(i * n, i * n + n)
        scores = lax.dot_general(
            query[at], keys[at], (((1,), (1,)), ((), ())), preferred_element_type=F32
        ) * (1.0 / (C**0.5))
        scores = jnp.where(seen, scores, -1e30)
        weights = jnp.exp(scores - jnp.max(scores, axis=1, keepdims=True))
        weights = (weights / jnp.sum(weights, axis=1, keepdims=True)).astype(BF)
        parts.append(dot(weights, values[at]).astype(BF))
    update = dot(jnp.concatenate(parts, axis=0), wo_ref[...])
    out = (mid.reshape(rows, C) + update).astype(BF)
    to = iota((rows, rows), 0)
    frame = to // pixels
    turn = (iota((rows, rows), 1) == (to % pixels) * T + (frame % 2) * P2 + frame // 2).astype(BF)
    out_ref[...] = dot(turn, out).astype(BF).reshape(T, pixels, C)


def local(latents, conv_weight, w_query, w_key, w_value, w_out):
    x = latents.reshape(16, 128, C)
    vmem = pl.BlockSpec(memory_space=pltpu.VMEM)
    smem = pl.BlockSpec(memory_space=pltpu.SMEM)
    whole = lambda *shape: pl.BlockSpec(shape, lambda i: (0,) * len(shape))
    exchange = lambda v, axes: lax.all_to_all(v[None], axes, split_axis=1, concat_axis=0, tiled=True)[:, 0]
    place = jnp.stack([lax.axis_index(TM), lax.axis_index("rows")]).astype(jnp.int32)

    row = jax.ShapeDtypeStruct((144, C), BF)
    up, down, own = pl.pallas_call(
        latent_stats_kernel,
        out_shape=(row, row, jax.ShapeDtypeStruct((16, C), BF)),
        in_specs=[vmem],
        out_specs=(vmem,) * 3,
        compiler_params=params(),
        cost_estimate=cost(2048 * C * 4, 2048 * C * 2),
        name="latent_stats",
    )(x.reshape(2048, C))
    around = lambda v, by: lax.ppermute(v, "rows", [(i, (i + by) % 4) for i in range(4)])
    up, down, far = around(up, 1), around(down, 3), around(own, 2)
    messages = pl.pallas_call(
        message_kernel,
        grid=(4,),
        out_shape=jax.ShapeDtypeStruct((32, MSG, C), BF),
        in_specs=[whole(16, 128, C), whole(144, C), whole(144, C), whole(16, C), whole(16, C)],
        out_specs=pl.BlockSpec((8, MSG, C), lambda i: (i, 0, 0)),
        scratch_shapes=[pltpu.VMEM((4, 18, 128, 128), F32), pltpu.VMEM((4, 2, 16 * 24, 128), F32)],
        compiler_params=params(),
        cost_estimate=cost(2**22, 6 * 2**20),
        name="messages",
    )(x, up, down, own, far)
    patch = exchange(messages, TM)
    weights = pl.pallas_call(
        weights_kernel,
        grid=(3, 3),
        out_shape=jax.ShapeDtypeStruct((4, 3, 3, C, C), BF),
        in_specs=[pl.BlockSpec((3, 1, 1, C, C), lambda b, e: (0, b, e, 0, 0))],
        out_specs=pl.BlockSpec((4, 1, 1, C, C), lambda b, e: (0, b, e, 0, 0)),
        compiler_params=params(),
        cost_estimate=cost(9 * 4 * C * C, 9 * 7 * C * C * 2),
        name="weights",
    )(conv_weight)

    mid, stats = pl.pallas_call(
        conv_kernel,
        grid=(4,),
        out_shape=(jax.ShapeDtypeStruct((S * S, 2, P2, C), BF), jax.ShapeDtypeStruct((8, P2, 128), F32)),
        in_specs=[smem, whole(T, MSG, C), pl.BlockSpec((1, 3, 3, C, C), lambda i: (i, 0, 0, 0, 0))],
        out_specs=(whole(S * S, 2, P2, C), whole(8, P2, 128)),
        scratch_shapes=[
            pltpu.VMEM((4, W, S, P2, 3 * C), BF),
            pltpu.VMEM((S * S, 2, P2, C), BF),
            pltpu.VMEM((S * S, 2, P2, C), F32),
            pltpu.VMEM((2, 2, P2, C), F32),
        ],
        compiler_params=params(),
        cost_estimate=cost(1024 * 36 * C * C * 2, 28 * 2**20),
        name="conv",
    )(place, patch, weights)
    parts = pl.pallas_call(
        merge_kernel,
        out_shape=jax.ShapeDtypeStruct((16, P2, 128), F32),
        in_specs=[vmem],
        out_specs=vmem,
        compiler_params=params(),
        name="merge",
    )(exchange(stats, ("core", "rows")))
    parts = exchange(parts, ("x", "y"))
    pixels = 16
    out = pl.pallas_call(
        attend_kernel,
        grid=(S * S // pixels,),
        out_shape=jax.ShapeDtypeStruct((T, S * S, C), BF),
        in_specs=[pl.BlockSpec((pixels, 2, P2, C), lambda i: (i, 0, 0, 0)), whole(16, P2, 128)] + [whole(C, C)] * 4,
        out_specs=pl.BlockSpec((T, pixels, C), lambda i: (0, i, 0)),
        scratch_shapes=[pltpu.VMEM((2, 2, P2, C), F32)],
        compiler_params=params(),
        cost_estimate=cost(2048 * C * C * 2 * 6, 8 * 2**20),
        name="attend",
    )(mid, parts, w_query, w_key, w_value, w_out)
    back = exchange(out, TM)
    back = back.reshape(16, 2, S, S, C).transpose(1, 2, 0, 3, 4)
    return back.reshape(1, 16, 128, C)


def solution(mesh):
    mesh = Mesh(mesh.devices.reshape(4, 4, 2, 4), TM + ("rows",))
    in_specs = (P(TM, "rows", None, None), P(), P(), P(), P(), P())
    out_specs = P(TM, "rows", None, None)
    return jax.shard_map(local, mesh=mesh, in_specs=in_specs, out_specs=out_specs, check_vma=False)
```

time: 201 us -> 177 us (0.88)
  starting transfers between devices: 40.1 us -> 14.8 us
  waiting for transfers between devices: 11.7 us -> 29.9 us
  Pallas kernels: 87.2 us -> 71.2 us
  blocking collectives: 50 us -> 55.5 us
  local copies, waits for them, and re-layouts: 9.28 us -> 4.03 us
    all_to_all x2 -> x1, waiting for transfers between devices: 0.01 us -> 26.5 us  [local(): lax.all_to_all(v[None], axes, split_axis=1, concat_axis=0, tiled=True)[:, 0]]
    ppermute x15 -> x3, starting transfers between devices: 26.5 us -> 5.89 us  [local(): lax.ppermute(v, 'rows', [(i, (i + by) % 4) for i in range(4)])]
    pallas_call x5 -> x3, Pallas kernels: 30.2 us -> 10.5 us  [the longest x1 4.85 us: local(): pl.pallas_call(message_kernel, grid=(4,), out_shape=jax.ShapeDtypeStruct(...]
    ppermute x15 -> x3, waiting for transfers between devices: 11.7 us -> 3.4 us  [local(): lax.ppermute(v, 'rows', [(i, (i + by) % 4) for i in range(4)])]
    all_to_all x2 -> x3, blocking collectives: 50 us -> 55.5 us  [local(): lax.all_to_all(v[None], axes, split_axis=1, concat_axis=0, tiled=True)[:, 0]]
    all_to_all x2 -> x1, starting transfers between devices: 13.7 us -> 8.93 us  [local(): lax.all_to_all(v[None], axes, split_axis=1, concat_axis=0, tiled=True)[:, 0]]
    pallas_call x1, Pallas kernels: 29 us -> 32.7 us  [local(): pl.pallas_call(conv_kernel, grid=(4,), out_shape=(jax.ShapeDtypeStruct((S...]
    another operation x1 -> x0, local copies, waits for them, and re-layouts: 3.19 us -> none  [local(): messages = x.reshape(2, S, 16, S, C).transpose(2, 0, 1, 3, 4)]
  transfers between devices with their start and end apart: 17 -> 4, of which waited for: 5 -> 2; matrix products, arithmetic and copies ran while one was open for 1% -> 0% of each run, Pallas kernels for 28% -> 9%
where the time goes in v3:
time: 177 us; the launch traced here: 176 us
  Pallas kernels  71.2 us (40%)
  blocking collectives  55.5 us (31%)
  waiting for transfers between devices  29.9 us (17%)
  starting transfers between devices  14.8 us (8%)
  local copies, waits for them, and re-layouts  4.03 us (2%)
    all_to_all x3, blocking collectives, local(): lax.all_to_all(v[None], axes, split_axis=1, concat_axis=0, tiled=True)[:, 0]  55.5 us
    pallas_call x1, Pallas kernels, local(): pl.pallas_call(conv_kernel, grid=(4,), out_shape=(jax.ShapeDtypeStruct((S...  32.7 us
    all_to_all x1, waiting for transfers between devices, local(): lax.all_to_all(v[None], axes, split_axis=1, concat_axis=0, tiled=True)[:, 0]  26.5 us
    pallas_call x1, Pallas kernels, local(): pl.pallas_call(weights_kernel, grid=(3, 3), out_shape=jax.ShapeDtypeStruc...  15.5 us
    pallas_call x1, Pallas kernels, local(): pl.pallas_call(attend_kernel, grid=(S * S // pixels,), out_shape=jax.Shap...  12.6 us
    all_to_all x1, starting transfers between devices, local(): lax.all_to_all(v[None], axes, split_axis=1, concat_axis=0, tiled=True)[:, 0]  8.93 us
    ppermute x3, starting transfers between devices, local(): lax.ppermute(v, 'rows', [(i, (i + by) % 4) for i in range(4)])  5.89 us
    pallas_call x1, Pallas kernels, local(): pl.pallas_call(message_kernel, grid=(4,), out_shape=jax.ShapeDtypeStruct(...  4.85 us
  transfers between devices with their start and end apart: 4, of which 2 were waited for; matrix products, arithmetic and copies ran while one was open for 0% of the time, Pallas kernels for 9%

profile of v3, /device:TPU:1, one launch (start us, length us, event | category | flops | bytes accessed | tf_op | source)
XLA Modules:
  0.0 176.1 jit_solution(7040394309914468096)
XLA Ops:
  0.0 4.1 %latent_stats.1 = (bf16[144,512]{1,0:T(8,128)(2,1)}, bf16[144,512]{1,0:T(8,128)(2,1)}, bf16[16,512]{1,0:T(8,128)(2,1)}) custom-call(bf16[2048,512]{1,0:T(8,128)(2,1)} %bitcast.25), custom_call_target="tpu_custom_call" | custom-call | flops 4194304 | bytes 2097152 | tf_op jit(solution)/shard_map/latent_stats/pallas_call | solution.py:305
  4.1 2.5 %collective-permute-start = (bf16[144,512]{1,0:T(8,128)(2,1)}, bf16[144,512]{1,0:T(8,128)(2,1)S(1)}, u32[]{:S(2)}, u32[]{:S(2)}) collective-permute-start(bf16[144,512]{1,0:T(8,128)(2,1)} %get-tuple-element.10), channel_id=1, source_target_pairs={{0,1},{1,2},{2,3},{3,0},{4,5},{5,6},{6,7},{7,4},{8,9},{9,10},{10,1... | collective-permute-start | bytes 442376 | tf_op jit(solution)/shard_map/ppermute | solution.py:314
  6.6 2.1 %collective-permute-start.1 = (bf16[144,512]{1,0:T(8,128)(2,1)}, bf16[144,512]{1,0:T(8,128)(2,1)S(1)}, u32[]{:S(2)}, u32[]{:S(2)}) collective-permute-start(bf16[144,512]{1,0:T(8,128)(2,1)} %get-tuple-element.11), channel_id=1, source_target_pairs={{0,3},{1,0},{2,1},{3,2},{4,7},{5,4},{6,5},{7,6},{8,11},{9,8},{10,9... | collective-permute-start | bytes 442376 | tf_op jit(solution)/shard_map/ppermute | solution.py:314
  8.7 1.3 collective-permute-start.2
  10.0 3.4 %collective-permute-done.2.far_ref = bf16[16,512]{1,0:T(8,128)(2,1)S(1)} collective-permute-done((bf16[16,512]{1,0:T(8,128)(2,1)}, bf16[16,512]{1,0:T(8,128)(2,1)S(1)}, u32[]{:S(2)}, u32[]{:S(2)}) %collective-permute-start.2) | collective-permute-done | bytes 16416 | tf_op jit(solution)/shard_map/ppermute | solution.py:314
  13.4 0.0 copy-start.3
  13.4 0.0 collective-permute-done.up_ref
  13.4 0.0 copy-start.1
  13.4 0.0 collective-permute-done.1.down_ref
  13.4 0.0 copy-start.2
  13.4 0.6 copy-done.3
  14.0 0.1 copy-done.1
  14.1 0.0 copy-done.2
  14.1 4.9 %messages.1 = bf16[32,104,512]{2,1,0:T(8,128)(2,1)} custom-call(bf16[16,128,512]{2,1,0:T(8,128)(2,1)} %bitcast.26, bf16[144,512]{1,0:T(8,128)(2,1)} %copy-done.1, bf16[144,512]{1,0:T(8,128)(2,1)} %copy-done.2, bf16[16,512]{1,0:T(8,128)(2,1)} %get-tuple-element.12.own_ref, bf16[16,512]{1,0:T(8,128)(2,1)} %copy-done.3), custom_call_target="tpu_custom_call" | custom-call | flops 4194304 | bytes 6291456 | tf_op jit(solution)/shard_map/messages/pallas_call | solution.py:316
  19.0 8.9 %all-to-all-start = ((bf16[1,32,104,512]{3,2,0,1:T(8,128)(2,1)}), bf16[1,32,104,512]{3,2,0,1:T(8,128)(2,1)S(1)}, u32[]{:S(2)}, u32[]{:S(2)}) async-start(bf16[1,32,104,512]{3,2,0,1:T(8,128)(2,1)} %bitcast.23), calls=%async_computation | async-start | bytes 6815744 | tf_op jit(solution)/shard_map/all_to_all | solution.py:301
  27.9 15.5 %weights.1.w_ref = bf16[4,3,3,512,512]{4,3,2,1,0:T(8,128)(2,1)} custom-call(bf16[3,3,3,512,512]{4,3,2,1,0:T(8,128)(2,1)} %w_ref.1), custom_call_target="tpu_custom_call" | custom-call | flops 9437184 | bytes 33030144 | tf_op jit(solution)/shard_map/weights/pallas_call | solution.py:328
  43.4 0.6 pad_add_fusion.place_ref
  44.0 26.5 %all-to-all-done = bf16[1,32,104,512]{3,2,0,1:T(8,128)(2,1)S(1)} async-done(((bf16[1,32,104,512]{3,2,0,1:T(8,128)(2,1)}), bf16[1,32,104,512]{3,2,0,1:T(8,128)(2,1)S(1)}, u32[]{:S(2)}, u32[]{:S(2)}) %all-to-all-start) | async-done | bytes 3407904 | tf_op jit(solution)/shard_map/all_to_all | solution.py:301
  70.5 0.0 copy-start
  70.5 1.8 %copy-done = bf16[1,32,104,512]{3,2,0,1:T(8,128)(2,1)} copy-done((bf16[1,32,104,512]{3,2,0,1:T(8,128)(2,1)}, bf16[1,32,104,512]{3,2,0,1:T(8,128)(2,1)S(1)}, u32[]{:S(2)}) %copy-start) | copy-done | bytes 3407896
  72.3 32.7 %conv.1 = (bf16[64,2,16,512]{3,2,1,0:T(8,128)(2,1)}, f32[8,16,128]{2,1,0:T(8,128)}) custom-call(s32[2]{0:T(128)} %pad_add_fusion.place_ref, bf16[32,104,512]{2,1,0:T(8,128)(2,1)} %bitcast.27, bf16[4,3,3,512,512]{4,3,2,1,0:T(8,128)(2,1)} %weights.1.w_ref), custom_call_target="tpu_custom_call" | custom-call | flops 19327352832 | bytes 29360128 | tf_op jit(solution)/shard_map/conv/pallas_call | solution.py:339
  104.9 9.8 %all_to_all.16 = f32[1,8,16,128]{3,2,0,1:T(8,128)} all-to-all(f32[1,8,16,128]{3,2,0,1:T(8,128)} %bitcast.32), channel_id=1, replica_groups=mesh['x'=4,'y'=4,'core'=2,'rows'=4] {'core','rows'}, dimensions={1} | all-to-all | bytes 131072 | tf_op jit(solution)/shard_map/all_to_all | solution.py:301
  114.7 1.6 merge.1
  116.3 12.0 %all_to_all.17 = f32[1,16,16,128]{3,2,0,1:T(8,128)} all-to-all(f32[1,16,16,128]{3,2,0,1:T(8,128)} %bitcast.29), channel_id=1, replica_groups=mesh['x'=4,'y'=4,'core'=2,'rows'=4] {'x','y'}, dimensions={1} | all-to-all | bytes 262144 | tf_op jit(solution)/shard_map/all_to_all | solution.py:301
  128.2 12.6 %attend.1 = bf16[32,64,512]{2,1,0:T(8,128)(2,1)} custom-call(bf16[64,2,16,512]{3,2,1,0:T(8,128)(2,1)} %get-tuple-element.13.mid_ref, f32[16,16,128]{2,1,0:T(8,128)} %bitcast.31, bf16[512,512]{1,0:T(8,128)(2,1)} %wq_ref.1, bf16[512,512]{1,0:T(8,128)(2,1)} %wk_ref.1, bf16[512,512]{1,0:T(8,128)(2,1)} %wv_ref.1, bf16[512,512]{1,0:T(8,128)(2,1)} %wo_ref.1), custom_call_target="tpu_custom_call" | custom-call | flops 6442450944 | bytes 8388608 | tf_op jit(solution)/shard_map/attend/pallas_call | solution.py:365
  140.8 33.7 %all_to_all.18 = bf16[1,32,64,512]{3,2,0,1:T(8,128)(2,1)S(1)} all-to-all(bf16[1,32,64,512]{3,2,0,1:T(8,128)(2,1)} %bitcast.28), channel_id=1, replica_groups=mesh['x'=4,'y'=4,'core'=2,'rows'=4] {'x','y','core'}, dimensions={1} | all-to-all | bytes 4194304 | tf_op jit(solution)/shard_map/all_to_all | solution.py:301
  174.5 1.5 copy.12
Async XLA Ops:
  4.1 9.3 %collective-permute-start = (bf16[144,512]{1,0:T(8,128)(2,1)}, bf16[144,512]{1,0:T(8,128)(2,1)S(1)}, u32[]{:S(2)}, u32[]{:S(2)}) collective-permute-start(bf16[144,512]{1,0:T(8,128)(2,1)} %get-tuple-element.10), channel_id=1, source_target_pairs={{0,1},{1,2},{2,3},{3,0},{4,5},{5,6},{6,7},{7,4},{8,9},{9,10},{10,1... | collective-permute-start | bytes 442376 | tf_op jit(solution)/shard_map/ppermute | solution.py:314
  6.6 6.8 %collective-permute-start.1 = (bf16[144,512]{1,0:T(8,128)(2,1)}, bf16[144,512]{1,0:T(8,128)(2,1)S(1)}, u32[]{:S(2)}, u32[]{:S(2)}) collective-permute-start(bf16[144,512]{1,0:T(8,128)(2,1)} %get-tuple-element.11), channel_id=1, source_target_pairs={{0,3},{1,0},{2,1},{3,2},{4,7},{5,4},{6,5},{7,6},{8,11},{9,8},{10,9... | collective-permute-start | bytes 442376 | tf_op jit(solution)/shard_map/ppermute | solution.py:314
  8.7 4.7 %collective-permute-start.2 = (bf16[16,512]{1,0:T(8,128)(2,1)}, bf16[16,512]{1,0:T(8,128)(2,1)S(1)}, u32[]{:S(2)}, u32[]{:S(2)}) collective-permute-start(bf16[16,512]{1,0:T(8,128)(2,1)} %get-tuple-element.12.own_ref), channel_id=1, source_target_pairs={{0,2},{1,3},{2,0},{3,1},{4,6},{5,7},{6,4},{7,5},{8,10},{9,11},{10,... | collective-permute-start | bytes 49160 | tf_op jit(solution)/shard_map/ppermute | solution.py:314
  13.4 0.6 copy-start.3
  13.4 0.7 copy-start.1
  13.4 0.7 copy-start.2
  19.0 51.5 %all-to-all-start = ((bf16[1,32,104,512]{3,2,0,1:T(8,128)(2,1)}), bf16[1,32,104,512]{3,2,0,1:T(8,128)(2,1)S(1)}, u32[]{:S(2)}, u32[]{:S(2)}) async-start(bf16[1,32,104,512]{3,2,0,1:T(8,128)(2,1)} %bitcast.23), calls=%async_computation | async-start | bytes 6815744 | tf_op jit(solution)/shard_map/all_to_all | solution.py:301
  70.5 1.8 %copy-start = (bf16[1,32,104,512]{3,2,0,1:T(8,128)(2,1)}, bf16[1,32,104,512]{3,2,0,1:T(8,128)(2,1)S(1)}, u32[]{:S(2)}) copy-start(bf16[1,32,104,512]{3,2,0,1:T(8,128)(2,1)S(1)} %all-to-all-done) | copy-start | bytes 10223620

commit v4 on v3

--- a/solution.py
+++ b/solution.py
@@ -137,12 +137,16 @@
 
 
 def weights_kernel(w_ref, out_ref):
-    g = [w_ref[i, 0, 0].astype(F32) for i in range(3)]
-    ends = (g[0] + g[2]) * 0.5
-    out_ref[0, 0, 0] = w_ref[0, 0, 0]
-    out_ref[1, 0, 0] = (ends + g[1] * 0.5).astype(BF)
-    out_ref[2, 0, 0] = (ends - g[1] * 0.5).astype(BF)
-    out_ref[3, 0, 0] = w_ref[2, 0, 0]
+    def products(g):
+        ends = (g[0] + g[2]) * 0.5
+        middle = g[1] * 0.5
+        return g[0], ends + middle, ends - middle, g[2]
+
+    w = [[w_ref[a, 0, e].astype(F32) for e in range(3)] for a in range(3)]
+    columns = [products(w[a]) for a in range(3)]
+    for l in range(4):
+        for j, v in enumerate(products([columns[a][l] for a in range(3)])):
+            out_ref[4 * j + l, 0] = v.astype(BF)
 
 
 def turned(in_ref, first, pixels):
@@ -169,85 +173,103 @@
         return jnp.where(start, 0.0, v).reshape(pixels, P2, C)
 
     even1, odd1 = before(even), before(odd)
-    return [v.astype(BF) for v in (even1 - even, odd1 + even, even - odd1, odd1 - odd)]
+    return even1 - even, odd1 + even, even - odd1, odd1 - odd
 
 
 def signs(j):
     return jnp.where(j == 3, 0.0, 1.0), jnp.where(j == 0, 0.0, jnp.where(j == 1, 1.0, -1.0))
 
 
-def conv_kernel(place_ref, in_ref, w_ref, mid_ref, stats_ref, terms, latent, y_ref, norm):
-    j = pl.program_id(0)
-
-    @pl.when(j == 0)
-    def _():
-        block, z = place_ref[0], place_ref[1]
-        half, column = block % 2, block // 2
-        above = (half == 0) & (z == 0)
-        below = (half == 1) & (z == 3)
-        tail = in_ref[:, 96:MSG, :].reshape(T * 8, C)
-        row = iota((T, T * 8), 0)
-        row = 2 * (row % P2) + row // P2
-        pieces = dot((iota((T, T * 8), 1) == row * 8 + 4).astype(BF), tail).astype(BF)
+def conv_kernel(place_ref, in_ref, w_ref, mid_ref, stats_ref, terms, sides, latent, y_ref, norm, held, sems):
+    def fetch(j, l):
+        slot = 4 * (j % 2) + l
+        return pltpu.make_async_copy(w_ref.at[4 * j + l], held.at[slot], sems.at[slot])
+
+    for j in range(2):
+        for l in range(4):
+            fetch(j, l).start()
+
+    block, z = place_ref[0], place_ref[1]
+    half, column = block % 2, block // 2
+    above = (half == 0) & (z == 0)
+    below = (half == 1) & (z == 3)
+    tail = in_ref[:, 96:MSG, :].reshape(T * 8, C)
+    row = iota((T, T * 8), 0)
+    row = 2 * (row % P2) + row // P2
+    pieces = dot((iota((T, T * 8), 1) == row * 8 + 4).astype(BF), tail).astype(BF)
+    for i in range(2):
+        norm[i] = sum(
+            dot(pieces[:, 128 * k : 128 * k + 128], from_groups(32 * i, BF)) for k in range(3)
+        ).reshape(2, P2, C)
+
+    for first, pixels in ((80, 16), (96, 8)):
+        act = activate(turned(in_ref, first, pixels), norm)
+        p = iota(act.shape, 0) + first
+        out = (column == 0) & (p < 90) | (column == 15) & (p >= 90)
+        out = out | above & ((p == 80) | (p == 90)) | below & ((p == 89) | (p == 99))
+        for j, v in enumerate(time_terms(jnp.where(out, 0.0, act))):
+            for q in range(pixels):
+                if first + q < 100:
+                    sides[j, (first + q - 80) // W, (first + q) % W] = v[q]
+    for k in range(W // 2):
+        values = turned(in_ref, 16 * k, 16)
+        act = activate(values, norm)
+        if k == 0:
+            act = jnp.where(above & (iota(act.shape, 0) < S), 0.0, act)
+        if k == W // 2 - 1:
+            act = jnp.where(below & (iota(act.shape, 0) >= S), 0.0, act)
         for i in range(2):
-            norm[i] = sum(
-                dot(pieces[:, 128 * k : 128 * k + 128], from_groups(32 * i, BF)) for k in range(3)
-            ).reshape(2, P2, C)
-
-        for k in range(W // 2):
-            values = turned(in_ref, 16 * k, 16)
-            act = activate(values, norm)
-            if k == 0:
-                act = jnp.where(above & (iota(act.shape, 0) < S), 0.0, act)
-            if k == W // 2 - 1:
-                act = jnp.where(below & (iota(act.shape, 0) >= S), 0.0, act)
-            for i in range(2):
-                r = 2 * k + i - 1
-                if 0 <= r < S:
-                    latent[S * r : S * r + S] = values[S * i : S * i + S].astype(BF)
-            at = slice(2 * k, 2 * k + 2)
-            for i, v in enumerate(time_terms(act)):
-                v = v.reshape(2, S, P2, C)
-                terms[i, at, 1:S, :, 0:C] = v[:, : S - 1]
-                terms[i, at, :, :, C : 2 * C] = v
-                terms[i, at, 0 : S - 1, :, 2 * C :] = v[:, 1:]
-        for first, pixels in ((80, 16), (96, 8)):
-            act = activate(turned(in_ref, first, pixels), norm)
-            p = iota(act.shape, 0) + first
-            out = (column == 0) & (p < 90) | (column == 15) & (p >= 90)
-            out = out | above & ((p == 80) | (p == 90)) | below & ((p == 89) | (p == 99))
-            for i, v in enumerate(time_terms(jnp.where(out, 0.0, act))):
-                for q in range(pixels):
-                    if first + q < 90:
-                        terms[i, first + q - 80, 0, :, 0:C] = v[q]
-                    elif first + q < 100:
-                        terms[i, first + q - 90, S - 1, :, 2 * C :] = v[q]
-        y_ref[...] = jnp.zeros_like(y_ref)
-
-    even, odd = signs(j)
-    for q in range(S // 2):
-        m = sum(
-            dot(terms[j, 2 * q + b : 2 * q + b + 2].reshape(2 * S * P2, 3 * C), w_ref[0, b].reshape(3 * C, C))
-            for b in range(3)
-        ).reshape(2 * S, P2, C)
-        at = slice(16 * q, 16 * q + 16)
-        y_ref[at, 0] += even * m
-        y_ref[at, 1] += odd * m
-
-    @pl.when(j == 3)
-    def _():
-        total = jnp.zeros((2, P2, C), F32)
-        for p in range(S * S):
-            v = (latent[p].astype(F32) + y_ref[p]).astype(BF)
-            mid_ref[p] = v
-            total = total + v.astype(F32)
-        mean = total * (1.0 / (S * S))
-        total = jnp.zeros((2, P2, C), F32)
-        for p in range(S * S):
-            off = mid_ref[p].astype(F32) - mean
-            total = total + off * off
-        stats = sum(group_stats(mean[i], total[i], float(S * S), 64 * i) for i in range(2))
-        stats_ref[...] = jnp.broadcast_to(stats[None], stats_ref.shape)
+            r = 2 * k + i - 1
+            if 0 <= r < S:
+                latent[S * r : S * r + S] = values[S * i : S * i + S].astype(BF)
+        at = slice(2 * k, 2 * k + 2)
+        for j, v in enumerate(time_terms(act)):
+            left, right = sides[j, 0, at][:, None], sides[j, 1, at][:, None]
+            v = jnp.concatenate([left, v.reshape(2, S, P2, C), right], axis=1).reshape(2, W // 2, 2, P2, C)
+            even, odd = v[:, :, 0], v[:, :, 1]
+            before, after, odd_before = even[:, :-1], even[:, 1:], odd[:, :-1]
+            for l, u in enumerate((before - after, odd_before + after, after - odd_before, odd_before - odd[:, 1:])):
+                terms[j, l, at] = u.astype(BF)
+    y_ref[...] = jnp.zeros_like(y_ref)
+
+    def term(j, _):
+        @pl.when((j == 1) | (j == 2))
+        def _():
+            for l in range(4):
+                fetch(j + 1, l).start()
+
+        even, odd = signs(j)
+        for q in range(2):
+            m = []
+            for l in range(4):
+                if q == 0:
+                    fetch(j, l).wait()
+                m.append(
+                    sum(
+                        dot(terms[j, l, 4 * q + b : 4 * q + b + 4].reshape(16 * P2, C), held[4 * (j % 2) + l, b])
+                        for b in range(3)
+                    ).reshape(4, 4, P2, C)
+                )
+            at = slice(4 * q, 4 * q + 4)
+            for c, v in enumerate((m[0] + m[1] + m[2], m[1] - m[2] - m[3])):
+                y_ref[at, :, c, 0] += even * v
+                y_ref[at, :, c, 1] += odd * v
+        return 0
+
+    lax.fori_loop(0, 4, term, 0)
+
+    total = jnp.zeros((2, P2, C), F32)
+    for p in range(S * S):
+        v = (latent[p].astype(F32) + y_ref[p // S, p % S // 2, p % 2]).astype(BF)
+        mid_ref[p] = v
+        total = total + v.astype(F32)
+    mean = total * (1.0 / (S * S))
+    total = jnp.zeros((2, P2, C), F32)
+    for p in range(S * S):
+        off = mid_ref[p].astype(F32) - mean
+        total = total + off * off
+    stats = sum(group_stats(mean[i], total[i], float(S * S), 64 * i) for i in range(2))
+    stats_ref[...] = jnp.broadcast_to(stats[None], stats_ref.shape)
 
 
 def merge_kernel(parts_ref, out_ref):
@@ -255,7 +277,7 @@
     out_ref[...] = jnp.broadcast_to(whole[None], out_ref.shape)
 
 
-def attend_kernel(mid_ref, parts_ref, wq_ref, wk_ref, wv_ref, wo_ref, out_ref, norm):
+def attend_kernel(mid_ref, parts_ref, score_ref, update_ref, out_ref, norm):
     @pl.when(pl.program_id(0) == 0)
     def _():
         count = float(S * S * 16 * 8)
@@ -268,9 +290,7 @@
     rows = pixels * T
     mid = mid_ref[...].astype(F32)
     flat = ((mid - norm[0][None]) * norm[1][None]).astype(BF).reshape(rows, C)
-    query = dot(flat, wq_ref[...]).astype(BF)
-    keys = dot(flat, wk_ref[...]).astype(BF)
-    values = dot(flat, wv_ref[...]).astype(BF)
+    query = dot(flat, score_ref[...]).astype(BF)
     n = 256
     row, column = iota((n, n), 0), iota((n, n), 1)
     frame = lambda v: 2 * (v % P2) + (v // P2) % 2
@@ -278,19 +298,19 @@
     parts = []
     for i in range(rows // n):
         at = slice(i * n, i * n + n)
-        scores = lax.dot_general(
-            query[at], keys[at], (((1,), (1,)), ((), ())), preferred_element_type=F32
-        ) * (1.0 / (C**0.5))
+        scores = lax.dot_general(query[at], flat[at], (((1,), (1,)), ((), ())), preferred_element_type=F32)
         scores = jnp.where(seen, scores, -1e30)
         weights = jnp.exp(scores - jnp.max(scores, axis=1, keepdims=True))
         weights = (weights / jnp.sum(weights, axis=1, keepdims=True)).astype(BF)
-        parts.append(dot(weights, values[at]).astype(BF))
-    update = dot(jnp.concatenate(parts, axis=0), wo_ref[...])
+        parts.append(dot(weights, flat[at]).astype(BF))
+    update = dot(jnp.concatenate(parts, axis=0), update_ref[...])
     out = (mid.reshape(rows, C) + update).astype(BF)
-    to = iota((rows, rows), 0)
-    frame = to // pixels
-    turn = (iota((rows, rows), 1) == (to % pixels) * T + (frame % 2) * P2 + frame // 2).astype(BF)
-    out_ref[...] = dot(turn, out).astype(BF).reshape(T, pixels, C)
+    to = iota((n, n), 0)
+    frame = to // S
+    turn = (iota((n, n), 1) == (to % S) * T + (frame % 2) * P2 + frame // 2).astype(BF)
+    for i in range(rows // (2 * n)):
+        pair = [dot(turn, out[(2 * i + k) * n : (2 * i + k + 1) * n]).reshape(T, S, C) for k in range(2)]
+        out_ref[:, 16 * i : 16 * i + 16, :] = jnp.concatenate(pair, axis=1).astype(BF)
 
 
 def local(latents, conv_weight, w_query, w_key, w_value, w_out):
@@ -327,29 +347,33 @@
     patch = exchange(messages, TM)
     weights = pl.pallas_call(
         weights_kernel,
-        grid=(3, 3),
-        out_shape=jax.ShapeDtypeStruct((4, 3, 3, C, C), BF),
-        in_specs=[pl.BlockSpec((3, 1, 1, C, C), lambda b, e: (0, b, e, 0, 0))],
-        out_specs=pl.BlockSpec((4, 1, 1, C, C), lambda b, e: (0, b, e, 0, 0)),
-        compiler_params=params(),
-        cost_estimate=cost(9 * 4 * C * C, 9 * 7 * C * C * 2),
+        grid=(3, 4),
+        out_shape=jax.ShapeDtypeStruct((16, 3, C, C), BF),
+        in_specs=[pl.BlockSpec((3, 1, 3, 128, C), lambda b, i: (0, b, 0, i, 0))],
+        out_specs=pl.BlockSpec((16, 1, 128, C), lambda b, i: (0, b, i, 0)),
+        compiler_params=params(),
+        cost_estimate=cost(9 * 8 * C * C, 75 * C * C * 2),
         name="weights",
     )(conv_weight)
+    score = dot(w_query, w_key.T) * (1.0 / C**0.5)
+    score, update = score.astype(BF), dot(w_value, w_out).astype(BF)
 
     mid, stats = pl.pallas_call(
         conv_kernel,
-        grid=(4,),
         out_shape=(jax.ShapeDtypeStruct((S * S, 2, P2, C), BF), jax.ShapeDtypeStruct((8, P2, 128), F32)),
-        in_specs=[smem, whole(T, MSG, C), pl.BlockSpec((1, 3, 3, C, C), lambda i: (i, 0, 0, 0, 0))],
-        out_specs=(whole(S * S, 2, P2, C), whole(8, P2, 128)),
+        in_specs=[smem, vmem, pl.BlockSpec(memory_space=pl.ANY)],
+        out_specs=(vmem, vmem),
         scratch_shapes=[
-            pltpu.VMEM((4, W, S, P2, 3 * C), BF),
+            pltpu.VMEM((4, 4, W, S // 2, P2, C), BF),
+            pltpu.VMEM((4, 2, W, P2, C), F32),
             pltpu.VMEM((S * S, 2, P2, C), BF),
-            pltpu.VMEM((S * S, 2, P2, C), F32),
+            pltpu.VMEM((S, S // 2, 2, 2, P2, C), F32),
             pltpu.VMEM((2, 2, P2, C), F32),
+            pltpu.VMEM((8, 3, C, C), BF),
+            pltpu.SemaphoreType.DMA((8,)),
         ],
         compiler_params=params(),
-        cost_estimate=cost(1024 * 36 * C * C * 2, 28 * 2**20),
+        cost_estimate=cost(512 * 48 * C * C * 2, 28 * 2**20),
         name="conv",
     )(place, patch, weights)
     parts = pl.pallas_call(
@@ -361,18 +385,18 @@
         name="merge",
     )(exchange(stats, ("core", "rows")))
     parts = exchange(parts, ("x", "y"))
-    pixels = 16
+    pixels = 32
     out = pl.pallas_call(
         attend_kernel,
         grid=(S * S // pixels,),
         out_shape=jax.ShapeDtypeStruct((T, S * S, C), BF),
-        in_specs=[pl.BlockSpec((pixels, 2, P2, C), lambda i: (i, 0, 0, 0)), whole(16, P2, 128)] + [whole(C, C)] * 4,
+        in_specs=[pl.BlockSpec((pixels, 2, P2, C), lambda i: (i, 0, 0, 0)), whole(16, P2, 128)] + [whole(C, C)] * 2,
         out_specs=pl.BlockSpec((T, pixels, C), lambda i: (0, i, 0)),
         scratch_shapes=[pltpu.VMEM((2, 2, P2, C), F32)],
         compiler_params=params(),
-        cost_estimate=cost(2048 * C * C * 2 * 6, 8 * 2**20),
+        cost_estimate=cost(2048 * C * C * 2 * 4, 8 * 2**20),
         name="attend",
-    )(mid, parts, w_query, w_key, w_value, w_out)
+    )(mid, parts, score, update)
     back = exchange(out, TM)
     back = back.reshape(16, 2, S, S, C).transpose(1, 2, 0, 3, 4)
     return back.reshape(1, 16, 128, C)

time: 177 us -> 168 us (0.949)
  blocking collectives: 55.5 us -> 33.7 us
  starting transfers between devices: 14.8 us -> 24.3 us
  waiting for transfers between devices: 29.9 us -> 35.9 us
  Pallas kernels: 71.2 us -> 66.2 us
  matrix products: 0 us -> 2.51 us
    all_to_all x3 -> x1, blocking collectives: 55.5 us -> 33.7 us  [local(): lax.all_to_all(v[None], axes, split_axis=1, concat_axis=0, tiled=True)[:, 0]]
    all_to_all x1 -> x3, starting transfers between devices: 8.93 us -> 18.4 us  [local(): lax.all_to_all(v[None], axes, split_axis=1, concat_axis=0, tiled=True)[:, 0]]
    all_to_all x1 -> x3, waiting for transfers between devices: 26.5 us -> 32.5 us  [local(): lax.all_to_all(v[None], axes, split_axis=1, concat_axis=0, tiled=True)[:, 0]]
    pallas_call x1, Pallas kernels: 12.6 us -> 8.53 us  [local(): pl.pallas_call(attend_kernel, grid=(S * S // pixels,), out_shape=jax.Shap...]
    dot_general x0 -> x2, matrix products: none -> 2.51 us  [dot(): return jnp.dot(a, b, preferred_element_type=F32, precision=precision)]
  transfers between devices with their start and end apart: 4 -> 6, of which waited for: 2 -> 4; matrix products, arithmetic and copies ran while one was open for 0% -> 2% of each run, Pallas kernels for 9% -> 11%
where the time goes in v4:
time: 168 us; the launch traced here: 167 us
  Pallas kernels  66.2 us (39%)
  waiting for transfers between devices  35.9 us (21%)
  blocking collectives  33.7 us (20%)
  starting transfers between devices  24.3 us (14%)
  local copies, waits for them, and re-layouts  3.52 us (2%)
  matrix products  2.51 us (1%)
    all_to_all x1, blocking collectives, local(): lax.all_to_all(v[None], axes, split_axis=1, concat_axis=0, tiled=True)[:, 0]  33.7 us
    all_to_all x3, waiting for transfers between devices, local(): lax.all_to_all(v[None], axes, split_axis=1, concat_axis=0, tiled=True)[:, 0]  32.5 us
    pallas_call x1, Pallas kernels, local(): pl.pallas_call(conv_kernel, out_shape=(jax.ShapeDtypeStruct((S * S, 2, P2...  28.4 us
    pallas_call x1, Pallas kernels, local(): pl.pallas_call(weights_kernel, grid=(3, 4), out_shape=jax.ShapeDtypeStruc...  18.6 us
    all_to_all x3, starting transfers between devices, local(): lax.all_to_all(v[None], axes, split_axis=1, concat_axis=0, tiled=True)[:, 0]  18.4 us
    pallas_call x1, Pallas kernels, local(): pl.pallas_call(attend_kernel, grid=(S * S // pixels,), out_shape=jax.Shap...  8.53 us
    ppermute x3, starting transfers between devices, local(): lax.ppermute(v, 'rows', [(i, (i + by) % 4) for i in range(4)])  5.89 us
    pallas_call x1, Pallas kernels, local(): pl.pallas_call(message_kernel, grid=(4,), out_shape=jax.ShapeDtypeStruct(...  4.87 us
  transfers between devices with their start and end apart: 6, of which 4 were waited for; matrix products, arithmetic and copies ran while one was open for 2% of the time, Pallas kernels for 11%

profile of v4, /device:TPU:1, one launch (start us, length us, event | category | flops | bytes accessed | tf_op | source)
XLA Modules:
  0.0 166.9 jit_solution(7028898011134300780)
XLA Ops:
  0.0 0.0 copy-start
  0.0 4.2 %latent_stats.1 = (bf16[144,512]{1,0:T(8,128)(2,1)}, bf16[144,512]{1,0:T(8,128)(2,1)}, bf16[16,512]{1,0:T(8,128)(2,1)}) custom-call(bf16[2048,512]{1,0:T(8,128)(2,1)} %bitcast.29), custom_call_target="tpu_custom_call" | custom-call | flops 4194304 | bytes 2097152 | tf_op jit(solution)/shard_map/latent_stats/pallas_call | solution.py:325
  4.2 2.5 %collective-permute-start = (bf16[144,512]{1,0:T(8,128)(2,1)}, bf16[144,512]{1,0:T(8,128)(2,1)S(1)}, u32[]{:S(2)}, u32[]{:S(2)}) collective-permute-start(bf16[144,512]{1,0:T(8,128)(2,1)} %get-tuple-element.10), channel_id=1, source_target_pairs={{0,1},{1,2},{2,3},{3,0},{4,5},{5,6},{6,7},{7,4},{8,9},{9,10},{10,1... | collective-permute-start | bytes 442376 | tf_op jit(solution)/shard_map/ppermute | solution.py:334
  6.6 2.1 %collective-permute-start.1 = (bf16[144,512]{1,0:T(8,128)(2,1)}, bf16[144,512]{1,0:T(8,128)(2,1)S(1)}, u32[]{:S(2)}, u32[]{:S(2)}) collective-permute-start(bf16[144,512]{1,0:T(8,128)(2,1)} %get-tuple-element.11), channel_id=1, source_target_pairs={{0,3},{1,0},{2,1},{3,2},{4,7},{5,4},{6,5},{7,6},{8,11},{9,8},{10,9... | collective-permute-start | bytes 442376 | tf_op jit(solution)/shard_map/ppermute | solution.py:334
  8.8 1.3 collective-permute-start.2
  10.1 3.4 %collective-permute-done.2.far_ref = bf16[16,512]{1,0:T(8,128)(2,1)S(1)} collective-permute-done((bf16[16,512]{1,0:T(8,128)(2,1)}, bf16[16,512]{1,0:T(8,128)(2,1)S(1)}, u32[]{:S(2)}, u32[]{:S(2)}) %collective-permute-start.2) | collective-permute-done | bytes 16416 | tf_op jit(solution)/shard_map/ppermute | solution.py:334
  13.5 0.0 copy-start.6
  13.5 0.0 collective-permute-done.up_ref
  13.5 0.0 copy-start.3
  13.5 0.0 collective-permute-done.1.down_ref
  13.5 0.0 copy-start.4
  13.5 0.6 copy-done.6
  14.0 0.1 copy-done.3
  14.1 0.0 copy-done.4
  14.2 4.9 %messages.1 = bf16[32,104,512]{2,1,0:T(8,128)(2,1)} custom-call(bf16[16,128,512]{2,1,0:T(8,128)(2,1)} %bitcast.30, bf16[144,512]{1,0:T(8,128)(2,1)} %copy-done.3, bf16[144,512]{1,0:T(8,128)(2,1)} %copy-done.4, bf16[16,512]{1,0:T(8,128)(2,1)} %get-tuple-element.12.own_ref, bf16[16,512]{1,0:T(8,128)(2,1)} %copy-done.6), custom_call_target="tpu_custom_call" | custom-call | flops 4194304 | bytes 6291456 | tf_op jit(solution)/shard_map/messages/pallas_call | solution.py:336
  19.0 9.0 %all-to-all-start = ((bf16[1,32,104,512]{3,2,0,1:T(8,128)(2,1)}), bf16[1,32,104,512]{3,2,0,1:T(8,128)(2,1)}, u32[]{:S(2)}, u32[]{:S(2)}) async-start(bf16[1,32,104,512]{3,2,0,1:T(8,128)(2,1)} %bitcast.27), calls=%async_computation | async-start | bytes 6815744 | tf_op jit(solution)/shard_map/all_to_all | solution.py:321
  28.0 18.6 %weights.1.w_ref = bf16[16,3,512,512]{3,2,1,0:T(8,128)(2,1)} custom-call(bf16[3,3,3,512,512]{4,3,2,1,0:T(8,128)(2,1)} %w_ref.1), custom_call_target="tpu_custom_call" | custom-call | flops 18874368 | bytes 39321600 | tf_op jit(solution)/shard_map/weights/pallas_call | solution.py:348
  46.6 0.6 pad_add_fusion.place_ref
  47.3 23.4 %all-to-all-done = bf16[1,32,104,512]{3,2,0,1:T(8,128)(2,1)} async-done(((bf16[1,32,104,512]{3,2,0,1:T(8,128)(2,1)}), bf16[1,32,104,512]{3,2,0,1:T(8,128)(2,1)}, u32[]{:S(2)}, u32[]{:S(2)}) %all-to-all-start) | async-done | bytes 3407904 | tf_op jit(solution)/shard_map/all_to_all | solution.py:321
  70.6 0.0 copy-start.1
  70.6 28.4 %conv.1 = (bf16[64,2,16,512]{3,2,1,0:T(8,128)(2,1)}, f32[8,16,128]{2,1,0:T(8,128)}) custom-call(s32[2]{0:T(128)} %pad_add_fusion.place_ref, bf16[32,104,512]{2,1,0:T(8,128)(2,1)} %bitcast.6.in_ref, bf16[16,3,512,512]{3,2,1,0:T(8,128)(2,1)} %weights.1.w_ref), custom_call_target="tpu_custom_call" | custom-call | flops 12884901888 | bytes 29360128 | tf_op jit(solution)/shard_map/conv/pallas_call | solution.py:361
  99.1 0.0 copy-start.7
  99.1 0.0 copy-start.8
  99.1 4.3 %all-to-all-start.1 = ((f32[1,8,16,128]{3,2,0,1:T(8,128)}), f32[1,8,16,128]{3,2,0,1:T(8,128)S(1)}, u32[]{:S(2)}, u32[]{:S(2)}) async-start(f32[1,8,16,128]{3,2,0,1:T(8,128)} %bitcast.35), calls=%async_computation.1 | async-start | bytes 131072 | tf_op jit(solution)/shard_map/all_to_all | solution.py:321
  103.4 0.0 copy-done
  103.4 0.0 copy-done.1
  103.4 1.2 convolution_convert_fusion.update_ref
  104.6 3.7 %all-to-all-done.1 = f32[1,8,16,128]{3,2,0,1:T(8,128)S(1)} async-done(((f32[1,8,16,128]{3,2,0,1:T(8,128)}), f32[1,8,16,128]{3,2,0,1:T(8,128)S(1)}, u32[]{:S(2)}, u32[]{:S(2)}) %all-to-all-start.1) | async-done | bytes 65568 | tf_op jit(solution)/shard_map/all_to_all | solution.py:321
  108.4 0.0 copy-start.2
  108.4 0.6 copy-done.2
  109.0 1.6 merge.1
  110.6 5.2 %all-to-all-start.2 = ((f32[1,16,16,128]{3,2,0,1:T(8,128)}), f32[1,16,16,128]{3,2,0,1:T(8,128)S(1)}, u32[]{:S(2)}, u32[]{:S(2)}) async-start(f32[1,16,16,128]{3,2,0,1:T(8,128)} %bitcast.32), calls=%async_computation.2 | async-start | bytes 262144 | tf_op jit(solution)/shard_map/all_to_all | solution.py:321
  115.8 0.0 copy-done.7
  115.8 0.0 copy-done.8
  115.8 1.3 fusion.score_ref
  117.0 5.4 %all-to-all-done.2 = f32[1,16,16,128]{3,2,0,1:T(8,128)S(1)} async-done(((f32[1,16,16,128]{3,2,0,1:T(8,128)}), f32[1,16,16,128]{3,2,0,1:T(8,128)S(1)}, u32[]{:S(2)}, u32[]{:S(2)}) %all-to-all-start.2) | async-done | bytes 131104 | tf_op jit(solution)/shard_map/all_to_all | solution.py:321
  122.4 0.0 copy-start.5
  122.4 0.7 copy-done.5
  123.1 8.5 %attend.1 = bf16[32,64,512]{2,1,0:T(8,128)(2,1)} custom-call(bf16[64,2,16,512]{3,2,1,0:T(8,128)(2,1)} %get-tuple-element.13.mid_ref, f32[16,16,128]{2,1,0:T(8,128)} %bitcast.34, bf16[512,512]{1,0:T(8,128)(2,1)} %fusion.score_ref, bf16[512,512]{1,0:T(8,128)(2,1)} %convolution_convert_fusion.update_ref), custom_call_target="tpu_custom_call" | custom-call | flops 4294967296 | bytes 8388608 | tf_op jit(solution)/shard_map/attend/pallas_call | solution.py:389
  131.6 33.7 %all_to_all.16 = bf16[1,32,64,512]{3,2,0,1:T(8,128)(2,1)S(1)} all-to-all(bf16[1,32,64,512]{3,2,0,1:T(8,128)(2,1)} %bitcast.31), channel_id=1, replica_groups=mesh['x'=4,'y'=4,'core'=2,'rows'=4] {'x','y','core'}, dimensions={1} | all-to-all | bytes 4194304 | tf_op jit(solution)/shard_map/all_to_all | solution.py:321
  165.3 1.5 copy.12
Async XLA Ops:
  0.0 103.4 %copy-start = (bf16[512,512]{1,0:T(8,128)(2,1)S(1)}, bf16[512,512]{1,0:T(8,128)(2,1)}, u32[]{:S(2)}) copy-start(bf16[512,512]{1,0:T(8,128)(2,1)} %param.10) | copy-start | bytes 1572868
  4.2 9.3 %collective-permute-start = (bf16[144,512]{1,0:T(8,128)(2,1)}, bf16[144,512]{1,0:T(8,128)(2,1)S(1)}, u32[]{:S(2)}, u32[]{:S(2)}) collective-permute-start(bf16[144,512]{1,0:T(8,128)(2,1)} %get-tuple-element.10), channel_id=1, source_target_pairs={{0,1},{1,2},{2,3},{3,0},{4,5},{5,6},{6,7},{7,4},{8,9},{9,10},{10,1... | collective-permute-start | bytes 442376 | tf_op jit(solution)/shard_map/ppermute | solution.py:334
  6.6 6.8 %collective-permute-start.1 = (bf16[144,512]{1,0:T(8,128)(2,1)}, bf16[144,512]{1,0:T(8,128)(2,1)S(1)}, u32[]{:S(2)}, u32[]{:S(2)}) collective-permute-start(bf16[144,512]{1,0:T(8,128)(2,1)} %get-tuple-element.11), channel_id=1, source_target_pairs={{0,3},{1,0},{2,1},{3,2},{4,7},{5,4},{6,5},{7,6},{8,11},{9,8},{10,9... | collective-permute-start | bytes 442376 | tf_op jit(solution)/shard_map/ppermute | solution.py:334
  8.8 4.7 %collective-permute-start.2 = (bf16[16,512]{1,0:T(8,128)(2,1)}, bf16[16,512]{1,0:T(8,128)(2,1)S(1)}, u32[]{:S(2)}, u32[]{:S(2)}) collective-permute-start(bf16[16,512]{1,0:T(8,128)(2,1)} %get-tuple-element.12.own_ref), channel_id=1, source_target_pairs={{0,2},{1,3},{2,0},{3,1},{4,6},{5,7},{6,4},{7,5},{8,10},{9,11},{10,... | collective-permute-start | bytes 49160 | tf_op jit(solution)/shard_map/ppermute | solution.py:334
  13.5 0.6 copy-start.6
  13.5 0.7 copy-start.3
  13.5 0.7 copy-start.4
  19.0 51.6 %all-to-all-start = ((bf16[1,32,104,512]{3,2,0,1:T(8,128)(2,1)}), bf16[1,32,104,512]{3,2,0,1:T(8,128)(2,1)}, u32[]{:S(2)}, u32[]{:S(2)}) async-start(bf16[1,32,104,512]{3,2,0,1:T(8,128)(2,1)} %bitcast.27), calls=%async_computation | async-start | bytes 6815744 | tf_op jit(solution)/shard_map/all_to_all | solution.py:321
  70.6 32.8 %copy-start.1 = (bf16[512,512]{1,0:T(8,128)(2,1)S(1)}, bf16[512,512]{1,0:T(8,128)(2,1)}, u32[]{:S(2)}) copy-start(bf16[512,512]{1,0:T(8,128)(2,1)} %param.11) | copy-start | bytes 1572868
  99.1 16.7 %copy-start.7 = (bf16[512,512]{1,0:T(8,128)(2,1)S(1)}, bf16[512,512]{1,0:T(8,128)(2,1)}, u32[]{:S(2)}) copy-start(bf16[512,512]{1,0:T(8,128)(2,1)} %param.8) | copy-start | bytes 1572868
  99.1 16.7 %copy-start.8 = (bf16[512,512]{1,0:T(8,128)(2,1)S(1)}, bf16[512,512]{1,0:T(8,128)(2,1)}, u32[]{:S(2)}) copy-start(bf16[512,512]{1,0:T(8,128)(2,1)} %param.9) | copy-start | bytes 1572868
  99.1 9.2 %all-to-all-start.1 = ((f32[1,8,16,128]{3,2,0,1:T(8,128)}), f32[1,8,16,128]{3,2,0,1:T(8,128)S(1)}, u32[]{:S(2)}, u32[]{:S(2)}) async-start(f32[1,8,16,128]{3,2,0,1:T(8,128)} %bitcast.35), calls=%async_computation.1 | async-start | bytes 131072 | tf_op jit(solution)/shard_map/all_to_all | solution.py:321
  108.4 0.6 copy-start.2
  110.6 11.9 %all-to-all-start.2 = ((f32[1,16,16,128]{3,2,0,1:T(8,128)}), f32[1,16,16,128]{3,2,0,1:T(8,128)S(1)}, u32[]{:S(2)}, u32[]{:S(2)}) async-start(f32[1,16,16,128]{3,2,0,1:T(8,128)} %bitcast.32), calls=%async_computation.2 | async-start | bytes 262144 | tf_op jit(solution)/shard_map/all_to_all | solution.py:321
  122.4 0.7 copy-start.5

commit v5 on v4

--- a/solution.py
+++ b/solution.py
@@ -154,7 +154,7 @@
     to, at = iota((rows, rows), 0), iota((rows, rows), 1)
     frame = 2 * (to % P2) + (to // P2) % 2
     turn = (at == frame * pixels + to // T).astype(BF)
-    values = in_ref[:, first : first + pixels, :].reshape(rows, C)
+    values = in_ref[:, pl.ds(first, pixels), :].reshape(rows, C)
     return dot(turn, values).reshape(pixels, 2, P2, C)
 
 
@@ -176,16 +176,12 @@
     return even1 - even, odd1 + even, even - odd1, odd1 - odd
 
 
-def signs(j):
-    return jnp.where(j == 3, 0.0, 1.0), jnp.where(j == 0, 0.0, jnp.where(j == 1, 1.0, -1.0))
-
-
-def conv_kernel(place_ref, in_ref, w_ref, mid_ref, stats_ref, terms, sides, latent, y_ref, norm, held, sems):
+def conv_kernel(place_ref, in_ref, w_ref, mid_ref, stats_ref, terms, sides, latent, sums, norm, held, sems):
     def fetch(j, l):
-        slot = 4 * (j % 2) + l
+        slot = 4 * (j % 3) + l
         return pltpu.make_async_copy(w_ref.at[4 * j + l], held.at[slot], sems.at[slot])
 
-    for j in range(2):
+    for j in range(3):
         for l in range(4):
             fetch(j, l).start()
 
@@ -211,18 +207,15 @@
             for q in range(pixels):
                 if first + q < 100:
                     sides[j, (first + q - 80) // W, (first + q) % W] = v[q]
-    for k in range(W // 2):
-        values = turned(in_ref, 16 * k, 16)
+
+    def two_rows(k, _):
+        first = pl.multiple_of(16 * k, 16)
+        values = turned(in_ref, first, 16)
+        latent[pl.ds(first, 16)] = values.astype(BF)
         act = activate(values, norm)
-        if k == 0:
-            act = jnp.where(above & (iota(act.shape, 0) < S), 0.0, act)
-        if k == W // 2 - 1:
-            act = jnp.where(below & (iota(act.shape, 0) >= S), 0.0, act)
-        for i in range(2):
-            r = 2 * k + i - 1
-            if 0 <= r < S:
-                latent[S * r : S * r + S] = values[S * i : S * i + S].astype(BF)
-        at = slice(2 * k, 2 * k + 2)
+        r = iota(act.shape, 0) // S + 2 * k
+        act = jnp.where(above & (r == 0) | below & (r == W - 1), 0.0, act)
+        at = pl.ds(2 * k, 2)
         for j, v in enumerate(time_terms(act)):
             left, right = sides[j, 0, at][:, None], sides[j, 1, at][:, None]
             v = jnp.concatenate([left, v.reshape(2, S, P2, C), right], axis=1).reshape(2, W // 2, 2, P2, C)
@@ -230,44 +223,51 @@
             before, after, odd_before = even[:, :-1], even[:, 1:], odd[:, :-1]
             for l, u in enumerate((before - after, odd_before + after, after - odd_before, odd_before - odd[:, 1:])):
                 terms[j, l, at] = u.astype(BF)
-    y_ref[...] = jnp.zeros_like(y_ref)
+        return 0
+
+    lax.fori_loop(0, W // 2, two_rows, 0)
 
     def term(j, _):
-        @pl.when((j == 1) | (j == 2))
+        @pl.when(j == 1)
         def _():
             for l in range(4):
-                fetch(j + 1, l).start()
-
-        even, odd = signs(j)
+                fetch(j + 2, l).start()
+
+        for l in range(4):
+            fetch(j, l).wait()
         for q in range(2):
             m = []
             for l in range(4):
-                if q == 0:
-                    fetch(j, l).wait()
-                m.append(
-                    sum(
-                        dot(terms[j, l, 4 * q + b : 4 * q + b + 4].reshape(16 * P2, C), held[4 * (j % 2) + l, b])
-                        for b in range(3)
-                    ).reshape(4, 4, P2, C)
-                )
-            at = slice(4 * q, 4 * q + 4)
-            for c, v in enumerate((m[0] + m[1] + m[2], m[1] - m[2] - m[3])):
-                y_ref[at, :, c, 0] += even * v
-                y_ref[at, :, c, 1] += odd * v
+                rows = [terms[j, l, 4 * q + b : 4 * q + b + 4].reshape(16 * P2, C) for b in range(3)]
+                weight = held[4 * (j % 3) + l].reshape(3 * C, C)
+                m.append(dot(jnp.concatenate(rows, axis=1), weight).reshape(4, 4, P2, C))
+            sums[j, 0, 4 * q : 4 * q + 4] = m[0] + m[1] + m[2]
+            sums[j, 1, 4 * q : 4 * q + 4] = m[1] - m[2] - m[3]
         return 0
 
     lax.fori_loop(0, 4, term, 0)
 
-    total = jnp.zeros((2, P2, C), F32)
-    for p in range(S * S):
-        v = (latent[p].astype(F32) + y_ref[p // S, p % S // 2, p % 2]).astype(BF)
-        mid_ref[p] = v
-        total = total + v.astype(F32)
-    mean = total * (1.0 / (S * S))
-    total = jnp.zeros((2, P2, C), F32)
-    for p in range(S * S):
-        off = mid_ref[p].astype(F32) - mean
-        total = total + off * off
+    def finish_row(r, total):
+        for c in range(S):
+            m = [sums[j, c % 2, r, c // 2] for j in range(4)]
+            for i, v in enumerate((m[0] + m[1] + m[2], m[1] - m[2] - m[3])):
+                v = (latent[S * r + S + c, i].astype(F32) + v).astype(BF)
+                mid_ref[S * r + c, i] = v
+                total[i] = total[i] + v.astype(F32)
+        return total
+
+    zero = jnp.zeros((P2, C), F32)
+    total = lax.fori_loop(0, S, finish_row, [zero, zero])
+    mean = [v * (1.0 / (S * S)) for v in total]
+
+    def squares(r, total):
+        for c in range(S):
+            for i in range(2):
+                off = mid_ref[S * r + c, i].astype(F32) - mean[i]
+                total[i] = total[i] + off * off
+        return total
+
+    total = lax.fori_loop(0, S, squares, [zero, zero])
     stats = sum(group_stats(mean[i], total[i], float(S * S), 64 * i) for i in range(2))
     stats_ref[...] = jnp.broadcast_to(stats[None], stats_ref.shape)
 
@@ -366,11 +366,11 @@
         scratch_shapes=[
             pltpu.VMEM((4, 4, W, S // 2, P2, C), BF),
             pltpu.VMEM((4, 2, W, P2, C), F32),
-            pltpu.VMEM((S * S, 2, P2, C), BF),
-            pltpu.VMEM((S, S // 2, 2, 2, P2, C), F32),
+            pltpu.VMEM((W * S, 2, P2, C), BF),
+            pltpu.VMEM((4, 2, S, S // 2, P2, C), F32),
             pltpu.VMEM((2, 2, P2, C), F32),
-            pltpu.VMEM((8, 3, C, C), BF),
-            pltpu.SemaphoreType.DMA((8,)),
+            pltpu.VMEM((12, 3, C, C), BF),
+            pltpu.SemaphoreType.DMA((12,)),
         ],
         compiler_params=params(),
         cost_estimate=cost(512 * 48 * C * C * 2, 28 * 2**20),

time: 168 us -> 166 us (0.988)
  Pallas kernels: 66.2 us -> 64 us
    pallas_call x1, Pallas kernels: 28.4 us -> 26.2 us  [local(): pl.pallas_call(conv_kernel, out_shape=(jax.ShapeDtypeStruct((S * S, 2, P2...]
where the time goes in v5:
time: 166 us; the launch traced here: 165 us
  Pallas kernels  64 us (39%)
  waiting for transfers between devices  36 us (22%)
  blocking collectives  33.7 us (20%)
  starting transfers between devices  24.3 us (15%)
  local copies, waits for them, and re-layouts  3.52 us (2%)
  matrix products  2.51 us (2%)
    all_to_all x1, blocking collectives, local(): lax.all_to_all(v[None], axes, split_axis=1, concat_axis=0, tiled=True)[:, 0]  33.7 us
    all_to_all x3, waiting for transfers between devices, local(): lax.all_to_all(v[None], axes, split_axis=1, concat_axis=0, tiled=True)[:, 0]  32.6 us
    pallas_call x1, Pallas kernels, local(): pl.pallas_call(conv_kernel, out_shape=(jax.ShapeDtypeStruct((S * S, 2, P2...  26.2 us
    pallas_call x1, Pallas kernels, local(): pl.pallas_call(weights_kernel, grid=(3, 4), out_shape=jax.ShapeDtypeStruc...  18.6 us
    all_to_all x3, starting transfers between devices, local(): lax.all_to_all(v[None], axes, split_axis=1, concat_axis=0, tiled=True)[:, 0]  18.4 us
    pallas_call x1, Pallas kernels, local(): pl.pallas_call(attend_kernel, grid=(S * S // pixels,), out_shape=jax.Shap...  8.52 us
    ppermute x3, starting transfers between devices, local(): lax.ppermute(v, 'rows', [(i, (i + by) % 4) for i in range(4)])  5.89 us
    pallas_call x1, Pallas kernels, local(): pl.pallas_call(message_kernel, grid=(4,), out_shape=jax.ShapeDtypeStruct(...  4.87 us
  transfers between devices with their start and end apart: 6, of which 4 were waited for; matrix products, arithmetic and copies ran while one was open for 2% of the time, Pallas kernels for 11%

profile of v5, /device:TPU:1, one launch (start us, length us, event | category | flops | bytes accessed | tf_op | source)
XLA Modules:
  0.0 164.7 jit_solution(13526287661651499093)
XLA Ops:
  0.0 0.0 copy-start
  0.0 4.2 %latent_stats.1 = (bf16[144,512]{1,0:T(8,128)(2,1)}, bf16[144,512]{1,0:T(8,128)(2,1)}, bf16[16,512]{1,0:T(8,128)(2,1)}) custom-call(bf16[2048,512]{1,0:T(8,128)(2,1)} %bitcast.29), custom_call_target="tpu_custom_call" | custom-call | flops 4194304 | bytes 2097152 | tf_op jit(solution)/shard_map/latent_stats/pallas_call | solution.py:325
  4.2 2.5 %collective-permute-start = (bf16[144,512]{1,0:T(8,128)(2,1)}, bf16[144,512]{1,0:T(8,128)(2,1)S(1)}, u32[]{:S(2)}, u32[]{:S(2)}) collective-permute-start(bf16[144,512]{1,0:T(8,128)(2,1)} %get-tuple-element.10), channel_id=1, source_target_pairs={{0,1},{1,2},{2,3},{3,0},{4,5},{5,6},{6,7},{7,4},{8,9},{9,10},{10,1... | collective-permute-start | bytes 442376 | tf_op jit(solution)/shard_map/ppermute | solution.py:334
  6.6 2.1 %collective-permute-start.1 = (bf16[144,512]{1,0:T(8,128)(2,1)}, bf16[144,512]{1,0:T(8,128)(2,1)S(1)}, u32[]{:S(2)}, u32[]{:S(2)}) collective-permute-start(bf16[144,512]{1,0:T(8,128)(2,1)} %get-tuple-element.11), channel_id=1, source_target_pairs={{0,3},{1,0},{2,1},{3,2},{4,7},{5,4},{6,5},{7,6},{8,11},{9,8},{10,9... | collective-permute-start | bytes 442376 | tf_op jit(solution)/shard_map/ppermute | solution.py:334
  8.8 1.3 collective-permute-start.2
  10.1 3.4 %collective-permute-done.2.far_ref = bf16[16,512]{1,0:T(8,128)(2,1)S(1)} collective-permute-done((bf16[16,512]{1,0:T(8,128)(2,1)}, bf16[16,512]{1,0:T(8,128)(2,1)S(1)}, u32[]{:S(2)}, u32[]{:S(2)}) %collective-permute-start.2) | collective-permute-done | bytes 16416 | tf_op jit(solution)/shard_map/ppermute | solution.py:334
  13.5 0.0 copy-start.6
  13.5 0.0 collective-permute-done.up_ref
  13.5 0.0 copy-start.3
  13.5 0.0 collective-permute-done.1.down_ref
  13.5 0.0 copy-start.4
  13.5 0.6 copy-done.6
  14.0 0.1 copy-done.3
  14.1 0.0 copy-done.4
  14.2 4.9 %messages.1 = bf16[32,104,512]{2,1,0:T(8,128)(2,1)} custom-call(bf16[16,128,512]{2,1,0:T(8,128)(2,1)} %bitcast.30, bf16[144,512]{1,0:T(8,128)(2,1)} %copy-done.3, bf16[144,512]{1,0:T(8,128)(2,1)} %copy-done.4, bf16[16,512]{1,0:T(8,128)(2,1)} %get-tuple-element.12.own_ref, bf16[16,512]{1,0:T(8,128)(2,1)} %copy-done.6), custom_call_target="tpu_custom_call" | custom-call | flops 4194304 | bytes 6291456 | tf_op jit(solution)/shard_map/messages/pallas_call | solution.py:336
  19.0 9.0 %all-to-all-start = ((bf16[1,32,104,512]{3,2,0,1:T(8,128)(2,1)}), bf16[1,32,104,512]{3,2,0,1:T(8,128)(2,1)}, u32[]{:S(2)}, u32[]{:S(2)}) async-start(bf16[1,32,104,512]{3,2,0,1:T(8,128)(2,1)} %bitcast.27), calls=%async_computation | async-start | bytes 6815744 | tf_op jit(solution)/shard_map/all_to_all | solution.py:321
  28.0 18.6 %weights.1.w_ref = bf16[16,3,512,512]{3,2,1,0:T(8,128)(2,1)} custom-call(bf16[3,3,3,512,512]{4,3,2,1,0:T(8,128)(2,1)} %w_ref.1), custom_call_target="tpu_custom_call" | custom-call | flops 18874368 | bytes 39321600 | tf_op jit(solution)/shard_map/weights/pallas_call | solution.py:348
  46.6 0.6 pad_add_fusion.place_ref
  47.2 23.5 %all-to-all-done = bf16[1,32,104,512]{3,2,0,1:T(8,128)(2,1)} async-done(((bf16[1,32,104,512]{3,2,0,1:T(8,128)(2,1)}), bf16[1,32,104,512]{3,2,0,1:T(8,128)(2,1)}, u32[]{:S(2)}, u32[]{:S(2)}) %all-to-all-start) | async-done | bytes 3407904 | tf_op jit(solution)/shard_map/all_to_all | solution.py:321
  70.7 0.0 copy-start.1
  70.7 26.2 %conv.1 = (bf16[64,2,16,512]{3,2,1,0:T(8,128)(2,1)}, f32[8,16,128]{2,1,0:T(8,128)}) custom-call(s32[2]{0:T(128)} %pad_add_fusion.place_ref, bf16[32,104,512]{2,1,0:T(8,128)(2,1)} %bitcast.6.in_ref, bf16[16,3,512,512]{3,2,1,0:T(8,128)(2,1)} %weights.1.w_ref), custom_call_target="tpu_custom_call" | custom-call | flops 12884901888 | bytes 29360128 | tf_op jit(solution)/shard_map/conv/pallas_call | solution.py:361
  97.0 0.0 copy-start.7
  97.0 0.0 copy-start.8
  97.0 4.3 %all-to-all-start.1 = ((f32[1,8,16,128]{3,2,0,1:T(8,128)}), f32[1,8,16,128]{3,2,0,1:T(8,128)S(1)}, u32[]{:S(2)}, u32[]{:S(2)}) async-start(f32[1,8,16,128]{3,2,0,1:T(8,128)} %bitcast.35), calls=%async_computation.1 | async-start | bytes 131072 | tf_op jit(solution)/shard_map/all_to_all | solution.py:321
  101.3 0.0 copy-done
  101.3 0.0 copy-done.1
  101.3 1.2 convolution_convert_fusion.update_ref
  102.5 3.7 %all-to-all-done.1 = f32[1,8,16,128]{3,2,0,1:T(8,128)S(1)} async-done(((f32[1,8,16,128]{3,2,0,1:T(8,128)}), f32[1,8,16,128]{3,2,0,1:T(8,128)S(1)}, u32[]{:S(2)}, u32[]{:S(2)}) %all-to-all-start.1) | async-done | bytes 65568 | tf_op jit(solution)/shard_map/all_to_all | solution.py:321
  106.2 0.0 copy-start.2
  106.2 0.6 copy-done.2
  106.8 1.6 merge.1
  108.4 5.1 %all-to-all-start.2 = ((f32[1,16,16,128]{3,2,0,1:T(8,128)}), f32[1,16,16,128]{3,2,0,1:T(8,128)S(1)}, u32[]{:S(2)}, u32[]{:S(2)}) async-start(f32[1,16,16,128]{3,2,0,1:T(8,128)} %bitcast.32), calls=%async_computation.2 | async-start | bytes 262144 | tf_op jit(solution)/shard_map/all_to_all | solution.py:321
  113.6 0.0 copy-done.7
  113.6 0.0 copy-done.8
  113.6 1.3 fusion.score_ref
  114.8 5.4 %all-to-all-done.2 = f32[1,16,16,128]{3,2,0,1:T(8,128)S(1)} async-done(((f32[1,16,16,128]{3,2,0,1:T(8,128)}), f32[1,16,16,128]{3,2,0,1:T(8,128)S(1)}, u32[]{:S(2)}, u32[]{:S(2)}) %all-to-all-start.2) | async-done | bytes 131104 | tf_op jit(solution)/shard_map/all_to_all | solution.py:321
  120.2 0.0 copy-start.5
  120.2 0.7 copy-done.5
  120.9 8.5 %attend.1 = bf16[32,64,512]{2,1,0:T(8,128)(2,1)} custom-call(bf16[64,2,16,512]{3,2,1,0:T(8,128)(2,1)} %get-tuple-element.13.mid_ref, f32[16,16,128]{2,1,0:T(8,128)} %bitcast.34, bf16[512,512]{1,0:T(8,128)(2,1)} %fusion.score_ref, bf16[512,512]{1,0:T(8,128)(2,1)} %convolution_convert_fusion.update_ref), custom_call_target="tpu_custom_call" | custom-call | flops 4294967296 | bytes 8388608 | tf_op jit(solution)/shard_map/attend/pallas_call | solution.py:389
  129.4 33.7 %all_to_all.16 = bf16[1,32,64,512]{3,2,0,1:T(8,128)(2,1)S(1)} all-to-all(bf16[1,32,64,512]{3,2,0,1:T(8,128)(2,1)} %bitcast.31), channel_id=1, replica_groups=mesh['x'=4,'y'=4,'core'=2,'rows'=4] {'x','y','core'}, dimensions={1} | all-to-all | bytes 4194304 | tf_op jit(solution)/shard_map/all_to_all | solution.py:321
  163.1 1.5 copy.12
Async XLA Ops:
  0.0 101.3 %copy-start = (bf16[512,512]{1,0:T(8,128)(2,1)S(1)}, bf16[512,512]{1,0:T(8,128)(2,1)}, u32[]{:S(2)}) copy-start(bf16[512,512]{1,0:T(8,128)(2,1)} %param.10) | copy-start | bytes 1572868
  4.2 9.3 %collective-permute-start = (bf16[144,512]{1,0:T(8,128)(2,1)}, bf16[144,512]{1,0:T(8,128)(2,1)S(1)}, u32[]{:S(2)}, u32[]{:S(2)}) collective-permute-start(bf16[144,512]{1,0:T(8,128)(2,1)} %get-tuple-element.10), channel_id=1, source_target_pairs={{0,1},{1,2},{2,3},{3,0},{4,5},{5,6},{6,7},{7,4},{8,9},{9,10},{10,1... | collective-permute-start | bytes 442376 | tf_op jit(solution)/shard_map/ppermute | solution.py:334
  6.6 6.8 %collective-permute-start.1 = (bf16[144,512]{1,0:T(8,128)(2,1)}, bf16[144,512]{1,0:T(8,128)(2,1)S(1)}, u32[]{:S(2)}, u32[]{:S(2)}) collective-permute-start(bf16[144,512]{1,0:T(8,128)(2,1)} %get-tuple-element.11), channel_id=1, source_target_pairs={{0,3},{1,0},{2,1},{3,2},{4,7},{5,4},{6,5},{7,6},{8,11},{9,8},{10,9... | collective-permute-start | bytes 442376 | tf_op jit(solution)/shard_map/ppermute | solution.py:334
  8.8 4.7 %collective-permute-start.2 = (bf16[16,512]{1,0:T(8,128)(2,1)}, bf16[16,512]{1,0:T(8,128)(2,1)S(1)}, u32[]{:S(2)}, u32[]{:S(2)}) collective-permute-start(bf16[16,512]{1,0:T(8,128)(2,1)} %get-tuple-element.12.own_ref), channel_id=1, source_target_pairs={{0,2},{1,3},{2,0},{3,1},{4,6},{5,7},{6,4},{7,5},{8,10},{9,11},{10,... | collective-permute-start | bytes 49160 | tf_op jit(solution)/shard_map/ppermute | solution.py:334
  13.5 0.6 copy-start.6
  13.5 0.7 copy-start.3
  13.5 0.7 copy-start.4
  19.0 51.7 %all-to-all-start = ((bf16[1,32,104,512]{3,2,0,1:T(8,128)(2,1)}), bf16[1,32,104,512]{3,2,0,1:T(8,128)(2,1)}, u32[]{:S(2)}, u32[]{:S(2)}) async-start(bf16[1,32,104,512]{3,2,0,1:T(8,128)(2,1)} %bitcast.27), calls=%async_computation | async-start | bytes 6815744 | tf_op jit(solution)/shard_map/all_to_all | solution.py:321
  70.7 30.6 %copy-start.1 = (bf16[512,512]{1,0:T(8,128)(2,1)S(1)}, bf16[512,512]{1,0:T(8,128)(2,1)}, u32[]{:S(2)}) copy-start(bf16[512,512]{1,0:T(8,128)(2,1)} %param.11) | copy-start | bytes 1572868
  97.0 16.6 %copy-start.7 = (bf16[512,512]{1,0:T(8,128)(2,1)S(1)}, bf16[512,512]{1,0:T(8,128)(2,1)}, u32[]{:S(2)}) copy-start(bf16[512,512]{1,0:T(8,128)(2,1)} %param.8) | copy-start | bytes 1572868
  97.0 16.6 %copy-start.8 = (bf16[512,512]{1,0:T(8,128)(2,1)S(1)}, bf16[512,512]{1,0:T(8,128)(2,1)}, u32[]{:S(2)}) copy-start(bf16[512,512]{1,0:T(8,128)(2,1)} %param.9) | copy-start | bytes 1572868
  97.0 9.2 %all-to-all-start.1 = ((f32[1,8,16,128]{3,2,0,1:T(8,128)}), f32[1,8,16,128]{3,2,0,1:T(8,128)S(1)}, u32[]{:S(2)}, u32[]{:S(2)}) async-start(f32[1,8,16,128]{3,2,0,1:T(8,128)} %bitcast.35), calls=%async_computation.1 | async-start | bytes 131072 | tf_op jit(solution)/shard_map/all_to_all | solution.py:321
  106.2 0.6 copy-start.2
  108.4 11.8 %all-to-all-start.2 = ((f32[1,16,16,128]{3,2,0,1:T(8,128)}), f32[1,16,16,128]{3,2,0,1:T(8,128)S(1)}, u32[]{:S(2)}, u32[]{:S(2)}) async-start(f32[1,16,16,128]{3,2,0,1:T(8,128)} %bitcast.32), calls=%async_computation.2 | async-start | bytes 262144 | tf_op jit(solution)/shard_map/all_to_all | solution.py:321
  120.2 0.7 copy-start.5

commit v6 on v5

--- a/solution.py
+++ b/solution.py
@@ -12,7 +12,7 @@
 S = 8
 W = S + 2
 P2 = T // 2
-MSG = 104
+RIM = 40
 TM = ("x", "y", "core")
 EPS = 1e-6
 BF, F32 = jnp.bfloat16, jnp.float32
@@ -101,39 +101,38 @@
     return jnp.where(is_mean, whole, lax.rsqrt(whole * (1.0 / count) + EPS))
 
 
-def message_kernel(x_ref, up_ref, down_ref, own_ref, far_ref, out_ref, wide, sides):
-    step = pl.program_id(0)
-
-    @pl.when(step == 0)
-    def _():
-        n = 2048.0 * 16.0
-        parts = [own_ref[...], far_ref[...], up_ref[128:, :], down_ref[128:, :]]
-        whole = merge(jnp.stack([join_terms(v)[:8] for v in parts]), n)
-        row = split_terms(jnp.where(iota(whole.shape, 1) < 64, finish(whole, 4.0 * n), 0.0))
-        for q in range(4):
-            lanes = slice(128 * q, 128 * q + 128)
-            wide[q, 0] = up_ref[:128, lanes].astype(F32)
-            wide[q, 17] = down_ref[:128, lanes].astype(F32)
-            wide[q, 1:17] = x_ref[:, :, lanes].astype(F32)
-            for half in range(2):
-                sides[q, half] = jnp.zeros((16 * 24, 128), F32)
-                sides[q, half, pl.ds(20, 16, stride=24), :] = jnp.broadcast_to(row[:1, lanes], (16, 128))
-                for r in range(W):
-                    left = wide[q, S * half + r, pl.ds(7, 15, stride=8), :]
-                    right = wide[q, S * half + r, pl.ds(8, 15, stride=8), :]
-                    sides[q, half, pl.ds(24 + r, 15, stride=24), :] = left
-                    sides[q, half, pl.ds(W + r, 15, stride=24), :] = right
-
+def inner_kernel(x_ref, out_ref):
+    x = x_ref[...].astype(F32).reshape(2, S, 4, S, C)
     for k in range(4):
         for half in range(2):
-            cb = 4 * step + k
-            cols = pl.ds(pl.multiple_of(8 * cb, 8), 8)
-            rows = pl.ds(pl.multiple_of(24 * cb, 8), 24)
-            for q in range(4):
-                main = wide[q, S * half : S * half + W, cols, :].reshape(W * S, 128)
-                side = sides[q, half, rows, :]
-                message = jnp.concatenate([main, side], axis=0).astype(BF)
-                out_ref[2 * k + half, :, 128 * q : 128 * q + 128] = message
+            out_ref[2 * k + half] = x[half, :, k].reshape(S * S, C).astype(BF)
+
+
+def rim_kernel(x_ref, up_ref, down_ref, own_ref, far_ref, out_ref):
+    pair = pl.program_id(0)
+    n = 2048.0 * 16.0
+    parts = [own_ref[...], far_ref[...], up_ref[128:, :], down_ref[128:, :]]
+    whole = merge(jnp.stack([join_terms(v)[:8] for v in parts]), n)
+    stats = split_terms(jnp.where(iota(whole.shape, 1) < 64, finish(whole, 4.0 * n), 0.0))[:1]
+    for odd in range(2):
+        start = 16 * pair if odd else 16 * pair - 16
+        start = jnp.clip(start, 0, 96)
+        first = 16 * pair + 8 * odd - 1 - start
+        start = pl.multiple_of(start, 16)
+        p, source = iota((RIM, W * 32), 0), iota((RIM, W * 32), 1)
+        r = jnp.where(p < 10, 0, jnp.where(p < 20, 9, jnp.where(p < 28, p - 19, p - 27)))
+        c = jnp.where(p < 10, p, jnp.where(p < 20, p - 10, jnp.where(p < 28, 0, 9)))
+        column = first + c
+        pick = (source == r * 32 + column) & (column >= 0) & (column < 32) & (p < 36)
+        pick = pick.astype(BF)
+        for half in range(2):
+            cols = pl.ds(start, 32)
+            if half == 0:
+                block = jnp.concatenate([up_ref[cols, :][None], x_ref[0:9, cols, :]], axis=0)
+            else:
+                block = jnp.concatenate([x_ref[7:16, cols, :], down_ref[cols, :][None]], axis=0)
+            message = dot(pick, block.reshape(W * 32, C))
+            out_ref[2 * odd + half] = jnp.where(iota((RIM, C), 0) == 36, stats, message).astype(BF)
 
 
 def weights_kernel(w_ref, out_ref):
@@ -176,7 +175,7 @@
     return even1 - even, odd1 + even, even - odd1, odd1 - odd
 
 
-def conv_kernel(place_ref, in_ref, w_ref, mid_ref, stats_ref, terms, sides, latent, sums, norm, held, sems):
+def conv_kernel(place_ref, in_ref, rim_ref, w_ref, mid_ref, stats_ref, terms, ends, sides, latent, sums, norm, held, sems):
     def fetch(j, l):
         slot = 4 * (j % 3) + l
         return pltpu.make_async_copy(w_ref.at[4 * j + l], held.at[slot], sems.at[slot])
@@ -189,7 +188,7 @@
     half, column = block % 2, block // 2
     above = (half == 0) & (z == 0)
     below = (half == 1) & (z == 3)
-    tail = in_ref[:, 96:MSG, :].reshape(T * 8, C)
+    tail = rim_ref[:, 32:RIM, :].reshape(T * 8, C)
     row = iota((T, T * 8), 0)
     row = 2 * (row % P2) + row // P2
     pieces = dot((iota((T, T * 8), 1) == row * 8 + 4).astype(BF), tail).astype(BF)
@@ -198,34 +197,42 @@
             dot(pieces[:, 128 * k : 128 * k + 128], from_groups(32 * i, BF)) for k in range(3)
         ).reshape(2, P2, C)
 
-    for first, pixels in ((80, 16), (96, 8)):
-        act = activate(turned(in_ref, first, pixels), norm)
+    for first, pixels in ((0, 16), (16, 16), (32, 8)):
+        act = activate(turned(rim_ref, first, pixels), norm)
         p = iota(act.shape, 0) + first
-        out = (column == 0) & (p < 90) | (column == 15) & (p >= 90)
-        out = out | above & ((p == 80) | (p == 90)) | below & ((p == 89) | (p == 99))
+        out = above & (p < 10) | below & (p >= 10) & (p < 20)
+        out = out | (column == 0) & ((p == 0) | (p == 10) | (p >= 20) & (p < 28))
+        out = out | (column == 15) & ((p == 9) | (p == 19) | (p >= 28))
         for j, v in enumerate(time_terms(jnp.where(out, 0.0, act))):
             for q in range(pixels):
-                if first + q < 100:
-                    sides[j, (first + q - 80) // W, (first + q) % W] = v[q]
+                p = first + q
+                if p < 20:
+                    ends[j, p // 10, p % 10] = v[q]
+                elif p < 36:
+                    sides[j, (p - 20) // S, (p - 20) % S] = v[q]
+
+    def columns(v, j, at):
+        v = v.reshape(2, W // 2, 2, P2, C)
+        even, odd = v[:, :, 0], v[:, :, 1]
+        before, after, odd_before = even[:, :-1], even[:, 1:], odd[:, :-1]
+        for l, u in enumerate((before - after, odd_before + after, after - odd_before, odd_before - odd[:, 1:])):
+            u = u.astype(BF)
+            for i, r in enumerate(at):
+                terms[j, l, r] = u[i]
+
+    for j in range(4):
+        columns(ends[j], j, (0, W - 1))
 
     def two_rows(k, _):
         first = pl.multiple_of(16 * k, 16)
         values = turned(in_ref, first, 16)
         latent[pl.ds(first, 16)] = values.astype(BF)
-        act = activate(values, norm)
-        r = iota(act.shape, 0) // S + 2 * k
-        act = jnp.where(above & (r == 0) | below & (r == W - 1), 0.0, act)
-        at = pl.ds(2 * k, 2)
-        for j, v in enumerate(time_terms(act)):
-            left, right = sides[j, 0, at][:, None], sides[j, 1, at][:, None]
-            v = jnp.concatenate([left, v.reshape(2, S, P2, C), right], axis=1).reshape(2, W // 2, 2, P2, C)
-            even, odd = v[:, :, 0], v[:, :, 1]
-            before, after, odd_before = even[:, :-1], even[:, 1:], odd[:, :-1]
-            for l, u in enumerate((before - after, odd_before + after, after - odd_before, odd_before - odd[:, 1:])):
-                terms[j, l, at] = u.astype(BF)
+        for j, v in enumerate(time_terms(activate(values, norm))):
+            left, right = (sides[j, i, pl.ds(2 * k, 2)][:, None] for i in range(2))
+            columns(jnp.concatenate([left, v.reshape(2, S, P2, C), right], axis=1), j, (2 * k + 1, 2 * k + 2))
         return 0
 
-    lax.fori_loop(0, W // 2, two_rows, 0)
+    lax.fori_loop(0, S // 2, two_rows, 0)
 
     def term(j, _):
         @pl.when(j == 1)
@@ -251,7 +258,7 @@
         for c in range(S):
             m = [sums[j, c % 2, r, c // 2] for j in range(4)]
             for i, v in enumerate((m[0] + m[1] + m[2], m[1] - m[2] - m[3])):
-                v = (latent[S * r + S + c, i].astype(F32) + v).astype(BF)
+                v = (latent[S * r + c, i].astype(F32) + v).astype(BF)
                 mid_ref[S * r + c, i] = v
                 total[i] = total[i] + v.astype(F32)
         return total
@@ -321,6 +328,17 @@
     exchange = lambda v, axes: lax.all_to_all(v[None], axes, split_axis=1, concat_axis=0, tiled=True)[:, 0]
     place = jnp.stack([lax.axis_index(TM), lax.axis_index("rows")]).astype(jnp.int32)
 
+    inner = pl.pallas_call(
+        inner_kernel,
+        grid=(4,),
+        out_shape=jax.ShapeDtypeStruct((32, S * S, C), BF),
+        in_specs=[pl.BlockSpec((16, 32, C), lambda i: (0, i, 0))],
+        out_specs=pl.BlockSpec((8, S * S, C), lambda i: (i, 0, 0)),
+        compiler_params=params(),
+        cost_estimate=cost(2**20, 4 * 2**20),
+        name="inner",
+    )(x)
+    patch = exchange(inner, TM)
     row = jax.ShapeDtypeStruct((144, C), BF)
     up, down, own = pl.pallas_call(
         latent_stats_kernel,
@@ -333,18 +351,18 @@
     )(x.reshape(2048, C))
     around = lambda v, by: lax.ppermute(v, "rows", [(i, (i + by) % 4) for i in range(4)])
     up, down, far = around(up, 1), around(down, 3), around(own, 2)
-    messages = pl.pallas_call(
-        message_kernel,
-        grid=(4,),
-        out_shape=jax.ShapeDtypeStruct((32, MSG, C), BF),
+    rim = pl.pallas_call(
+        rim_kernel,
+        grid=(8,),
+        out_shape=jax.ShapeDtypeStruct((32, RIM, C), BF),
         in_specs=[whole(16, 128, C), whole(144, C), whole(144, C), whole(16, C), whole(16, C)],
-        out_specs=pl.BlockSpec((8, MSG, C), lambda i: (i, 0, 0)),
-        scratch_shapes=[pltpu.VMEM((4, 18, 128, 128), F32), pltpu.VMEM((4, 2, 16 * 24, 128), F32)],
-        compiler_params=params(),
-        cost_estimate=cost(2**22, 6 * 2**20),
-        name="messages",
+        out_specs=pl.BlockSpec((4, RIM, C), lambda i: (i, 0, 0)),
+        compiler_params=params(),
+        cost_estimate=cost(32 * RIM * 320 * C * 2, 4 * 2**20),
+        name="rim",
     )(x, up, down, own, far)
-    patch = exchange(messages, TM)
+    rim, patch, conv_weight = lax.optimization_barrier((rim, patch, conv_weight))
+    rim = exchange(rim, TM)
     weights = pl.pallas_call(
         weights_kernel,
         grid=(3, 4),
@@ -361,12 +379,13 @@
     mid, stats = pl.pallas_call(
         conv_kernel,
         out_shape=(jax.ShapeDtypeStruct((S * S, 2, P2, C), BF), jax.ShapeDtypeStruct((8, P2, 128), F32)),
-        in_specs=[smem, vmem, pl.BlockSpec(memory_space=pl.ANY)],
+        in_specs=[smem, vmem, vmem, pl.BlockSpec(memory_space=pl.ANY)],
         out_specs=(vmem, vmem),
         scratch_shapes=[
             pltpu.VMEM((4, 4, W, S // 2, P2, C), BF),
             pltpu.VMEM((4, 2, W, P2, C), F32),
-            pltpu.VMEM((W * S, 2, P2, C), BF),
+            pltpu.VMEM((4, 2, S, P2, C), F32),
+            pltpu.VMEM((S * S, 2, P2, C), BF),
             pltpu.VMEM((4, 2, S, S // 2, P2, C), F32),
             pltpu.VMEM((2, 2, P2, C), F32),
             pltpu.VMEM((12, 3, C, C), BF),
@@ -375,7 +394,7 @@
         compiler_params=params(),
         cost_estimate=cost(512 * 48 * C * C * 2, 28 * 2**20),
         name="conv",
-    )(place, patch, weights)
+    )(place, patch, rim, weights)
     parts = pl.pallas_call(
         merge_kernel,
         out_shape=jax.ShapeDtypeStruct((16, P2, 128), F32),

time: 166 us -> 163 us (0.982)
  waiting for transfers between devices: 36 us -> 21.4 us
  starting transfers between devices: 24.3 us -> 30.8 us
  Pallas kernels: 64 us -> 68.6 us
    all_to_all x3 -> x4, waiting for transfers between devices: 32.6 us -> 17.2 us  [local(): lax.all_to_all(v[None], axes, split_axis=1, concat_axis=0, tiled=True)[:, 0]]
    all_to_all x3 -> x4, starting transfers between devices: 18.4 us -> 25.7 us  [local(): lax.all_to_all(v[None], axes, split_axis=1, concat_axis=0, tiled=True)[:, 0]]
    pallas_call x1 -> x2, Pallas kernels: 4.87 us -> 10 us  [the longest x1 6.19 us: local(): pl.pallas_call(rim_kernel, grid=(8,), out_shape=jax.ShapeDtypeStruct((32,...]
  transfers between devices with their start and end apart: 6 -> 7, of which waited for: 4 -> 5; matrix products, arithmetic and copies ran while one was open for 2% -> 2% of each run, Pallas kernels for 11% -> 18%
where the time goes in v6:
time: 163 us; the launch traced here: 162 us
  Pallas kernels  68.6 us (42%)
  blocking collectives  33.7 us (21%)
  starting transfers between devices  30.8 us (19%)
  waiting for transfers between devices  21.4 us (13%)
  local copies, waits for them, and re-layouts  4.18 us (3%)
  matrix products  2.52 us (2%)
    all_to_all x1, blocking collectives, local(): lax.all_to_all(v[None], axes, split_axis=1, concat_axis=0, tiled=True)[:, 0]  33.7 us
    pallas_call x1, Pallas kernels, local(): pl.pallas_call(conv_kernel, out_shape=(jax.ShapeDtypeStruct((S * S, 2, P2...  25.8 us
    all_to_all x4, starting transfers between devices, local(): lax.all_to_all(v[None], axes, split_axis=1, concat_axis=0, tiled=True)[:, 0]  25.7 us
    pallas_call x1, Pallas kernels, local(): pl.pallas_call(weights_kernel, grid=(3, 4), out_shape=jax.ShapeDtypeStruc...  18.6 us
    all_to_all x4, waiting for transfers between devices, local(): lax.all_to_all(v[None], axes, split_axis=1, concat_axis=0, tiled=True)[:, 0]  17.2 us
    pallas_call x1, Pallas kernels, local(): pl.pallas_call(attend_kernel, grid=(S * S // pixels,), out_shape=jax.Shap...  8.49 us
    pallas_call x1, Pallas kernels, local(): pl.pallas_call(rim_kernel, grid=(8,), out_shape=jax.ShapeDtypeStruct((32,...  6.19 us
    ppermute x3, starting transfers between devices, local(): lax.ppermute(v, 'rows', [(i, (i + by) % 4) for i in range(4)])  5.06 us
  transfers between devices with their start and end apart: 7, of which 5 were waited for; matrix products, arithmetic and copies ran while one was open for 2% of the time, Pallas kernels for 18%

profile of v6, /device:TPU:1, one launch (start us, length us, event | category | flops | bytes accessed | tf_op | source)
XLA Modules:
  0.0 161.9 jit_solution(8354431078199263365)
XLA Ops:
  0.0 0.0 copy-start
  0.0 3.8 %inner.1 = bf16[32,64,512]{2,1,0:T(8,128)(2,1)} custom-call(bf16[16,128,512]{2,1,0:T(8,128)(2,1)} %bitcast.31), custom_call_target="tpu_custom_call" | custom-call | flops 1048576 | bytes 4194304 | tf_op jit(solution)/shard_map/inner/pallas_call | solution.py:331
  3.8 8.6 %all-to-all-start = ((bf16[1,32,64,512]{3,2,0,1:T(8,128)(2,1)}), bf16[1,32,64,512]{3,2,0,1:T(8,128)(2,1)S(1)}, u32[]{:S(2)}, u32[]{:S(2)}) async-start(bf16[1,32,64,512]{3,2,0,1:T(8,128)(2,1)} %bitcast.34), calls=%async_computation | async-start | bytes 4194304 | tf_op jit(solution)/shard_map/all_to_all | solution.py:328
  12.4 4.1 %latent_stats.1 = (bf16[144,512]{1,0:T(8,128)(2,1)}, bf16[144,512]{1,0:T(8,128)(2,1)}, bf16[16,512]{1,0:T(8,128)(2,1)}) custom-call(bf16[2048,512]{1,0:T(8,128)(2,1)} %bitcast.32), custom_call_target="tpu_custom_call" | custom-call | flops 4194304 | bytes 2097152 | tf_op jit(solution)/shard_map/latent_stats/pallas_call | solution.py:343
  16.6 1.6 %collective-permute-start = (bf16[144,512]{1,0:T(8,128)(2,1)}, bf16[144,512]{1,0:T(8,128)(2,1)S(1)}, u32[]{:S(2)}, u32[]{:S(2)}) collective-permute-start(bf16[144,512]{1,0:T(8,128)(2,1)} %get-tuple-element.13), channel_id=1, source_target_pairs={{0,1},{1,2},{2,3},{3,0},{4,5},{5,6},{6,7},{7,4},{8,9},{9,10},{10,1... | collective-permute-start | bytes 442376 | tf_op jit(solution)/shard_map/ppermute | solution.py:352
  18.2 2.1 %collective-permute-start.1 = (bf16[144,512]{1,0:T(8,128)(2,1)}, bf16[144,512]{1,0:T(8,128)(2,1)S(1)}, u32[]{:S(2)}, u32[]{:S(2)}) collective-permute-start(bf16[144,512]{1,0:T(8,128)(2,1)} %get-tuple-element.14), channel_id=1, source_target_pairs={{0,3},{1,0},{2,1},{3,2},{4,7},{5,4},{6,5},{7,6},{8,11},{9,8},{10,9... | collective-permute-start | bytes 442376 | tf_op jit(solution)/shard_map/ppermute | solution.py:352
  20.3 1.3 collective-permute-start.2
  21.6 4.2 %collective-permute-done.2.far_ref = bf16[16,512]{1,0:T(8,128)(2,1)S(1)} collective-permute-done((bf16[16,512]{1,0:T(8,128)(2,1)}, bf16[16,512]{1,0:T(8,128)(2,1)S(1)}, u32[]{:S(2)}, u32[]{:S(2)}) %collective-permute-start.2) | collective-permute-done | bytes 16416 | tf_op jit(solution)/shard_map/ppermute | solution.py:352
  25.8 0.0 copy-start.7
  25.8 0.0 collective-permute-done.up_ref
  25.8 0.0 copy-start.4
  25.8 0.0 collective-permute-done.1.down_ref
  25.8 0.6 copy-done.7
  26.4 0.1 copy-done.4
  26.5 0.0 copy-start.5
  26.5 0.7 copy-done.5
  27.2 6.2 %rim.1 = bf16[32,40,512]{2,1,0:T(8,128)(2,1)} custom-call(bf16[16,128,512]{2,1,0:T(8,128)(2,1)} %bitcast.33, bf16[144,512]{1,0:T(8,128)(2,1)} %copy-done.4, bf16[144,512]{1,0:T(8,128)(2,1)} %copy-done.5, bf16[16,512]{1,0:T(8,128)(2,1)} %get-tuple-element.15.own_ref, bf16[16,512]{1,0:T(8,128)(2,1)} %copy-done.7), custom_call_target="tpu_custom_call" | custom-call | flops 419430400 | bytes 4194304 | tf_op jit(solution)/shard_map/rim/pallas_call | solution.py:354
  33.3 7.4 %all-to-all-done = bf16[1,32,64,512]{3,2,0,1:T(8,128)(2,1)S(1)} async-done(((bf16[1,32,64,512]{3,2,0,1:T(8,128)(2,1)}), bf16[1,32,64,512]{3,2,0,1:T(8,128)(2,1)S(1)}, u32[]{:S(2)}, u32[]{:S(2)}) %all-to-all-start) | async-done | bytes 2097184 | tf_op jit(solution)/shard_map/all_to_all | solution.py:328
  40.7 0.0 copy-start.1
  40.7 5.1 %all-to-all-start.1 = ((bf16[1,32,40,512]{3,2,0,1:T(8,128)(2,1)}), bf16[1,32,40,512]{3,2,0,1:T(8,128)(2,1)}, u32[]{:S(2)}, u32[]{:S(2)}) async-start(bf16[1,32,40,512]{3,2,0,1:T(8,128)(2,1)} %bitcast.36), calls=%async_computation.1 | async-start | bytes 2621440 | tf_op jit(solution)/shard_map/all_to_all | solution.py:328
  45.9 0.7 pad_add_fusion.place_ref
  46.5 18.6 %weights.1.w_ref = bf16[16,3,512,512]{3,2,1,0:T(8,128)(2,1)} custom-call(bf16[3,3,3,512,512]{4,3,2,1,0:T(8,128)(2,1)} %w_ref), custom_call_target="tpu_custom_call" | custom-call | flops 18874368 | bytes 39321600 | tf_op jit(solution)/shard_map/weights/pallas_call | solution.py:366
  65.2 0.0 copy-done.1
  65.2 0.7 all-to-all-done.1
  65.8 0.0 copy-start.2
  65.8 25.8 %conv.1 = (bf16[64,2,16,512]{3,2,1,0:T(8,128)(2,1)}, f32[8,16,128]{2,1,0:T(8,128)}) custom-call(s32[2]{0:T(128)} %pad_add_fusion.place_ref, bf16[32,64,512]{2,1,0:T(8,128)(2,1)} %bitcast.37, bf16[32,40,512]{2,1,0:T(8,128)(2,1)} %bitcast.9.rim_ref, bf16[16,3,512,512]{3,2,1,0:T(8,128)(2,1)} %weights.1.w_ref), custom_call_target="tpu_custom_call" | custom-call | flops 12884901888 | bytes 29360128 | tf_op jit(solution)/shard_map/conv/pallas_call | solution.py:379
  91.6 0.0 copy-start.8
  91.6 0.0 copy-start.9
  91.7 5.8 %all-to-all-start.2 = ((f32[1,8,16,128]{3,2,0,1:T(8,128)}), f32[1,8,16,128]{3,2,0,1:T(8,128)S(1)}, u32[]{:S(2)}, u32[]{:S(2)}) async-start(f32[1,8,16,128]{3,2,0,1:T(8,128)} %bitcast.42), calls=%async_computation.2 | async-start | bytes 131072 | tf_op jit(solution)/shard_map/all_to_all | solution.py:328
  97.5 0.0 copy-done
  97.5 0.0 copy-done.2
  97.5 1.2 convolution_convert_fusion.update_ref
  98.7 3.7 %all-to-all-done.2 = f32[1,8,16,128]{3,2,0,1:T(8,128)S(1)} async-done(((f32[1,8,16,128]{3,2,0,1:T(8,128)}), f32[1,8,16,128]{3,2,0,1:T(8,128)S(1)}, u32[]{:S(2)}, u32[]{:S(2)}) %all-to-all-start.2) | async-done | bytes 65568 | tf_op jit(solution)/shard_map/all_to_all | solution.py:328
  102.5 0.0 copy-start.3
  102.5 0.6 copy-done.3
  103.1 1.6 merge.1
  104.7 6.1 %all-to-all-start.3 = ((f32[1,16,16,128]{3,2,0,1:T(8,128)}), f32[1,16,16,128]{3,2,0,1:T(8,128)S(1)}, u32[]{:S(2)}, u32[]{:S(2)}) async-start(f32[1,16,16,128]{3,2,0,1:T(8,128)} %bitcast.39), calls=%async_computation.3 | async-start | bytes 262144 | tf_op jit(solution)/shard_map/all_to_all | solution.py:328
  110.8 0.0 copy-done.8
  110.8 0.0 copy-done.9
  110.8 1.3 fusion.score_ref
  112.1 5.4 %all-to-all-done.3 = f32[1,16,16,128]{3,2,0,1:T(8,128)S(1)} async-done(((f32[1,16,16,128]{3,2,0,1:T(8,128)}), f32[1,16,16,128]{3,2,0,1:T(8,128)S(1)}, u32[]{:S(2)}, u32[]{:S(2)}) %all-to-all-start.3) | async-done | bytes 131104 | tf_op jit(solution)/shard_map/all_to_all | solution.py:328
  117.5 0.0 copy-start.6
  117.5 0.7 copy-done.6
  118.2 8.5 %attend.1 = bf16[32,64,512]{2,1,0:T(8,128)(2,1)} custom-call(bf16[64,2,16,512]{3,2,1,0:T(8,128)(2,1)} %get-tuple-element.19.mid_ref, f32[16,16,128]{2,1,0:T(8,128)} %bitcast.41, bf16[512,512]{1,0:T(8,128)(2,1)} %fusion.score_ref, bf16[512,512]{1,0:T(8,128)(2,1)} %convolution_convert_fusion.update_ref), custom_call_target="tpu_custom_call" | custom-call | flops 4294967296 | bytes 8388608 | tf_op jit(solution)/shard_map/attend/pallas_call | solution.py:408
  126.7 33.7 %all_to_all.20 = bf16[1,32,64,512]{3,2,0,1:T(8,128)(2,1)S(1)} all-to-all(bf16[1,32,64,512]{3,2,0,1:T(8,128)(2,1)} %bitcast.38), channel_id=1, replica_groups=mesh['x'=4,'y'=4,'core'=2,'rows'=4] {'x','y','core'}, dimensions={1} | all-to-all | bytes 4194304 | tf_op jit(solution)/shard_map/all_to_all | solution.py:328
  160.4 1.5 copy.13
Async XLA Ops:
  0.0 97.5 %copy-start = (bf16[512,512]{1,0:T(8,128)(2,1)S(1)}, bf16[512,512]{1,0:T(8,128)(2,1)}, u32[]{:S(2)}) copy-start(bf16[512,512]{1,0:T(8,128)(2,1)} %param.10) | copy-start | bytes 1572868
  3.8 36.9 %all-to-all-start = ((bf16[1,32,64,512]{3,2,0,1:T(8,128)(2,1)}), bf16[1,32,64,512]{3,2,0,1:T(8,128)(2,1)S(1)}, u32[]{:S(2)}, u32[]{:S(2)}) async-start(bf16[1,32,64,512]{3,2,0,1:T(8,128)(2,1)} %bitcast.34), calls=%async_computation | async-start | bytes 4194304 | tf_op jit(solution)/shard_map/all_to_all | solution.py:328
  16.6 9.3 %collective-permute-start = (bf16[144,512]{1,0:T(8,128)(2,1)}, bf16[144,512]{1,0:T(8,128)(2,1)S(1)}, u32[]{:S(2)}, u32[]{:S(2)}) collective-permute-start(bf16[144,512]{1,0:T(8,128)(2,1)} %get-tuple-element.13), channel_id=1, source_target_pairs={{0,1},{1,2},{2,3},{3,0},{4,5},{5,6},{6,7},{7,4},{8,9},{9,10},{10,1... | collective-permute-start | bytes 442376 | tf_op jit(solution)/shard_map/ppermute | solution.py:352
  18.2 7.6 %collective-permute-start.1 = (bf16[144,512]{1,0:T(8,128)(2,1)}, bf16[144,512]{1,0:T(8,128)(2,1)S(1)}, u32[]{:S(2)}, u32[]{:S(2)}) collective-permute-start(bf16[144,512]{1,0:T(8,128)(2,1)} %get-tuple-element.14), channel_id=1, source_target_pairs={{0,3},{1,0},{2,1},{3,2},{4,7},{5,4},{6,5},{7,6},{8,11},{9,8},{10,9... | collective-permute-start | bytes 442376 | tf_op jit(solution)/shard_map/ppermute | solution.py:352
  20.3 5.5 %collective-permute-start.2 = (bf16[16,512]{1,0:T(8,128)(2,1)}, bf16[16,512]{1,0:T(8,128)(2,1)S(1)}, u32[]{:S(2)}, u32[]{:S(2)}) collective-permute-start(bf16[16,512]{1,0:T(8,128)(2,1)} %get-tuple-element.15.own_ref), channel_id=1, source_target_pairs={{0,2},{1,3},{2,0},{3,1},{4,6},{5,7},{6,4},{7,5},{8,10},{9,11},{10,... | collective-permute-start | bytes 49160 | tf_op jit(solution)/shard_map/ppermute | solution.py:352
  25.8 0.6 copy-start.7
  25.8 0.7 copy-start.4
  26.5 0.7 copy-start.5
  40.7 24.4 %copy-start.1 = (bf16[1,32,64,512]{3,2,0,1:T(8,128)(2,1)}, bf16[1,32,64,512]{3,2,0,1:T(8,128)(2,1)S(1)}, u32[]{:S(2)}) copy-start(bf16[1,32,64,512]{3,2,0,1:T(8,128)(2,1)S(1)} %all-to-all-done) | copy-start | bytes 6291460
  40.7 25.1 %all-to-all-start.1 = ((bf16[1,32,40,512]{3,2,0,1:T(8,128)(2,1)}), bf16[1,32,40,512]{3,2,0,1:T(8,128)(2,1)}, u32[]{:S(2)}, u32[]{:S(2)}) async-start(bf16[1,32,40,512]{3,2,0,1:T(8,128)(2,1)} %bitcast.36), calls=%async_computation.1 | async-start | bytes 2621440 | tf_op jit(solution)/shard_map/all_to_all | solution.py:328
  65.8 31.7 %copy-start.2 = (bf16[512,512]{1,0:T(8,128)(2,1)S(1)}, bf16[512,512]{1,0:T(8,128)(2,1)}, u32[]{:S(2)}) copy-start(bf16[512,512]{1,0:T(8,128)(2,1)} %param.11) | copy-start | bytes 1572868
  91.6 19.2 %copy-start.8 = (bf16[512,512]{1,0:T(8,128)(2,1)S(1)}, bf16[512,512]{1,0:T(8,128)(2,1)}, u32[]{:S(2)}) copy-start(bf16[512,512]{1,0:T(8,128)(2,1)} %param.8) | copy-start | bytes 1572868
  91.6 19.2 %copy-start.9 = (bf16[512,512]{1,0:T(8,128)(2,1)S(1)}, bf16[512,512]{1,0:T(8,128)(2,1)}, u32[]{:S(2)}) copy-start(bf16[512,512]{1,0:T(8,128)(2,1)} %param.9) | copy-start | bytes 1572868
  91.7 10.8 %all-to-all-start.2 = ((f32[1,8,16,128]{3,2,0,1:T(8,128)}), f32[1,8,16,128]{3,2,0,1:T(8,128)S(1)}, u32[]{:S(2)}, u32[]{:S(2)}) async-start(f32[1,8,16,128]{3,2,0,1:T(8,128)} %bitcast.42), calls=%async_computation.2 | async-start | bytes 131072 | tf_op jit(solution)/shard_map/all_to_all | solution.py:328
  102.5 0.6 copy-start.3
  104.7 12.8 %all-to-all-start.3 = ((f32[1,16,16,128]{3,2,0,1:T(8,128)}), f32[1,16,16,128]{3,2,0,1:T(8,128)S(1)}, u32[]{:S(2)}, u32[]{:S(2)}) async-start(f32[1,16,16,128]{3,2,0,1:T(8,128)} %bitcast.39), calls=%async_computation.3 | async-start | bytes 262144 | tf_op jit(solution)/shard_map/all_to_all | solution.py:328
  117.5 0.7 copy-start.6

commit v7 on v6

--- a/solution.py
+++ b/solution.py
@@ -12,7 +12,7 @@
 S = 8
 W = S + 2
 P2 = T // 2
-RIM = 40
+RIM = 24
 TM = ("x", "y", "core")
 EPS = 1e-6
 BF, F32 = jnp.bfloat16, jnp.float32
@@ -120,10 +120,10 @@
         first = 16 * pair + 8 * odd - 1 - start
         start = pl.multiple_of(start, 16)
         p, source = iota((RIM, W * 32), 0), iota((RIM, W * 32), 1)
-        r = jnp.where(p < 10, 0, jnp.where(p < 20, 9, jnp.where(p < 28, p - 19, p - 27)))
-        c = jnp.where(p < 10, p, jnp.where(p < 20, p - 10, jnp.where(p < 28, 0, 9)))
+        r = jnp.where(p < 16, p % S + 1, jnp.where(p < 18, 0, 9))
+        c = jnp.where(p < 16, jnp.where(p < 8, 0, 9), jnp.where(p % 2 == 0, 0, 9))
         column = first + c
-        pick = (source == r * 32 + column) & (column >= 0) & (column < 32) & (p < 36)
+        pick = (source == r * 32 + column) & (column >= 0) & (column < 32) & (p < 20)
         pick = pick.astype(BF)
         for half in range(2):
             cols = pl.ds(start, 32)
@@ -132,7 +132,7 @@
             else:
                 block = jnp.concatenate([x_ref[7:16, cols, :], down_ref[cols, :][None]], axis=0)
             message = dot(pick, block.reshape(W * 32, C))
-            out_ref[2 * odd + half] = jnp.where(iota((RIM, C), 0) == 36, stats, message).astype(BF)
+            out_ref[2 * odd + half] = jnp.where(iota((RIM, C), 0) == 20, stats, message).astype(BF)
 
 
 def weights_kernel(w_ref, out_ref):
@@ -145,7 +145,13 @@
     columns = [products(w[a]) for a in range(3)]
     for l in range(4):
         for j, v in enumerate(products([columns[a][l] for a in range(3)])):
-            out_ref[4 * j + l, 0] = v.astype(BF)
+            out_ref[4 * j + l] = v.astype(BF)
+
+
+def products_kernel(wq_ref, wk_ref, wv_ref, wo_ref, score_ref, update_ref):
+    score = lax.dot_general(wq_ref[...], wk_ref[...], (((1,), (1,)), ((), ())), preferred_element_type=F32)
+    score_ref[...] = (score * (1.0 / C**0.5)).astype(BF)
+    update_ref[...] = dot(wv_ref[...], wo_ref[...]).astype(BF)
 
 
 def turned(in_ref, first, pixels):
@@ -175,20 +181,30 @@
     return even1 - even, odd1 + even, even - odd1, odd1 - odd
 
 
-def conv_kernel(place_ref, in_ref, rim_ref, w_ref, mid_ref, stats_ref, terms, ends, sides, latent, sums, norm, held, sems):
+def conv_kernel(
+    place_ref, in_ref, rim_ref, core_ref, band_ref, w0, w1, w2, mid_ref, stats_ref,
+    terms, ends, sides, latent, sums, norm, held, sems,
+):
     def fetch(j, l):
         slot = 4 * (j % 3) + l
-        return pltpu.make_async_copy(w_ref.at[4 * j + l], held.at[slot], sems.at[slot])
+        return [
+            pltpu.make_async_copy(w.at[4 * j + l], held.at[slot, b], sems.at[slot, b])
+            for b, w in enumerate((w0, w1, w2))
+        ]
+
+    def start(j):
+        for l in range(4):
+            for copy in fetch(j, l):
+                copy.start()
 
     for j in range(3):
-        for l in range(4):
-            fetch(j, l).start()
+        start(j)
 
     block, z = place_ref[0], place_ref[1]
     half, column = block % 2, block // 2
     above = (half == 0) & (z == 0)
     below = (half == 1) & (z == 3)
-    tail = rim_ref[:, 32:RIM, :].reshape(T * 8, C)
+    tail = rim_ref[:, 16:RIM, :].reshape(T * 8, C)
     row = iota((T, T * 8), 0)
     row = 2 * (row % P2) + row // P2
     pieces = dot((iota((T, T * 8), 1) == row * 8 + 4).astype(BF), tail).astype(BF)
@@ -197,19 +213,24 @@
             dot(pieces[:, 128 * k : 128 * k + 128], from_groups(32 * i, BF)) for k in range(3)
         ).reshape(2, P2, C)
 
-    for first, pixels in ((0, 16), (16, 16), (32, 8)):
+    for first, pixels in ((0, 16), (16, 8)):
         act = activate(turned(rim_ref, first, pixels), norm)
         p = iota(act.shape, 0) + first
-        out = above & (p < 10) | below & (p >= 10) & (p < 20)
-        out = out | (column == 0) & ((p == 0) | (p == 10) | (p >= 20) & (p < 28))
-        out = out | (column == 15) & ((p == 9) | (p == 19) | (p >= 28))
+        out = (column == 0) & ((p < 8) | (p == 16) | (p == 18))
+        out = out | (column == 15) & ((p >= 8) & (p < 16) | (p == 17) | (p == 19))
+        out = out | above & ((p == 16) | (p == 17)) | below & (p >= 18)
         for j, v in enumerate(time_terms(jnp.where(out, 0.0, act))):
-            for q in range(pixels):
+            for q in range(min(pixels, 20 - first)):
                 p = first + q
-                if p < 20:
-                    ends[j, p // 10, p % 10] = v[q]
-                elif p < 36:
-                    sides[j, (p - 20) // S, (p - 20) % S] = v[q]
+                if p < 16:
+                    sides[j, p // S, p % S] = v[q]
+                else:
+                    ends[j, (p - 16) // 2, (p % 2) * (W - 1)] = v[q]
+    core, band = turned(core_ref, 0, S), turned(band_ref, 0, S)
+    for i, values in enumerate((jnp.where(half == 0, band, core), jnp.where(half == 0, core, band))):
+        act = jnp.where(below if i else above, 0.0, activate(values, norm))
+        for j, v in enumerate(time_terms(act)):
+            ends[j, i, 1 : S + 1] = v
 
     def columns(v, j, at):
         v = v.reshape(2, W // 2, 2, P2, C)
@@ -237,11 +258,11 @@
     def term(j, _):
         @pl.when(j == 1)
         def _():
-            for l in range(4):
-                fetch(j + 2, l).start()
+            start(j + 2)
 
         for l in range(4):
-            fetch(j, l).wait()
+            for copy in fetch(j, l):
+                copy.wait()
         for q in range(2):
             m = []
             for l in range(4):
@@ -349,6 +370,16 @@
         cost_estimate=cost(2048 * C * 4, 2048 * C * 2),
         name="latent_stats",
     )(x.reshape(2048, C))
+    own, *products = lax.optimization_barrier((own, w_query, w_key, w_value, w_out))
+    score, update = pl.pallas_call(
+        products_kernel,
+        out_shape=(jax.ShapeDtypeStruct((C, C), BF),) * 2,
+        in_specs=[vmem] * 4,
+        out_specs=(vmem,) * 2,
+        compiler_params=params(),
+        cost_estimate=cost(2 * 2 * C**3, 6 * C * C * 2),
+        name="products",
+    )(*products)
     around = lambda v, by: lax.ppermute(v, "rows", [(i, (i + by) % 4) for i in range(4)])
     up, down, far = around(up, 1), around(down, 3), around(own, 2)
     rim = pl.pallas_call(
@@ -361,25 +392,35 @@
         cost_estimate=cost(32 * RIM * 320 * C * 2, 4 * 2**20),
         name="rim",
     )(x, up, down, own, far)
-    rim, patch, conv_weight = lax.optimization_barrier((rim, patch, conv_weight))
+    def combine(b, conv_weight):
+        return pl.pallas_call(
+            weights_kernel,
+            grid=(4,),
+            out_shape=jax.ShapeDtypeStruct((16, C, C), BF),
+            in_specs=[pl.BlockSpec((3, 1, 3, 128, C), lambda i: (0, b, 0, i, 0))],
+            out_specs=pl.BlockSpec((16, 128, C), lambda i: (0, i, 0)),
+            compiler_params=params(),
+            cost_estimate=cost(3 * 8 * C * C, 25 * C * C * 2),
+            name="weights",
+        )(conv_weight)
+
+    rim, early = lax.optimization_barrier((rim, conv_weight))
+    weights = [combine(0, early)]
+    rim, patch = lax.optimization_barrier((rim, patch))
     rim = exchange(rim, TM)
-    weights = pl.pallas_call(
-        weights_kernel,
-        grid=(3, 4),
-        out_shape=jax.ShapeDtypeStruct((16, 3, C, C), BF),
-        in_specs=[pl.BlockSpec((3, 1, 3, 128, C), lambda b, i: (0, b, 0, i, 0))],
-        out_specs=pl.BlockSpec((16, 1, 128, C), lambda b, i: (0, b, i, 0)),
-        compiler_params=params(),
-        cost_estimate=cost(9 * 8 * C * C, 75 * C * C * 2),
-        name="weights",
-    )(conv_weight)
-    score = dot(w_query, w_key.T) * (1.0 / C**0.5)
-    score, update = score.astype(BF), dot(w_value, w_out).astype(BF)
+    first = lax.axis_index("core") == 0
+    row = lambda at: lax.dynamic_slice_in_dim(patch, at, S, axis=1)
+    core, band = row(jnp.where(first, S * S - S, 0)), row(jnp.where(first, 0, S * S - S))
+    core = lax.ppermute(core, "core", [(0, 1), (1, 0)])
+    pairs = [(4 + i, i + 1) for i in range(3)] + [(i + 1, 4 + i) for i in range(3)]
+    band = lax.ppermute(band, ("core", "rows"), pairs)
+    core, band, late = lax.optimization_barrier((core, band, conv_weight))
+    weights += [combine(b, late) for b in (1, 2)]
 
     mid, stats = pl.pallas_call(
         conv_kernel,
         out_shape=(jax.ShapeDtypeStruct((S * S, 2, P2, C), BF), jax.ShapeDtypeStruct((8, P2, 128), F32)),
-        in_specs=[smem, vmem, vmem, pl.BlockSpec(memory_space=pl.ANY)],
+        in_specs=[smem] + [vmem] * 4 + [pl.BlockSpec(memory_space=pl.ANY)] * 3,
         out_specs=(vmem, vmem),
         scratch_shapes=[
             pltpu.VMEM((4, 4, W, S // 2, P2, C), BF),
@@ -389,12 +430,12 @@
             pltpu.VMEM((4, 2, S, S // 2, P2, C), F32),
             pltpu.VMEM((2, 2, P2, C), F32),
             pltpu.VMEM((12, 3, C, C), BF),
-            pltpu.SemaphoreType.DMA((12,)),
+            pltpu.SemaphoreType.DMA((12, 3)),
         ],
         compiler_params=params(),
         cost_estimate=cost(512 * 48 * C * C * 2, 28 * 2**20),
         name="conv",
-    )(place, patch, rim, weights)
+    )(place, patch, rim, core, band, *weights)
     parts = pl.pallas_call(
         merge_kernel,
         out_shape=jax.ShapeDtypeStruct((16, P2, 128), F32),

time: 163 us -> 169 us (1.037)
  blocking collectives: 33.7 us -> 43.8 us
  waiting for transfers between devices: 21.4 us -> 15.5 us
  Pallas kernels: 68.6 us -> 74.4 us
  matrix products: 2.52 us -> 0 us
  starting transfers between devices: 30.8 us -> 29.1 us
    all_to_all x1 -> x2, blocking collectives: 33.7 us -> 43.8 us  [local(): lax.all_to_all(v[None], axes, split_axis=1, concat_axis=0, tiled=True)[:, 0]]
    all_to_all x4 -> x3, waiting for transfers between devices: 17.2 us -> 11.3 us  [local(): lax.all_to_all(v[None], axes, split_axis=1, concat_axis=0, tiled=True)[:, 0]]
    all_to_all x4 -> x3, starting transfers between devices: 25.7 us -> 19.8 us  [local(): lax.all_to_all(v[None], axes, split_axis=1, concat_axis=0, tiled=True)[:, 0]]
    pallas_call x1 -> x4, Pallas kernels: 18.6 us -> 24.4 us  [the longest x3 21.3 us: combine(): pl.pallas_call(weights_kernel, grid=(4,), out_shape=jax.ShapeDtypeStruct(...]
    ppermute x0 -> x2, starting transfers between devices: none -> 4.19 us  [the longest x1 3.76 us: local(): band = lax.ppermute(band, ('core', 'rows'), pairs)]
    dot_general x2 -> x0, matrix products: 2.52 us -> none  [dot(): return jnp.dot(a, b, preferred_element_type=F32, precision=precision)]
  transfers between devices with their start and end apart: 7 -> 8, of which waited for: 5 -> 3; matrix products, arithmetic and copies ran while one was open for 2% -> 0% of each run, Pallas kernels for 18% -> 21%
where the time goes in v7:
time: 169 us; the launch traced here: 168 us
  Pallas kernels  74.4 us (44%)
  blocking collectives  43.8 us (26%)
  starting transfers between devices  29.1 us (17%)
  waiting for transfers between devices  15.5 us (9%)
  local copies, waits for them, and re-layouts  4.44 us (3%)
    all_to_all x2, blocking collectives, local(): lax.all_to_all(v[None], axes, split_axis=1, concat_axis=0, tiled=True)[:, 0]  43.8 us
    pallas_call x1, Pallas kernels, local(): pl.pallas_call(conv_kernel, out_shape=(jax.ShapeDtypeStruct((S * S, 2, P2...  26.1 us
    pallas_call x3, Pallas kernels, combine(): pl.pallas_call(weights_kernel, grid=(4,), out_shape=jax.ShapeDtypeStruct(...  21.3 us
    all_to_all x3, starting transfers between devices, local(): lax.all_to_all(v[None], axes, split_axis=1, concat_axis=0, tiled=True)[:, 0]  19.8 us
    all_to_all x3, waiting for transfers between devices, local(): lax.all_to_all(v[None], axes, split_axis=1, concat_axis=0, tiled=True)[:, 0]  11.3 us
    pallas_call x1, Pallas kernels, local(): pl.pallas_call(attend_kernel, grid=(S * S // pixels,), out_shape=jax.Shap...  8.5 us
    pallas_call x1, Pallas kernels, local(): pl.pallas_call(rim_kernel, grid=(8,), out_shape=jax.ShapeDtypeStruct((32,...  5.96 us
    ppermute x3, starting transfers between devices, local(): lax.ppermute(v, 'rows', [(i, (i + by) % 4) for i in range(4)])  5.06 us
  transfers between devices with their start and end apart: 8, of which 3 were waited for; matrix products, arithmetic and copies ran while one was open for 0% of the time, Pallas kernels for 21%

profile of v7, /device:TPU:1, one launch (start us, length us, event | category | flops | bytes accessed | tf_op | source)
XLA Modules:
  0.0 167.9 jit_solution(4629803860979184893)
XLA Ops:
  0.0 3.8 %inner.1 = bf16[32,64,512]{2,1,0:T(8,128)(2,1)} custom-call(bf16[16,128,512]{2,1,0:T(8,128)(2,1)} %bitcast.27), custom_call_target="tpu_custom_call" | custom-call | flops 1048576 | bytes 4194304 | tf_op jit(solution)/shard_map/inner/pallas_call | solution.py:352
  3.8 8.6 %all-to-all-start = ((bf16[1,32,64,512]{3,2,0,1:T(8,128)(2,1)}), bf16[1,32,64,512]{3,2,0,1:T(8,128)(2,1)S(1)}, u32[]{:S(2)}, u32[]{:S(2)}) async-start(bf16[1,32,64,512]{3,2,0,1:T(8,128)(2,1)} %bitcast.30), calls=%async_computation | async-start | bytes 4194304 | tf_op jit(solution)/shard_map/all_to_all | solution.py:349
  12.4 4.1 %latent_stats.1 = (bf16[144,512]{1,0:T(8,128)(2,1)}, bf16[144,512]{1,0:T(8,128)(2,1)}, bf16[16,512]{1,0:T(8,128)(2,1)}) custom-call(bf16[2048,512]{1,0:T(8,128)(2,1)} %bitcast.28), custom_call_target="tpu_custom_call" | custom-call | flops 4194304 | bytes 2097152 | tf_op jit(solution)/shard_map/latent_stats/pallas_call | solution.py:364
  16.5 1.6 collective-permute-start
  18.1 2.1 %collective-permute-start.1 = (bf16[144,512]{1,0:T(8,128)(2,1)}, bf16[144,512]{1,0:T(8,128)(2,1)S(1)}, u32[]{:S(2)}, u32[]{:S(2)}) collective-permute-start(bf16[144,512]{1,0:T(8,128)(2,1)} %get-tuple-element.25), channel_id=1, source_target_pairs={{0,3},{1,0},{2,1},{3,2},{4,7},{5,4},{6,5},{7,6},{8,11},{9,8},{10,9... | collective-permute-start | bytes 442376 | tf_op jit(solution)/shard_map/ppermute | solution.py:383
  20.3 1.3 collective-permute-start.2
  21.6 4.2 %collective-permute-done.2.far_ref = bf16[16,512]{1,0:T(8,128)(2,1)S(1)} collective-permute-done((bf16[16,512]{1,0:T(8,128)(2,1)}, bf16[16,512]{1,0:T(8,128)(2,1)S(1)}, u32[]{:S(2)}, u32[]{:S(2)}) %collective-permute-start.2) | collective-permute-done | bytes 16416 | tf_op jit(solution)/shard_map/ppermute | solution.py:383
  25.8 0.0 copy-start.5
  25.8 0.0 collective-permute-done.up_ref
  25.8 0.0 copy-start.2
  25.8 0.0 collective-permute-done.1.down_ref
  25.8 0.6 copy-done.5
  26.3 0.1 copy-done.2
  26.4 0.0 copy-start.3
  26.4 0.7 copy-done.3
  27.1 6.0 %rim.1 = bf16[32,24,512]{2,1,0:T(8,128)(2,1)} custom-call(bf16[16,128,512]{2,1,0:T(8,128)(2,1)} %bitcast.29, bf16[144,512]{1,0:T(8,128)(2,1)} %copy-done.2, bf16[144,512]{1,0:T(8,128)(2,1)} %copy-done.3, bf16[16,512]{1,0:T(8,128)(2,1)} %get-tuple-element.27.own_ref, bf16[16,512]{1,0:T(8,128)(2,1)} %copy-done.5), custom_call_target="tpu_custom_call" | custom-call | flops 251658240 | bytes 4194304 | tf_op jit(solution)/shard_map/rim/pallas_call | solution.py:385
  33.0 7.6 %all-to-all-done = bf16[1,32,64,512]{3,2,0,1:T(8,128)(2,1)S(1)} async-done(((bf16[1,32,64,512]{3,2,0,1:T(8,128)(2,1)}), bf16[1,32,64,512]{3,2,0,1:T(8,128)(2,1)S(1)}, u32[]{:S(2)}, u32[]{:S(2)}) %all-to-all-start) | async-done | bytes 2097184 | tf_op jit(solution)/shard_map/all_to_all | solution.py:349
  40.7 0.0 copy-start
  40.7 4.4 %all-to-all-start.1 = ((bf16[1,32,24,512]{3,2,0,1:T(8,128)(2,1)}), bf16[1,32,24,512]{3,2,0,1:T(8,128)(2,1)S(1)}, u32[]{:S(2)}, u32[]{:S(2)}) async-start(bf16[1,32,24,512]{3,2,0,1:T(8,128)(2,1)} %bitcast.34), calls=%async_computation.1 | async-start | bytes 1572864 | tf_op jit(solution)/shard_map/all_to_all | solution.py:349
  45.2 0.4 collective-permute-start.3
  45.6 3.8 %collective-permute-start.4 = (bf16[32,8,512]{2,1,0:T(8,128)(2,1)S(1)}, bf16[32,8,512]{2,1,0:T(8,128)(2,1)}, u32[]{:S(2)}, u32[]{:S(2)}) collective-permute-start(bf16[32,8,512]{2,1,0:T(8,128)(2,1)S(1)} %get-tuple-element.43), channel_id=1, source_target_pairs={{4,1},{5,2},{6,3},{1,4},{2,5},{3,6},{12,9},{13,10},{14,11},{9,12},... | collective-permute-start | bytes 786440 | tf_op jit(solution)/shard_map/ppermute | solution.py:416
  49.4 0.6 pad_add_fusion.place_ref
  50.0 7.1 %weights.3.w0 = bf16[16,512,512]{2,1,0:T(8,128)(2,1)} custom-call(bf16[3,3,3,512,512]{4,3,2,1,0:T(8,128)(2,1)} %w_ref.2), custom_call_target="tpu_custom_call" | custom-call | flops 6291456 | bytes 13107200 | tf_op jit(solution)/shard_map/weights/pallas_call | solution.py:396
  57.1 0.0 copy-done
  57.1 0.0 collective-permute-done.3.core_ref
  57.1 0.0 collective-permute-done.4.band_ref
  57.1 7.1 %weights.4.w1 = bf16[16,512,512]{2,1,0:T(8,128)(2,1)} custom-call(bf16[3,3,3,512,512]{4,3,2,1,0:T(8,128)(2,1)} %w_ref.2), custom_call_target="tpu_custom_call" | custom-call | flops 6291456 | bytes 13107200 | tf_op jit(solution)/shard_map/weights/pallas_call | solution.py:396
  64.2 7.1 %weights.5.w2 = bf16[16,512,512]{2,1,0:T(8,128)(2,1)} custom-call(bf16[3,3,3,512,512]{4,3,2,1,0:T(8,128)(2,1)} %w_ref.2), custom_call_target="tpu_custom_call" | custom-call | flops 6291456 | bytes 13107200 | tf_op jit(solution)/shard_map/weights/pallas_call | solution.py:396
  71.3 0.0 all-to-all-done.1
  71.3 0.0 copy-start.1
  71.3 0.9 copy-done.1
  72.2 26.1 %conv.1 = (bf16[64,2,16,512]{3,2,1,0:T(8,128)(2,1)}, f32[8,16,128]{2,1,0:T(8,128)}) custom-call(s32[2]{0:T(128)} %pad_add_fusion.place_ref, bf16[32,64,512]{2,1,0:T(8,128)(2,1)} %bitcast.33, bf16[32,24,512]{2,1,0:T(8,128)(2,1)} %bitcast.36, bf16[32,8,512]{2,1,0:T(8,128)(2,1)} %collective-permute-done.3.core_ref, ...), custom_call_target="tpu_custom_call" | custom-call | flops 12884901888 | bytes 29360128 | tf_op jit(solution)/shard_map/conv/pallas_call | solution.py:420
  98.3 10.1 %all_to_all.20 = f32[1,8,16,128]{3,2,0,1:T(8,128)} all-to-all(f32[1,8,16,128]{3,2,0,1:T(8,128)} %bitcast.40), channel_id=1, replica_groups=mesh['x'=4,'y'=4,'core'=2,'rows'=4] {'core','rows'}, dimensions={1} | all-to-all | bytes 131072 | tf_op jit(solution)/shard_map/all_to_all | solution.py:349
  108.4 1.6 merge.1
  109.9 6.8 %all-to-all-start.3 = ((f32[1,16,16,128]{3,2,0,1:T(8,128)}), f32[1,16,16,128]{3,2,0,1:T(8,128)S(1)}, u32[]{:S(2)}, u32[]{:S(2)}) async-start(f32[1,16,16,128]{3,2,0,1:T(8,128)} %bitcast.37), calls=%async_computation.3 | async-start | bytes 262144 | tf_op jit(solution)/shard_map/all_to_all | solution.py:349
  116.8 3.1 %products.1 = (bf16[512,512]{1,0:T(8,128)(2,1)}, bf16[512,512]{1,0:T(8,128)(2,1)}) custom-call(bf16[512,512]{1,0:T(8,128)(2,1)} %wq_ref, bf16[512,512]{1,0:T(8,128)(2,1)} %wk_ref, bf16[512,512]{1,0:T(8,128)(2,1)} %wv_ref, bf16[512,512]{1,0:T(8,128)(2,1)} %wo_ref), custom_call_target="tpu_custom_call" | custom-call | flops 536870912 | bytes 3145728 | tf_op jit(solution)/shard_map/products/pallas_call | solution.py:374
  119.8 3.6 %all-to-all-done.3 = f32[1,16,16,128]{3,2,0,1:T(8,128)S(1)} async-done(((f32[1,16,16,128]{3,2,0,1:T(8,128)}), f32[1,16,16,128]{3,2,0,1:T(8,128)S(1)}, u32[]{:S(2)}, u32[]{:S(2)}) %all-to-all-start.3) | async-done | bytes 131104 | tf_op jit(solution)/shard_map/all_to_all | solution.py:349
  123.4 0.0 copy-start.4
  123.4 0.7 copy-done.4
  124.1 8.5 %attend.1 = bf16[32,64,512]{2,1,0:T(8,128)(2,1)} custom-call(bf16[64,2,16,512]{3,2,1,0:T(8,128)(2,1)} %get-tuple-element.35.mid_ref, f32[16,16,128]{2,1,0:T(8,128)} %bitcast.39, bf16[512,512]{1,0:T(8,128)(2,1)} %get-tuple-element.41.score_ref, bf16[512,512]{1,0:T(8,128)(2,1)} %get-tuple-element.42.update_ref), custom_call_target="tpu_custom_call" | custom-call | flops 4294967296 | bytes 8388608 | tf_op jit(solution)/shard_map/attend/pallas_call | solution.py:449
  132.6 33.7 %all_to_all.21 = bf16[1,32,64,512]{3,2,0,1:T(8,128)(2,1)S(1)} all-to-all(bf16[1,32,64,512]{3,2,0,1:T(8,128)(2,1)} %bitcast.35), channel_id=1, replica_groups=mesh['x'=4,'y'=4,'core'=2,'rows'=4] {'x','y','core'}, dimensions={1} | all-to-all | bytes 4194304 | tf_op jit(solution)/shard_map/all_to_all | solution.py:349
  166.3 1.5 copy.13
  (1 shorter events, 0.0 us)
Async XLA Ops:
  3.8 36.9 %all-to-all-start = ((bf16[1,32,64,512]{3,2,0,1:T(8,128)(2,1)}), bf16[1,32,64,512]{3,2,0,1:T(8,128)(2,1)S(1)}, u32[]{:S(2)}, u32[]{:S(2)}) async-start(bf16[1,32,64,512]{3,2,0,1:T(8,128)(2,1)} %bitcast.30), calls=%async_computation | async-start | bytes 4194304 | tf_op jit(solution)/shard_map/all_to_all | solution.py:349
  16.5 9.3 %collective-permute-start = (bf16[144,512]{1,0:T(8,128)(2,1)}, bf16[144,512]{1,0:T(8,128)(2,1)S(1)}, u32[]{:S(2)}, u32[]{:S(2)}) collective-permute-start(bf16[144,512]{1,0:T(8,128)(2,1)} %get-tuple-element.24), channel_id=1, source_target_pairs={{0,1},{1,2},{2,3},{3,0},{4,5},{5,6},{6,7},{7,4},{8,9},{9,10},{10,1... | collective-permute-start | bytes 442376 | tf_op jit(solution)/shard_map/ppermute | solution.py:383
  18.1 7.6 %collective-permute-start.1 = (bf16[144,512]{1,0:T(8,128)(2,1)}, bf16[144,512]{1,0:T(8,128)(2,1)S(1)}, u32[]{:S(2)}, u32[]{:S(2)}) collective-permute-start(bf16[144,512]{1,0:T(8,128)(2,1)} %get-tuple-element.25), channel_id=1, source_target_pairs={{0,3},{1,0},{2,1},{3,2},{4,7},{5,4},{6,5},{7,6},{8,11},{9,8},{10,9... | collective-permute-start | bytes 442376 | tf_op jit(solution)/shard_map/ppermute | solution.py:383
  20.3 5.5 %collective-permute-start.2 = (bf16[16,512]{1,0:T(8,128)(2,1)}, bf16[16,512]{1,0:T(8,128)(2,1)S(1)}, u32[]{:S(2)}, u32[]{:S(2)}) collective-permute-start(bf16[16,512]{1,0:T(8,128)(2,1)} %get-tuple-element.27.own_ref), channel_id=1, source_target_pairs={{0,2},{1,3},{2,0},{3,1},{4,6},{5,7},{6,4},{7,5},{8,10},{9,11},{10,... | collective-permute-start | bytes 49160 | tf_op jit(solution)/shard_map/ppermute | solution.py:383
  25.8 0.6 copy-start.5
  25.8 0.6 copy-start.2
  26.4 0.7 copy-start.3
  40.7 16.4 %copy-start = (bf16[1,32,64,512]{3,2,0,1:T(8,128)(2,1)}, bf16[1,32,64,512]{3,2,0,1:T(8,128)(2,1)S(1)}, u32[]{:S(2)}) copy-start(bf16[1,32,64,512]{3,2,0,1:T(8,128)(2,1)S(1)} %all-to-all-done) | copy-start | bytes 6291460
  40.7 30.6 %all-to-all-start.1 = ((bf16[1,32,24,512]{3,2,0,1:T(8,128)(2,1)}), bf16[1,32,24,512]{3,2,0,1:T(8,128)(2,1)S(1)}, u32[]{:S(2)}, u32[]{:S(2)}) async-start(bf16[1,32,24,512]{3,2,0,1:T(8,128)(2,1)} %bitcast.34), calls=%async_computation.1 | async-start | bytes 1572864 | tf_op jit(solution)/shard_map/all_to_all | solution.py:349
  45.2 11.9 %collective-permute-start.3 = (bf16[32,8,512]{2,1,0:T(8,128)(2,1)S(1)}, bf16[32,8,512]{2,1,0:T(8,128)(2,1)}, u32[]{:S(2)}, u32[]{:S(2)}) collective-permute-start(bf16[32,8,512]{2,1,0:T(8,128)(2,1)S(1)} %get-tuple-element.44), channel_id=1, source_target_pairs={{0,4},{4,0},{1,5},{5,1},{2,6},{6,2},{3,7},{7,3},{8,12},{12,8},{9,1... | collective-permute-start | bytes 786440 | tf_op jit(solution)/shard_map/ppermute | solution.py:414
  45.6 11.5 %collective-permute-start.4 = (bf16[32,8,512]{2,1,0:T(8,128)(2,1)S(1)}, bf16[32,8,512]{2,1,0:T(8,128)(2,1)}, u32[]{:S(2)}, u32[]{:S(2)}) collective-permute-start(bf16[32,8,512]{2,1,0:T(8,128)(2,1)S(1)} %get-tuple-element.43), channel_id=1, source_target_pairs={{4,1},{5,2},{6,3},{1,4},{2,5},{3,6},{12,9},{13,10},{14,11},{9,12},... | collective-permute-start | bytes 786440 | tf_op jit(solution)/shard_map/ppermute | solution.py:416
  71.3 0.9 copy-start.1
  109.9 13.5 %all-to-all-start.3 = ((f32[1,16,16,128]{3,2,0,1:T(8,128)}), f32[1,16,16,128]{3,2,0,1:T(8,128)S(1)}, u32[]{:S(2)}, u32[]{:S(2)}) async-start(f32[1,16,16,128]{3,2,0,1:T(8,128)} %bitcast.37), calls=%async_computation.3 | async-start | bytes 262144 | tf_op jit(solution)/shard_map/all_to_all | solution.py:349
  123.4 0.7 copy-start.4

commit v8 on v7

--- a/solution.py
+++ b/solution.py
@@ -15,6 +15,7 @@
 RIM = 24
 TM = ("x", "y", "core")
 EPS = 1e-6
+COMBINED = {(i // 4, i % 4): n for n, i in enumerate(i for i in range(16) if i not in (0, 3, 12, 15))}
 BF, F32 = jnp.bfloat16, jnp.float32
 HI = lax.Precision.HIGHEST
 
@@ -108,31 +109,28 @@
             out_ref[2 * k + half] = x[half, :, k].reshape(S * S, C).astype(BF)
 
 
-def rim_kernel(x_ref, up_ref, down_ref, own_ref, far_ref, out_ref):
-    pair = pl.program_id(0)
+def rim_kernel(x_ref, up_ref, down_ref, own_ref, far_ref, out_ref, wide, rim):
     n = 2048.0 * 16.0
     parts = [own_ref[...], far_ref[...], up_ref[128:, :], down_ref[128:, :]]
     whole = merge(jnp.stack([join_terms(v)[:8] for v in parts]), n)
     stats = split_terms(jnp.where(iota(whole.shape, 1) < 64, finish(whole, 4.0 * n), 0.0))[:1]
-    for odd in range(2):
-        start = 16 * pair if odd else 16 * pair - 16
-        start = jnp.clip(start, 0, 96)
-        first = 16 * pair + 8 * odd - 1 - start
-        start = pl.multiple_of(start, 16)
-        p, source = iota((RIM, W * 32), 0), iota((RIM, W * 32), 1)
-        r = jnp.where(p < 16, p % S + 1, jnp.where(p < 18, 0, 9))
-        c = jnp.where(p < 16, jnp.where(p < 8, 0, 9), jnp.where(p % 2 == 0, 0, 9))
-        column = first + c
-        pick = (source == r * 32 + column) & (column >= 0) & (column < 32) & (p < 20)
-        pick = pick.astype(BF)
+    rim[...] = jnp.zeros_like(rim)
+
+    def lanes(q):
+        at = slice(128 * q, 128 * q + 128)
+        wide[0] = up_ref[:128, at].astype(F32)
+        wide[17] = down_ref[:128, at].astype(F32)
+        wide[1:17] = x_ref[:, :, at].astype(F32)
         for half in range(2):
-            cols = pl.ds(start, 32)
-            if half == 0:
-                block = jnp.concatenate([up_ref[cols, :][None], x_ref[0:9, cols, :]], axis=0)
-            else:
-                block = jnp.concatenate([x_ref[7:16, cols, :], down_ref[cols, :][None]], axis=0)
-            message = dot(pick, block.reshape(W * 32, C))
-            out_ref[2 * odd + half] = jnp.where(iota((RIM, C), 0) == 20, stats, message).astype(BF)
+            rim[half, pl.ds(20, 16, stride=RIM), :] = jnp.broadcast_to(stats[:, at], (16, 128))
+            for r in range(W):
+                left, right = (16, 17) if r == 0 else (18, 19) if r == W - 1 else (r - 1, S + r - 1)
+                rim[half, pl.ds(RIM + left, 15, stride=RIM), :] = wide[S * half + r, pl.ds(S - 1, 15, stride=S), :]
+                rim[half, pl.ds(right, 15, stride=RIM), :] = wide[S * half + r, pl.ds(S, 15, stride=S), :]
+            out_ref[:, half, :, at] = rim[half].reshape(16, RIM, 128).astype(BF)
+
+    for q in range(4):
+        lanes(q)
 
 
 def weights_kernel(w_ref, out_ref):
@@ -145,7 +143,8 @@
     columns = [products(w[a]) for a in range(3)]
     for l in range(4):
         for j, v in enumerate(products([columns[a][l] for a in range(3)])):
-            out_ref[4 * j + l] = v.astype(BF)
+            if (j, l) in COMBINED:
+                out_ref[COMBINED[j, l]] = v.astype(BF)
 
 
 def products_kernel(wq_ref, wk_ref, wv_ref, wo_ref, score_ref, update_ref):
@@ -182,20 +181,18 @@
 
 
 def conv_kernel(
-    place_ref, in_ref, rim_ref, core_ref, band_ref, w0, w1, w2, mid_ref, stats_ref,
+    place_ref, in_ref, rim_ref, core_ref, band_ref, plain_ref, w0, w1, w2, mid_ref, stats_ref,
     terms, ends, sides, latent, sums, norm, held, sems,
 ):
-    def fetch(j, l):
+    def arrival(j, l, b, source):
         slot = 4 * (j % 3) + l
-        return [
-            pltpu.make_async_copy(w.at[4 * j + l], held.at[slot, b], sems.at[slot, b])
-            for b, w in enumerate((w0, w1, w2))
-        ]
+        return pltpu.make_async_copy(source, held.at[slot, b], sems.at[slot, b])
 
     def start(j):
         for l in range(4):
-            for copy in fetch(j, l):
-                copy.start()
+            for b, w in enumerate((w0, w1, w2)):
+                summed = (j, l) in COMBINED
+                arrival(j, l, b, w.at[COMBINED[j, l]] if summed else plain_ref.at[2 * j // 3, b, 2 * l // 3]).start()
 
     for j in range(3):
         start(j)
@@ -258,11 +255,11 @@
     def term(j, _):
         @pl.when(j == 1)
         def _():
-            start(j + 2)
+            start(3)
 
         for l in range(4):
-            for copy in fetch(j, l):
-                copy.wait()
+            for b in range(3):
+                arrival(j, l, b, w0.at[0]).wait()
         for q in range(2):
             m = []
             for l in range(4):
@@ -382,31 +379,32 @@
     )(*products)
     around = lambda v, by: lax.ppermute(v, "rows", [(i, (i + by) % 4) for i in range(4)])
     up, down, far = around(up, 1), around(down, 3), around(own, 2)
+    wide_x, score, update = lax.optimization_barrier((x, score, update))
     rim = pl.pallas_call(
         rim_kernel,
-        grid=(8,),
-        out_shape=jax.ShapeDtypeStruct((32, RIM, C), BF),
-        in_specs=[whole(16, 128, C), whole(144, C), whole(144, C), whole(16, C), whole(16, C)],
-        out_specs=pl.BlockSpec((4, RIM, C), lambda i: (i, 0, 0)),
-        compiler_params=params(),
-        cost_estimate=cost(32 * RIM * 320 * C * 2, 4 * 2**20),
+        out_shape=jax.ShapeDtypeStruct((16, 2, RIM, C), BF),
+        in_specs=[vmem] * 5,
+        out_specs=vmem,
+        scratch_shapes=[pltpu.VMEM((18, 128, 128), F32), pltpu.VMEM((2, 16 * RIM, 128), F32)],
+        compiler_params=params(),
+        cost_estimate=cost(2**22, 4 * 2**20),
         name="rim",
-    )(x, up, down, own, far)
+    )(wide_x, up, down, own, far).reshape(32, RIM, C)
+
     def combine(b, conv_weight):
         return pl.pallas_call(
             weights_kernel,
             grid=(4,),
-            out_shape=jax.ShapeDtypeStruct((16, C, C), BF),
+            out_shape=jax.ShapeDtypeStruct((12, C, C), BF),
             in_specs=[pl.BlockSpec((3, 1, 3, 128, C), lambda i: (0, b, 0, i, 0))],
-            out_specs=pl.BlockSpec((16, 128, C), lambda i: (0, i, 0)),
+            out_specs=pl.BlockSpec((12, 128, C), lambda i: (0, i, 0)),
             compiler_params=params(),
-            cost_estimate=cost(3 * 8 * C * C, 25 * C * C * 2),
+            cost_estimate=cost(3 * 8 * C * C, 21 * C * C * 2),
             name="weights",
         )(conv_weight)
 
     rim, early = lax.optimization_barrier((rim, conv_weight))
-    weights = [combine(0, early)]
-    rim, patch = lax.optimization_barrier((rim, patch))
+    rim, patch, *weights = lax.optimization_barrier((rim, patch, combine(0, early)))
     rim = exchange(rim, TM)
     first = lax.axis_index("core") == 0
     row = lambda at: lax.dynamic_slice_in_dim(patch, at, S, axis=1)
@@ -420,7 +418,7 @@
     mid, stats = pl.pallas_call(
         conv_kernel,
         out_shape=(jax.ShapeDtypeStruct((S * S, 2, P2, C), BF), jax.ShapeDtypeStruct((8, P2, 128), F32)),
-        in_specs=[smem] + [vmem] * 4 + [pl.BlockSpec(memory_space=pl.ANY)] * 3,
+        in_specs=[smem] + [vmem] * 4 + [pl.BlockSpec(memory_space=pl.ANY)] * 4,
         out_specs=(vmem, vmem),
         scratch_shapes=[
             pltpu.VMEM((4, 4, W, S // 2, P2, C), BF),
@@ -435,7 +433,7 @@
         compiler_params=params(),
         cost_estimate=cost(512 * 48 * C * C * 2, 28 * 2**20),
         name="conv",
-    )(place, patch, rim, core, band, *weights)
+    )(place, patch, rim, core, band, conv_weight, *weights)
     parts = pl.pallas_call(
         merge_kernel,
         out_shape=jax.ShapeDtypeStruct((16, P2, 128), F32),

time: 169 us -> 164 us (0.970)
  blocking collectives: 43.8 us -> 57.7 us
  waiting for transfers between devices: 15.5 us -> 8.29 us
  starting transfers between devices: 29.1 us -> 22.1 us
  Pallas kernels: 74.4 us -> 70 us
    all_to_all x2 -> x3, blocking collectives: 43.8 us -> 57.7 us  [local(): lax.all_to_all(v[None], axes, split_axis=1, concat_axis=0, tiled=True)[:, 0]]
    all_to_all x3 -> x2, waiting for transfers between devices: 11.3 us -> 3.72 us  [local(): lax.all_to_all(v[None], axes, split_axis=1, concat_axis=0, tiled=True)[:, 0]]
    all_to_all x3 -> x2, starting transfers between devices: 19.8 us -> 13 us  [local(): lax.all_to_all(v[None], axes, split_axis=1, concat_axis=0, tiled=True)[:, 0]]
    ppermute x1, waiting for transfers between devices: 0.01 us -> 3.44 us  [local(): band = lax.ppermute(band, ('core', 'rows'), pairs)]
    ppermute x3, waiting for transfers between devices: 4.19 us -> 1.13 us  [local(): lax.ppermute(v, 'rows', [(i, (i + by) % 4) for i in range(4)])]
    pallas_call x1, Pallas kernels: 5.96 us -> 3.4 us  [local(): pl.pallas_call(rim_kernel, out_shape=jax.ShapeDtypeStruct((16, 2, RIM, C)...]
    pallas_call x3, Pallas kernels: 21.3 us -> 19.4 us  [combine(): pl.pallas_call(weights_kernel, grid=(4,), out_shape=jax.ShapeDtypeStruct(...]
  transfers between devices with their start and end apart: 8 -> 7, of which waited for: 3 -> 3; matrix products, arithmetic and copies ran while one was open for 0% -> 0% of each run, Pallas kernels for 21% -> 18%
where the time goes in v8:
time: 164 us; the launch traced here: 163 us
  Pallas kernels  70 us (43%)
  blocking collectives  57.7 us (35%)
  starting transfers between devices  22.1 us (13%)
  waiting for transfers between devices  8.29 us (5%)
  local copies, waits for them, and re-layouts  3.78 us (2%)
    all_to_all x3, blocking collectives, local(): lax.all_to_all(v[None], axes, split_axis=1, concat_axis=0, tiled=True)[:, 0]  57.7 us
    pallas_call x1, Pallas kernels, local(): pl.pallas_call(conv_kernel, out_shape=(jax.ShapeDtypeStruct((S * S, 2, P2...  26 us
    pallas_call x3, Pallas kernels, combine(): pl.pallas_call(weights_kernel, grid=(4,), out_shape=jax.ShapeDtypeStruct(...  19.4 us
    all_to_all x2, starting transfers between devices, local(): lax.all_to_all(v[None], axes, split_axis=1, concat_axis=0, tiled=True)[:, 0]  13 us
    pallas_call x1, Pallas kernels, local(): pl.pallas_call(attend_kernel, grid=(S * S // pixels,), out_shape=jax.Shap...  8.5 us
    ppermute x3, starting transfers between devices, local(): lax.ppermute(v, 'rows', [(i, (i + by) % 4) for i in range(4)])  5.06 us
    pallas_call x1, Pallas kernels, local(): pl.pallas_call(latent_stats_kernel, out_shape=(row, row, jax.ShapeDtypeSt...  4.15 us
    ppermute x1, starting transfers between devices, local(): band = lax.ppermute(band, ('core', 'rows'), pairs)  3.78 us
  transfers between devices with their start and end apart: 7, of which 3 were waited for; matrix products, arithmetic and copies ran while one was open for 0% of the time, Pallas kernels for 18%

profile of v8, /device:TPU:1, one launch (start us, length us, event | category | flops | bytes accessed | tf_op | source)
XLA Modules:
  0.0 162.6 jit_solution(3375276679520330101)
XLA Ops:
  0.0 3.8 %inner.1 = bf16[32,64,512]{2,1,0:T(8,128)(2,1)} custom-call(bf16[16,128,512]{2,1,0:T(8,128)(2,1)} %bitcast.26), custom_call_target="tpu_custom_call" | custom-call | flops 1048576 | bytes 4194304 | tf_op jit(solution)/shard_map/inner/pallas_call | solution.py:349
  3.8 8.6 %all-to-all-start = ((bf16[1,32,64,512]{3,2,0,1:T(8,128)(2,1)}), bf16[1,32,64,512]{3,2,0,1:T(8,128)(2,1)S(1)}, u32[]{:S(2)}, u32[]{:S(2)}) async-start(bf16[1,32,64,512]{3,2,0,1:T(8,128)(2,1)} %bitcast.29), calls=%async_computation | async-start | bytes 4194304 | tf_op jit(solution)/shard_map/all_to_all | solution.py:346
  12.4 4.2 %latent_stats.1 = (bf16[144,512]{1,0:T(8,128)(2,1)}, bf16[144,512]{1,0:T(8,128)(2,1)}, bf16[16,512]{1,0:T(8,128)(2,1)}) custom-call(bf16[2048,512]{1,0:T(8,128)(2,1)} %bitcast.27), custom_call_target="tpu_custom_call" | custom-call | flops 4194304 | bytes 2097152 | tf_op jit(solution)/shard_map/latent_stats/pallas_call | solution.py:361
  16.5 1.6 %collective-permute-start = (bf16[144,512]{1,0:T(8,128)(2,1)}, bf16[144,512]{1,0:T(8,128)(2,1)S(1)}, u32[]{:S(2)}, u32[]{:S(2)}) collective-permute-start(bf16[144,512]{1,0:T(8,128)(2,1)} %get-tuple-element.36), channel_id=1, source_target_pairs={{0,1},{1,2},{2,3},{3,0},{4,5},{5,6},{6,7},{7,4},{8,9},{9,10},{10,1... | collective-permute-start | bytes 442376 | tf_op jit(solution)/shard_map/ppermute | solution.py:380
  18.2 2.1 %collective-permute-start.1 = (bf16[144,512]{1,0:T(8,128)(2,1)}, bf16[144,512]{1,0:T(8,128)(2,1)S(1)}, u32[]{:S(2)}, u32[]{:S(2)}) collective-permute-start(bf16[144,512]{1,0:T(8,128)(2,1)} %get-tuple-element.37), channel_id=1, source_target_pairs={{0,3},{1,0},{2,1},{3,2},{4,7},{5,4},{6,5},{7,6},{8,11},{9,8},{10,9... | collective-permute-start | bytes 442376 | tf_op jit(solution)/shard_map/ppermute | solution.py:380
  20.3 1.3 collective-permute-start.2
  21.6 3.1 %products.1 = (bf16[512,512]{1,0:T(8,128)(2,1)}, bf16[512,512]{1,0:T(8,128)(2,1)}) custom-call(bf16[512,512]{1,0:T(8,128)(2,1)} %wq_ref, bf16[512,512]{1,0:T(8,128)(2,1)} %wk_ref, bf16[512,512]{1,0:T(8,128)(2,1)} %wv_ref, bf16[512,512]{1,0:T(8,128)(2,1)} %wo_ref), custom_call_target="tpu_custom_call" | custom-call | flops 536870912 | bytes 3145728 | tf_op jit(solution)/shard_map/products/pallas_call | solution.py:371
  24.7 1.1 collective-permute-done.2.far_ref
  25.8 0.0 copy-start.4
  25.8 0.0 collective-permute-done.up_ref
  25.8 0.0 copy-start.2
  25.8 0.0 collective-permute-done.1.down_ref
  25.8 0.6 copy-done.4
  26.4 0.1 copy-done.2
  26.4 0.0 copy-start.3
  26.4 0.7 copy-done.3
  27.1 3.4 %rim.1 = bf16[16,2,24,512]{3,2,1,0:T(8,128)(2,1)} custom-call(bf16[16,128,512]{2,1,0:T(8,128)(2,1)} %bitcast.28, bf16[144,512]{1,0:T(8,128)(2,1)} %copy-done.2, bf16[144,512]{1,0:T(8,128)(2,1)} %copy-done.3, bf16[16,512]{1,0:T(8,128)(2,1)} %get-tuple-element.38.own_ref, bf16[16,512]{1,0:T(8,128)(2,1)} %copy-done.4), custom_call_target="tpu_custom_call" | custom-call | flops 4194304 | bytes 4194304 | tf_op jit(solution)/shard_map/rim/pallas_call | solution.py:383
  30.5 6.5 %weights.3.w0 = bf16[12,512,512]{2,1,0:T(8,128)(2,1)} custom-call(bf16[3,3,3,512,512]{4,3,2,1,0:T(8,128)(2,1)} %plain_ref.1), custom_call_target="tpu_custom_call" | custom-call | flops 6291456 | bytes 11010048 | tf_op jit(solution)/shard_map/weights/pallas_call | solution.py:395
  37.0 3.7 %all-to-all-done = bf16[1,32,64,512]{3,2,0,1:T(8,128)(2,1)S(1)} async-done(((bf16[1,32,64,512]{3,2,0,1:T(8,128)(2,1)}), bf16[1,32,64,512]{3,2,0,1:T(8,128)(2,1)S(1)}, u32[]{:S(2)}, u32[]{:S(2)}) %all-to-all-start) | async-done | bytes 2097184 | tf_op jit(solution)/shard_map/all_to_all | solution.py:346
  40.7 0.0 copy-start
  40.7 4.4 %all-to-all-start.1 = ((bf16[1,32,24,512]{3,2,0,1:T(8,128)(2,1)}), bf16[1,32,24,512]{3,2,0,1:T(8,128)(2,1)S(1)}, u32[]{:S(2)}, u32[]{:S(2)}) async-start(bf16[1,32,24,512]{3,2,0,1:T(8,128)(2,1)} %bitcast.8), calls=%async_computation.1 | async-start | bytes 1572864 | tf_op jit(solution)/shard_map/all_to_all | solution.py:346
  45.2 3.8 %collective-permute-start.4 = (bf16[32,8,512]{2,1,0:T(8,128)(2,1)S(1)}, bf16[32,8,512]{2,1,0:T(8,128)(2,1)}, u32[]{:S(2)}, u32[]{:S(2)}) collective-permute-start(bf16[32,8,512]{2,1,0:T(8,128)(2,1)S(1)} %get-tuple-element.51), channel_id=1, source_target_pairs={{4,1},{5,2},{6,3},{1,4},{2,5},{3,6},{12,9},{13,10},{14,11},{9,12},... | collective-permute-start | bytes 786440 | tf_op jit(solution)/shard_map/ppermute | solution.py:414
  49.0 0.3 collective-permute-start.3
  49.3 0.6 pad_add_fusion.place_ref
  49.9 3.4 %collective-permute-done.4.band_ref = bf16[32,8,512]{2,1,0:T(8,128)(2,1)} collective-permute-done((bf16[32,8,512]{2,1,0:T(8,128)(2,1)S(1)}, bf16[32,8,512]{2,1,0:T(8,128)(2,1)}, u32[]{:S(2)}, u32[]{:S(2)}) %collective-permute-start.4) | collective-permute-done | bytes 262176 | tf_op jit(solution)/shard_map/ppermute | solution.py:414
  53.3 0.0 collective-permute-done.3.core_ref
  53.3 6.5 %weights.5.w2 = bf16[12,512,512]{2,1,0:T(8,128)(2,1)} custom-call(bf16[3,3,3,512,512]{4,3,2,1,0:T(8,128)(2,1)} %plain_ref.1), custom_call_target="tpu_custom_call" | custom-call | flops 6291456 | bytes 11010048 | tf_op jit(solution)/shard_map/weights/pallas_call | solution.py:395
  59.8 0.0 copy-done
  59.8 6.5 %weights.4.w1 = bf16[12,512,512]{2,1,0:T(8,128)(2,1)} custom-call(bf16[3,3,3,512,512]{4,3,2,1,0:T(8,128)(2,1)} %plain_ref.1), custom_call_target="tpu_custom_call" | custom-call | flops 6291456 | bytes 11010048 | tf_op jit(solution)/shard_map/weights/pallas_call | solution.py:395
  66.3 0.0 all-to-all-done.1
  66.3 0.0 copy-start.1
  66.3 0.9 copy-done.1
  67.2 26.0 %conv.1 = (bf16[64,2,16,512]{3,2,1,0:T(8,128)(2,1)}, f32[8,16,128]{2,1,0:T(8,128)}) custom-call(s32[2]{0:T(128)} %pad_add_fusion.place_ref, bf16[32,64,512]{2,1,0:T(8,128)(2,1)} %bitcast.32, bf16[32,24,512]{2,1,0:T(8,128)(2,1)} %bitcast.34, bf16[32,8,512]{2,1,0:T(8,128)(2,1)} %collective-permute-done.3.core_ref, ...), custom_call_target="tpu_custom_call" | custom-call | flops 12884901888 | bytes 29360128 | tf_op jit(solution)/shard_map/conv/pallas_call | solution.py:418
  93.2 10.4 %all_to_all.20 = f32[1,8,16,128]{3,2,0,1:T(8,128)} all-to-all(f32[1,8,16,128]{3,2,0,1:T(8,128)} %bitcast.38), channel_id=1, replica_groups=mesh['x'=4,'y'=4,'core'=2,'rows'=4] {'core','rows'}, dimensions={1} | all-to-all | bytes 131072 | tf_op jit(solution)/shard_map/all_to_all | solution.py:346
  103.6 1.6 merge.1
  105.2 13.6 %all_to_all.21 = f32[1,16,16,128]{3,2,0,1:T(8,128)} all-to-all(f32[1,16,16,128]{3,2,0,1:T(8,128)} %bitcast.35), channel_id=1, replica_groups=mesh['x'=4,'y'=4,'core'=2,'rows'=4] {'x','y'}, dimensions={1} | all-to-all | bytes 262144 | tf_op jit(solution)/shard_map/all_to_all | solution.py:346
  118.8 8.5 %attend.1 = bf16[32,64,512]{2,1,0:T(8,128)(2,1)} custom-call(bf16[64,2,16,512]{3,2,1,0:T(8,128)(2,1)} %get-tuple-element.47.mid_ref, f32[16,16,128]{2,1,0:T(8,128)} %bitcast.37, bf16[512,512]{1,0:T(8,128)(2,1)} %get-tuple-element.49.score_ref, bf16[512,512]{1,0:T(8,128)(2,1)} %get-tuple-element.50.update_ref), custom_call_target="tpu_custom_call" | custom-call | flops 4294967296 | bytes 8388608 | tf_op jit(solution)/shard_map/attend/pallas_call | solution.py:447
  127.3 33.7 %all_to_all.22 = bf16[1,32,64,512]{3,2,0,1:T(8,128)(2,1)S(1)} all-to-all(bf16[1,32,64,512]{3,2,0,1:T(8,128)(2,1)} %bitcast.33), channel_id=1, replica_groups=mesh['x'=4,'y'=4,'core'=2,'rows'=4] {'x','y','core'}, dimensions={1} | all-to-all | bytes 4194304 | tf_op jit(solution)/shard_map/all_to_all | solution.py:346
  161.1 1.5 copy.12
  (1 shorter events, 0.0 us)
Async XLA Ops:
  3.8 36.9 %all-to-all-start = ((bf16[1,32,64,512]{3,2,0,1:T(8,128)(2,1)}), bf16[1,32,64,512]{3,2,0,1:T(8,128)(2,1)S(1)}, u32[]{:S(2)}, u32[]{:S(2)}) async-start(bf16[1,32,64,512]{3,2,0,1:T(8,128)(2,1)} %bitcast.29), calls=%async_computation | async-start | bytes 4194304 | tf_op jit(solution)/shard_map/all_to_all | solution.py:346
  16.5 9.3 %collective-permute-start = (bf16[144,512]{1,0:T(8,128)(2,1)}, bf16[144,512]{1,0:T(8,128)(2,1)S(1)}, u32[]{:S(2)}, u32[]{:S(2)}) collective-permute-start(bf16[144,512]{1,0:T(8,128)(2,1)} %get-tuple-element.36), channel_id=1, source_target_pairs={{0,1},{1,2},{2,3},{3,0},{4,5},{5,6},{6,7},{7,4},{8,9},{9,10},{10,1... | collective-permute-start | bytes 442376 | tf_op jit(solution)/shard_map/ppermute | solution.py:380
  18.2 7.6 %collective-permute-start.1 = (bf16[144,512]{1,0:T(8,128)(2,1)}, bf16[144,512]{1,0:T(8,128)(2,1)S(1)}, u32[]{:S(2)}, u32[]{:S(2)}) collective-permute-start(bf16[144,512]{1,0:T(8,128)(2,1)} %get-tuple-element.37), channel_id=1, source_target_pairs={{0,3},{1,0},{2,1},{3,2},{4,7},{5,4},{6,5},{7,6},{8,11},{9,8},{10,9... | collective-permute-start | bytes 442376 | tf_op jit(solution)/shard_map/ppermute | solution.py:380
  20.3 5.5 %collective-permute-start.2 = (bf16[16,512]{1,0:T(8,128)(2,1)}, bf16[16,512]{1,0:T(8,128)(2,1)S(1)}, u32[]{:S(2)}, u32[]{:S(2)}) collective-permute-start(bf16[16,512]{1,0:T(8,128)(2,1)} %get-tuple-element.38.own_ref), channel_id=1, source_target_pairs={{0,2},{1,3},{2,0},{3,1},{4,6},{5,7},{6,4},{7,5},{8,10},{9,11},{10,... | collective-permute-start | bytes 49160 | tf_op jit(solution)/shard_map/ppermute | solution.py:380
  25.8 0.6 copy-start.4
  25.8 0.7 copy-start.2
  26.4 0.7 copy-start.3
  40.7 19.1 %copy-start = (bf16[1,32,64,512]{3,2,0,1:T(8,128)(2,1)}, bf16[1,32,64,512]{3,2,0,1:T(8,128)(2,1)S(1)}, u32[]{:S(2)}) copy-start(bf16[1,32,64,512]{3,2,0,1:T(8,128)(2,1)S(1)} %all-to-all-done) | copy-start | bytes 6291460
  40.7 25.6 %all-to-all-start.1 = ((bf16[1,32,24,512]{3,2,0,1:T(8,128)(2,1)}), bf16[1,32,24,512]{3,2,0,1:T(8,128)(2,1)S(1)}, u32[]{:S(2)}, u32[]{:S(2)}) async-start(bf16[1,32,24,512]{3,2,0,1:T(8,128)(2,1)} %bitcast.8), calls=%async_computation.1 | async-start | bytes 1572864 | tf_op jit(solution)/shard_map/all_to_all | solution.py:346
  45.2 8.1 %collective-permute-start.4 = (bf16[32,8,512]{2,1,0:T(8,128)(2,1)S(1)}, bf16[32,8,512]{2,1,0:T(8,128)(2,1)}, u32[]{:S(2)}, u32[]{:S(2)}) collective-permute-start(bf16[32,8,512]{2,1,0:T(8,128)(2,1)S(1)} %get-tuple-element.51), channel_id=1, source_target_pairs={{4,1},{5,2},{6,3},{1,4},{2,5},{3,6},{12,9},{13,10},{14,11},{9,12},... | collective-permute-start | bytes 786440 | tf_op jit(solution)/shard_map/ppermute | solution.py:414
  49.0 4.3 %collective-permute-start.3 = (bf16[32,8,512]{2,1,0:T(8,128)(2,1)S(1)}, bf16[32,8,512]{2,1,0:T(8,128)(2,1)}, u32[]{:S(2)}, u32[]{:S(2)}) collective-permute-start(bf16[32,8,512]{2,1,0:T(8,128)(2,1)S(1)} %get-tuple-element.52), channel_id=1, source_target_pairs={{0,4},{4,0},{1,5},{5,1},{2,6},{6,2},{3,7},{7,3},{8,12},{12,8},{9,1... | collective-permute-start | bytes 786440 | tf_op jit(solution)/shard_map/ppermute | solution.py:412
  66.3 0.9 copy-start.1

commit v9 on v8

--- a/solution.py
+++ b/solution.py
@@ -103,8 +103,8 @@
 
 
 def inner_kernel(x_ref, out_ref):
-    x = x_ref[...].astype(F32).reshape(2, S, 4, S, C)
-    for k in range(4):
+    x = x_ref[...].astype(F32).reshape(2, S, 8, S, C)
+    for k in range(8):
         for half in range(2):
             out_ref[2 * k + half] = x[half, :, k].reshape(S * S, C).astype(BF)
 
@@ -133,24 +133,26 @@
         lanes(q)
 
 
-def weights_kernel(w_ref, out_ref):
+def weights_kernel(w_ref, *refs):
+    out_ref = refs[-1]
+
     def products(g):
         ends = (g[0] + g[2]) * 0.5
         middle = g[1] * 0.5
         return g[0], ends + middle, ends - middle, g[2]
 
-    w = [[w_ref[a, 0, e].astype(F32) for e in range(3)] for a in range(3)]
-    columns = [products(w[a]) for a in range(3)]
-    for l in range(4):
-        for j, v in enumerate(products([columns[a][l] for a in range(3)])):
-            if (j, l) in COMBINED:
-                out_ref[COMBINED[j, l]] = v.astype(BF)
-
-
-def products_kernel(wq_ref, wk_ref, wv_ref, wo_ref, score_ref, update_ref):
-    score = lax.dot_general(wq_ref[...], wk_ref[...], (((1,), (1,)), ((), ())), preferred_element_type=F32)
-    score_ref[...] = (score * (1.0 / C**0.5)).astype(BF)
-    update_ref[...] = dot(wv_ref[...], wo_ref[...]).astype(BF)
+    def rows(i, _):
+        at = pl.ds(pl.multiple_of(16 * i, 16), 16)
+        for q in range(4):
+            lanes = slice(128 * q, 128 * q + 128)
+            columns = [products([w_ref[a, 0, e, at, lanes].astype(F32) for e in range(3)]) for a in range(3)]
+            for l in range(4):
+                for j, v in enumerate(products([columns[a][l] for a in range(3)])):
+                    if (j, l) in COMBINED:
+                        out_ref[COMBINED[j, l], 0, at, lanes] = v.astype(BF)
+        return 0
+
+    lax.fori_loop(0, 16, rows, 0)
 
 
 def turned(in_ref, first, pixels):
@@ -181,7 +183,7 @@
 
 
 def conv_kernel(
-    place_ref, in_ref, rim_ref, core_ref, band_ref, plain_ref, w0, w1, w2, mid_ref, stats_ref,
+    place_ref, in_ref, rim_ref, core_ref, band_ref, plain_ref, sums_ref, mid_ref, stats_ref,
     terms, ends, sides, latent, sums, norm, held, sems,
 ):
     def arrival(j, l, b, source):
@@ -190,9 +192,10 @@
 
     def start(j):
         for l in range(4):
-            for b, w in enumerate((w0, w1, w2)):
+            for b in range(3):
                 summed = (j, l) in COMBINED
-                arrival(j, l, b, w.at[COMBINED[j, l]] if summed else plain_ref.at[2 * j // 3, b, 2 * l // 3]).start()
+                source = sums_ref.at[COMBINED[j, l], b] if summed else plain_ref.at[2 * j // 3, b, 2 * l // 3]
+                arrival(j, l, b, source).start()
 
     for j in range(3):
         start(j)
@@ -259,7 +262,7 @@
 
         for l in range(4):
             for b in range(3):
-                arrival(j, l, b, w0.at[0]).wait()
+                arrival(j, l, b, sums_ref.at[0, 0]).wait()
         for q in range(2):
             m = []
             for l in range(4):
@@ -348,10 +351,10 @@
 
     inner = pl.pallas_call(
         inner_kernel,
-        grid=(4,),
+        grid=(2,),
         out_shape=jax.ShapeDtypeStruct((32, S * S, C), BF),
-        in_specs=[pl.BlockSpec((16, 32, C), lambda i: (0, i, 0))],
-        out_specs=pl.BlockSpec((8, S * S, C), lambda i: (i, 0, 0)),
+        in_specs=[pl.BlockSpec((16, 64, C), lambda i: (0, i, 0))],
+        out_specs=pl.BlockSpec((16, S * S, C), lambda i: (i, 0, 0)),
         compiler_params=params(),
         cost_estimate=cost(2**20, 4 * 2**20),
         name="inner",
@@ -367,19 +370,8 @@
         cost_estimate=cost(2048 * C * 4, 2048 * C * 2),
         name="latent_stats",
     )(x.reshape(2048, C))
-    own, *products = lax.optimization_barrier((own, w_query, w_key, w_value, w_out))
-    score, update = pl.pallas_call(
-        products_kernel,
-        out_shape=(jax.ShapeDtypeStruct((C, C), BF),) * 2,
-        in_specs=[vmem] * 4,
-        out_specs=(vmem,) * 2,
-        compiler_params=params(),
-        cost_estimate=cost(2 * 2 * C**3, 6 * C * C * 2),
-        name="products",
-    )(*products)
     around = lambda v, by: lax.ppermute(v, "rows", [(i, (i + by) % 4) for i in range(4)])
     up, down, far = around(up, 1), around(down, 3), around(own, 2)
-    wide_x, score, update = lax.optimization_barrier((x, score, update))
     rim = pl.pallas_call(
         rim_kernel,
         out_shape=jax.ShapeDtypeStruct((16, 2, RIM, C), BF),
@@ -389,36 +381,40 @@
         compiler_params=params(),
         cost_estimate=cost(2**22, 4 * 2**20),
         name="rim",
-    )(wide_x, up, down, own, far).reshape(32, RIM, C)
-
-    def combine(b, conv_weight):
+    )(x, up, down, own, far).reshape(32, RIM, C)
+
+    def combine(first, conv_weight, *before):
         return pl.pallas_call(
             weights_kernel,
-            grid=(4,),
-            out_shape=jax.ShapeDtypeStruct((12, C, C), BF),
-            in_specs=[pl.BlockSpec((3, 1, 3, 128, C), lambda i: (0, b, 0, i, 0))],
-            out_specs=pl.BlockSpec((12, 128, C), lambda i: (0, i, 0)),
+            grid=(3,),
+            out_shape=jax.ShapeDtypeStruct((12, 3, C, C), BF),
+            in_specs=[pl.BlockSpec((3, 1, 3, 256, C), lambda i: (0, (i + first) // 2, 0, (i + first) % 2, 0))]
+            + [pl.BlockSpec(memory_space=pl.ANY)] * len(before),
+            out_specs=pl.BlockSpec((12, 1, 256, C), lambda i: (0, (i + first) // 2, (i + first) % 2, 0)),
+            input_output_aliases={1: 0} if before else {},
             compiler_params=params(),
-            cost_estimate=cost(3 * 8 * C * C, 21 * C * C * 2),
+            cost_estimate=cost(4 * 8 * C * C, 32 * C * C * 2),
             name="weights",
-        )(conv_weight)
+        )(conv_weight, *before)
 
     rim, early = lax.optimization_barrier((rim, conv_weight))
-    rim, patch, *weights = lax.optimization_barrier((rim, patch, combine(0, early)))
+    rim, patch, weights = lax.optimization_barrier((rim, patch, combine(0, early)))
     rim = exchange(rim, TM)
     first = lax.axis_index("core") == 0
     row = lambda at: lax.dynamic_slice_in_dim(patch, at, S, axis=1)
     core, band = row(jnp.where(first, S * S - S, 0)), row(jnp.where(first, 0, S * S - S))
+    core, band, late = lax.optimization_barrier((core, band, conv_weight))
     core = lax.ppermute(core, "core", [(0, 1), (1, 0)])
     pairs = [(4 + i, i + 1) for i in range(3)] + [(i + 1, 4 + i) for i in range(3)]
     band = lax.ppermute(band, ("core", "rows"), pairs)
-    core, band, late = lax.optimization_barrier((core, band, conv_weight))
-    weights += [combine(b, late) for b in (1, 2)]
+    weights = combine(3, late, weights)
+    score = (dot(w_query, w_key.T) * (1.0 / C**0.5)).astype(BF)
+    update = dot(w_value, w_out).astype(BF)
 
     mid, stats = pl.pallas_call(
         conv_kernel,
         out_shape=(jax.ShapeDtypeStruct((S * S, 2, P2, C), BF), jax.ShapeDtypeStruct((8, P2, 128), F32)),
-        in_specs=[smem] + [vmem] * 4 + [pl.BlockSpec(memory_space=pl.ANY)] * 4,
+        in_specs=[smem] + [vmem] * 4 + [pl.BlockSpec(memory_space=pl.ANY)] * 2,
         out_specs=(vmem, vmem),
         scratch_shapes=[
             pltpu.VMEM((4, 4, W, S // 2, P2, C), BF),
@@ -433,7 +429,7 @@
         compiler_params=params(),
         cost_estimate=cost(512 * 48 * C * C * 2, 28 * 2**20),
         name="conv",
-    )(place, patch, rim, core, band, conv_weight, *weights)
+    )(place, patch, rim, core, band, conv_weight, weights)
     parts = pl.pallas_call(
         merge_kernel,
         out_shape=jax.ShapeDtypeStruct((16, P2, 128), F32),

time: 164 us -> 157 us (0.957)
  blocking collectives: 57.7 us -> 33.7 us
  starting transfers between devices: 22.1 us -> 33.6 us
  waiting for transfers between devices: 8.29 us -> 15.1 us
  Pallas kernels: 70 us -> 64.2 us
  matrix products: 0 us -> 2.52 us
  local copies, waits for them, and re-layouts: 3.78 us -> 5.87 us
    all_to_all x3 -> x1, blocking collectives: 57.7 us -> 33.7 us  [local(): lax.all_to_all(v[None], axes, split_axis=1, concat_axis=0, tiled=True)[:, 0]]
    all_to_all x2 -> x4, starting transfers between devices: 13 us -> 25.4 us  [local(): lax.all_to_all(v[None], axes, split_axis=1, concat_axis=0, tiled=True)[:, 0]]
    all_to_all x2 -> x4, waiting for transfers between devices: 3.72 us -> 10.9 us  [local(): lax.all_to_all(v[None], axes, split_axis=1, concat_axis=0, tiled=True)[:, 0]]
    pallas_call x5 -> x3, Pallas kernels: 26.3 us -> 20.5 us  [the longest x2 17.8 us: combine(): pl.pallas_call(weights_kernel, grid=(3,), out_shape=jax.ShapeDtypeStruct(...]
    ppermute x1, waiting for transfers between devices: 3.44 us -> 0.01 us  [local(): band = lax.ppermute(band, ('core', 'rows'), pairs)]
    ppermute x3, waiting for transfers between devices: 1.13 us -> 4.19 us  [local(): lax.ppermute(v, 'rows', [(i, (i + by) % 4) for i in range(4)])]
    dot_general x0 -> x2, matrix products: none -> 2.52 us  [dot(): return jnp.dot(a, b, preferred_element_type=F32, precision=precision)]
    unnamed x10 -> x22, local copies, waits for them, and re-layouts: 2.19 us -> 3.48 us
  transfers between devices with their start and end apart: 7 -> 9, of which waited for: 3 -> 5; matrix products, arithmetic and copies ran while one was open for 0% -> 3% of each run, Pallas kernels for 18% -> 16%
where the time goes in v9:
time: 157 us; the launch traced here: 156 us
  Pallas kernels  64.2 us (41%)
  blocking collectives  33.7 us (21%)
  starting transfers between devices  33.6 us (21%)
  waiting for transfers between devices  15.1 us (10%)
  local copies, waits for them, and re-layouts  5.87 us (4%)
  matrix products  2.52 us (2%)
    all_to_all x1, blocking collectives, local(): lax.all_to_all(v[None], axes, split_axis=1, concat_axis=0, tiled=True)[:, 0]  33.7 us
    pallas_call x1, Pallas kernels, local(): pl.pallas_call(conv_kernel, out_shape=(jax.ShapeDtypeStruct((S * S, 2, P2...  26.1 us
    all_to_all x4, starting transfers between devices, local(): lax.all_to_all(v[None], axes, split_axis=1, concat_axis=0, tiled=True)[:, 0]  25.4 us
    pallas_call x2, Pallas kernels, combine(): pl.pallas_call(weights_kernel, grid=(3,), out_shape=jax.ShapeDtypeStruct(...  17.8 us
    all_to_all x4, waiting for transfers between devices, local(): lax.all_to_all(v[None], axes, split_axis=1, concat_axis=0, tiled=True)[:, 0]  10.9 us
    pallas_call x1, Pallas kernels, local(): pl.pallas_call(attend_kernel, grid=(S * S // pixels,), out_shape=jax.Shap...  8.5 us
    ppermute x3, starting transfers between devices, local(): lax.ppermute(v, 'rows', [(i, (i + by) % 4) for i in range(4)])  5.06 us
    ppermute x3, waiting for transfers between devices, local(): lax.ppermute(v, 'rows', [(i, (i + by) % 4) for i in range(4)])  4.19 us
  transfers between devices with their start and end apart: 9, of which 5 were waited for; matrix products, arithmetic and copies ran while one was open for 3% of the time, Pallas kernels for 16%

profile of v9, /device:TPU:1, one launch (start us, length us, event | category | flops | bytes accessed | tf_op | source)
XLA Modules:
  0.0 155.8 jit_solution(8106532592561305951)
XLA Ops:
  0.0 0.0 copy-start
  0.0 2.7 %inner.1 = bf16[32,64,512]{2,1,0:T(8,128)(2,1)} custom-call(bf16[16,128,512]{2,1,0:T(8,128)(2,1)} %bitcast.30), custom_call_target="tpu_custom_call" | custom-call | flops 1048576 | bytes 4194304 | tf_op jit(solution)/shard_map/inner/pallas_call | solution.py:352
  2.7 8.6 %all-to-all-start = ((bf16[1,32,64,512]{3,2,0,1:T(8,128)(2,1)}), bf16[1,32,64,512]{3,2,0,1:T(8,128)(2,1)S(1)}, u32[]{:S(2)}, u32[]{:S(2)}) async-start(bf16[1,32,64,512]{3,2,0,1:T(8,128)(2,1)} %bitcast.33), calls=%async_computation | async-start | bytes 4194304 | tf_op jit(solution)/shard_map/all_to_all | solution.py:349
  11.3 4.1 %latent_stats.1 = (bf16[144,512]{1,0:T(8,128)(2,1)}, bf16[144,512]{1,0:T(8,128)(2,1)}, bf16[16,512]{1,0:T(8,128)(2,1)}) custom-call(bf16[2048,512]{1,0:T(8,128)(2,1)} %bitcast.31), custom_call_target="tpu_custom_call" | custom-call | flops 4194304 | bytes 2097152 | tf_op jit(solution)/shard_map/latent_stats/pallas_call | solution.py:364
  15.4 1.6 %collective-permute-start = (bf16[144,512]{1,0:T(8,128)(2,1)}, bf16[144,512]{1,0:T(8,128)(2,1)S(1)}, u32[]{:S(2)}, u32[]{:S(2)}) collective-permute-start(bf16[144,512]{1,0:T(8,128)(2,1)} %get-tuple-element.18), channel_id=1, source_target_pairs={{0,1},{1,2},{2,3},{3,0},{4,5},{5,6},{6,7},{7,4},{8,9},{9,10},{10,1... | collective-permute-start | bytes 442376 | tf_op jit(solution)/shard_map/ppermute | solution.py:373
  17.0 2.1 %collective-permute-start.1 = (bf16[144,512]{1,0:T(8,128)(2,1)}, bf16[144,512]{1,0:T(8,128)(2,1)S(1)}, u32[]{:S(2)}, u32[]{:S(2)}) collective-permute-start(bf16[144,512]{1,0:T(8,128)(2,1)} %get-tuple-element.19), channel_id=1, source_target_pairs={{0,3},{1,0},{2,1},{3,2},{4,7},{5,4},{6,5},{7,6},{8,11},{9,8},{10,9... | collective-permute-start | bytes 442376 | tf_op jit(solution)/shard_map/ppermute | solution.py:373
  19.2 1.3 collective-permute-start.2
  20.5 4.2 %collective-permute-done.2.far_ref = bf16[16,512]{1,0:T(8,128)(2,1)S(1)} collective-permute-done((bf16[16,512]{1,0:T(8,128)(2,1)}, bf16[16,512]{1,0:T(8,128)(2,1)S(1)}, u32[]{:S(2)}, u32[]{:S(2)}) %collective-permute-start.2) | collective-permute-done | bytes 16416 | tf_op jit(solution)/shard_map/ppermute | solution.py:373
  24.6 0.0 copy-start.9
  24.6 0.0 collective-permute-done.up_ref
  24.6 0.0 copy-start.6
  24.6 0.0 collective-permute-done.1.down_ref
  24.7 0.6 copy-done.9
  25.2 0.1 copy-done.6
  25.3 0.6 copy-done.7
  26.0 3.4 %rim.1 = bf16[16,2,24,512]{3,2,1,0:T(8,128)(2,1)} custom-call(bf16[16,128,512]{2,1,0:T(8,128)(2,1)} %bitcast.32, bf16[144,512]{1,0:T(8,128)(2,1)} %copy-done.6, bf16[144,512]{1,0:T(8,128)(2,1)} %copy-done.7, bf16[16,512]{1,0:T(8,128)(2,1)} %get-tuple-element.20.own_ref, bf16[16,512]{1,0:T(8,128)(2,1)} %copy-done.9), custom_call_target="tpu_custom_call" | custom-call | flops 4194304 | bytes 4194304 | tf_op jit(solution)/shard_map/rim/pallas_call | solution.py:375
  29.4 8.9 %weights.2.refs_0_ = bf16[12,3,512,512]{3,2,1,0:T(8,128)(2,1)} custom-call(bf16[3,3,3,512,512]{4,3,2,1,0:T(8,128)(2,1)} %plain_ref.1), custom_call_target="tpu_custom_call" | custom-call | flops 8388608 | bytes 16777216 | tf_op jit(solution)/shard_map/weights/pallas_call | solution.py:387
  38.3 1.3 all-to-all-done
  39.6 6.8 %all-to-all-start.1 = ((bf16[1,32,24,512]{3,2,0,1:T(8,128)(2,1)}), bf16[1,32,24,512]{3,2,0,1:T(8,128)(2,1)S(1)}, u32[]{:S(2)}, u32[]{:S(2)}) async-start(bf16[1,32,24,512]{3,2,0,1:T(8,128)(2,1)} %bitcast.8), calls=%async_computation.1 | async-start | bytes 1572864 | tf_op jit(solution)/shard_map/all_to_all | solution.py:349
  46.4 0.9 constant_dynamic-slice_fusion
  47.2 0.2 collective-permute-start.3
  47.5 2.9 %collective-permute-start.4 = (bf16[32,8,512]{2,1,0:T(8,128)(2,1)}, bf16[32,8,512]{2,1,0:T(8,128)(2,1)}, u32[]{:S(2)}, u32[]{:S(2)}) collective-permute-start(bf16[32,8,512]{2,1,0:T(8,128)(2,1)} %get-tuple-element.26), channel_id=1, source_target_pairs={{4,1},{5,2},{6,3},{1,4},{2,5},{3,6},{12,9},{13,10},{14,11},{9,12},... | collective-permute-start | bytes 786440 | tf_op jit(solution)/shard_map/ppermute | solution.py:409
  50.4 0.6 pad_add_fusion.place_ref
  51.0 8.9 %weights.3.sums_ref = bf16[12,3,512,512]{3,2,1,0:T(8,128)(2,1)} custom-call(bf16[3,3,3,512,512]{4,3,2,1,0:T(8,128)(2,1)} %plain_ref.1, bf16[12,3,512,512]{3,2,1,0:T(8,128)(2,1)} %weights.2.refs_0_), custom_call_target="tpu_custom_call", output_to_operand_aliasing={{}: (1, {})} | custom-call | flops 8388608 | bytes 16777216 | tf_op jit(solution)/shard_map/weights/pallas_call | solution.py:387
  59.9 0.0 copy-done.1
  59.9 0.0 collective-permute-done.3.core_ref
  59.9 0.0 collective-permute-done.4.band_ref
  59.9 0.7 all-to-all-done.1
  60.6 0.9 copy-done.2
  61.5 26.1 %conv.1 = (bf16[64,2,16,512]{3,2,1,0:T(8,128)(2,1)}, f32[8,16,128]{2,1,0:T(8,128)}) custom-call(s32[2]{0:T(128)} %pad_add_fusion.place_ref, bf16[32,64,512]{2,1,0:T(8,128)(2,1)} %bitcast.36, bf16[32,24,512]{2,1,0:T(8,128)(2,1)} %bitcast.38, bf16[32,8,512]{2,1,0:T(8,128)(2,1)} %collective-permute-done.3.core_ref, ...), custom_call_target="tpu_custom_call" | custom-call | flops 12884901888 | bytes 29360128 | tf_op jit(solution)/shard_map/conv/pallas_call | solution.py:414
  87.6 0.0 copy-start.3
  87.6 0.0 copy-start.4
  87.6 3.4 %all-to-all-start.2 = ((f32[1,8,16,128]{3,2,0,1:T(8,128)}), f32[1,8,16,128]{3,2,0,1:T(8,128)S(1)}, u32[]{:S(2)}, u32[]{:S(2)}) async-start(f32[1,8,16,128]{3,2,0,1:T(8,128)} %bitcast.42), calls=%async_computation.2 | async-start | bytes 131072 | tf_op jit(solution)/shard_map/all_to_all | solution.py:349
  91.0 0.0 copy-done
  91.0 0.0 copy-done.10
  91.1 1.3 fusion.score_ref
  92.3 3.5 %all-to-all-done.2 = f32[1,8,16,128]{3,2,0,1:T(8,128)S(1)} async-done(((f32[1,8,16,128]{3,2,0,1:T(8,128)}), f32[1,8,16,128]{3,2,0,1:T(8,128)S(1)}, u32[]{:S(2)}, u32[]{:S(2)}) %all-to-all-start.2) | async-done | bytes 65568 | tf_op jit(solution)/shard_map/all_to_all | solution.py:349
  95.9 0.6 copy-done.5
  96.5 1.6 %merge.1 = f32[16,16,128]{2,1,0:T(8,128)} custom-call(f32[8,16,128]{2,1,0:T(8,128)} %bitcast.40), custom_call_target="tpu_custom_call" | custom-call | tf_op jit(solution)/shard_map/merge/pallas_call | solution.py:433
  98.1 6.6 %all-to-all-start.3 = ((f32[1,16,16,128]{3,2,0,1:T(8,128)}), f32[1,16,16,128]{3,2,0,1:T(8,128)S(1)}, u32[]{:S(2)}, u32[]{:S(2)}) async-start(f32[1,16,16,128]{3,2,0,1:T(8,128)} %bitcast.39), calls=%async_computation.3 | async-start | bytes 262144 | tf_op jit(solution)/shard_map/all_to_all | solution.py:349
  104.7 0.0 copy-done.3
  104.7 0.0 copy-done.4
  104.7 1.2 convolution_convert_fusion.update_ref
  105.9 5.4 %all-to-all-done.3 = f32[1,16,16,128]{3,2,0,1:T(8,128)S(1)} async-done(((f32[1,16,16,128]{3,2,0,1:T(8,128)}), f32[1,16,16,128]{3,2,0,1:T(8,128)S(1)}, u32[]{:S(2)}, u32[]{:S(2)}) %all-to-all-start.3) | async-done | bytes 131104 | tf_op jit(solution)/shard_map/all_to_all | solution.py:349
  111.3 0.6 copy-done.8
  112.0 8.5 %attend.1 = bf16[32,64,512]{2,1,0:T(8,128)(2,1)} custom-call(bf16[64,2,16,512]{3,2,1,0:T(8,128)(2,1)} %get-tuple-element.29.mid_ref, f32[16,16,128]{2,1,0:T(8,128)} %bitcast.41, bf16[512,512]{1,0:T(8,128)(2,1)} %fusion.score_ref, bf16[512,512]{1,0:T(8,128)(2,1)} %convolution_convert_fusion.update_ref), custom_call_target="tpu_custom_call" | custom-call | flops 4294967296 | bytes 8388608 | tf_op jit(solution)/shard_map/attend/pallas_call | solution.py:443
  120.5 33.7 %all_to_all.20 = bf16[1,32,64,512]{3,2,0,1:T(8,128)(2,1)S(1)} all-to-all(bf16[1,32,64,512]{3,2,0,1:T(8,128)(2,1)} %bitcast.37), channel_id=1, replica_groups=mesh['x'=4,'y'=4,'core'=2,'rows'=4] {'x','y','core'}, dimensions={1} | all-to-all | bytes 4194304 | tf_op jit(solution)/shard_map/all_to_all | solution.py:349
  154.2 1.5 copy.13
  (6 shorter events, 0.0 us)
Async XLA Ops:
  0.0 91.0 %copy-start = (bf16[512,512]{1,0:T(8,128)(2,1)S(1)}, bf16[512,512]{1,0:T(8,128)(2,1)}, u32[]{:S(2)}) copy-start(bf16[512,512]{1,0:T(8,128)(2,1)} %param.8) | copy-start | bytes 1572868
  2.7 36.9 %all-to-all-start = ((bf16[1,32,64,512]{3,2,0,1:T(8,128)(2,1)}), bf16[1,32,64,512]{3,2,0,1:T(8,128)(2,1)S(1)}, u32[]{:S(2)}, u32[]{:S(2)}) async-start(bf16[1,32,64,512]{3,2,0,1:T(8,128)(2,1)} %bitcast.33), calls=%async_computation | async-start | bytes 4194304 | tf_op jit(solution)/shard_map/all_to_all | solution.py:349
  15.4 9.3 %collective-permute-start = (bf16[144,512]{1,0:T(8,128)(2,1)}, bf16[144,512]{1,0:T(8,128)(2,1)S(1)}, u32[]{:S(2)}, u32[]{:S(2)}) collective-permute-start(bf16[144,512]{1,0:T(8,128)(2,1)} %get-tuple-element.18), channel_id=1, source_target_pairs={{0,1},{1,2},{2,3},{3,0},{4,5},{5,6},{6,7},{7,4},{8,9},{9,10},{10,1... | collective-permute-start | bytes 442376 | tf_op jit(solution)/shard_map/ppermute | solution.py:373
  17.0 7.6 %collective-permute-start.1 = (bf16[144,512]{1,0:T(8,128)(2,1)}, bf16[144,512]{1,0:T(8,128)(2,1)S(1)}, u32[]{:S(2)}, u32[]{:S(2)}) collective-permute-start(bf16[144,512]{1,0:T(8,128)(2,1)} %get-tuple-element.19), channel_id=1, source_target_pairs={{0,3},{1,0},{2,1},{3,2},{4,7},{5,4},{6,5},{7,6},{8,11},{9,8},{10,9... | collective-permute-start | bytes 442376 | tf_op jit(solution)/shard_map/ppermute | solution.py:373
  19.2 5.5 %collective-permute-start.2 = (bf16[16,512]{1,0:T(8,128)(2,1)}, bf16[16,512]{1,0:T(8,128)(2,1)S(1)}, u32[]{:S(2)}, u32[]{:S(2)}) collective-permute-start(bf16[16,512]{1,0:T(8,128)(2,1)} %get-tuple-element.20.own_ref), channel_id=1, source_target_pairs={{0,2},{1,3},{2,0},{3,1},{4,6},{5,7},{6,4},{7,5},{8,10},{9,11},{10,... | collective-permute-start | bytes 49160 | tf_op jit(solution)/shard_map/ppermute | solution.py:373
  24.6 0.6 copy-start.9
  24.6 0.7 copy-start.6
  25.3 0.7 copy-start.7
  39.6 20.3 %copy-start.1 = (bf16[1,32,64,512]{3,2,0,1:T(8,128)(2,1)}, bf16[1,32,64,512]{3,2,0,1:T(8,128)(2,1)S(1)}, u32[]{:S(2)}) copy-start(bf16[1,32,64,512]{3,2,0,1:T(8,128)(2,1)S(1)} %all-to-all-done) | copy-start | bytes 6291460
  39.6 21.0 %all-to-all-start.1 = ((bf16[1,32,24,512]{3,2,0,1:T(8,128)(2,1)}), bf16[1,32,24,512]{3,2,0,1:T(8,128)(2,1)S(1)}, u32[]{:S(2)}, u32[]{:S(2)}) async-start(bf16[1,32,24,512]{3,2,0,1:T(8,128)(2,1)} %bitcast.8), calls=%async_computation.1 | async-start | bytes 1572864 | tf_op jit(solution)/shard_map/all_to_all | solution.py:349
  47.2 12.7 %collective-permute-start.3 = (bf16[32,8,512]{2,1,0:T(8,128)(2,1)}, bf16[32,8,512]{2,1,0:T(8,128)(2,1)}, u32[]{:S(2)}, u32[]{:S(2)}) collective-permute-start(bf16[32,8,512]{2,1,0:T(8,128)(2,1)} %get-tuple-element.25), channel_id=1, source_target_pairs={{0,4},{4,0},{1,5},{5,1},{2,6},{6,2},{3,7},{7,3},{8,12},{12,8},{9,1... | collective-permute-start | bytes 786440 | tf_op jit(solution)/shard_map/ppermute | solution.py:407
  47.5 12.4 %collective-permute-start.4 = (bf16[32,8,512]{2,1,0:T(8,128)(2,1)}, bf16[32,8,512]{2,1,0:T(8,128)(2,1)}, u32[]{:S(2)}, u32[]{:S(2)}) collective-permute-start(bf16[32,8,512]{2,1,0:T(8,128)(2,1)} %get-tuple-element.26), channel_id=1, source_target_pairs={{4,1},{5,2},{6,3},{1,4},{2,5},{3,6},{12,9},{13,10},{14,11},{9,12},... | collective-permute-start | bytes 786440 | tf_op jit(solution)/shard_map/ppermute | solution.py:409
  60.6 0.9 copy-start.2
  61.5 29.6 %copy-start.10 = (bf16[512,512]{1,0:T(8,128)(2,1)S(1)}, bf16[512,512]{1,0:T(8,128)(2,1)}, u32[]{:S(2)}) copy-start(bf16[512,512]{1,0:T(8,128)(2,1)} %param.9) | copy-start | bytes 1572868
  87.6 17.1 %copy-start.3 = (bf16[512,512]{1,0:T(8,128)(2,1)S(1)}, bf16[512,512]{1,0:T(8,128)(2,1)}, u32[]{:S(2)}) copy-start(bf16[512,512]{1,0:T(8,128)(2,1)} %param.10) | copy-start | bytes 1572868
  87.6 17.1 %copy-start.4 = (bf16[512,512]{1,0:T(8,128)(2,1)S(1)}, bf16[512,512]{1,0:T(8,128)(2,1)}, u32[]{:S(2)}) copy-start(bf16[512,512]{1,0:T(8,128)(2,1)} %param.11) | copy-start | bytes 1572868
  87.6 8.3 %all-to-all-start.2 = ((f32[1,8,16,128]{3,2,0,1:T(8,128)}), f32[1,8,16,128]{3,2,0,1:T(8,128)S(1)}, u32[]{:S(2)}, u32[]{:S(2)}) async-start(f32[1,8,16,128]{3,2,0,1:T(8,128)} %bitcast.42), calls=%async_computation.2 | async-start | bytes 131072 | tf_op jit(solution)/shard_map/all_to_all | solution.py:349
  95.9 0.6 copy-start.5
  98.1 13.2 %all-to-all-start.3 = ((f32[1,16,16,128]{3,2,0,1:T(8,128)}), f32[1,16,16,128]{3,2,0,1:T(8,128)S(1)}, u32[]{:S(2)}, u32[]{:S(2)}) async-start(f32[1,16,16,128]{3,2,0,1:T(8,128)} %bitcast.39), calls=%async_computation.3 | async-start | bytes 262144 | tf_op jit(solution)/shard_map/all_to_all | solution.py:349
  111.3 0.6 copy-start.8

commit v10 on v9

--- a/solution.py
+++ b/solution.py
@@ -72,21 +72,20 @@
 
 def latent_stats_kernel(x_ref, up_ref, down_ref, out_ref):
     n = x_ref.shape[0]
-    step = 256
-
-    def add(i, total):
-        rows = x_ref[pl.ds(pl.multiple_of(i * step, step), step), :].astype(F32)
-        return total + jnp.sum(rows.reshape(step // 8, 8, C), axis=0)
-
-    total = lax.fori_loop(0, n // step, add, jnp.zeros((8, C), F32))
-    mean = jnp.sum(total, axis=0, keepdims=True) * (1.0 / n)
-
-    def add_square(i, total):
-        rows = x_ref[pl.ds(pl.multiple_of(i * step, step), step), :].astype(F32) - mean
-        return total + jnp.sum((rows * rows).reshape(step // 8, 8, C), axis=0)
-
-    total = lax.fori_loop(0, n // step, add_square, jnp.zeros((8, C), F32))
-    m2 = jnp.sum(total, axis=0, keepdims=True)
+    step = 64
+
+    pivot = x_ref[:16, :].astype(F32)[:1]
+
+    def add(i, totals):
+        rows = x_ref[pl.ds(pl.multiple_of(i * step, step), step), :].astype(F32) - pivot
+        rows = rows.reshape(step // 8, 8, C)
+        return totals[0] + jnp.sum(rows, axis=0), totals[1] + jnp.sum(rows * rows, axis=0)
+
+    zero = jnp.zeros((8, C), F32)
+    totals = lax.fori_loop(0, n // step, add, (zero, zero))
+    off = jnp.sum(totals[0], axis=0, keepdims=True) * (1.0 / n)
+    mean = pivot + off
+    m2 = jnp.sum(totals[1], axis=0, keepdims=True) - n * off * off
     wide = lambda v: jnp.broadcast_to(v, (8, C))
     row = split_terms(group_stats(wide(mean), wide(m2), float(n), 0))
     row = jnp.concatenate([row, jnp.zeros_like(row)], axis=0).astype(BF)
@@ -275,27 +274,26 @@
 
     lax.fori_loop(0, 4, term, 0)
 
-    def finish_row(r, total):
+    def pixel(r, c):
+        m = [sums[j, c % 2, r, c // 2] for j in range(4)]
+        m = m[0] + m[1] + m[2], m[1] - m[2] - m[3]
+        return [(latent[S * r + c, i].astype(F32) + m[i]).astype(BF) for i in range(2)]
+
+    pivot = [v.astype(F32) for v in pixel(0, 0)]
+
+    def finish_row(r, totals):
         for c in range(S):
-            m = [sums[j, c % 2, r, c // 2] for j in range(4)]
-            for i, v in enumerate((m[0] + m[1] + m[2], m[1] - m[2] - m[3])):
-                v = (latent[S * r + c, i].astype(F32) + v).astype(BF)
+            for i, v in enumerate(pixel(r, c)):
                 mid_ref[S * r + c, i] = v
-                total[i] = total[i] + v.astype(F32)
-        return total
-
-    zero = jnp.zeros((P2, C), F32)
-    total = lax.fori_loop(0, S, finish_row, [zero, zero])
-    mean = [v * (1.0 / (S * S)) for v in total]
-
-    def squares(r, total):
-        for c in range(S):
-            for i in range(2):
-                off = mid_ref[S * r + c, i].astype(F32) - mean[i]
-                total[i] = total[i] + off * off
-        return total
-
-    total = lax.fori_loop(0, S, squares, [zero, zero])
+                off = v.astype(F32) - pivot[i]
+                totals[i] = totals[i] + off
+                totals[2 + i] = totals[2 + i] + off * off
+        return totals
+
+    totals = lax.fori_loop(0, S, finish_row, [jnp.zeros((P2, C), F32)] * 4)
+    off = [v * (1.0 / (S * S)) for v in totals[:2]]
+    mean = [pivot[i] + off[i] for i in range(2)]
+    total = [totals[2 + i] - S * S * off[i] * off[i] for i in range(2)]
     stats = sum(group_stats(mean[i], total[i], float(S * S), 64 * i) for i in range(2))
     stats_ref[...] = jnp.broadcast_to(stats[None], stats_ref.shape)
 
@@ -329,7 +327,7 @@
         scores = lax.dot_general(query[at], flat[at], (((1,), (1,)), ((), ())), preferred_element_type=F32)
         scores = jnp.where(seen, scores, -1e30)
         weights = jnp.exp(scores - jnp.max(scores, axis=1, keepdims=True))
-        weights = (weights / jnp.sum(weights, axis=1, keepdims=True)).astype(BF)
+        weights = (weights * (1.0 / jnp.sum(weights, axis=1, keepdims=True))).astype(BF)
         parts.append(dot(weights, flat[at]).astype(BF))
     update = dot(jnp.concatenate(parts, axis=0), update_ref[...])
     out = (mid.reshape(rows, C) + update).astype(BF)
@@ -370,8 +368,24 @@
         cost_estimate=cost(2048 * C * 4, 2048 * C * 2),
         name="latent_stats",
     )(x.reshape(2048, C))
+    def combine(first, count, conv_weight, *before):
+        return pl.pallas_call(
+            weights_kernel,
+            grid=(count,),
+            out_shape=jax.ShapeDtypeStruct((12, 3, C, C), BF),
+            in_specs=[pl.BlockSpec((3, 1, 3, 256, C), lambda i: (0, (i + first) // 2, 0, (i + first) % 2, 0))]
+            + [pl.BlockSpec(memory_space=pl.ANY)] * len(before),
+            out_specs=pl.BlockSpec((12, 1, 256, C), lambda i: (0, (i + first) // 2, (i + first) % 2, 0)),
+            input_output_aliases={1: 0} if before else {},
+            compiler_params=params(),
+            cost_estimate=cost(count * C * C, count * 11 * C * C * 2),
+            name="weights",
+        )(conv_weight, *before)
+
     around = lambda v, by: lax.ppermute(v, "rows", [(i, (i + by) % 4) for i in range(4)])
     up, down, far = around(up, 1), around(down, 3), around(own, 2)
+    _, early = lax.optimization_barrier((own, conv_weight))
+    rim_x, weights = lax.optimization_barrier((x, combine(0, 1, early)))
     rim = pl.pallas_call(
         rim_kernel,
         out_shape=jax.ShapeDtypeStruct((16, 2, RIM, C), BF),
@@ -381,24 +395,10 @@
         compiler_params=params(),
         cost_estimate=cost(2**22, 4 * 2**20),
         name="rim",
-    )(x, up, down, own, far).reshape(32, RIM, C)
-
-    def combine(first, conv_weight, *before):
-        return pl.pallas_call(
-            weights_kernel,
-            grid=(3,),
-            out_shape=jax.ShapeDtypeStruct((12, 3, C, C), BF),
-            in_specs=[pl.BlockSpec((3, 1, 3, 256, C), lambda i: (0, (i + first) // 2, 0, (i + first) % 2, 0))]
-            + [pl.BlockSpec(memory_space=pl.ANY)] * len(before),
-            out_specs=pl.BlockSpec((12, 1, 256, C), lambda i: (0, (i + first) // 2, (i + first) % 2, 0)),
-            input_output_aliases={1: 0} if before else {},
-            compiler_params=params(),
-            cost_estimate=cost(4 * 8 * C * C, 32 * C * C * 2),
-            name="weights",
-        )(conv_weight, *before)
+    )(rim_x, up, down, own, far).reshape(32, RIM, C)
 
     rim, early = lax.optimization_barrier((rim, conv_weight))
-    rim, patch, weights = lax.optimization_barrier((rim, patch, combine(0, early)))
+    rim, patch, weights = lax.optimization_barrier((rim, patch, combine(1, 2, early, weights)))
     rim = exchange(rim, TM)
     first = lax.axis_index("core") == 0
     row = lambda at: lax.dynamic_slice_in_dim(patch, at, S, axis=1)
@@ -407,7 +407,7 @@
     core = lax.ppermute(core, "core", [(0, 1), (1, 0)])
     pairs = [(4 + i, i + 1) for i in range(3)] + [(i + 1, 4 + i) for i in range(3)]
     band = lax.ppermute(band, ("core", "rows"), pairs)
-    weights = combine(3, late, weights)
+    weights = combine(3, 3, late, weights)
     score = (dot(w_query, w_key.T) * (1.0 / C**0.5)).astype(BF)
     update = dot(w_value, w_out).astype(BF)
 

time: 157 us -> 156 us (level)
    ppermute x3, waiting for transfers between devices: 4.19 us -> 0.01 us  [local(): lax.ppermute(v, 'rows', [(i, (i + by) % 4) for i in range(4)])]
    all_to_all x4, waiting for transfers between devices: 10.9 us -> 13.8 us  [local(): lax.all_to_all(v[None], axes, split_axis=1, concat_axis=0, tiled=True)[:, 0]]
    pallas_call x2 -> x3, Pallas kernels: 17.8 us -> 18.8 us  [combine(): pl.pallas_call(weights_kernel, grid=(count,), out_shape=jax.ShapeDtypeStr...]
  transfers between devices with their start and end apart: 9 -> 9, of which waited for: 5 -> 3; matrix products, arithmetic and copies ran while one was open for 3% -> 3% of each run, Pallas kernels for 16% -> 17%
where the time goes in v10:
time: 156 us; the launch traced here: 155 us
  Pallas kernels  64.9 us (42%)
  starting transfers between devices  33.9 us (22%)
  blocking collectives  33.7 us (22%)
  waiting for transfers between devices  13.8 us (9%)
  local copies, waits for them, and re-layouts  5.86 us (4%)
  matrix products  2.51 us (2%)
    all_to_all x1, blocking collectives, local(): lax.all_to_all(v[None], axes, split_axis=1, concat_axis=0, tiled=True)[:, 0]  33.7 us
    pallas_call x1, Pallas kernels, local(): pl.pallas_call(conv_kernel, out_shape=(jax.ShapeDtypeStruct((S * S, 2, P2...  26 us
    all_to_all x4, starting transfers between devices, local(): lax.all_to_all(v[None], axes, split_axis=1, concat_axis=0, tiled=True)[:, 0]  24.9 us
    pallas_call x3, Pallas kernels, combine(): pl.pallas_call(weights_kernel, grid=(count,), out_shape=jax.ShapeDtypeStr...  18.8 us
    all_to_all x4, waiting for transfers between devices, local(): lax.all_to_all(v[None], axes, split_axis=1, concat_axis=0, tiled=True)[:, 0]  13.8 us
    pallas_call x1, Pallas kernels, local(): pl.pallas_call(attend_kernel, grid=(S * S // pixels,), out_shape=jax.Shap...  8.5 us
    ppermute x3, starting transfers between devices, local(): lax.ppermute(v, 'rows', [(i, (i + by) % 4) for i in range(4)])  5.06 us
    pallas_call x1, Pallas kernels, local(): pl.pallas_call(latent_stats_kernel, out_shape=(row, row, jax.ShapeDtypeSt...  3.93 us
  transfers between devices with their start and end apart: 9, of which 3 were waited for; matrix products, arithmetic and copies ran while one was open for 3% of the time, Pallas kernels for 17%

profile of v10, /device:TPU:1, one launch (start us, length us, event | category | flops | bytes accessed | tf_op | source)
XLA Modules:
  0.0 155.5 jit_solution(7333170420957204393)
XLA Ops:
  0.0 0.0 copy-start
  0.0 2.7 %inner.1 = bf16[32,64,512]{2,1,0:T(8,128)(2,1)} custom-call(bf16[16,128,512]{2,1,0:T(8,128)(2,1)} %bitcast.30), custom_call_target="tpu_custom_call" | custom-call | flops 1048576 | bytes 4194304 | tf_op jit(solution)/shard_map/inner/pallas_call | solution.py:350
  2.7 8.6 %all-to-all-start = ((bf16[1,32,64,512]{3,2,0,1:T(8,128)(2,1)}), bf16[1,32,64,512]{3,2,0,1:T(8,128)(2,1)S(1)}, u32[]{:S(2)}, u32[]{:S(2)}) async-start(bf16[1,32,64,512]{3,2,0,1:T(8,128)(2,1)} %bitcast.33), calls=%async_computation | async-start | bytes 4194304 | tf_op jit(solution)/shard_map/all_to_all | solution.py:347
  11.3 3.9 %latent_stats.1 = (bf16[144,512]{1,0:T(8,128)(2,1)}, bf16[144,512]{1,0:T(8,128)(2,1)}, bf16[16,512]{1,0:T(8,128)(2,1)}) custom-call(bf16[2048,512]{1,0:T(8,128)(2,1)} %bitcast.31), custom_call_target="tpu_custom_call" | custom-call | flops 4194304 | bytes 2097152 | tf_op jit(solution)/shard_map/latent_stats/pallas_call | solution.py:362
  15.2 1.6 %collective-permute-start = (bf16[144,512]{1,0:T(8,128)(2,1)}, bf16[144,512]{1,0:T(8,128)(2,1)S(1)}, u32[]{:S(2)}, u32[]{:S(2)}) collective-permute-start(bf16[144,512]{1,0:T(8,128)(2,1)} %get-tuple-element.24), channel_id=1, source_target_pairs={{0,1},{1,2},{2,3},{3,0},{4,5},{5,6},{6,7},{7,4},{8,9},{9,10},{10,1... | collective-permute-start | bytes 442376 | tf_op jit(solution)/shard_map/ppermute | solution.py:385
  16.8 2.1 %collective-permute-start.1 = (bf16[144,512]{1,0:T(8,128)(2,1)}, bf16[144,512]{1,0:T(8,128)(2,1)S(1)}, u32[]{:S(2)}, u32[]{:S(2)}) collective-permute-start(bf16[144,512]{1,0:T(8,128)(2,1)} %get-tuple-element.25), channel_id=1, source_target_pairs={{0,3},{1,0},{2,1},{3,2},{4,7},{5,4},{6,5},{7,6},{8,11},{9,8},{10,9... | collective-permute-start | bytes 442376 | tf_op jit(solution)/shard_map/ppermute | solution.py:385
  19.0 1.3 collective-permute-start.2
  20.3 4.4 %weights.3.refs_0_ = bf16[12,3,512,512]{3,2,1,0:T(8,128)(2,1)} custom-call(bf16[3,3,3,512,512]{4,3,2,1,0:T(8,128)(2,1)} %plain_ref.1), custom_call_target="tpu_custom_call" | custom-call | flops 262144 | bytes 5767168 | tf_op jit(solution)/shard_map/weights/pallas_call | solution.py:372
  24.7 0.0 collective-permute-done.2.far_ref
  24.7 0.0 collective-permute-done.up_ref
  24.7 0.0 copy-start.6
  24.7 0.0 collective-permute-done.1.down_ref
  24.7 0.6 copy-done.9
  25.3 0.1 copy-done.6
  25.4 0.7 copy-done.7
  26.0 3.4 %rim.1 = bf16[16,2,24,512]{3,2,1,0:T(8,128)(2,1)} custom-call(bf16[16,128,512]{2,1,0:T(8,128)(2,1)} %bitcast.32, bf16[144,512]{1,0:T(8,128)(2,1)} %copy-done.6, bf16[144,512]{1,0:T(8,128)(2,1)} %copy-done.7, bf16[16,512]{1,0:T(8,128)(2,1)} %get-tuple-element.21.own_ref, bf16[16,512]{1,0:T(8,128)(2,1)} %copy-done.9), custom_call_target="tpu_custom_call" | custom-call | flops 4194304 | bytes 4194304 | tf_op jit(solution)/shard_map/rim/pallas_call | solution.py:389
  29.4 5.5 %weights.4.refs_0_ = bf16[12,3,512,512]{3,2,1,0:T(8,128)(2,1)} custom-call(bf16[3,3,3,512,512]{4,3,2,1,0:T(8,128)(2,1)} %plain_ref.1, bf16[12,3,512,512]{3,2,1,0:T(8,128)(2,1)} %weights.3.refs_0_), custom_call_target="tpu_custom_call", output_to_operand_aliasing={{}: (1, {})} | custom-call | flops 524288 | bytes 11534336 | tf_op jit(solution)/shard_map/weights/pallas_call | solution.py:372
  34.9 4.7 %all-to-all-done = bf16[1,32,64,512]{3,2,0,1:T(8,128)(2,1)S(1)} async-done(((bf16[1,32,64,512]{3,2,0,1:T(8,128)(2,1)}), bf16[1,32,64,512]{3,2,0,1:T(8,128)(2,1)S(1)}, u32[]{:S(2)}, u32[]{:S(2)}) %all-to-all-start) | async-done | bytes 2097184 | tf_op jit(solution)/shard_map/all_to_all | solution.py:347
  39.6 4.4 %all-to-all-start.1 = ((bf16[1,32,24,512]{3,2,0,1:T(8,128)(2,1)}), bf16[1,32,24,512]{3,2,0,1:T(8,128)(2,1)S(1)}, u32[]{:S(2)}, u32[]{:S(2)}) async-start(bf16[1,32,24,512]{3,2,0,1:T(8,128)(2,1)} %bitcast.8), calls=%async_computation.1 | async-start | bytes 1572864 | tf_op jit(solution)/shard_map/all_to_all | solution.py:347
  44.0 0.9 constant_dynamic-slice_fusion
  44.9 0.3 collective-permute-start.3
  45.2 3.6 %collective-permute-start.4 = (bf16[32,8,512]{2,1,0:T(8,128)(2,1)}, bf16[32,8,512]{2,1,0:T(8,128)(2,1)}, u32[]{:S(2)}, u32[]{:S(2)}) collective-permute-start(bf16[32,8,512]{2,1,0:T(8,128)(2,1)} %get-tuple-element.32), channel_id=1, source_target_pairs={{4,1},{5,2},{6,3},{1,4},{2,5},{3,6},{12,9},{13,10},{14,11},{9,12},... | collective-permute-start | bytes 786440 | tf_op jit(solution)/shard_map/ppermute | solution.py:409
  48.8 0.6 pad_add_fusion.place_ref
  49.4 8.9 %weights.5.sums_ref = bf16[12,3,512,512]{3,2,1,0:T(8,128)(2,1)} custom-call(bf16[3,3,3,512,512]{4,3,2,1,0:T(8,128)(2,1)} %plain_ref.1, bf16[12,3,512,512]{3,2,1,0:T(8,128)(2,1)} %weights.4.refs_0_), custom_call_target="tpu_custom_call", output_to_operand_aliasing={{}: (1, {})} | custom-call | flops 786432 | bytes 17301504 | tf_op jit(solution)/shard_map/weights/pallas_call | solution.py:372
  58.3 0.0 copy-done.1
  58.3 0.0 collective-permute-done.3.core_ref
  58.3 0.0 collective-permute-done.4.band_ref
  58.3 0.0 all-to-all-done.1
  58.3 0.0 copy-start.2
  58.4 0.9 copy-done.2
  59.2 26.0 %conv.1 = (bf16[64,2,16,512]{3,2,1,0:T(8,128)(2,1)}, f32[8,16,128]{2,1,0:T(8,128)}) custom-call(s32[2]{0:T(128)} %pad_add_fusion.place_ref, bf16[32,64,512]{2,1,0:T(8,128)(2,1)} %bitcast.36, bf16[32,24,512]{2,1,0:T(8,128)(2,1)} %bitcast.38, bf16[32,8,512]{2,1,0:T(8,128)(2,1)} %collective-permute-done.3.core_ref, ...), custom_call_target="tpu_custom_call" | custom-call | flops 12884901888 | bytes 29360128 | tf_op jit(solution)/shard_map/conv/pallas_call | solution.py:414
  85.2 0.0 copy-start.3
  85.2 0.0 copy-start.4
  85.3 5.6 %all-to-all-start.2 = ((f32[1,8,16,128]{3,2,0,1:T(8,128)}), f32[1,8,16,128]{3,2,0,1:T(8,128)S(1)}, u32[]{:S(2)}, u32[]{:S(2)}) async-start(f32[1,8,16,128]{3,2,0,1:T(8,128)} %bitcast.42), calls=%async_computation.2 | async-start | bytes 131072 | tf_op jit(solution)/shard_map/all_to_all | solution.py:347
  90.8 0.0 copy-done
  90.8 0.0 copy-done.10
  90.8 1.3 fusion.score_ref
  92.1 3.7 %all-to-all-done.2 = f32[1,8,16,128]{3,2,0,1:T(8,128)S(1)} async-done(((f32[1,8,16,128]{3,2,0,1:T(8,128)}), f32[1,8,16,128]{3,2,0,1:T(8,128)S(1)}, u32[]{:S(2)}, u32[]{:S(2)}) %all-to-all-start.2) | async-done | bytes 65568 | tf_op jit(solution)/shard_map/all_to_all | solution.py:347
  95.8 0.6 copy-done.5
  96.4 1.6 %merge.1 = f32[16,16,128]{2,1,0:T(8,128)} custom-call(f32[8,16,128]{2,1,0:T(8,128)} %bitcast.40), custom_call_target="tpu_custom_call" | custom-call | tf_op jit(solution)/shard_map/merge/pallas_call | solution.py:433
  98.0 6.4 %all-to-all-start.3 = ((f32[1,16,16,128]{3,2,0,1:T(8,128)}), f32[1,16,16,128]{3,2,0,1:T(8,128)S(1)}, u32[]{:S(2)}, u32[]{:S(2)}) async-start(f32[1,16,16,128]{3,2,0,1:T(8,128)} %bitcast.39), calls=%async_computation.3 | async-start | bytes 262144 | tf_op jit(solution)/shard_map/all_to_all | solution.py:347
  104.4 0.0 copy-done.3
  104.4 1.2 convolution_convert_fusion.update_ref
  105.6 5.4 %all-to-all-done.3 = f32[1,16,16,128]{3,2,0,1:T(8,128)S(1)} async-done(((f32[1,16,16,128]{3,2,0,1:T(8,128)}), f32[1,16,16,128]{3,2,0,1:T(8,128)S(1)}, u32[]{:S(2)}, u32[]{:S(2)}) %all-to-all-start.3) | async-done | bytes 131104 | tf_op jit(solution)/shard_map/all_to_all | solution.py:347
  111.1 0.6 copy-done.8
  111.7 8.5 %attend.1 = bf16[32,64,512]{2,1,0:T(8,128)(2,1)} custom-call(bf16[64,2,16,512]{3,2,1,0:T(8,128)(2,1)} %get-tuple-element.35.mid_ref, f32[16,16,128]{2,1,0:T(8,128)} %bitcast.41, bf16[512,512]{1,0:T(8,128)(2,1)} %fusion.score_ref, bf16[512,512]{1,0:T(8,128)(2,1)} %convolution_convert_fusion.update_ref), custom_call_target="tpu_custom_call" | custom-call | flops 4294967296 | bytes 8388608 | tf_op jit(solution)/shard_map/attend/pallas_call | solution.py:443
  120.2 33.7 %all_to_all.20 = bf16[1,32,64,512]{3,2,0,1:T(8,128)(2,1)S(1)} all-to-all(bf16[1,32,64,512]{3,2,0,1:T(8,128)(2,1)} %bitcast.37), channel_id=1, replica_groups=mesh['x'=4,'y'=4,'core'=2,'rows'=4] {'x','y','core'}, dimensions={1} | all-to-all | bytes 4194304 | tf_op jit(solution)/shard_map/all_to_all | solution.py:347
  153.9 1.5 copy.14
  (7 shorter events, 0.0 us)
Async XLA Ops:
  0.0 90.8 %copy-start = (bf16[512,512]{1,0:T(8,128)(2,1)S(1)}, bf16[512,512]{1,0:T(8,128)(2,1)}, u32[]{:S(2)}) copy-start(bf16[512,512]{1,0:T(8,128)(2,1)} %param.8) | copy-start | bytes 1572868
  2.7 36.9 %all-to-all-start = ((bf16[1,32,64,512]{3,2,0,1:T(8,128)(2,1)}), bf16[1,32,64,512]{3,2,0,1:T(8,128)(2,1)S(1)}, u32[]{:S(2)}, u32[]{:S(2)}) async-start(bf16[1,32,64,512]{3,2,0,1:T(8,128)(2,1)} %bitcast.33), calls=%async_computation | async-start | bytes 4194304 | tf_op jit(solution)/shard_map/all_to_all | solution.py:347
  15.2 9.5 %collective-permute-start = (bf16[144,512]{1,0:T(8,128)(2,1)}, bf16[144,512]{1,0:T(8,128)(2,1)S(1)}, u32[]{:S(2)}, u32[]{:S(2)}) collective-permute-start(bf16[144,512]{1,0:T(8,128)(2,1)} %get-tuple-element.24), channel_id=1, source_target_pairs={{0,1},{1,2},{2,3},{3,0},{4,5},{5,6},{6,7},{7,4},{8,9},{9,10},{10,1... | collective-permute-start | bytes 442376 | tf_op jit(solution)/shard_map/ppermute | solution.py:385
  16.8 7.9 %collective-permute-start.1 = (bf16[144,512]{1,0:T(8,128)(2,1)}, bf16[144,512]{1,0:T(8,128)(2,1)S(1)}, u32[]{:S(2)}, u32[]{:S(2)}) collective-permute-start(bf16[144,512]{1,0:T(8,128)(2,1)} %get-tuple-element.25), channel_id=1, source_target_pairs={{0,3},{1,0},{2,1},{3,2},{4,7},{5,4},{6,5},{7,6},{8,11},{9,8},{10,9... | collective-permute-start | bytes 442376 | tf_op jit(solution)/shard_map/ppermute | solution.py:385
  19.0 5.7 %collective-permute-start.2 = (bf16[16,512]{1,0:T(8,128)(2,1)}, bf16[16,512]{1,0:T(8,128)(2,1)S(1)}, u32[]{:S(2)}, u32[]{:S(2)}) collective-permute-start(bf16[16,512]{1,0:T(8,128)(2,1)} %get-tuple-element.21.own_ref), channel_id=1, source_target_pairs={{0,2},{1,3},{2,0},{3,1},{4,6},{5,7},{6,4},{7,5},{8,10},{9,11},{10,... | collective-permute-start | bytes 49160 | tf_op jit(solution)/shard_map/ppermute | solution.py:385
  24.7 0.6 copy-start.9
  24.7 0.7 copy-start.6
  25.4 0.7 copy-start.7
  39.6 18.8 %copy-start.1 = (bf16[1,32,64,512]{3,2,0,1:T(8,128)(2,1)}, bf16[1,32,64,512]{3,2,0,1:T(8,128)(2,1)S(1)}, u32[]{:S(2)}) copy-start(bf16[1,32,64,512]{3,2,0,1:T(8,128)(2,1)S(1)} %all-to-all-done) | copy-start | bytes 6291460
  39.6 18.8 %all-to-all-start.1 = ((bf16[1,32,24,512]{3,2,0,1:T(8,128)(2,1)}), bf16[1,32,24,512]{3,2,0,1:T(8,128)(2,1)S(1)}, u32[]{:S(2)}, u32[]{:S(2)}) async-start(bf16[1,32,24,512]{3,2,0,1:T(8,128)(2,1)} %bitcast.8), calls=%async_computation.1 | async-start | bytes 1572864 | tf_op jit(solution)/shard_map/all_to_all | solution.py:347
  44.9 13.5 %collective-permute-start.3 = (bf16[32,8,512]{2,1,0:T(8,128)(2,1)}, bf16[32,8,512]{2,1,0:T(8,128)(2,1)}, u32[]{:S(2)}, u32[]{:S(2)}) collective-permute-start(bf16[32,8,512]{2,1,0:T(8,128)(2,1)} %get-tuple-element.31), channel_id=1, source_target_pairs={{0,4},{4,0},{1,5},{5,1},{2,6},{6,2},{3,7},{7,3},{8,12},{12,8},{9,1... | collective-permute-start | bytes 786440 | tf_op jit(solution)/shard_map/ppermute | solution.py:407
  45.2 13.1 %collective-permute-start.4 = (bf16[32,8,512]{2,1,0:T(8,128)(2,1)}, bf16[32,8,512]{2,1,0:T(8,128)(2,1)}, u32[]{:S(2)}, u32[]{:S(2)}) collective-permute-start(bf16[32,8,512]{2,1,0:T(8,128)(2,1)} %get-tuple-element.32), channel_id=1, source_target_pairs={{4,1},{5,2},{6,3},{1,4},{2,5},{3,6},{12,9},{13,10},{14,11},{9,12},... | collective-permute-start | bytes 786440 | tf_op jit(solution)/shard_map/ppermute | solution.py:409
  58.3 0.9 copy-start.2
  59.2 31.6 %copy-start.10 = (bf16[512,512]{1,0:T(8,128)(2,1)S(1)}, bf16[512,512]{1,0:T(8,128)(2,1)}, u32[]{:S(2)}) copy-start(bf16[512,512]{1,0:T(8,128)(2,1)} %param.9) | copy-start | bytes 1572868
  85.2 19.1 %copy-start.3 = (bf16[512,512]{1,0:T(8,128)(2,1)S(1)}, bf16[512,512]{1,0:T(8,128)(2,1)}, u32[]{:S(2)}) copy-start(bf16[512,512]{1,0:T(8,128)(2,1)} %param.10) | copy-start | bytes 1572868
  85.2 19.1 %copy-start.4 = (bf16[512,512]{1,0:T(8,128)(2,1)S(1)}, bf16[512,512]{1,0:T(8,128)(2,1)}, u32[]{:S(2)}) copy-start(bf16[512,512]{1,0:T(8,128)(2,1)} %param.11) | copy-start | bytes 1572868
  85.3 10.5 %all-to-all-start.2 = ((f32[1,8,16,128]{3,2,0,1:T(8,128)}), f32[1,8,16,128]{3,2,0,1:T(8,128)S(1)}, u32[]{:S(2)}, u32[]{:S(2)}) async-start(f32[1,8,16,128]{3,2,0,1:T(8,128)} %bitcast.42), calls=%async_computation.2 | async-start | bytes 131072 | tf_op jit(solution)/shard_map/all_to_all | solution.py:347
  95.8 0.6 copy-start.5
  98.0 13.0 %all-to-all-start.3 = ((f32[1,16,16,128]{3,2,0,1:T(8,128)}), f32[1,16,16,128]{3,2,0,1:T(8,128)S(1)}, u32[]{:S(2)}, u32[]{:S(2)}) async-start(f32[1,16,16,128]{3,2,0,1:T(8,128)} %bitcast.39), calls=%async_computation.3 | async-start | bytes 262144 | tf_op jit(solution)/shard_map/all_to_all | solution.py:347
  111.1 0.6 copy-start.8

commit v11 on v10

--- a/solution.py
+++ b/solution.py
@@ -17,15 +17,14 @@
 EPS = 1e-6
 COMBINED = {(i // 4, i % 4): n for n, i in enumerate(i for i in range(16) if i not in (0, 3, 12, 15))}
 BF, F32 = jnp.bfloat16, jnp.float32
-HI = lax.Precision.HIGHEST
 
 
 def iota(shape, dim):
     return lax.broadcasted_iota(jnp.int32, shape, dim)
 
 
-def dot(a, b, precision=None):
-    return jnp.dot(a, b, preferred_element_type=F32, precision=precision)
+def dot(a, b):
+    return jnp.dot(a, b, preferred_element_type=F32)
 
 
 def params():
@@ -36,18 +35,30 @@
     return pl.CostEstimate(flops=flops, bytes_accessed=nbytes, transcendentals=0)
 
 
+def bf16_terms(v):
+    high = v.astype(BF).astype(F32)
+    middle = (v - high).astype(BF).astype(F32)
+    return [high, middle, v - high - middle]
+
+
+def pick_dot(v, ones):
+    n = v.shape[0]
+    parts = dot(jnp.concatenate(bf16_terms(v), axis=0).astype(BF), ones)
+    return parts[:n] + parts[n : 2 * n] + parts[2 * n :]
+
+
 def to_groups(lane):
-    return (iota((C, 128), 0) // 16 + lane == iota((C, 128), 1)).astype(F32)
-
-
-def from_groups(lane, dtype=F32):
-    return (iota((128, C), 1) // 16 + lane == iota((128, C), 0)).astype(dtype)
-
-
-def group_stats(mean, m2, count, lane):
-    group_mean = dot(mean, to_groups(lane), HI) * (1.0 / 16.0)
-    off = mean - dot(group_mean, from_groups(lane), HI)
-    return group_mean + dot(m2 + count * (off * off), to_groups(lane + 32), HI)
+    return (iota((C, 128), 0) // 16 + lane == iota((C, 128), 1)).astype(BF)
+
+
+def from_groups(lane):
+    return (iota((128, C), 1) // 16 + lane == iota((128, C), 0)).astype(BF)
+
+
+def group_stats(mean, m2, count):
+    group_mean = pick_dot(mean, to_groups(0)) * (1.0 / 16.0)
+    off = mean - pick_dot(group_mean, from_groups(0))
+    return group_mean + pick_dot(m2 + count * (off * off), to_groups(32))
 
 
 def merge(parts, count):
@@ -61,9 +72,7 @@
 
 
 def split_terms(v):
-    high = v.astype(BF).astype(F32)
-    middle = (v - high).astype(BF).astype(F32)
-    return jnp.concatenate([high, middle, v - high - middle, jnp.zeros_like(v)], axis=1)
+    return jnp.concatenate(bf16_terms(v) + [jnp.zeros_like(v)], axis=1)
 
 
 def join_terms(v):
@@ -87,7 +96,7 @@
     mean = pivot + off
     m2 = jnp.sum(totals[1], axis=0, keepdims=True) - n * off * off
     wide = lambda v: jnp.broadcast_to(v, (8, C))
-    row = split_terms(group_stats(wide(mean), wide(m2), float(n), 0))
+    row = split_terms(group_stats(wide(mean), wide(m2), float(n)))
     row = jnp.concatenate([row, jnp.zeros_like(row)], axis=0).astype(BF)
     out_ref[...] = row
     up_ref[:128, :] = x_ref[n - 128 :, :]
@@ -209,7 +218,7 @@
     pieces = dot((iota((T, T * 8), 1) == row * 8 + 4).astype(BF), tail).astype(BF)
     for i in range(2):
         norm[i] = sum(
-            dot(pieces[:, 128 * k : 128 * k + 128], from_groups(32 * i, BF)) for k in range(3)
+            dot(pieces[:, 128 * k : 128 * k + 128], from_groups(32 * i)) for k in range(3)
         ).reshape(2, P2, C)
 
     for first, pixels in ((0, 16), (16, 8)):
@@ -294,7 +303,8 @@
     off = [v * (1.0 / (S * S)) for v in totals[:2]]
     mean = [pivot[i] + off[i] for i in range(2)]
     total = [totals[2 + i] - S * S * off[i] * off[i] for i in range(2)]
-    stats = sum(group_stats(mean[i], total[i], float(S * S), 64 * i) for i in range(2))
+    stats = group_stats(jnp.concatenate(mean, axis=0), jnp.concatenate(total, axis=0), float(S * S))
+    stats = stats[:P2] + pltpu.roll(stats[P2:], 64, 1)
     stats_ref[...] = jnp.broadcast_to(stats[None], stats_ref.shape)
 
 
@@ -308,9 +318,9 @@
     def _():
         count = float(S * S * 16 * 8)
         whole = finish(merge(parts_ref[...], count), 16.0 * count)
+        both = jnp.concatenate([whole, pltpu.roll(whole, 64, 1)], axis=0)
         for i in range(2):
-            for j in range(2):
-                norm[i, j] = dot(whole, from_groups(64 * j + 32 * i), HI)
+            norm[i] = pick_dot(both, from_groups(32 * i)).reshape(2, P2, C)
 
     pixels = mid_ref.shape[0]
     rows = pixels * T
@@ -398,7 +408,7 @@
     )(rim_x, up, down, own, far).reshape(32, RIM, C)
 
     rim, early = lax.optimization_barrier((rim, conv_weight))
-    rim, patch, weights = lax.optimization_barrier((rim, patch, combine(1, 2, early, weights)))
+    rim, patch, weights = lax.optimization_barrier((rim, patch, combine(1, 3, early, weights)))
     rim = exchange(rim, TM)
     first = lax.axis_index("core") == 0
     row = lambda at: lax.dynamic_slice_in_dim(patch, at, S, axis=1)
@@ -407,7 +417,7 @@
     core = lax.ppermute(core, "core", [(0, 1), (1, 0)])
     pairs = [(4 + i, i + 1) for i in range(3)] + [(i + 1, 4 + i) for i in range(3)]
     band = lax.ppermute(band, ("core", "rows"), pairs)
-    weights = combine(3, 3, late, weights)
+    weights = combine(4, 2, late, weights)
     score = (dot(w_query, w_key.T) * (1.0 / C**0.5)).astype(BF)
     update = dot(w_value, w_out).astype(BF)
 

time: 156 us -> 153 us (0.981)
  starting transfers between devices: 33.9 us -> 30.5 us
    all_to_all x4, starting transfers between devices: 24.9 us -> 22.4 us  [local(): lax.all_to_all(v[None], axes, split_axis=1, concat_axis=0, tiled=True)[:, 0]]
  transfers between devices with their start and end apart: 9 -> 9, of which waited for: 3 -> 4; matrix products, arithmetic and copies ran while one was open for 3% -> 3% of each run, Pallas kernels for 17% -> 17%
where the time goes in v11:
time: 153 us; the launch traced here: 152 us
  Pallas kernels  63.9 us (42%)
  blocking collectives  33.7 us (22%)
  starting transfers between devices  30.5 us (20%)
  waiting for transfers between devices  14.6 us (10%)
  local copies, waits for them, and re-layouts  5.87 us (4%)
  matrix products  2.52 us (2%)
    all_to_all x1, blocking collectives, local(): lax.all_to_all(v[None], axes, split_axis=1, concat_axis=0, tiled=True)[:, 0]  33.7 us
    pallas_call x1, Pallas kernels, local(): pl.pallas_call(conv_kernel, out_shape=(jax.ShapeDtypeStruct((S * S, 2, P2...  25.4 us
    all_to_all x4, starting transfers between devices, local(): lax.all_to_all(v[None], axes, split_axis=1, concat_axis=0, tiled=True)[:, 0]  22.4 us
    pallas_call x3, Pallas kernels, combine(): pl.pallas_call(weights_kernel, grid=(count,), out_shape=jax.ShapeDtypeStr...  18.8 us
    all_to_all x4, waiting for transfers between devices, local(): lax.all_to_all(v[None], axes, split_axis=1, concat_axis=0, tiled=True)[:, 0]  14.6 us
    pallas_call x1, Pallas kernels, local(): pl.pallas_call(attend_kernel, grid=(S * S // pixels,), out_shape=jax.Shap...  8.29 us
    ppermute x3, starting transfers between devices, local(): lax.ppermute(v, 'rows', [(i, (i + by) % 4) for i in range(4)])  5.06 us
    pallas_call x1, Pallas kernels, local(): pl.pallas_call(latent_stats_kernel, out_shape=(row, row, jax.ShapeDtypeSt...  3.64 us
  transfers between devices with their start and end apart: 9, of which 4 were waited for; matrix products, arithmetic and copies ran while one was open for 3% of the time, Pallas kernels for 17%

profile of v11, /device:TPU:1, one launch (start us, length us, event | category | flops | bytes accessed | tf_op | source)
XLA Modules:
  0.0 151.9 jit_solution(16801777629104018086)
XLA Ops:
  0.0 0.0 copy-start
  0.0 2.7 %inner.1 = bf16[32,64,512]{2,1,0:T(8,128)(2,1)} custom-call(bf16[16,128,512]{2,1,0:T(8,128)(2,1)} %bitcast.30), custom_call_target="tpu_custom_call" | custom-call | flops 1048576 | bytes 4194304 | tf_op jit(solution)/shard_map/inner/pallas_call | solution.py:360
  2.7 8.6 %all-to-all-start = ((bf16[1,32,64,512]{3,2,0,1:T(8,128)(2,1)}), bf16[1,32,64,512]{3,2,0,1:T(8,128)(2,1)S(1)}, u32[]{:S(2)}, u32[]{:S(2)}) async-start(bf16[1,32,64,512]{3,2,0,1:T(8,128)(2,1)} %bitcast.33), calls=%async_computation | async-start | bytes 4194304 | tf_op jit(solution)/shard_map/all_to_all | solution.py:357
  11.3 3.6 %latent_stats.1 = (bf16[144,512]{1,0:T(8,128)(2,1)}, bf16[144,512]{1,0:T(8,128)(2,1)}, bf16[16,512]{1,0:T(8,128)(2,1)}) custom-call(bf16[2048,512]{1,0:T(8,128)(2,1)} %bitcast.31), custom_call_target="tpu_custom_call" | custom-call | flops 4194304 | bytes 2097152 | tf_op jit(solution)/shard_map/latent_stats/pallas_call | solution.py:372
  14.9 1.6 %collective-permute-start = (bf16[144,512]{1,0:T(8,128)(2,1)}, bf16[144,512]{1,0:T(8,128)(2,1)S(1)}, u32[]{:S(2)}, u32[]{:S(2)}) collective-permute-start(bf16[144,512]{1,0:T(8,128)(2,1)} %get-tuple-element.24), channel_id=1, source_target_pairs={{0,1},{1,2},{2,3},{3,0},{4,5},{5,6},{6,7},{7,4},{8,9},{9,10},{10,1... | collective-permute-start | bytes 442376 | tf_op jit(solution)/shard_map/ppermute | solution.py:395
  16.5 2.1 %collective-permute-start.1 = (bf16[144,512]{1,0:T(8,128)(2,1)}, bf16[144,512]{1,0:T(8,128)(2,1)S(1)}, u32[]{:S(2)}, u32[]{:S(2)}) collective-permute-start(bf16[144,512]{1,0:T(8,128)(2,1)} %get-tuple-element.25), channel_id=1, source_target_pairs={{0,3},{1,0},{2,1},{3,2},{4,7},{5,4},{6,5},{7,6},{8,11},{9,8},{10,9... | collective-permute-start | bytes 442376 | tf_op jit(solution)/shard_map/ppermute | solution.py:395
  18.7 1.3 collective-permute-start.2
  20.0 4.4 %weights.3.refs_0_ = bf16[12,3,512,512]{3,2,1,0:T(8,128)(2,1)} custom-call(bf16[3,3,3,512,512]{4,3,2,1,0:T(8,128)(2,1)} %plain_ref.1), custom_call_target="tpu_custom_call" | custom-call | flops 262144 | bytes 5767168 | tf_op jit(solution)/shard_map/weights/pallas_call | solution.py:382
  24.4 0.0 collective-permute-done.2.far_ref
  24.4 0.0 collective-permute-done.up_ref
  24.4 0.0 copy-start.6
  24.4 0.0 collective-permute-done.1.down_ref
  24.4 0.6 copy-done.9
  25.0 0.1 copy-done.6
  25.1 0.7 copy-done.7
  25.7 3.4 %rim.1 = bf16[16,2,24,512]{3,2,1,0:T(8,128)(2,1)} custom-call(bf16[16,128,512]{2,1,0:T(8,128)(2,1)} %bitcast.32, bf16[144,512]{1,0:T(8,128)(2,1)} %copy-done.6, bf16[144,512]{1,0:T(8,128)(2,1)} %copy-done.7, bf16[16,512]{1,0:T(8,128)(2,1)} %get-tuple-element.21.own_ref, bf16[16,512]{1,0:T(8,128)(2,1)} %copy-done.9), custom_call_target="tpu_custom_call" | custom-call | flops 4194304 | bytes 4194304 | tf_op jit(solution)/shard_map/rim/pallas_call | solution.py:399
  29.1 8.9 %weights.4.refs_0_ = bf16[12,3,512,512]{3,2,1,0:T(8,128)(2,1)} custom-call(bf16[3,3,3,512,512]{4,3,2,1,0:T(8,128)(2,1)} %plain_ref.1, bf16[12,3,512,512]{3,2,1,0:T(8,128)(2,1)} %weights.3.refs_0_), custom_call_target="tpu_custom_call", output_to_operand_aliasing={{}: (1, {})} | custom-call | flops 786432 | bytes 17301504 | tf_op jit(solution)/shard_map/weights/pallas_call | solution.py:382
  38.1 1.5 all-to-all-done
  39.6 6.7 %all-to-all-start.1 = ((bf16[1,32,24,512]{3,2,0,1:T(8,128)(2,1)}), bf16[1,32,24,512]{3,2,0,1:T(8,128)(2,1)S(1)}, u32[]{:S(2)}, u32[]{:S(2)}) async-start(bf16[1,32,24,512]{3,2,0,1:T(8,128)(2,1)} %bitcast.8), calls=%async_computation.1 | async-start | bytes 1572864 | tf_op jit(solution)/shard_map/all_to_all | solution.py:357
  46.3 0.9 constant_dynamic-slice_fusion
  47.2 0.2 collective-permute-start.3
  47.4 2.8 %collective-permute-start.4 = (bf16[32,8,512]{2,1,0:T(8,128)(2,1)}, bf16[32,8,512]{2,1,0:T(8,128)(2,1)}, u32[]{:S(2)}, u32[]{:S(2)}) collective-permute-start(bf16[32,8,512]{2,1,0:T(8,128)(2,1)} %get-tuple-element.32), channel_id=1, source_target_pairs={{4,1},{5,2},{6,3},{1,4},{2,5},{3,6},{12,9},{13,10},{14,11},{9,12},... | collective-permute-start | bytes 786440 | tf_op jit(solution)/shard_map/ppermute | solution.py:419
  50.2 0.6 pad_add_fusion.place_ref
  50.8 5.5 %weights.5.sums_ref = bf16[12,3,512,512]{3,2,1,0:T(8,128)(2,1)} custom-call(bf16[3,3,3,512,512]{4,3,2,1,0:T(8,128)(2,1)} %plain_ref.1, bf16[12,3,512,512]{3,2,1,0:T(8,128)(2,1)} %weights.4.refs_0_), custom_call_target="tpu_custom_call", output_to_operand_aliasing={{}: (1, {})} | custom-call | flops 524288 | bytes 11534336 | tf_op jit(solution)/shard_map/weights/pallas_call | solution.py:382
  56.3 0.0 copy-done.1
  56.3 0.0 collective-permute-done.3.core_ref
  56.3 0.0 collective-permute-done.4.band_ref
  56.3 4.2 %all-to-all-done.1 = bf16[1,32,24,512]{3,2,0,1:T(8,128)(2,1)S(1)} async-done(((bf16[1,32,24,512]{3,2,0,1:T(8,128)(2,1)}), bf16[1,32,24,512]{3,2,0,1:T(8,128)(2,1)S(1)}, u32[]{:S(2)}, u32[]{:S(2)}) %all-to-all-start.1) | async-done | bytes 786464 | tf_op jit(solution)/shard_map/all_to_all | solution.py:357
  60.5 0.9 copy-done.2
  61.4 25.4 %conv.1 = (bf16[64,2,16,512]{3,2,1,0:T(8,128)(2,1)}, f32[8,16,128]{2,1,0:T(8,128)}) custom-call(s32[2]{0:T(128)} %pad_add_fusion.place_ref, bf16[32,64,512]{2,1,0:T(8,128)(2,1)} %bitcast.36, bf16[32,24,512]{2,1,0:T(8,128)(2,1)} %bitcast.38, bf16[32,8,512]{2,1,0:T(8,128)(2,1)} %collective-permute-done.3.core_ref, ...), custom_call_target="tpu_custom_call" | custom-call | flops 12884901888 | bytes 29360128 | tf_op jit(solution)/shard_map/conv/pallas_call | solution.py:424
  86.9 0.0 copy-start.3
  86.9 0.0 copy-start.4
  86.9 3.4 %all-to-all-start.2 = ((f32[1,8,16,128]{3,2,0,1:T(8,128)}), f32[1,8,16,128]{3,2,0,1:T(8,128)S(1)}, u32[]{:S(2)}, u32[]{:S(2)}) async-start(f32[1,8,16,128]{3,2,0,1:T(8,128)} %bitcast.42), calls=%async_computation.2 | async-start | bytes 131072 | tf_op jit(solution)/shard_map/all_to_all | solution.py:357
  90.3 0.0 copy-done
  90.3 0.0 copy-done.10
  90.3 1.3 fusion.score_ref
  91.6 3.6 %all-to-all-done.2 = f32[1,8,16,128]{3,2,0,1:T(8,128)S(1)} async-done(((f32[1,8,16,128]{3,2,0,1:T(8,128)}), f32[1,8,16,128]{3,2,0,1:T(8,128)S(1)}, u32[]{:S(2)}, u32[]{:S(2)}) %all-to-all-start.2) | async-done | bytes 65568 | tf_op jit(solution)/shard_map/all_to_all | solution.py:357
  95.2 0.6 copy-done.5
  95.9 1.6 %merge.1 = f32[16,16,128]{2,1,0:T(8,128)} custom-call(f32[8,16,128]{2,1,0:T(8,128)} %bitcast.40), custom_call_target="tpu_custom_call" | custom-call | tf_op jit(solution)/shard_map/merge/pallas_call | solution.py:443
  97.5 3.7 %all-to-all-start.3 = ((f32[1,16,16,128]{3,2,0,1:T(8,128)}), f32[1,16,16,128]{3,2,0,1:T(8,128)S(1)}, u32[]{:S(2)}, u32[]{:S(2)}) async-start(f32[1,16,16,128]{3,2,0,1:T(8,128)} %bitcast.39), calls=%async_computation.3 | async-start | bytes 262144 | tf_op jit(solution)/shard_map/all_to_all | solution.py:357
  101.2 0.0 copy-done.3
  101.2 0.0 copy-done.4
  101.2 1.2 convolution_convert_fusion.update_ref
  102.4 5.2 %all-to-all-done.3 = f32[1,16,16,128]{3,2,0,1:T(8,128)S(1)} async-done(((f32[1,16,16,128]{3,2,0,1:T(8,128)}), f32[1,16,16,128]{3,2,0,1:T(8,128)S(1)}, u32[]{:S(2)}, u32[]{:S(2)}) %all-to-all-start.3) | async-done | bytes 131104 | tf_op jit(solution)/shard_map/all_to_all | solution.py:357
  107.7 0.6 copy-done.8
  108.3 8.3 %attend.1 = bf16[32,64,512]{2,1,0:T(8,128)(2,1)} custom-call(bf16[64,2,16,512]{3,2,1,0:T(8,128)(2,1)} %get-tuple-element.35.mid_ref, f32[16,16,128]{2,1,0:T(8,128)} %bitcast.41, bf16[512,512]{1,0:T(8,128)(2,1)} %fusion.score_ref, bf16[512,512]{1,0:T(8,128)(2,1)} %convolution_convert_fusion.update_ref), custom_call_target="tpu_custom_call" | custom-call | flops 4294967296 | bytes 8388608 | tf_op jit(solution)/shard_map/attend/pallas_call | solution.py:453
  116.6 33.7 %all_to_all.20 = bf16[1,32,64,512]{3,2,0,1:T(8,128)(2,1)S(1)} all-to-all(bf16[1,32,64,512]{3,2,0,1:T(8,128)(2,1)} %bitcast.37), channel_id=1, replica_groups=mesh['x'=4,'y'=4,'core'=2,'rows'=4] {'x','y','core'}, dimensions={1} | all-to-all | bytes 4194304 | tf_op jit(solution)/shard_map/all_to_all | solution.py:357
  150.3 1.5 %copy.14 = bf16[2,8,16,8,512]{4,3,2,1,0:T(8,128)(2,1)} copy(bf16[2,8,16,8,512]{4,3,1,0,2:T(8,128)(2,1)S(1)} %bitcast.34) | data formatting | bytes 4194304 | tf_op jit(solution)/shard_map/transpose | solution.py:465
  (7 shorter events, 0.0 us)
Async XLA Ops:
  0.0 90.3 %copy-start = (bf16[512,512]{1,0:T(8,128)(2,1)S(1)}, bf16[512,512]{1,0:T(8,128)(2,1)}, u32[]{:S(2)}) copy-start(bf16[512,512]{1,0:T(8,128)(2,1)} %param.8) | copy-start | bytes 1572868
  2.7 36.9 %all-to-all-start = ((bf16[1,32,64,512]{3,2,0,1:T(8,128)(2,1)}), bf16[1,32,64,512]{3,2,0,1:T(8,128)(2,1)S(1)}, u32[]{:S(2)}, u32[]{:S(2)}) async-start(bf16[1,32,64,512]{3,2,0,1:T(8,128)(2,1)} %bitcast.33), calls=%async_computation | async-start | bytes 4194304 | tf_op jit(solution)/shard_map/all_to_all | solution.py:357
  14.9 9.5 %collective-permute-start = (bf16[144,512]{1,0:T(8,128)(2,1)}, bf16[144,512]{1,0:T(8,128)(2,1)S(1)}, u32[]{:S(2)}, u32[]{:S(2)}) collective-permute-start(bf16[144,512]{1,0:T(8,128)(2,1)} %get-tuple-element.24), channel_id=1, source_target_pairs={{0,1},{1,2},{2,3},{3,0},{4,5},{5,6},{6,7},{7,4},{8,9},{9,10},{10,1... | collective-permute-start | bytes 442376 | tf_op jit(solution)/shard_map/ppermute | solution.py:395
  16.5 7.9 %collective-permute-start.1 = (bf16[144,512]{1,0:T(8,128)(2,1)}, bf16[144,512]{1,0:T(8,128)(2,1)S(1)}, u32[]{:S(2)}, u32[]{:S(2)}) collective-permute-start(bf16[144,512]{1,0:T(8,128)(2,1)} %get-tuple-element.25), channel_id=1, source_target_pairs={{0,3},{1,0},{2,1},{3,2},{4,7},{5,4},{6,5},{7,6},{8,11},{9,8},{10,9... | collective-permute-start | bytes 442376 | tf_op jit(solution)/shard_map/ppermute | solution.py:395
  18.7 5.7 %collective-permute-start.2 = (bf16[16,512]{1,0:T(8,128)(2,1)}, bf16[16,512]{1,0:T(8,128)(2,1)S(1)}, u32[]{:S(2)}, u32[]{:S(2)}) collective-permute-start(bf16[16,512]{1,0:T(8,128)(2,1)} %get-tuple-element.21.own_ref), channel_id=1, source_target_pairs={{0,2},{1,3},{2,0},{3,1},{4,6},{5,7},{6,4},{7,5},{8,10},{9,11},{10,... | collective-permute-start | bytes 49160 | tf_op jit(solution)/shard_map/ppermute | solution.py:395
  24.4 0.6 copy-start.9
  24.4 0.7 copy-start.6
  25.1 0.7 copy-start.7
  39.6 16.7 %copy-start.1 = (bf16[1,32,64,512]{3,2,0,1:T(8,128)(2,1)}, bf16[1,32,64,512]{3,2,0,1:T(8,128)(2,1)S(1)}, u32[]{:S(2)}) copy-start(bf16[1,32,64,512]{3,2,0,1:T(8,128)(2,1)S(1)} %all-to-all-done) | copy-start | bytes 6291460
  39.6 20.9 %all-to-all-start.1 = ((bf16[1,32,24,512]{3,2,0,1:T(8,128)(2,1)}), bf16[1,32,24,512]{3,2,0,1:T(8,128)(2,1)S(1)}, u32[]{:S(2)}, u32[]{:S(2)}) async-start(bf16[1,32,24,512]{3,2,0,1:T(8,128)(2,1)} %bitcast.8), calls=%async_computation.1 | async-start | bytes 1572864 | tf_op jit(solution)/shard_map/all_to_all | solution.py:357
  47.2 9.1 %collective-permute-start.3 = (bf16[32,8,512]{2,1,0:T(8,128)(2,1)}, bf16[32,8,512]{2,1,0:T(8,128)(2,1)}, u32[]{:S(2)}, u32[]{:S(2)}) collective-permute-start(bf16[32,8,512]{2,1,0:T(8,128)(2,1)} %get-tuple-element.31), channel_id=1, source_target_pairs={{0,4},{4,0},{1,5},{5,1},{2,6},{6,2},{3,7},{7,3},{8,12},{12,8},{9,1... | collective-permute-start | bytes 786440 | tf_op jit(solution)/shard_map/ppermute | solution.py:417
  47.4 8.9 %collective-permute-start.4 = (bf16[32,8,512]{2,1,0:T(8,128)(2,1)}, bf16[32,8,512]{2,1,0:T(8,128)(2,1)}, u32[]{:S(2)}, u32[]{:S(2)}) collective-permute-start(bf16[32,8,512]{2,1,0:T(8,128)(2,1)} %get-tuple-element.32), channel_id=1, source_target_pairs={{4,1},{5,2},{6,3},{1,4},{2,5},{3,6},{12,9},{13,10},{14,11},{9,12},... | collective-permute-start | bytes 786440 | tf_op jit(solution)/shard_map/ppermute | solution.py:419
  60.5 0.9 copy-start.2
  61.4 28.9 %copy-start.10 = (bf16[512,512]{1,0:T(8,128)(2,1)S(1)}, bf16[512,512]{1,0:T(8,128)(2,1)}, u32[]{:S(2)}) copy-start(bf16[512,512]{1,0:T(8,128)(2,1)} %param.9) | copy-start | bytes 1572868
  86.9 14.3 %copy-start.3 = (bf16[512,512]{1,0:T(8,128)(2,1)S(1)}, bf16[512,512]{1,0:T(8,128)(2,1)}, u32[]{:S(2)}) copy-start(bf16[512,512]{1,0:T(8,128)(2,1)} %param.10) | copy-start | bytes 1572868
  86.9 14.3 %copy-start.4 = (bf16[512,512]{1,0:T(8,128)(2,1)S(1)}, bf16[512,512]{1,0:T(8,128)(2,1)}, u32[]{:S(2)}) copy-start(bf16[512,512]{1,0:T(8,128)(2,1)} %param.11) | copy-start | bytes 1572868
  86.9 8.4 %all-to-all-start.2 = ((f32[1,8,16,128]{3,2,0,1:T(8,128)}), f32[1,8,16,128]{3,2,0,1:T(8,128)S(1)}, u32[]{:S(2)}, u32[]{:S(2)}) async-start(f32[1,8,16,128]{3,2,0,1:T(8,128)} %bitcast.42), calls=%async_computation.2 | async-start | bytes 131072 | tf_op jit(solution)/shard_map/all_to_all | solution.py:357
  95.2 0.6 copy-start.5
  97.5 10.2 %all-to-all-start.3 = ((f32[1,16,16,128]{3,2,0,1:T(8,128)}), f32[1,16,16,128]{3,2,0,1:T(8,128)S(1)}, u32[]{:S(2)}, u32[]{:S(2)}) async-start(f32[1,16,16,128]{3,2,0,1:T(8,128)} %bitcast.39), calls=%async_computation.3 | async-start | bytes 262144 | tf_op jit(solution)/shard_map/all_to_all | solution.py:357
  107.7 0.6 copy-start.8

commit v12 on v11

--- a/solution.py
+++ b/solution.py
@@ -48,11 +48,11 @@
 
 
 def to_groups(lane):
-    return (iota((C, 128), 0) // 16 + lane == iota((C, 128), 1)).astype(BF)
+    return ((iota((C, 128), 0) >> 4) + lane == iota((C, 128), 1)).astype(BF)
 
 
 def from_groups(lane):
-    return (iota((128, C), 1) // 16 + lane == iota((128, C), 0)).astype(BF)
+    return ((iota((128, C), 1) >> 4) + lane == iota((128, C), 0)).astype(BF)
 
 
 def group_stats(mean, m2, count):
@@ -67,7 +67,7 @@
     mean = total * (1.0 / n)
     off = parts - mean[None]
     between = pltpu.roll(jnp.sum(off * off, axis=0), 32, 1)
-    is_mean = (iota(total.shape, 1) // 32) % 2 == 0
+    is_mean = (iota(total.shape, 1) & 32) == 0
     return jnp.where(is_mean, mean, total + count * between)
 
 
@@ -106,7 +106,7 @@
 
 
 def finish(whole, count):
-    is_mean = (iota(whole.shape, 1) // 32) % 2 == 0
+    is_mean = (iota(whole.shape, 1) & 32) == 0
     return jnp.where(is_mean, whole, lax.rsqrt(whole * (1.0 / count) + EPS))
 
 
@@ -163,12 +163,18 @@
     lax.fori_loop(0, 16, rows, 0)
 
 
-def turned(in_ref, first, pixels):
+def frame_of(v):
+    return ((v & (P2 - 1)) << 1) | ((v >> 4) & 1)
+
+
+def turn_matrix(pixels):
     rows = pixels * T
-    to, at = iota((rows, rows), 0), iota((rows, rows), 1)
-    frame = 2 * (to % P2) + (to // P2) % 2
-    turn = (at == frame * pixels + to // T).astype(BF)
-    values = in_ref[:, pl.ds(first, pixels), :].reshape(rows, C)
+    to = iota((rows, 1), 0)
+    return (iota((rows, rows), 1) == frame_of(to) * pixels + (to >> 5)).astype(BF)
+
+
+def turned(in_ref, first, pixels, turn):
+    values = in_ref[:, pl.ds(first, pixels), :].reshape(pixels * T, C)
     return dot(turn, values).reshape(pixels, 2, P2, C)
 
 
@@ -180,7 +186,7 @@
 def time_terms(act):
     pixels = act.shape[0]
     even, odd = act[:, 0], act[:, 1]
-    start = iota((pixels * P2, C), 0) % P2 == 0
+    start = (iota((pixels * P2, C), 0) & (P2 - 1)) == 0
 
     def before(v):
         v = pltpu.roll(v.reshape(pixels * P2, C), 1, 0)
@@ -192,7 +198,7 @@
 
 def conv_kernel(
     place_ref, in_ref, rim_ref, core_ref, band_ref, plain_ref, sums_ref, mid_ref, stats_ref,
-    terms, ends, sides, latent, sums, norm, held, sems,
+    terms, ends, sides, latent, sums, norm, wide_turn, held, sems,
 ):
     def arrival(j, l, b, source):
         slot = 4 * (j % 3) + l
@@ -221,20 +227,23 @@
             dot(pieces[:, 128 * k : 128 * k + 128], from_groups(32 * i)) for k in range(3)
         ).reshape(2, P2, C)
 
+    wide_turn[...] = turn_matrix(16)
+    turn = turn_matrix(S)
+    left, right = column == 0, column == 15
     for first, pixels in ((0, 16), (16, 8)):
-        act = activate(turned(rim_ref, first, pixels), norm)
-        p = iota(act.shape, 0) + first
-        out = (column == 0) & ((p < 8) | (p == 16) | (p == 18))
-        out = out | (column == 15) & ((p >= 8) & (p < 16) | (p == 17) | (p == 19))
-        out = out | above & ((p == 16) | (p == 17)) | below & (p >= 18)
-        for j, v in enumerate(time_terms(jnp.where(out, 0.0, act))):
+        act = activate(turned(rim_ref, first, pixels, wide_turn[...] if pixels == 16 else turn), norm)
+        for j, v in enumerate(time_terms(act)):
             for q in range(min(pixels, 20 - first)):
                 p = first + q
+                out = left if p < 8 or p in (16, 18) else right
+                if p >= 16:
+                    out = out | (above if p < 18 else below)
+                value = v[q] * jnp.where(out, 0.0, 1.0)
                 if p < 16:
-                    sides[j, p // S, p % S] = v[q]
+                    sides[j, p // S, p % S] = value
                 else:
-                    ends[j, (p - 16) // 2, (p % 2) * (W - 1)] = v[q]
-    core, band = turned(core_ref, 0, S), turned(band_ref, 0, S)
+                    ends[j, (p - 16) // 2, (p % 2) * (W - 1)] = value
+    core, band = turned(core_ref, 0, S, turn), turned(band_ref, 0, S, turn)
     for i, values in enumerate((jnp.where(half == 0, band, core), jnp.where(half == 0, core, band))):
         act = jnp.where(below if i else above, 0.0, activate(values, norm))
         for j, v in enumerate(time_terms(act)):
@@ -254,7 +263,7 @@
 
     def two_rows(k, _):
         first = pl.multiple_of(16 * k, 16)
-        values = turned(in_ref, first, 16)
+        values = turned(in_ref, first, 16, wide_turn[...])
         latent[pl.ds(first, 16)] = values.astype(BF)
         for j, v in enumerate(time_terms(activate(values, norm))):
             left, right = (sides[j, i, pl.ds(2 * k, 2)][:, None] for i in range(2))
@@ -328,9 +337,9 @@
     flat = ((mid - norm[0][None]) * norm[1][None]).astype(BF).reshape(rows, C)
     query = dot(flat, score_ref[...]).astype(BF)
     n = 256
-    row, column = iota((n, n), 0), iota((n, n), 1)
-    frame = lambda v: 2 * (v % P2) + (v // P2) % 2
-    seen = (row // T == column // T) & (frame(row) >= frame(column))
+    key = lambda v: ((v >> 5) << 6) + frame_of(v)
+    apart = key(iota((n, 1), 0)) - key(iota((1, n), 1))
+    seen = (apart >= 0) & (apart < T)
     parts = []
     for i in range(rows // n):
         at = slice(i * n, i * n + n)
@@ -341,9 +350,9 @@
         parts.append(dot(weights, flat[at]).astype(BF))
     update = dot(jnp.concatenate(parts, axis=0), update_ref[...])
     out = (mid.reshape(rows, C) + update).astype(BF)
-    to = iota((n, n), 0)
-    frame = to // S
-    turn = (iota((n, n), 1) == (to % S) * T + (frame % 2) * P2 + frame // 2).astype(BF)
+    to = iota((n, 1), 0)
+    frame = to >> 3
+    turn = (iota((n, n), 1) == (to & (S - 1)) * T + (frame & 1) * P2 + (frame >> 1)).astype(BF)
     for i in range(rows // (2 * n)):
         pair = [dot(turn, out[(2 * i + k) * n : (2 * i + k + 1) * n]).reshape(T, S, C) for k in range(2)]
         out_ref[:, 16 * i : 16 * i + 16, :] = jnp.concatenate(pair, axis=1).astype(BF)
@@ -433,6 +442,7 @@
             pltpu.VMEM((S * S, 2, P2, C), BF),
             pltpu.VMEM((4, 2, S, S // 2, P2, C), F32),
             pltpu.VMEM((2, 2, P2, C), F32),
+            pltpu.VMEM((16 * T, 16 * T), BF),
             pltpu.VMEM((12, 3, C, C), BF),
             pltpu.SemaphoreType.DMA((12, 3)),
         ],

time: 153 us -> 153 us (level)
  no operation moved by 1% of the time
where the time goes in v12:
time: 153 us; the launch traced here: 152 us
  Pallas kernels  64 us (42%)
  blocking collectives  33.7 us (22%)
  starting transfers between devices  30.5 us (20%)
  waiting for transfers between devices  14.6 us (10%)
  local copies, waits for them, and re-layouts  5.87 us (4%)
  matrix products  2.52 us (2%)
    all_to_all x1, blocking collectives, local(): lax.all_to_all(v[None], axes, split_axis=1, concat_axis=0, tiled=True)[:, 0]  33.7 us
    pallas_call x1, Pallas kernels, local(): pl.pallas_call(conv_kernel, out_shape=(jax.ShapeDtypeStruct((S * S, 2, P2...  25.5 us
    all_to_all x4, starting transfers between devices, local(): lax.all_to_all(v[None], axes, split_axis=1, concat_axis=0, tiled=True)[:, 0]  22.4 us
    pallas_call x3, Pallas kernels, combine(): pl.pallas_call(weights_kernel, grid=(count,), out_shape=jax.ShapeDtypeStr...  18.8 us
    all_to_all x4, waiting for transfers between devices, local(): lax.all_to_all(v[None], axes, split_axis=1, concat_axis=0, tiled=True)[:, 0]  14.6 us
    pallas_call x1, Pallas kernels, local(): pl.pallas_call(attend_kernel, grid=(S * S // pixels,), out_shape=jax.Shap...  8.3 us
    ppermute x3, starting transfers between devices, local(): lax.ppermute(v, 'rows', [(i, (i + by) % 4) for i in range(4)])  5.06 us
    pallas_call x1, Pallas kernels, local(): pl.pallas_call(latent_stats_kernel, out_shape=(row, row, jax.ShapeDtypeSt...  3.64 us
  transfers between devices with their start and end apart: 9, of which 4 were waited for; matrix products, arithmetic and copies ran while one was open for 3% of the time, Pallas kernels for 17%

profile of v12, /device:TPU:1, one launch (start us, length us, event | category | flops | bytes accessed | tf_op | source)
XLA Modules:
  0.0 152.0 jit_solution(5522308984663720575)
XLA Ops:
  0.0 0.0 copy-start
  0.0 2.7 %inner.1 = bf16[32,64,512]{2,1,0:T(8,128)(2,1)} custom-call(bf16[16,128,512]{2,1,0:T(8,128)(2,1)} %bitcast.30), custom_call_target="tpu_custom_call" | custom-call | flops 1048576 | bytes 4194304 | tf_op jit(solution)/shard_map/inner/pallas_call | solution.py:369
  2.7 8.6 %all-to-all-start = ((bf16[1,32,64,512]{3,2,0,1:T(8,128)(2,1)}), bf16[1,32,64,512]{3,2,0,1:T(8,128)(2,1)S(1)}, u32[]{:S(2)}, u32[]{:S(2)}) async-start(bf16[1,32,64,512]{3,2,0,1:T(8,128)(2,1)} %bitcast.33), calls=%async_computation | async-start | bytes 4194304 | tf_op jit(solution)/shard_map/all_to_all | solution.py:366
  11.3 3.6 %latent_stats.1 = (bf16[144,512]{1,0:T(8,128)(2,1)}, bf16[144,512]{1,0:T(8,128)(2,1)}, bf16[16,512]{1,0:T(8,128)(2,1)}) custom-call(bf16[2048,512]{1,0:T(8,128)(2,1)} %bitcast.31), custom_call_target="tpu_custom_call" | custom-call | flops 4194304 | bytes 2097152 | tf_op jit(solution)/shard_map/latent_stats/pallas_call | solution.py:381
  14.9 1.6 %collective-permute-start = (bf16[144,512]{1,0:T(8,128)(2,1)}, bf16[144,512]{1,0:T(8,128)(2,1)S(1)}, u32[]{:S(2)}, u32[]{:S(2)}) collective-permute-start(bf16[144,512]{1,0:T(8,128)(2,1)} %get-tuple-element.24), channel_id=1, source_target_pairs={{0,1},{1,2},{2,3},{3,0},{4,5},{5,6},{6,7},{7,4},{8,9},{9,10},{10,1... | collective-permute-start | bytes 442376 | tf_op jit(solution)/shard_map/ppermute | solution.py:404
  16.5 2.1 %collective-permute-start.1 = (bf16[144,512]{1,0:T(8,128)(2,1)}, bf16[144,512]{1,0:T(8,128)(2,1)S(1)}, u32[]{:S(2)}, u32[]{:S(2)}) collective-permute-start(bf16[144,512]{1,0:T(8,128)(2,1)} %get-tuple-element.25), channel_id=1, source_target_pairs={{0,3},{1,0},{2,1},{3,2},{4,7},{5,4},{6,5},{7,6},{8,11},{9,8},{10,9... | collective-permute-start | bytes 442376 | tf_op jit(solution)/shard_map/ppermute | solution.py:404
  18.7 1.3 collective-permute-start.2
  20.0 4.4 %weights.3.refs_0_ = bf16[12,3,512,512]{3,2,1,0:T(8,128)(2,1)} custom-call(bf16[3,3,3,512,512]{4,3,2,1,0:T(8,128)(2,1)} %plain_ref.1), custom_call_target="tpu_custom_call" | custom-call | flops 262144 | bytes 5767168 | tf_op jit(solution)/shard_map/weights/pallas_call | solution.py:391
  24.4 0.0 collective-permute-done.2.far_ref
  24.4 0.0 collective-permute-done.up_ref
  24.4 0.0 copy-start.6
  24.4 0.0 collective-permute-done.1.down_ref
  24.4 0.6 copy-done.9
  25.0 0.1 copy-done.6
  25.1 0.7 copy-done.7
  25.7 3.4 %rim.1 = bf16[16,2,24,512]{3,2,1,0:T(8,128)(2,1)} custom-call(bf16[16,128,512]{2,1,0:T(8,128)(2,1)} %bitcast.32, bf16[144,512]{1,0:T(8,128)(2,1)} %copy-done.6, bf16[144,512]{1,0:T(8,128)(2,1)} %copy-done.7, bf16[16,512]{1,0:T(8,128)(2,1)} %get-tuple-element.21.own_ref, bf16[16,512]{1,0:T(8,128)(2,1)} %copy-done.9), custom_call_target="tpu_custom_call" | custom-call | flops 4194304 | bytes 4194304 | tf_op jit(solution)/shard_map/rim/pallas_call | solution.py:408
  29.1 8.9 %weights.4.refs_0_ = bf16[12,3,512,512]{3,2,1,0:T(8,128)(2,1)} custom-call(bf16[3,3,3,512,512]{4,3,2,1,0:T(8,128)(2,1)} %plain_ref.1, bf16[12,3,512,512]{3,2,1,0:T(8,128)(2,1)} %weights.3.refs_0_), custom_call_target="tpu_custom_call", output_to_operand_aliasing={{}: (1, {})} | custom-call | flops 786432 | bytes 17301504 | tf_op jit(solution)/shard_map/weights/pallas_call | solution.py:391
  38.1 1.5 all-to-all-done
  39.6 6.7 %all-to-all-start.1 = ((bf16[1,32,24,512]{3,2,0,1:T(8,128)(2,1)}), bf16[1,32,24,512]{3,2,0,1:T(8,128)(2,1)S(1)}, u32[]{:S(2)}, u32[]{:S(2)}) async-start(bf16[1,32,24,512]{3,2,0,1:T(8,128)(2,1)} %bitcast.8), calls=%async_computation.1 | async-start | bytes 1572864 | tf_op jit(solution)/shard_map/all_to_all | solution.py:366
  46.3 0.9 constant_dynamic-slice_fusion
  47.2 0.2 collective-permute-start.3
  47.4 2.8 %collective-permute-start.4 = (bf16[32,8,512]{2,1,0:T(8,128)(2,1)}, bf16[32,8,512]{2,1,0:T(8,128)(2,1)}, u32[]{:S(2)}, u32[]{:S(2)}) collective-permute-start(bf16[32,8,512]{2,1,0:T(8,128)(2,1)} %get-tuple-element.32), channel_id=1, source_target_pairs={{4,1},{5,2},{6,3},{1,4},{2,5},{3,6},{12,9},{13,10},{14,11},{9,12},... | collective-permute-start | bytes 786440 | tf_op jit(solution)/shard_map/ppermute | solution.py:428
  50.2 0.6 pad_add_fusion.place_ref
  50.8 5.5 %weights.5.sums_ref = bf16[12,3,512,512]{3,2,1,0:T(8,128)(2,1)} custom-call(bf16[3,3,3,512,512]{4,3,2,1,0:T(8,128)(2,1)} %plain_ref.1, bf16[12,3,512,512]{3,2,1,0:T(8,128)(2,1)} %weights.4.refs_0_), custom_call_target="tpu_custom_call", output_to_operand_aliasing={{}: (1, {})} | custom-call | flops 524288 | bytes 11534336 | tf_op jit(solution)/shard_map/weights/pallas_call | solution.py:391
  56.3 0.0 copy-done.1
  56.3 0.0 collective-permute-done.3.core_ref
  56.3 0.0 collective-permute-done.4.band_ref
  56.3 4.2 %all-to-all-done.1 = bf16[1,32,24,512]{3,2,0,1:T(8,128)(2,1)S(1)} async-done(((bf16[1,32,24,512]{3,2,0,1:T(8,128)(2,1)}), bf16[1,32,24,512]{3,2,0,1:T(8,128)(2,1)S(1)}, u32[]{:S(2)}, u32[]{:S(2)}) %all-to-all-start.1) | async-done | bytes 786464 | tf_op jit(solution)/shard_map/all_to_all | solution.py:366
  60.5 0.9 copy-done.2
  61.4 25.5 %conv.1 = (bf16[64,2,16,512]{3,2,1,0:T(8,128)(2,1)}, f32[8,16,128]{2,1,0:T(8,128)}) custom-call(s32[2]{0:T(128)} %pad_add_fusion.place_ref, bf16[32,64,512]{2,1,0:T(8,128)(2,1)} %bitcast.36, bf16[32,24,512]{2,1,0:T(8,128)(2,1)} %bitcast.38, bf16[32,8,512]{2,1,0:T(8,128)(2,1)} %collective-permute-done.3.core_ref, ...), custom_call_target="tpu_custom_call" | custom-call | flops 12884901888 | bytes 29360128 | tf_op jit(solution)/shard_map/conv/pallas_call | solution.py:433
  87.0 0.0 copy-start.3
  87.0 0.0 copy-start.4
  87.0 3.4 %all-to-all-start.2 = ((f32[1,8,16,128]{3,2,0,1:T(8,128)}), f32[1,8,16,128]{3,2,0,1:T(8,128)S(1)}, u32[]{:S(2)}, u32[]{:S(2)}) async-start(f32[1,8,16,128]{3,2,0,1:T(8,128)} %bitcast.42), calls=%async_computation.2 | async-start | bytes 131072 | tf_op jit(solution)/shard_map/all_to_all | solution.py:366
  90.4 0.0 copy-done
  90.4 0.0 copy-done.10
  90.5 1.3 fusion.score_ref
  91.7 3.6 %all-to-all-done.2 = f32[1,8,16,128]{3,2,0,1:T(8,128)S(1)} async-done(((f32[1,8,16,128]{3,2,0,1:T(8,128)}), f32[1,8,16,128]{3,2,0,1:T(8,128)S(1)}, u32[]{:S(2)}, u32[]{:S(2)}) %all-to-all-start.2) | async-done | bytes 65568 | tf_op jit(solution)/shard_map/all_to_all | solution.py:366
  95.3 0.6 copy-done.5
  96.0 1.6 %merge.1 = f32[16,16,128]{2,1,0:T(8,128)} custom-call(f32[8,16,128]{2,1,0:T(8,128)} %bitcast.40), custom_call_target="tpu_custom_call" | custom-call | tf_op jit(solution)/shard_map/merge/pallas_call | solution.py:453
  97.6 3.7 %all-to-all-start.3 = ((f32[1,16,16,128]{3,2,0,1:T(8,128)}), f32[1,16,16,128]{3,2,0,1:T(8,128)S(1)}, u32[]{:S(2)}, u32[]{:S(2)}) async-start(f32[1,16,16,128]{3,2,0,1:T(8,128)} %bitcast.39), calls=%async_computation.3 | async-start | bytes 262144 | tf_op jit(solution)/shard_map/all_to_all | solution.py:366
  101.3 0.0 copy-done.3
  101.3 0.0 copy-done.4
  101.3 1.2 convolution_convert_fusion.update_ref
  102.5 5.2 %all-to-all-done.3 = f32[1,16,16,128]{3,2,0,1:T(8,128)S(1)} async-done(((f32[1,16,16,128]{3,2,0,1:T(8,128)}), f32[1,16,16,128]{3,2,0,1:T(8,128)S(1)}, u32[]{:S(2)}, u32[]{:S(2)}) %all-to-all-start.3) | async-done | bytes 131104 | tf_op jit(solution)/shard_map/all_to_all | solution.py:366
  107.8 0.6 copy-done.8
  108.4 8.3 %attend.1 = bf16[32,64,512]{2,1,0:T(8,128)(2,1)} custom-call(bf16[64,2,16,512]{3,2,1,0:T(8,128)(2,1)} %get-tuple-element.35.mid_ref, f32[16,16,128]{2,1,0:T(8,128)} %bitcast.41, bf16[512,512]{1,0:T(8,128)(2,1)} %fusion.score_ref, bf16[512,512]{1,0:T(8,128)(2,1)} %convolution_convert_fusion.update_ref), custom_call_target="tpu_custom_call" | custom-call | flops 4294967296 | bytes 8388608 | tf_op jit(solution)/shard_map/attend/pallas_call | solution.py:463
  116.7 33.7 %all_to_all.20 = bf16[1,32,64,512]{3,2,0,1:T(8,128)(2,1)S(1)} all-to-all(bf16[1,32,64,512]{3,2,0,1:T(8,128)(2,1)} %bitcast.37), channel_id=1, replica_groups=mesh['x'=4,'y'=4,'core'=2,'rows'=4] {'x','y','core'}, dimensions={1} | all-to-all | bytes 4194304 | tf_op jit(solution)/shard_map/all_to_all | solution.py:366
  150.4 1.5 %copy.14 = bf16[2,8,16,8,512]{4,3,2,1,0:T(8,128)(2,1)} copy(bf16[2,8,16,8,512]{4,3,1,0,2:T(8,128)(2,1)S(1)} %bitcast.34) | data formatting | bytes 4194304 | tf_op jit(solution)/shard_map/transpose | solution.py:475
  (7 shorter events, 0.0 us)
Async XLA Ops:
  0.0 90.4 %copy-start = (bf16[512,512]{1,0:T(8,128)(2,1)S(1)}, bf16[512,512]{1,0:T(8,128)(2,1)}, u32[]{:S(2)}) copy-start(bf16[512,512]{1,0:T(8,128)(2,1)} %param.8) | copy-start | bytes 1572868
  2.7 36.9 %all-to-all-start = ((bf16[1,32,64,512]{3,2,0,1:T(8,128)(2,1)}), bf16[1,32,64,512]{3,2,0,1:T(8,128)(2,1)S(1)}, u32[]{:S(2)}, u32[]{:S(2)}) async-start(bf16[1,32,64,512]{3,2,0,1:T(8,128)(2,1)} %bitcast.33), calls=%async_computation | async-start | bytes 4194304 | tf_op jit(solution)/shard_map/all_to_all | solution.py:366
  14.9 9.5 %collective-permute-start = (bf16[144,512]{1,0:T(8,128)(2,1)}, bf16[144,512]{1,0:T(8,128)(2,1)S(1)}, u32[]{:S(2)}, u32[]{:S(2)}) collective-permute-start(bf16[144,512]{1,0:T(8,128)(2,1)} %get-tuple-element.24), channel_id=1, source_target_pairs={{0,1},{1,2},{2,3},{3,0},{4,5},{5,6},{6,7},{7,4},{8,9},{9,10},{10,1... | collective-permute-start | bytes 442376 | tf_op jit(solution)/shard_map/ppermute | solution.py:404
  16.5 7.9 %collective-permute-start.1 = (bf16[144,512]{1,0:T(8,128)(2,1)}, bf16[144,512]{1,0:T(8,128)(2,1)S(1)}, u32[]{:S(2)}, u32[]{:S(2)}) collective-permute-start(bf16[144,512]{1,0:T(8,128)(2,1)} %get-tuple-element.25), channel_id=1, source_target_pairs={{0,3},{1,0},{2,1},{3,2},{4,7},{5,4},{6,5},{7,6},{8,11},{9,8},{10,9... | collective-permute-start | bytes 442376 | tf_op jit(solution)/shard_map/ppermute | solution.py:404
  18.7 5.7 %collective-permute-start.2 = (bf16[16,512]{1,0:T(8,128)(2,1)}, bf16[16,512]{1,0:T(8,128)(2,1)S(1)}, u32[]{:S(2)}, u32[]{:S(2)}) collective-permute-start(bf16[16,512]{1,0:T(8,128)(2,1)} %get-tuple-element.21.own_ref), channel_id=1, source_target_pairs={{0,2},{1,3},{2,0},{3,1},{4,6},{5,7},{6,4},{7,5},{8,10},{9,11},{10,... | collective-permute-start | bytes 49160 | tf_op jit(solution)/shard_map/ppermute | solution.py:404
  24.4 0.6 copy-start.9
  24.4 0.7 copy-start.6
  25.1 0.7 copy-start.7
  39.6 16.7 %copy-start.1 = (bf16[1,32,64,512]{3,2,0,1:T(8,128)(2,1)}, bf16[1,32,64,512]{3,2,0,1:T(8,128)(2,1)S(1)}, u32[]{:S(2)}) copy-start(bf16[1,32,64,512]{3,2,0,1:T(8,128)(2,1)S(1)} %all-to-all-done) | copy-start | bytes 6291460
  39.6 20.9 %all-to-all-start.1 = ((bf16[1,32,24,512]{3,2,0,1:T(8,128)(2,1)}), bf16[1,32,24,512]{3,2,0,1:T(8,128)(2,1)S(1)}, u32[]{:S(2)}, u32[]{:S(2)}) async-start(bf16[1,32,24,512]{3,2,0,1:T(8,128)(2,1)} %bitcast.8), calls=%async_computation.1 | async-start | bytes 1572864 | tf_op jit(solution)/shard_map/all_to_all | solution.py:366
  47.2 9.1 %collective-permute-start.3 = (bf16[32,8,512]{2,1,0:T(8,128)(2,1)}, bf16[32,8,512]{2,1,0:T(8,128)(2,1)}, u32[]{:S(2)}, u32[]{:S(2)}) collective-permute-start(bf16[32,8,512]{2,1,0:T(8,128)(2,1)} %get-tuple-element.31), channel_id=1, source_target_pairs={{0,4},{4,0},{1,5},{5,1},{2,6},{6,2},{3,7},{7,3},{8,12},{12,8},{9,1... | collective-permute-start | bytes 786440 | tf_op jit(solution)/shard_map/ppermute | solution.py:426
  47.4 8.9 %collective-permute-start.4 = (bf16[32,8,512]{2,1,0:T(8,128)(2,1)}, bf16[32,8,512]{2,1,0:T(8,128)(2,1)}, u32[]{:S(2)}, u32[]{:S(2)}) collective-permute-start(bf16[32,8,512]{2,1,0:T(8,128)(2,1)} %get-tuple-element.32), channel_id=1, source_target_pairs={{4,1},{5,2},{6,3},{1,4},{2,5},{3,6},{12,9},{13,10},{14,11},{9,12},... | collective-permute-start | bytes 786440 | tf_op jit(solution)/shard_map/ppermute | solution.py:428
  60.5 0.9 copy-start.2
  61.4 29.0 %copy-start.10 = (bf16[512,512]{1,0:T(8,128)(2,1)S(1)}, bf16[512,512]{1,0:T(8,128)(2,1)}, u32[]{:S(2)}) copy-start(bf16[512,512]{1,0:T(8,128)(2,1)} %param.9) | copy-start | bytes 1572868
  87.0 14.3 %copy-start.3 = (bf16[512,512]{1,0:T(8,128)(2,1)S(1)}, bf16[512,512]{1,0:T(8,128)(2,1)}, u32[]{:S(2)}) copy-start(bf16[512,512]{1,0:T(8,128)(2,1)} %param.10) | copy-start | bytes 1572868
  87.0 14.3 %copy-start.4 = (bf16[512,512]{1,0:T(8,128)(2,1)S(1)}, bf16[512,512]{1,0:T(8,128)(2,1)}, u32[]{:S(2)}) copy-start(bf16[512,512]{1,0:T(8,128)(2,1)} %param.11) | copy-start | bytes 1572868
  87.0 8.4 %all-to-all-start.2 = ((f32[1,8,16,128]{3,2,0,1:T(8,128)}), f32[1,8,16,128]{3,2,0,1:T(8,128)S(1)}, u32[]{:S(2)}, u32[]{:S(2)}) async-start(f32[1,8,16,128]{3,2,0,1:T(8,128)} %bitcast.42), calls=%async_computation.2 | async-start | bytes 131072 | tf_op jit(solution)/shard_map/all_to_all | solution.py:366
  95.3 0.6 copy-start.5
  97.6 10.2 %all-to-all-start.3 = ((f32[1,16,16,128]{3,2,0,1:T(8,128)}), f32[1,16,16,128]{3,2,0,1:T(8,128)S(1)}, u32[]{:S(2)}, u32[]{:S(2)}) async-start(f32[1,16,16,128]{3,2,0,1:T(8,128)} %bitcast.39), calls=%async_computation.3 | async-start | bytes 262144 | tf_op jit(solution)/shard_map/all_to_all | solution.py:366
  107.8 0.6 copy-start.8

commit v13 on v11

--- a/solution.py
+++ b/solution.py
@@ -27,8 +27,8 @@
     return jnp.dot(a, b, preferred_element_type=F32)
 
 
-def params():
-    return pltpu.CompilerParams(vmem_limit_bytes=56 * 2**20)
+def params(mib):
+    return pltpu.CompilerParams(vmem_limit_bytes=mib * 2**20)
 
 
 def cost(flops, nbytes):
@@ -363,7 +363,7 @@
         out_shape=jax.ShapeDtypeStruct((32, S * S, C), BF),
         in_specs=[pl.BlockSpec((16, 64, C), lambda i: (0, i, 0))],
         out_specs=pl.BlockSpec((16, S * S, C), lambda i: (i, 0, 0)),
-        compiler_params=params(),
+        compiler_params=params(16),
         cost_estimate=cost(2**20, 4 * 2**20),
         name="inner",
     )(x)
@@ -374,7 +374,7 @@
         out_shape=(row, row, jax.ShapeDtypeStruct((16, C), BF)),
         in_specs=[vmem],
         out_specs=(vmem,) * 3,
-        compiler_params=params(),
+        compiler_params=params(12),
         cost_estimate=cost(2048 * C * 4, 2048 * C * 2),
         name="latent_stats",
     )(x.reshape(2048, C))
@@ -387,7 +387,7 @@
             + [pl.BlockSpec(memory_space=pl.ANY)] * len(before),
             out_specs=pl.BlockSpec((12, 1, 256, C), lambda i: (0, (i + first) // 2, (i + first) % 2, 0)),
             input_output_aliases={1: 0} if before else {},
-            compiler_params=params(),
+            compiler_params=params(24),
             cost_estimate=cost(count * C * C, count * 11 * C * C * 2),
             name="weights",
         )(conv_weight, *before)
@@ -402,7 +402,7 @@
         in_specs=[vmem] * 5,
         out_specs=vmem,
         scratch_shapes=[pltpu.VMEM((18, 128, 128), F32), pltpu.VMEM((2, 16 * RIM, 128), F32)],
-        compiler_params=params(),
+        compiler_params=params(16),
         cost_estimate=cost(2**22, 4 * 2**20),
         name="rim",
     )(rim_x, up, down, own, far).reshape(32, RIM, C)
@@ -436,7 +436,7 @@
             pltpu.VMEM((12, 3, C, C), BF),
             pltpu.SemaphoreType.DMA((12, 3)),
         ],
-        compiler_params=params(),
+        compiler_params=params(48),
         cost_estimate=cost(512 * 48 * C * C * 2, 28 * 2**20),
         name="conv",
     )(place, patch, rim, core, band, conv_weight, weights)
@@ -445,7 +445,7 @@
         out_shape=jax.ShapeDtypeStruct((16, P2, 128), F32),
         in_specs=[vmem],
         out_specs=vmem,
-        compiler_params=params(),
+        compiler_params=params(4),
         name="merge",
     )(exchange(stats, ("core", "rows")))
     parts = exchange(parts, ("x", "y"))
@@ -457,7 +457,7 @@
         in_specs=[pl.BlockSpec((pixels, 2, P2, C), lambda i: (i, 0, 0, 0)), whole(16, P2, 128)] + [whole(C, C)] * 2,
         out_specs=pl.BlockSpec((T, pixels, C), lambda i: (0, i, 0)),
         scratch_shapes=[pltpu.VMEM((2, 2, P2, C), F32)],
-        compiler_params=params(),
+        compiler_params=params(24),
         cost_estimate=cost(2048 * C * C * 2 * 4, 8 * 2**20),
         name="attend",
     )(mid, parts, score, update)

time: 153 us -> 153 us (level)
  Pallas kernels: 63.9 us -> 47.8 us
  local copies, waits for them, and re-layouts: 5.87 us -> 18.6 us
  starting transfers between devices: 30.5 us -> 34.3 us
  waiting for transfers between devices: 14.6 us -> 17.1 us
  matrix products: 2.52 us -> 0.9 us
    unnamed x22, local copies, waits for them, and re-layouts: 3.47 us -> 15.9 us
    pallas_call x3, Pallas kernels: 18.8 us -> 12.9 us  [combine(): pl.pallas_call(weights_kernel, grid=(count,), out_shape=jax.ShapeDtypeStr...]
    all_to_all x4, starting transfers between devices: 22.4 us -> 25.1 us  [local(): lax.all_to_all(v[None], axes, split_axis=1, concat_axis=0, tiled=True)[:, 0]]
    all_to_all x4, waiting for transfers between devices: 14.6 us -> 17.1 us  [local(): lax.all_to_all(v[None], axes, split_axis=1, concat_axis=0, tiled=True)[:, 0]]
    pallas_call x1, Pallas kernels: 8.29 us -> 5.83 us  [local(): pl.pallas_call(attend_kernel, grid=(S * S // pixels,), out_shape=jax.Shap...]
    pallas_call x1, Pallas kernels: 2.67 us -> 0.33 us  [local(): pl.pallas_call(inner_kernel, grid=(2,), out_shape=jax.ShapeDtypeStruct((3...]
    pallas_call x1, Pallas kernels: 3.64 us -> 1.3 us  [local(): pl.pallas_call(latent_stats_kernel, out_shape=(row, row, jax.ShapeDtypeSt...]
    pallas_call x1, Pallas kernels: 3.41 us -> 1.69 us  [local(): pl.pallas_call(rim_kernel, out_shape=jax.ShapeDtypeStruct((16, 2, RIM, C)...]
  transfers between devices with their start and end apart: 9 -> 9, of which waited for: 4 -> 3; matrix products, arithmetic and copies ran while one was open for 3% -> 1% of each run, Pallas kernels for 17% -> 10%
where the time goes in v13:
time: 153 us; the launch traced here: 152 us
  Pallas kernels  47.8 us (31%)
  starting transfers between devices  34.3 us (22%)
  blocking collectives  33.4 us (22%)
  local copies, waits for them, and re-layouts  18.6 us (12%)
  waiting for transfers between devices  17.1 us (11%)
    all_to_all x1, blocking collectives, local(): lax.all_to_all(v[None], axes, split_axis=1, concat_axis=0, tiled=True)[:, 0]  33.4 us
    all_to_all x4, starting transfers between devices, local(): lax.all_to_all(v[None], axes, split_axis=1, concat_axis=0, tiled=True)[:, 0]  25.1 us
    pallas_call x1, Pallas kernels, local(): pl.pallas_call(conv_kernel, out_shape=(jax.ShapeDtypeStruct((S * S, 2, P2...  25 us
    all_to_all x4, waiting for transfers between devices, local(): lax.all_to_all(v[None], axes, split_axis=1, concat_axis=0, tiled=True)[:, 0]  17.1 us
    unnamed x22, local copies, waits for them, and re-layouts  15.9 us
    pallas_call x3, Pallas kernels, combine(): pl.pallas_call(weights_kernel, grid=(count,), out_shape=jax.ShapeDtypeStr...  12.9 us
    pallas_call x1, Pallas kernels, local(): pl.pallas_call(attend_kernel, grid=(S * S // pixels,), out_shape=jax.Shap...  5.83 us
    ppermute x3, starting transfers between devices, local(): lax.ppermute(v, 'rows', [(i, (i + by) % 4) for i in range(4)])  5.13 us
  transfers between devices with their start and end apart: 9, of which 3 were waited for; matrix products, arithmetic and copies ran while one was open for 1% of the time, Pallas kernels for 10%

profile of v13, /device:TPU:1, one launch (start us, length us, event | category | flops | bytes accessed | tf_op | source)
XLA Modules:
  0.0 152.3 jit_solution(3969547769810899292)
XLA Ops:
  0.0 0.0 copy-start
  0.0 1.6 %copy-done.3 = bf16[1,16,128,512]{3,2,1,0:T(8,128)(2,1)S(1)} copy-done((bf16[1,16,128,512]{3,2,1,0:T(8,128)(2,1)S(1)}, bf16[1,16,128,512]{3,2,1,0:T(8,128)(2,1)}, u32[]{:S(2)}) %copy-start.3) | copy-done | bytes 2097176
  1.7 0.3 inner.1
  2.0 0.0 copy-start.5
  2.0 1.3 copy-done.5
  3.3 8.8 %all-to-all-start = ((bf16[1,32,64,512]{3,2,0,1:T(8,128)(2,1)}), bf16[1,32,64,512]{3,2,0,1:T(8,128)(2,1)}, u32[]{:S(2)}, u32[]{:S(2)}) async-start(bf16[1,32,64,512]{3,2,0,1:T(8,128)(2,1)} %bitcast.33), calls=%async_computation | async-start | bytes 4194304 | tf_op jit(solution)/shard_map/all_to_all | solution.py:357
  12.1 0.0 copy-done.4
  12.1 1.3 latent_stats.1
  13.4 1.7 %collective-permute-start = (bf16[144,512]{1,0:T(8,128)(2,1)S(1)}, bf16[144,512]{1,0:T(8,128)(2,1)S(1)}, u32[]{:S(2)}, u32[]{:S(2)}) collective-permute-start(bf16[144,512]{1,0:T(8,128)(2,1)S(1)} %get-tuple-element.24), channel_id=1, source_target_pairs={{0,1},{1,2},{2,3},{3,0},{4,5},{5,6},{6,7},{7,4},{8,9},{9,10},{10,1... | collective-permute-start | bytes 442376 | tf_op jit(solution)/shard_map/ppermute | solution.py:395
  15.1 2.2 %collective-permute-start.1 = (bf16[144,512]{1,0:T(8,128)(2,1)S(1)}, bf16[144,512]{1,0:T(8,128)(2,1)S(1)}, u32[]{:S(2)}, u32[]{:S(2)}) collective-permute-start(bf16[144,512]{1,0:T(8,128)(2,1)S(1)} %get-tuple-element.25), channel_id=1, source_target_pairs={{0,3},{1,0},{2,1},{3,2},{4,7},{5,4},{6,5},{7,6},{8,11},{9,8},{10,9... | collective-permute-start | bytes 442376 | tf_op jit(solution)/shard_map/ppermute | solution.py:395
  17.3 1.2 collective-permute-start.2
  18.5 5.0 %copy-done.1 = bf16[3,3,3,512,512]{4,3,2,1,0:T(8,128)(2,1)S(1)} copy-done((bf16[3,3,3,512,512]{4,3,2,1,0:T(8,128)(2,1)S(1)}, bf16[3,3,3,512,512]{4,3,2,1,0:T(8,128)(2,1)}, u32[]{:S(2)}) %copy-start.1) | copy-done | bytes 14155800
  23.6 2.9 %weights.3.refs_0_ = bf16[12,3,512,512]{3,2,1,0:T(8,128)(2,1)} custom-call(bf16[3,3,3,512,512]{4,3,2,1,0:T(8,128)(2,1)S(1)} %copy-done.1), custom_call_target="tpu_custom_call" | custom-call | flops 262144 | bytes 5767168 | tf_op jit(solution)/shard_map/weights/pallas_call | solution.py:382
  26.5 0.0 collective-permute-done.2.far_ref
  26.5 0.0 collective-permute-done.up_ref
  26.5 0.0 collective-permute-done.1.down_ref
  26.5 1.7 %rim.1 = bf16[16,2,24,512]{3,2,1,0:T(8,128)(2,1)} custom-call(bf16[16,128,512]{2,1,0:T(8,128)(2,1)S(1)} %bitcast.32, bf16[144,512]{1,0:T(8,128)(2,1)S(1)} %collective-permute-done.up_ref, bf16[144,512]{1,0:T(8,128)(2,1)S(1)} %collective-permute-done.1.down_ref, bf16[16,512]{1,0:T(8,128)(2,1)S(1)} %get-tuple-element.21.own_ref, ...), custom_call_target="tpu_custom_call" | custom-call | flops 4194304 | bytes 4194304 | tf_op jit(solution)/shard_map/rim/pallas_call | solution.py:399
  28.2 5.9 %weights.4.refs_0_ = bf16[12,3,512,512]{3,2,1,0:T(8,128)(2,1)} custom-call(bf16[3,3,3,512,512]{4,3,2,1,0:T(8,128)(2,1)S(1)} %copy-done.1, bf16[12,3,512,512]{3,2,1,0:T(8,128)(2,1)} %weights.3.refs_0_), custom_call_target="tpu_custom_call", output_to_operand_aliasing={{}: (1, {})} | custom-call | flops 786432 | bytes 17301504 | tf_op jit(solution)/shard_map/weights/pallas_call | solution.py:382
  34.0 6.4 %all-to-all-done = bf16[1,32,64,512]{3,2,0,1:T(8,128)(2,1)} async-done(((bf16[1,32,64,512]{3,2,0,1:T(8,128)(2,1)}), bf16[1,32,64,512]{3,2,0,1:T(8,128)(2,1)}, u32[]{:S(2)}, u32[]{:S(2)}) %all-to-all-start) | async-done | bytes 2097184 | tf_op jit(solution)/shard_map/all_to_all | solution.py:357
  40.4 4.4 %all-to-all-start.1 = ((bf16[1,32,24,512]{3,2,0,1:T(8,128)(2,1)}), bf16[1,32,24,512]{3,2,0,1:T(8,128)(2,1)S(1)}, u32[]{:S(2)}, u32[]{:S(2)}) async-start(bf16[1,32,24,512]{3,2,0,1:T(8,128)(2,1)} %bitcast.8), calls=%async_computation.1 | async-start | bytes 1572864 | tf_op jit(solution)/shard_map/all_to_all | solution.py:357
  44.9 1.1 constant_dynamic-slice_fusion
  46.0 0.4 collective-permute-start.3
  46.4 3.6 %collective-permute-start.4 = (bf16[32,8,512]{2,1,0:T(8,128)(2,1)S(1)}, bf16[32,8,512]{2,1,0:T(8,128)(2,1)S(1)}, u32[]{:S(2)}, u32[]{:S(2)}) collective-permute-start(bf16[32,8,512]{2,1,0:T(8,128)(2,1)S(1)} %get-tuple-element.32), channel_id=1, source_target_pairs={{4,1},{5,2},{6,3},{1,4},{2,5},{3,6},{12,9},{13,10},{14,11},{9,12},... | collective-permute-start | bytes 786440 | tf_op jit(solution)/shard_map/ppermute | solution.py:419
  50.0 0.1 pad_add_fusion.place_ref
  50.1 5.0 %copy-done.2 = bf16[3,3,3,512,512]{4,3,2,1,0:T(8,128)(2,1)S(1)} copy-done((bf16[3,3,3,512,512]{4,3,2,1,0:T(8,128)(2,1)S(1)}, bf16[3,3,3,512,512]{4,3,2,1,0:T(8,128)(2,1)}, u32[]{:S(2)}) %copy-start.2) | copy-done | bytes 14155800
  55.1 4.1 %weights.5.sums_ref = bf16[12,3,512,512]{3,2,1,0:T(8,128)(2,1)} custom-call(bf16[3,3,3,512,512]{4,3,2,1,0:T(8,128)(2,1)S(1)} %copy-done.2, bf16[12,3,512,512]{3,2,1,0:T(8,128)(2,1)} %weights.4.refs_0_), custom_call_target="tpu_custom_call", output_to_operand_aliasing={{}: (1, {})} | custom-call | flops 524288 | bytes 11534336 | tf_op jit(solution)/shard_map/weights/pallas_call | solution.py:382
  59.2 0.0 collective-permute-done.3.core_ref
  59.2 0.0 collective-permute-done.4.band_ref
  59.2 0.0 all-to-all-done.1
  59.3 0.0 copy-start.10
  59.3 25.0 %conv.1 = (bf16[64,2,16,512]{3,2,1,0:T(8,128)(2,1)S(1)}, f32[8,16,128]{2,1,0:T(8,128)}) custom-call(s32[2]{0:T(128)S(1)} %pad_add_fusion.place_ref, bf16[32,64,512]{2,1,0:T(8,128)(2,1)} %bitcast.7.in_ref, bf16[32,24,512]{2,1,0:T(8,128)(2,1)S(1)} %bitcast.35, bf16[32,8,512]{2,1,0:T(8,128)(2,1)S(1)} %collective-permute-done.3.core_ref, ...), custom_call_target="tpu_custom_call" | custom-call | flops 12884901888 | bytes 29360128 | tf_op jit(solution)/shard_map/conv/pallas_call | solution.py:424
  84.3 0.0 copy-start.6
  84.3 1.3 copy-done.6
  85.6 5.5 %all-to-all-start.2 = ((f32[1,8,16,128]{3,2,0,1:T(8,128)}), f32[1,8,16,128]{3,2,0,1:T(8,128)S(1)}, u32[]{:S(2)}, u32[]{:S(2)}) async-start(f32[1,8,16,128]{3,2,0,1:T(8,128)} %bitcast.11), calls=%async_computation.2 | async-start | bytes 131072 | tf_op jit(solution)/shard_map/all_to_all | solution.py:357
  91.1 0.0 copy-done
  91.1 0.0 copy-done.10
  91.1 0.5 fusion.score_ref
  91.6 4.5 %all-to-all-done.2 = f32[1,8,16,128]{3,2,0,1:T(8,128)S(1)} async-done(((f32[1,8,16,128]{3,2,0,1:T(8,128)}), f32[1,8,16,128]{3,2,0,1:T(8,128)S(1)}, u32[]{:S(2)}, u32[]{:S(2)}) %all-to-all-start.2) | async-done | bytes 65568 | tf_op jit(solution)/shard_map/all_to_all | solution.py:357
  96.1 0.7 merge.1
  96.8 6.4 %all-to-all-start.3 = ((f32[1,16,16,128]{3,2,0,1:T(8,128)}), f32[1,16,16,128]{3,2,0,1:T(8,128)S(1)}, u32[]{:S(2)}, u32[]{:S(2)}) async-start(f32[1,16,16,128]{3,2,0,1:T(8,128)} %bitcast.14), calls=%async_computation.3 | async-start | bytes 262144 | tf_op jit(solution)/shard_map/all_to_all | solution.py:357
  103.2 0.0 copy-done.8
  103.2 0.0 copy-done.9
  103.2 0.4 convolution_convert_fusion.update_ref
  103.7 6.2 %all-to-all-done.3 = f32[1,16,16,128]{3,2,0,1:T(8,128)S(1)} async-done(((f32[1,16,16,128]{3,2,0,1:T(8,128)}), f32[1,16,16,128]{3,2,0,1:T(8,128)S(1)}, u32[]{:S(2)}, u32[]{:S(2)}) %all-to-all-start.3) | async-done | bytes 131104 | tf_op jit(solution)/shard_map/all_to_all | solution.py:357
  109.9 1.6 %copy-done.7 = bf16[64,2,16,512]{3,2,1,0:T(8,128)(2,1)S(1)} copy-done((bf16[64,2,16,512]{3,2,1,0:T(8,128)(2,1)S(1)}, bf16[64,2,16,512]{3,2,1,0:T(8,128)(2,1)}, u32[]{:S(2)}) %copy-start.7) | copy-done | bytes 2097176
  111.5 5.8 %attend.1 = bf16[32,64,512]{2,1,0:T(8,128)(2,1)S(1)} custom-call(bf16[64,2,16,512]{3,2,1,0:T(8,128)(2,1)S(1)} %copy-done.7, f32[16,16,128]{2,1,0:T(8,128)S(1)} %bitcast.37, bf16[512,512]{1,0:T(8,128)(2,1)S(1)} %fusion.score_ref, bf16[512,512]{1,0:T(8,128)(2,1)S(1)} %convolution_convert_fusion.update_ref), custom_call_target="tpu_custom_call" | custom-call | flops 4294967296 | bytes 8388608 | tf_op jit(solution)/shard_map/attend/pallas_call | solution.py:453
  117.3 33.4 %all_to_all.20 = bf16[1,32,64,512]{3,2,0,1:T(8,128)(2,1)S(1)} all-to-all(bf16[1,32,64,512]{3,2,0,1:T(8,128)(2,1)S(1)} %bitcast.34), channel_id=1, replica_groups=mesh['x'=4,'y'=4,'core'=2,'rows'=4] {'x','y','core'}, dimensions={1} | all-to-all | bytes 4194304 | tf_op jit(solution)/shard_map/all_to_all | solution.py:357
  150.8 1.5 %copy.14 = bf16[2,8,16,8,512]{4,3,2,1,0:T(8,128)(2,1)} copy(bf16[2,8,16,8,512]{4,3,1,0,2:T(8,128)(2,1)S(1)} %bitcast.38) | data formatting | bytes 4194304 | tf_op jit(solution)/shard_map/transpose | solution.py:465
  (7 shorter events, 0.0 us)
Async XLA Ops:
  0.0 91.1 %copy-start = (bf16[512,512]{1,0:T(8,128)(2,1)S(1)}, bf16[512,512]{1,0:T(8,128)(2,1)}, u32[]{:S(2)}) copy-start(bf16[512,512]{1,0:T(8,128)(2,1)} %param.8) | copy-start | bytes 1572868
  0.0 1.6 %copy-start.3 = (bf16[1,16,128,512]{3,2,1,0:T(8,128)(2,1)S(1)}, bf16[1,16,128,512]{3,2,1,0:T(8,128)(2,1)}, u32[]{:S(2)}) copy-start(bf16[1,16,128,512]{3,2,1,0:T(8,128)(2,1)} %param.6) | copy-start | bytes 6291460
  2.0 1.3 copy-start.5
  3.3 8.8 %copy-start.4 = (bf16[1,16,128,512]{3,2,1,0:T(8,128)(2,1)S(1)}, bf16[1,16,128,512]{3,2,1,0:T(8,128)(2,1)}, u32[]{:S(2)}) copy-start(bf16[1,16,128,512]{3,2,1,0:T(8,128)(2,1)} %param.6) | copy-start | bytes 6291460
  3.3 37.1 %all-to-all-start = ((bf16[1,32,64,512]{3,2,0,1:T(8,128)(2,1)}), bf16[1,32,64,512]{3,2,0,1:T(8,128)(2,1)}, u32[]{:S(2)}, u32[]{:S(2)}) async-start(bf16[1,32,64,512]{3,2,0,1:T(8,128)(2,1)} %bitcast.33), calls=%async_computation | async-start | bytes 4194304 | tf_op jit(solution)/shard_map/all_to_all | solution.py:357
  13.4 13.1 %collective-permute-start = (bf16[144,512]{1,0:T(8,128)(2,1)S(1)}, bf16[144,512]{1,0:T(8,128)(2,1)S(1)}, u32[]{:S(2)}, u32[]{:S(2)}) collective-permute-start(bf16[144,512]{1,0:T(8,128)(2,1)S(1)} %get-tuple-element.24), channel_id=1, source_target_pairs={{0,1},{1,2},{2,3},{3,0},{4,5},{5,6},{6,7},{7,4},{8,9},{9,10},{10,1... | collective-permute-start | bytes 442376 | tf_op jit(solution)/shard_map/ppermute | solution.py:395
  15.1 11.4 %collective-permute-start.1 = (bf16[144,512]{1,0:T(8,128)(2,1)S(1)}, bf16[144,512]{1,0:T(8,128)(2,1)S(1)}, u32[]{:S(2)}, u32[]{:S(2)}) collective-permute-start(bf16[144,512]{1,0:T(8,128)(2,1)S(1)} %get-tuple-element.25), channel_id=1, source_target_pairs={{0,3},{1,0},{2,1},{3,2},{4,7},{5,4},{6,5},{7,6},{8,11},{9,8},{10,9... | collective-permute-start | bytes 442376 | tf_op jit(solution)/shard_map/ppermute | solution.py:395
  17.3 9.1 %collective-permute-start.2 = (bf16[16,512]{1,0:T(8,128)(2,1)S(1)}, bf16[16,512]{1,0:T(8,128)(2,1)S(1)}, u32[]{:S(2)}, u32[]{:S(2)}) collective-permute-start(bf16[16,512]{1,0:T(8,128)(2,1)S(1)} %get-tuple-element.21.own_ref), channel_id=1, source_target_pairs={{0,2},{1,3},{2,0},{3,1},{4,6},{5,7},{6,4},{7,5},{8,10},{9,11},{10,... | collective-permute-start | bytes 49160 | tf_op jit(solution)/shard_map/ppermute | solution.py:395
  18.5 5.0 %copy-start.1 = (bf16[3,3,3,512,512]{4,3,2,1,0:T(8,128)(2,1)S(1)}, bf16[3,3,3,512,512]{4,3,2,1,0:T(8,128)(2,1)}, u32[]{:S(2)}) copy-start(bf16[3,3,3,512,512]{4,3,2,1,0:T(8,128)(2,1)} %plain_ref.1) | copy-start | bytes 42467332
  40.4 18.8 %all-to-all-start.1 = ((bf16[1,32,24,512]{3,2,0,1:T(8,128)(2,1)}), bf16[1,32,24,512]{3,2,0,1:T(8,128)(2,1)S(1)}, u32[]{:S(2)}, u32[]{:S(2)}) async-start(bf16[1,32,24,512]{3,2,0,1:T(8,128)(2,1)} %bitcast.8), calls=%async_computation.1 | async-start | bytes 1572864 | tf_op jit(solution)/shard_map/all_to_all | solution.py:357
  46.0 13.3 %collective-permute-start.3 = (bf16[32,8,512]{2,1,0:T(8,128)(2,1)S(1)}, bf16[32,8,512]{2,1,0:T(8,128)(2,1)S(1)}, u32[]{:S(2)}, u32[]{:S(2)}) collective-permute-start(bf16[32,8,512]{2,1,0:T(8,128)(2,1)S(1)} %get-tuple-element.31), channel_id=1, source_target_pairs={{0,4},{4,0},{1,5},{5,1},{2,6},{6,2},{3,7},{7,3},{8,12},{12,8},{9,1... | collective-permute-start | bytes 786440 | tf_op jit(solution)/shard_map/ppermute | solution.py:417
  46.4 12.8 %collective-permute-start.4 = (bf16[32,8,512]{2,1,0:T(8,128)(2,1)S(1)}, bf16[32,8,512]{2,1,0:T(8,128)(2,1)S(1)}, u32[]{:S(2)}, u32[]{:S(2)}) collective-permute-start(bf16[32,8,512]{2,1,0:T(8,128)(2,1)S(1)} %get-tuple-element.32), channel_id=1, source_target_pairs={{4,1},{5,2},{6,3},{1,4},{2,5},{3,6},{12,9},{13,10},{14,11},{9,12},... | collective-permute-start | bytes 786440 | tf_op jit(solution)/shard_map/ppermute | solution.py:419
  50.1 5.0 %copy-start.2 = (bf16[3,3,3,512,512]{4,3,2,1,0:T(8,128)(2,1)S(1)}, bf16[3,3,3,512,512]{4,3,2,1,0:T(8,128)(2,1)}, u32[]{:S(2)}) copy-start(bf16[3,3,3,512,512]{4,3,2,1,0:T(8,128)(2,1)} %plain_ref.1) | copy-start | bytes 42467332
  59.3 31.8 %copy-start.10 = (bf16[512,512]{1,0:T(8,128)(2,1)S(1)}, bf16[512,512]{1,0:T(8,128)(2,1)}, u32[]{:S(2)}) copy-start(bf16[512,512]{1,0:T(8,128)(2,1)} %param.9) | copy-start | bytes 1572868
  84.3 1.3 copy-start.6
  85.6 17.6 %copy-start.8 = (bf16[512,512]{1,0:T(8,128)(2,1)S(1)}, bf16[512,512]{1,0:T(8,128)(2,1)}, u32[]{:S(2)}) copy-start(bf16[512,512]{1,0:T(8,128)(2,1)} %param.10) | copy-start | bytes 1572868
  85.6 17.7 %copy-start.9 = (bf16[512,512]{1,0:T(8,128)(2,1)S(1)}, bf16[512,512]{1,0:T(8,128)(2,1)}, u32[]{:S(2)}) copy-start(bf16[512,512]{1,0:T(8,128)(2,1)} %param.11) | copy-start | bytes 1572868
  85.6 10.5 %all-to-all-start.2 = ((f32[1,8,16,128]{3,2,0,1:T(8,128)}), f32[1,8,16,128]{3,2,0,1:T(8,128)S(1)}, u32[]{:S(2)}, u32[]{:S(2)}) async-start(f32[1,8,16,128]{3,2,0,1:T(8,128)} %bitcast.11), calls=%async_computation.2 | async-start | bytes 131072 | tf_op jit(solution)/shard_map/all_to_all | solution.py:357
  96.8 13.1 %all-to-all-start.3 = ((f32[1,16,16,128]{3,2,0,1:T(8,128)}), f32[1,16,16,128]{3,2,0,1:T(8,128)S(1)}, u32[]{:S(2)}, u32[]{:S(2)}) async-start(f32[1,16,16,128]{3,2,0,1:T(8,128)} %bitcast.14), calls=%async_computation.3 | async-start | bytes 262144 | tf_op jit(solution)/shard_map/all_to_all | solution.py:357
  109.9 1.6 %copy-start.7 = (bf16[64,2,16,512]{3,2,1,0:T(8,128)(2,1)S(1)}, bf16[64,2,16,512]{3,2,1,0:T(8,128)(2,1)}, u32[]{:S(2)}) copy-start(bf16[64,2,16,512]{3,2,1,0:T(8,128)(2,1)} %copy-done.6) | copy-start | bytes 6291460

commit v14 on v13

--- a/solution.py
+++ b/solution.py
@@ -363,7 +363,7 @@
         out_shape=jax.ShapeDtypeStruct((32, S * S, C), BF),
         in_specs=[pl.BlockSpec((16, 64, C), lambda i: (0, i, 0))],
         out_specs=pl.BlockSpec((16, S * S, C), lambda i: (i, 0, 0)),
-        compiler_params=params(16),
+        compiler_params=params(56),
         cost_estimate=cost(2**20, 4 * 2**20),
         name="inner",
     )(x)
@@ -387,7 +387,7 @@
             + [pl.BlockSpec(memory_space=pl.ANY)] * len(before),
             out_specs=pl.BlockSpec((12, 1, 256, C), lambda i: (0, (i + first) // 2, (i + first) % 2, 0)),
             input_output_aliases={1: 0} if before else {},
-            compiler_params=params(24),
+            compiler_params=params(56),
             cost_estimate=cost(count * C * C, count * 11 * C * C * 2),
             name="weights",
         )(conv_weight, *before)
@@ -436,7 +436,7 @@
             pltpu.VMEM((12, 3, C, C), BF),
             pltpu.SemaphoreType.DMA((12, 3)),
         ],
-        compiler_params=params(48),
+        compiler_params=params(56),
         cost_estimate=cost(512 * 48 * C * C * 2, 28 * 2**20),
         name="conv",
     )(place, patch, rim, core, band, conv_weight, weights)

time: 153 us -> 149 us (0.974)
  local copies, waits for them, and re-layouts: 18.6 us -> 5.11 us
  Pallas kernels: 47.8 us -> 56.4 us
  waiting for transfers between devices: 17.1 us -> 20.5 us
  starting transfers between devices: 34.3 us -> 31.6 us
    unnamed x22 -> x18, local copies, waits for them, and re-layouts: 15.9 us -> 2.49 us
    pallas_call x3, Pallas kernels: 12.9 us -> 18.7 us  [combine(): pl.pallas_call(weights_kernel, grid=(count,), out_shape=jax.ShapeDtypeStr...]
    all_to_all x4, waiting for transfers between devices: 17.1 us -> 20.5 us  [local(): lax.all_to_all(v[None], axes, split_axis=1, concat_axis=0, tiled=True)[:, 0]]
    all_to_all x4, starting transfers between devices: 25.1 us -> 22.5 us  [local(): lax.all_to_all(v[None], axes, split_axis=1, concat_axis=0, tiled=True)[:, 0]]
    pallas_call x1, Pallas kernels: 0.33 us -> 2.67 us  [local(): pl.pallas_call(inner_kernel, grid=(2,), out_shape=jax.ShapeDtypeStruct((3...]
  transfers between devices with their start and end apart: 9 -> 9, of which waited for: 3 -> 4; matrix products, arithmetic and copies ran while one was open for 1% -> 2% of each run, Pallas kernels for 10% -> 15%
where the time goes in v14:
time: 149 us
  Pallas kernels  56.4 us (38%)
  blocking collectives  33.4 us (22%)
  starting transfers between devices  31.6 us (21%)
  waiting for transfers between devices  20.5 us (14%)
  local copies, waits for them, and re-layouts  5.11 us (3%)
    all_to_all x1, blocking collectives, local(): lax.all_to_all(v[None], axes, split_axis=1, concat_axis=0, tiled=True)[:, 0]  33.4 us
    pallas_call x1, Pallas kernels, local(): pl.pallas_call(conv_kernel, out_shape=(jax.ShapeDtypeStruct((S * S, 2, P2...  25.4 us
    all_to_all x4, starting transfers between devices, local(): lax.all_to_all(v[None], axes, split_axis=1, concat_axis=0, tiled=True)[:, 0]  22.5 us
    all_to_all x4, waiting for transfers between devices, local(): lax.all_to_all(v[None], axes, split_axis=1, concat_axis=0, tiled=True)[:, 0]  20.5 us
    pallas_call x3, Pallas kernels, combine(): pl.pallas_call(weights_kernel, grid=(count,), out_shape=jax.ShapeDtypeStr...  18.7 us
    pallas_call x1, Pallas kernels, local(): pl.pallas_call(attend_kernel, grid=(S * S // pixels,), out_shape=jax.Shap...  5.83 us
    ppermute x3, starting transfers between devices, local(): lax.ppermute(v, 'rows', [(i, (i + by) % 4) for i in range(4)])  5.13 us
    ppermute x1, starting transfers between devices, local(): band = lax.ppermute(band, ('core', 'rows'), pairs)  3.58 us
  transfers between devices with their start and end apart: 9, of which 4 were waited for; matrix products, arithmetic and copies ran while one was open for 2% of the time, Pallas kernels for 15%

profile of v14, /device:TPU:1, one launch (start us, length us, event | category | flops | bytes accessed | tf_op | source)
XLA Modules:
  0.0 148.8 jit_solution(17141853413376626996)
XLA Ops:
  0.0 0.0 copy-start
  0.0 2.7 %inner.1 = bf16[32,64,512]{2,1,0:T(8,128)(2,1)} custom-call(bf16[16,128,512]{2,1,0:T(8,128)(2,1)} %bitcast.30), custom_call_target="tpu_custom_call" | custom-call | flops 1048576 | bytes 4194304 | tf_op jit(solution)/shard_map/inner/pallas_call | solution.py:360
  2.7 8.8 %all-to-all-start = ((bf16[1,32,64,512]{3,2,0,1:T(8,128)(2,1)}), bf16[1,32,64,512]{3,2,0,1:T(8,128)(2,1)}, u32[]{:S(2)}, u32[]{:S(2)}) async-start(bf16[1,32,64,512]{3,2,0,1:T(8,128)(2,1)} %bitcast.36), calls=%async_computation | async-start | bytes 4194304 | tf_op jit(solution)/shard_map/all_to_all | solution.py:357
  11.5 0.0 copy-done.1
  11.5 1.3 latent_stats.1
  12.8 1.7 %collective-permute-start = (bf16[144,512]{1,0:T(8,128)(2,1)S(1)}, bf16[144,512]{1,0:T(8,128)(2,1)S(1)}, u32[]{:S(2)}, u32[]{:S(2)}) collective-permute-start(bf16[144,512]{1,0:T(8,128)(2,1)S(1)} %get-tuple-element.24), channel_id=1, source_target_pairs={{0,1},{1,2},{2,3},{3,0},{4,5},{5,6},{6,7},{7,4},{8,9},{9,10},{10,1... | collective-permute-start | bytes 442376 | tf_op jit(solution)/shard_map/ppermute | solution.py:395
  14.5 2.2 %collective-permute-start.1 = (bf16[144,512]{1,0:T(8,128)(2,1)S(1)}, bf16[144,512]{1,0:T(8,128)(2,1)S(1)}, u32[]{:S(2)}, u32[]{:S(2)}) collective-permute-start(bf16[144,512]{1,0:T(8,128)(2,1)S(1)} %get-tuple-element.25), channel_id=1, source_target_pairs={{0,3},{1,0},{2,1},{3,2},{4,7},{5,4},{6,5},{7,6},{8,11},{9,8},{10,9... | collective-permute-start | bytes 442376 | tf_op jit(solution)/shard_map/ppermute | solution.py:395
  16.7 1.2 collective-permute-start.2
  17.9 4.4 %weights.3.refs_0_ = bf16[12,3,512,512]{3,2,1,0:T(8,128)(2,1)} custom-call(bf16[3,3,3,512,512]{4,3,2,1,0:T(8,128)(2,1)} %plain_ref.1), custom_call_target="tpu_custom_call" | custom-call | flops 262144 | bytes 5767168 | tf_op jit(solution)/shard_map/weights/pallas_call | solution.py:382
  22.3 0.0 collective-permute-done.2.far_ref
  22.3 0.0 collective-permute-done.up_ref
  22.3 0.0 collective-permute-done.1.down_ref
  22.3 1.7 %rim.1 = bf16[16,2,24,512]{3,2,1,0:T(8,128)(2,1)} custom-call(bf16[16,128,512]{2,1,0:T(8,128)(2,1)S(1)} %bitcast.32, bf16[144,512]{1,0:T(8,128)(2,1)S(1)} %collective-permute-done.up_ref, bf16[144,512]{1,0:T(8,128)(2,1)S(1)} %collective-permute-done.1.down_ref, bf16[16,512]{1,0:T(8,128)(2,1)S(1)} %get-tuple-element.21.own_ref, ...), custom_call_target="tpu_custom_call" | custom-call | flops 4194304 | bytes 4194304 | tf_op jit(solution)/shard_map/rim/pallas_call | solution.py:399
  24.0 8.9 %weights.4.refs_0_ = bf16[12,3,512,512]{3,2,1,0:T(8,128)(2,1)} custom-call(bf16[3,3,3,512,512]{4,3,2,1,0:T(8,128)(2,1)} %plain_ref.1, bf16[12,3,512,512]{3,2,1,0:T(8,128)(2,1)} %weights.3.refs_0_), custom_call_target="tpu_custom_call", output_to_operand_aliasing={{}: (1, {})} | custom-call | flops 786432 | bytes 17301504 | tf_op jit(solution)/shard_map/weights/pallas_call | solution.py:382
  32.9 6.9 %all-to-all-done = bf16[1,32,64,512]{3,2,0,1:T(8,128)(2,1)} async-done(((bf16[1,32,64,512]{3,2,0,1:T(8,128)(2,1)}), bf16[1,32,64,512]{3,2,0,1:T(8,128)(2,1)}, u32[]{:S(2)}, u32[]{:S(2)}) %all-to-all-start) | async-done | bytes 2097184 | tf_op jit(solution)/shard_map/all_to_all | solution.py:357
  39.8 4.4 %all-to-all-start.1 = ((bf16[1,32,24,512]{3,2,0,1:T(8,128)(2,1)}), bf16[1,32,24,512]{3,2,0,1:T(8,128)(2,1)S(1)}, u32[]{:S(2)}, u32[]{:S(2)}) async-start(bf16[1,32,24,512]{3,2,0,1:T(8,128)(2,1)} %bitcast.8), calls=%async_computation.1 | async-start | bytes 1572864 | tf_op jit(solution)/shard_map/all_to_all | solution.py:357
  44.3 1.1 constant_dynamic-slice_fusion
  45.3 0.4 collective-permute-start.3
  45.8 3.6 %collective-permute-start.4 = (bf16[32,8,512]{2,1,0:T(8,128)(2,1)S(1)}, bf16[32,8,512]{2,1,0:T(8,128)(2,1)S(1)}, u32[]{:S(2)}, u32[]{:S(2)}) collective-permute-start(bf16[32,8,512]{2,1,0:T(8,128)(2,1)S(1)} %get-tuple-element.32), channel_id=1, source_target_pairs={{4,1},{5,2},{6,3},{1,4},{2,5},{3,6},{12,9},{13,10},{14,11},{9,12},... | collective-permute-start | bytes 786440 | tf_op jit(solution)/shard_map/ppermute | solution.py:419
  49.4 0.7 pad_add_fusion.place_ref
  50.0 5.5 %weights.5.sums_ref = bf16[12,3,512,512]{3,2,1,0:T(8,128)(2,1)} custom-call(bf16[3,3,3,512,512]{4,3,2,1,0:T(8,128)(2,1)} %plain_ref.1, bf16[12,3,512,512]{3,2,1,0:T(8,128)(2,1)} %weights.4.refs_0_), custom_call_target="tpu_custom_call", output_to_operand_aliasing={{}: (1, {})} | custom-call | flops 524288 | bytes 11534336 | tf_op jit(solution)/shard_map/weights/pallas_call | solution.py:382
  55.5 0.0 collective-permute-done.3.core_ref
  55.5 0.0 copy-start.7
  55.5 0.0 collective-permute-done.4.band_ref
  55.5 0.0 copy-start.8
  55.5 3.1 %all-to-all-done.1 = bf16[1,32,24,512]{3,2,0,1:T(8,128)(2,1)S(1)} async-done(((bf16[1,32,24,512]{3,2,0,1:T(8,128)(2,1)}), bf16[1,32,24,512]{3,2,0,1:T(8,128)(2,1)S(1)}, u32[]{:S(2)}, u32[]{:S(2)}) %all-to-all-start.1) | async-done | bytes 786464 | tf_op jit(solution)/shard_map/all_to_all | solution.py:357
  58.6 0.0 copy-start.3
  58.6 0.0 copy-done.7
  58.6 0.0 copy-done.8
  58.6 0.9 copy-done.3
  59.5 25.4 %conv.1 = (bf16[64,2,16,512]{3,2,1,0:T(8,128)(2,1)}, f32[8,16,128]{2,1,0:T(8,128)}) custom-call(s32[2]{0:T(128)} %pad_add_fusion.place_ref, bf16[32,64,512]{2,1,0:T(8,128)(2,1)} %bitcast.7.in_ref, bf16[32,24,512]{2,1,0:T(8,128)(2,1)} %bitcast.38, bf16[32,8,512]{2,1,0:T(8,128)(2,1)} %copy-done.7, bf16[32,8,512]{2,1,0:T(8,128)(2,1)} %copy-done.8, ...), custom_call_target="tpu_custom_call" | custom-call | flops 12884901888 | bytes 29360128 | tf_op jit(solution)/shard_map/conv/pallas_call | solution.py:424
  84.9 0.0 copy-start.4
  84.9 0.0 copy-start.5
  84.9 5.6 %all-to-all-start.2 = ((f32[1,8,16,128]{3,2,0,1:T(8,128)}), f32[1,8,16,128]{3,2,0,1:T(8,128)S(1)}, u32[]{:S(2)}, u32[]{:S(2)}) async-start(f32[1,8,16,128]{3,2,0,1:T(8,128)} %bitcast.39), calls=%async_computation.2 | async-start | bytes 131072 | tf_op jit(solution)/shard_map/all_to_all | solution.py:357
  90.5 0.0 copy-done
  90.5 0.0 copy-done.6
  90.5 0.5 fusion.score_ref
  91.0 4.5 %all-to-all-done.2 = f32[1,8,16,128]{3,2,0,1:T(8,128)S(1)} async-done(((f32[1,8,16,128]{3,2,0,1:T(8,128)}), f32[1,8,16,128]{3,2,0,1:T(8,128)S(1)}, u32[]{:S(2)}, u32[]{:S(2)}) %all-to-all-start.2) | async-done | bytes 65568 | tf_op jit(solution)/shard_map/all_to_all | solution.py:357
  95.5 0.7 merge.1
  96.2 3.7 %all-to-all-start.3 = ((f32[1,16,16,128]{3,2,0,1:T(8,128)}), f32[1,16,16,128]{3,2,0,1:T(8,128)S(1)}, u32[]{:S(2)}, u32[]{:S(2)}) async-start(f32[1,16,16,128]{3,2,0,1:T(8,128)} %bitcast.14), calls=%async_computation.3 | async-start | bytes 262144 | tf_op jit(solution)/shard_map/all_to_all | solution.py:357
  99.9 0.0 copy-done.4
  99.9 0.0 copy-done.5
  99.9 0.4 convolution_convert_fusion.update_ref
  100.4 6.0 %all-to-all-done.3 = f32[1,16,16,128]{3,2,0,1:T(8,128)S(1)} async-done(((f32[1,16,16,128]{3,2,0,1:T(8,128)}), f32[1,16,16,128]{3,2,0,1:T(8,128)S(1)}, u32[]{:S(2)}, u32[]{:S(2)}) %all-to-all-start.3) | async-done | bytes 131104 | tf_op jit(solution)/shard_map/all_to_all | solution.py:357
  106.4 1.6 %copy-done.2 = bf16[64,2,16,512]{3,2,1,0:T(8,128)(2,1)S(1)} copy-done((bf16[64,2,16,512]{3,2,1,0:T(8,128)(2,1)S(1)}, bf16[64,2,16,512]{3,2,1,0:T(8,128)(2,1)}, u32[]{:S(2)}) %copy-start.2) | copy-done | bytes 2097176
  107.9 5.8 %attend.1 = bf16[32,64,512]{2,1,0:T(8,128)(2,1)S(1)} custom-call(bf16[64,2,16,512]{3,2,1,0:T(8,128)(2,1)S(1)} %copy-done.2, f32[16,16,128]{2,1,0:T(8,128)S(1)} %bitcast.35, bf16[512,512]{1,0:T(8,128)(2,1)S(1)} %fusion.score_ref, bf16[512,512]{1,0:T(8,128)(2,1)S(1)} %convolution_convert_fusion.update_ref), custom_call_target="tpu_custom_call" | custom-call | flops 4294967296 | bytes 8388608 | tf_op jit(solution)/shard_map/attend/pallas_call | solution.py:453
  113.8 33.4 %all_to_all.20 = bf16[1,32,64,512]{3,2,0,1:T(8,128)(2,1)S(1)} all-to-all(bf16[1,32,64,512]{3,2,0,1:T(8,128)(2,1)S(1)} %bitcast.33), channel_id=1, replica_groups=mesh['x'=4,'y'=4,'core'=2,'rows'=4] {'x','y','core'}, dimensions={1} | all-to-all | bytes 4194304 | tf_op jit(solution)/shard_map/all_to_all | solution.py:357
  147.2 1.5 %copy.14 = bf16[2,8,16,8,512]{4,3,2,1,0:T(8,128)(2,1)} copy(bf16[2,8,16,8,512]{4,3,1,0,2:T(8,128)(2,1)S(1)} %bitcast.37) | data formatting | bytes 4194304 | tf_op jit(solution)/shard_map/transpose | solution.py:465
  (3 shorter events, 0.0 us)
Async XLA Ops:
  0.0 90.5 %copy-start = (bf16[512,512]{1,0:T(8,128)(2,1)S(1)}, bf16[512,512]{1,0:T(8,128)(2,1)}, u32[]{:S(2)}) copy-start(bf16[512,512]{1,0:T(8,128)(2,1)} %param.8) | copy-start | bytes 1572868
  2.7 8.8 %copy-start.1 = (bf16[1,16,128,512]{3,2,1,0:T(8,128)(2,1)S(1)}, bf16[1,16,128,512]{3,2,1,0:T(8,128)(2,1)}, u32[]{:S(2)}) copy-start(bf16[1,16,128,512]{3,2,1,0:T(8,128)(2,1)} %param.6) | copy-start | bytes 6291460
  2.7 37.1 %all-to-all-start = ((bf16[1,32,64,512]{3,2,0,1:T(8,128)(2,1)}), bf16[1,32,64,512]{3,2,0,1:T(8,128)(2,1)}, u32[]{:S(2)}, u32[]{:S(2)}) async-start(bf16[1,32,64,512]{3,2,0,1:T(8,128)(2,1)} %bitcast.36), calls=%async_computation | async-start | bytes 4194304 | tf_op jit(solution)/shard_map/all_to_all | solution.py:357
  12.8 9.5 %collective-permute-start = (bf16[144,512]{1,0:T(8,128)(2,1)S(1)}, bf16[144,512]{1,0:T(8,128)(2,1)S(1)}, u32[]{:S(2)}, u32[]{:S(2)}) collective-permute-start(bf16[144,512]{1,0:T(8,128)(2,1)S(1)} %get-tuple-element.24), channel_id=1, source_target_pairs={{0,1},{1,2},{2,3},{3,0},{4,5},{5,6},{6,7},{7,4},{8,9},{9,10},{10,1... | collective-permute-start | bytes 442376 | tf_op jit(solution)/shard_map/ppermute | solution.py:395
  14.5 7.8 %collective-permute-start.1 = (bf16[144,512]{1,0:T(8,128)(2,1)S(1)}, bf16[144,512]{1,0:T(8,128)(2,1)S(1)}, u32[]{:S(2)}, u32[]{:S(2)}) collective-permute-start(bf16[144,512]{1,0:T(8,128)(2,1)S(1)} %get-tuple-element.25), channel_id=1, source_target_pairs={{0,3},{1,0},{2,1},{3,2},{4,7},{5,4},{6,5},{7,6},{8,11},{9,8},{10,9... | collective-permute-start | bytes 442376 | tf_op jit(solution)/shard_map/ppermute | solution.py:395
  16.7 5.6 %collective-permute-start.2 = (bf16[16,512]{1,0:T(8,128)(2,1)S(1)}, bf16[16,512]{1,0:T(8,128)(2,1)S(1)}, u32[]{:S(2)}, u32[]{:S(2)}) collective-permute-start(bf16[16,512]{1,0:T(8,128)(2,1)S(1)} %get-tuple-element.21.own_ref), channel_id=1, source_target_pairs={{0,2},{1,3},{2,0},{3,1},{4,6},{5,7},{6,4},{7,5},{8,10},{9,11},{10,... | collective-permute-start | bytes 49160 | tf_op jit(solution)/shard_map/ppermute | solution.py:395
  39.8 18.8 %all-to-all-start.1 = ((bf16[1,32,24,512]{3,2,0,1:T(8,128)(2,1)}), bf16[1,32,24,512]{3,2,0,1:T(8,128)(2,1)S(1)}, u32[]{:S(2)}, u32[]{:S(2)}) async-start(bf16[1,32,24,512]{3,2,0,1:T(8,128)(2,1)} %bitcast.8), calls=%async_computation.1 | async-start | bytes 1572864 | tf_op jit(solution)/shard_map/all_to_all | solution.py:357
  45.3 10.2 %collective-permute-start.3 = (bf16[32,8,512]{2,1,0:T(8,128)(2,1)S(1)}, bf16[32,8,512]{2,1,0:T(8,128)(2,1)S(1)}, u32[]{:S(2)}, u32[]{:S(2)}) collective-permute-start(bf16[32,8,512]{2,1,0:T(8,128)(2,1)S(1)} %get-tuple-element.31), channel_id=1, source_target_pairs={{0,4},{4,0},{1,5},{5,1},{2,6},{6,2},{3,7},{7,3},{8,12},{12,8},{9,1... | collective-permute-start | bytes 786440 | tf_op jit(solution)/shard_map/ppermute | solution.py:417
  45.8 9.7 %collective-permute-start.4 = (bf16[32,8,512]{2,1,0:T(8,128)(2,1)S(1)}, bf16[32,8,512]{2,1,0:T(8,128)(2,1)S(1)}, u32[]{:S(2)}, u32[]{:S(2)}) collective-permute-start(bf16[32,8,512]{2,1,0:T(8,128)(2,1)S(1)} %get-tuple-element.32), channel_id=1, source_target_pairs={{4,1},{5,2},{6,3},{1,4},{2,5},{3,6},{12,9},{13,10},{14,11},{9,12},... | collective-permute-start | bytes 786440 | tf_op jit(solution)/shard_map/ppermute | solution.py:419
  55.5 3.1 %copy-start.7 = (bf16[32,8,512]{2,1,0:T(8,128)(2,1)}, bf16[32,8,512]{2,1,0:T(8,128)(2,1)S(1)}, u32[]{:S(2)}) copy-start(bf16[32,8,512]{2,1,0:T(8,128)(2,1)S(1)} %collective-permute-done.3.core_ref) | copy-start | bytes 786436
  55.5 3.1 %copy-start.8 = (bf16[32,8,512]{2,1,0:T(8,128)(2,1)}, bf16[32,8,512]{2,1,0:T(8,128)(2,1)S(1)}, u32[]{:S(2)}) copy-start(bf16[32,8,512]{2,1,0:T(8,128)(2,1)S(1)} %collective-permute-done.4.band_ref) | copy-start | bytes 786436
  58.6 0.9 copy-start.3
  59.5 31.0 %copy-start.6 = (bf16[512,512]{1,0:T(8,128)(2,1)S(1)}, bf16[512,512]{1,0:T(8,128)(2,1)}, u32[]{:S(2)}) copy-start(bf16[512,512]{1,0:T(8,128)(2,1)} %param.9) | copy-start | bytes 1572868
  84.9 15.0 %copy-start.4 = (bf16[512,512]{1,0:T(8,128)(2,1)S(1)}, bf16[512,512]{1,0:T(8,128)(2,1)}, u32[]{:S(2)}) copy-start(bf16[512,512]{1,0:T(8,128)(2,1)} %param.10) | copy-start | bytes 1572868
  84.9 15.0 %copy-start.5 = (bf16[512,512]{1,0:T(8,128)(2,1)S(1)}, bf16[512,512]{1,0:T(8,128)(2,1)}, u32[]{:S(2)}) copy-start(bf16[512,512]{1,0:T(8,128)(2,1)} %param.11) | copy-start | bytes 1572868
  84.9 10.5 %all-to-all-start.2 = ((f32[1,8,16,128]{3,2,0,1:T(8,128)}), f32[1,8,16,128]{3,2,0,1:T(8,128)S(1)}, u32[]{:S(2)}, u32[]{:S(2)}) async-start(f32[1,8,16,128]{3,2,0,1:T(8,128)} %bitcast.39), calls=%async_computation.2 | async-start | bytes 131072 | tf_op jit(solution)/shard_map/all_to_all | solution.py:357
  96.2 10.2 %all-to-all-start.3 = ((f32[1,16,16,128]{3,2,0,1:T(8,128)}), f32[1,16,16,128]{3,2,0,1:T(8,128)S(1)}, u32[]{:S(2)}, u32[]{:S(2)}) async-start(f32[1,16,16,128]{3,2,0,1:T(8,128)} %bitcast.14), calls=%async_computation.3 | async-start | bytes 262144 | tf_op jit(solution)/shard_map/all_to_all | solution.py:357
  106.4 1.6 %copy-start.2 = (bf16[64,2,16,512]{3,2,1,0:T(8,128)(2,1)S(1)}, bf16[64,2,16,512]{3,2,1,0:T(8,128)(2,1)}, u32[]{:S(2)}) copy-start(bf16[64,2,16,512]{3,2,1,0:T(8,128)(2,1)} %get-tuple-element.35.mid_ref) | copy-start | bytes 6291460

commit v15 on v14

--- a/solution.py
+++ b/solution.py
@@ -408,7 +408,7 @@
     )(rim_x, up, down, own, far).reshape(32, RIM, C)
 
     rim, early = lax.optimization_barrier((rim, conv_weight))
-    rim, patch, weights = lax.optimization_barrier((rim, patch, combine(1, 3, early, weights)))
+    rim, patch, weights = lax.optimization_barrier((rim, patch, combine(1, 4, early, weights)))
     rim = exchange(rim, TM)
     first = lax.axis_index("core") == 0
     row = lambda at: lax.dynamic_slice_in_dim(patch, at, S, axis=1)
@@ -417,7 +417,7 @@
     core = lax.ppermute(core, "core", [(0, 1), (1, 0)])
     pairs = [(4 + i, i + 1) for i in range(3)] + [(i + 1, 4 + i) for i in range(3)]
     band = lax.ppermute(band, ("core", "rows"), pairs)
-    weights = combine(4, 2, late, weights)
+    weights = combine(5, 1, late, weights)
     score = (dot(w_query, w_key.T) * (1.0 / C**0.5)).astype(BF)
     update = dot(w_value, w_out).astype(BF)
 

time: 149 us -> 149 us (level)
  no operation moved by 1% of the time
where the time goes in v15:
time: 149 us
  Pallas kernels  56.4 us (38%)
  blocking collectives  33.3 us (22%)
  starting transfers between devices  31.6 us (21%)
  waiting for transfers between devices  20.4 us (14%)
  local copies, waits for them, and re-layouts  5.11 us (3%)
    all_to_all x1, blocking collectives, local(): lax.all_to_all(v[None], axes, split_axis=1, concat_axis=0, tiled=True)[:, 0]  33.3 us
    pallas_call x1, Pallas kernels, local(): pl.pallas_call(conv_kernel, out_shape=(jax.ShapeDtypeStruct((S * S, 2, P2...  25.4 us
    all_to_all x4, starting transfers between devices, local(): lax.all_to_all(v[None], axes, split_axis=1, concat_axis=0, tiled=True)[:, 0]  22.5 us
    all_to_all x4, waiting for transfers between devices, local(): lax.all_to_all(v[None], axes, split_axis=1, concat_axis=0, tiled=True)[:, 0]  20.4 us
    pallas_call x3, Pallas kernels, combine(): pl.pallas_call(weights_kernel, grid=(count,), out_shape=jax.ShapeDtypeStr...  18.8 us
    pallas_call x1, Pallas kernels, local(): pl.pallas_call(attend_kernel, grid=(S * S // pixels,), out_shape=jax.Shap...  5.83 us
    ppermute x3, starting transfers between devices, local(): lax.ppermute(v, 'rows', [(i, (i + by) % 4) for i in range(4)])  5.13 us
    ppermute x1, starting transfers between devices, local(): band = lax.ppermute(band, ('core', 'rows'), pairs)  3.58 us
  transfers between devices with their start and end apart: 9, of which 4 were waited for; matrix products, arithmetic and copies ran while one was open for 2% of the time, Pallas kernels for 15%

profile of v15, /device:TPU:1, one launch (start us, length us, event | category | flops | bytes accessed | tf_op | source)
XLA Modules:
  0.0 148.6 jit_solution(3293084949082214442)
XLA Ops:
  0.0 0.0 copy-start
  0.0 2.7 %inner.1 = bf16[32,64,512]{2,1,0:T(8,128)(2,1)} custom-call(bf16[16,128,512]{2,1,0:T(8,128)(2,1)} %bitcast.30), custom_call_target="tpu_custom_call" | custom-call | flops 1048576 | bytes 4194304 | tf_op jit(solution)/shard_map/inner/pallas_call | solution.py:360
  2.7 8.8 %all-to-all-start = ((bf16[1,32,64,512]{3,2,0,1:T(8,128)(2,1)}), bf16[1,32,64,512]{3,2,0,1:T(8,128)(2,1)}, u32[]{:S(2)}, u32[]{:S(2)}) async-start(bf16[1,32,64,512]{3,2,0,1:T(8,128)(2,1)} %bitcast.36), calls=%async_computation | async-start | bytes 4194304 | tf_op jit(solution)/shard_map/all_to_all | solution.py:357
  11.5 0.0 copy-done.1
  11.5 1.3 latent_stats.1
  12.8 1.7 %collective-permute-start = (bf16[144,512]{1,0:T(8,128)(2,1)S(1)}, bf16[144,512]{1,0:T(8,128)(2,1)S(1)}, u32[]{:S(2)}, u32[]{:S(2)}) collective-permute-start(bf16[144,512]{1,0:T(8,128)(2,1)S(1)} %get-tuple-element.24), channel_id=1, source_target_pairs={{0,1},{1,2},{2,3},{3,0},{4,5},{5,6},{6,7},{7,4},{8,9},{9,10},{10,1... | collective-permute-start | bytes 442376 | tf_op jit(solution)/shard_map/ppermute | solution.py:395
  14.5 2.2 %collective-permute-start.1 = (bf16[144,512]{1,0:T(8,128)(2,1)S(1)}, bf16[144,512]{1,0:T(8,128)(2,1)S(1)}, u32[]{:S(2)}, u32[]{:S(2)}) collective-permute-start(bf16[144,512]{1,0:T(8,128)(2,1)S(1)} %get-tuple-element.25), channel_id=1, source_target_pairs={{0,3},{1,0},{2,1},{3,2},{4,7},{5,4},{6,5},{7,6},{8,11},{9,8},{10,9... | collective-permute-start | bytes 442376 | tf_op jit(solution)/shard_map/ppermute | solution.py:395
  16.7 1.2 collective-permute-start.2
  17.9 4.4 %weights.3.refs_0_ = bf16[12,3,512,512]{3,2,1,0:T(8,128)(2,1)} custom-call(bf16[3,3,3,512,512]{4,3,2,1,0:T(8,128)(2,1)} %plain_ref.1), custom_call_target="tpu_custom_call" | custom-call | flops 262144 | bytes 5767168 | tf_op jit(solution)/shard_map/weights/pallas_call | solution.py:382
  22.3 0.0 collective-permute-done.2.far_ref
  22.3 0.0 collective-permute-done.up_ref
  22.3 0.0 collective-permute-done.1.down_ref
  22.3 1.7 %rim.1 = bf16[16,2,24,512]{3,2,1,0:T(8,128)(2,1)} custom-call(bf16[16,128,512]{2,1,0:T(8,128)(2,1)S(1)} %bitcast.32, bf16[144,512]{1,0:T(8,128)(2,1)S(1)} %collective-permute-done.up_ref, bf16[144,512]{1,0:T(8,128)(2,1)S(1)} %collective-permute-done.1.down_ref, bf16[16,512]{1,0:T(8,128)(2,1)S(1)} %get-tuple-element.21.own_ref, ...), custom_call_target="tpu_custom_call" | custom-call | flops 4194304 | bytes 4194304 | tf_op jit(solution)/shard_map/rim/pallas_call | solution.py:399
  24.0 10.0 %weights.4.refs_0_ = bf16[12,3,512,512]{3,2,1,0:T(8,128)(2,1)} custom-call(bf16[3,3,3,512,512]{4,3,2,1,0:T(8,128)(2,1)} %plain_ref.1, bf16[12,3,512,512]{3,2,1,0:T(8,128)(2,1)} %weights.3.refs_0_), custom_call_target="tpu_custom_call", output_to_operand_aliasing={{}: (1, {})} | custom-call | flops 1048576 | bytes 23068672 | tf_op jit(solution)/shard_map/weights/pallas_call | solution.py:382
  34.0 5.8 %all-to-all-done = bf16[1,32,64,512]{3,2,0,1:T(8,128)(2,1)} async-done(((bf16[1,32,64,512]{3,2,0,1:T(8,128)(2,1)}), bf16[1,32,64,512]{3,2,0,1:T(8,128)(2,1)}, u32[]{:S(2)}, u32[]{:S(2)}) %all-to-all-start) | async-done | bytes 2097184 | tf_op jit(solution)/shard_map/all_to_all | solution.py:357
  39.8 4.4 %all-to-all-start.1 = ((bf16[1,32,24,512]{3,2,0,1:T(8,128)(2,1)}), bf16[1,32,24,512]{3,2,0,1:T(8,128)(2,1)S(1)}, u32[]{:S(2)}, u32[]{:S(2)}) async-start(bf16[1,32,24,512]{3,2,0,1:T(8,128)(2,1)} %bitcast.8), calls=%async_computation.1 | async-start | bytes 1572864 | tf_op jit(solution)/shard_map/all_to_all | solution.py:357
  44.3 1.1 constant_dynamic-slice_fusion
  45.3 0.4 collective-permute-start.3
  45.8 3.6 %collective-permute-start.4 = (bf16[32,8,512]{2,1,0:T(8,128)(2,1)S(1)}, bf16[32,8,512]{2,1,0:T(8,128)(2,1)S(1)}, u32[]{:S(2)}, u32[]{:S(2)}) collective-permute-start(bf16[32,8,512]{2,1,0:T(8,128)(2,1)S(1)} %get-tuple-element.32), channel_id=1, source_target_pairs={{4,1},{5,2},{6,3},{1,4},{2,5},{3,6},{12,9},{13,10},{14,11},{9,12},... | collective-permute-start | bytes 786440 | tf_op jit(solution)/shard_map/ppermute | solution.py:419
  49.4 0.7 pad_add_fusion.place_ref
  50.0 4.4 %weights.5.sums_ref = bf16[12,3,512,512]{3,2,1,0:T(8,128)(2,1)} custom-call(bf16[3,3,3,512,512]{4,3,2,1,0:T(8,128)(2,1)} %plain_ref.1, bf16[12,3,512,512]{3,2,1,0:T(8,128)(2,1)} %weights.4.refs_0_), custom_call_target="tpu_custom_call", output_to_operand_aliasing={{}: (1, {})} | custom-call | flops 262144 | bytes 5767168 | tf_op jit(solution)/shard_map/weights/pallas_call | solution.py:382
  54.4 0.0 collective-permute-done.3.core_ref
  54.4 0.0 copy-start.7
  54.4 0.0 collective-permute-done.4.band_ref
  54.4 0.0 copy-start.8
  54.4 4.2 %all-to-all-done.1 = bf16[1,32,24,512]{3,2,0,1:T(8,128)(2,1)S(1)} async-done(((bf16[1,32,24,512]{3,2,0,1:T(8,128)(2,1)}), bf16[1,32,24,512]{3,2,0,1:T(8,128)(2,1)S(1)}, u32[]{:S(2)}, u32[]{:S(2)}) %all-to-all-start.1) | async-done | bytes 786464 | tf_op jit(solution)/shard_map/all_to_all | solution.py:357
  58.6 0.0 copy-start.3
  58.6 0.0 copy-done.7
  58.6 0.0 copy-done.8
  58.6 0.9 copy-done.3
  59.5 25.4 %conv.1 = (bf16[64,2,16,512]{3,2,1,0:T(8,128)(2,1)}, f32[8,16,128]{2,1,0:T(8,128)}) custom-call(s32[2]{0:T(128)} %pad_add_fusion.place_ref, bf16[32,64,512]{2,1,0:T(8,128)(2,1)} %bitcast.7.in_ref, bf16[32,24,512]{2,1,0:T(8,128)(2,1)} %bitcast.38, bf16[32,8,512]{2,1,0:T(8,128)(2,1)} %copy-done.7, bf16[32,8,512]{2,1,0:T(8,128)(2,1)} %copy-done.8, ...), custom_call_target="tpu_custom_call" | custom-call | flops 12884901888 | bytes 29360128 | tf_op jit(solution)/shard_map/conv/pallas_call | solution.py:424
  84.9 0.0 copy-start.4
  84.9 0.0 copy-start.5
  84.9 5.6 %all-to-all-start.2 = ((f32[1,8,16,128]{3,2,0,1:T(8,128)}), f32[1,8,16,128]{3,2,0,1:T(8,128)S(1)}, u32[]{:S(2)}, u32[]{:S(2)}) async-start(f32[1,8,16,128]{3,2,0,1:T(8,128)} %bitcast.39), calls=%async_computation.2 | async-start | bytes 131072 | tf_op jit(solution)/shard_map/all_to_all | solution.py:357
  90.5 0.0 copy-done
  90.5 0.0 copy-done.6
  90.5 0.5 fusion.score_ref
  91.0 4.5 %all-to-all-done.2 = f32[1,8,16,128]{3,2,0,1:T(8,128)S(1)} async-done(((f32[1,8,16,128]{3,2,0,1:T(8,128)}), f32[1,8,16,128]{3,2,0,1:T(8,128)S(1)}, u32[]{:S(2)}, u32[]{:S(2)}) %all-to-all-start.2) | async-done | bytes 65568 | tf_op jit(solution)/shard_map/all_to_all | solution.py:357
  95.5 0.7 merge.1
  96.2 3.7 %all-to-all-start.3 = ((f32[1,16,16,128]{3,2,0,1:T(8,128)}), f32[1,16,16,128]{3,2,0,1:T(8,128)S(1)}, u32[]{:S(2)}, u32[]{:S(2)}) async-start(f32[1,16,16,128]{3,2,0,1:T(8,128)} %bitcast.14), calls=%async_computation.3 | async-start | bytes 262144 | tf_op jit(solution)/shard_map/all_to_all | solution.py:357
  99.9 0.0 copy-done.4
  99.9 0.0 copy-done.5
  99.9 0.4 convolution_convert_fusion.update_ref
  100.4 6.0 %all-to-all-done.3 = f32[1,16,16,128]{3,2,0,1:T(8,128)S(1)} async-done(((f32[1,16,16,128]{3,2,0,1:T(8,128)}), f32[1,16,16,128]{3,2,0,1:T(8,128)S(1)}, u32[]{:S(2)}, u32[]{:S(2)}) %all-to-all-start.3) | async-done | bytes 131104 | tf_op jit(solution)/shard_map/all_to_all | solution.py:357
  106.4 1.6 %copy-done.2 = bf16[64,2,16,512]{3,2,1,0:T(8,128)(2,1)S(1)} copy-done((bf16[64,2,16,512]{3,2,1,0:T(8,128)(2,1)S(1)}, bf16[64,2,16,512]{3,2,1,0:T(8,128)(2,1)}, u32[]{:S(2)}) %copy-start.2) | copy-done | bytes 2097176
  107.9 5.8 %attend.1 = bf16[32,64,512]{2,1,0:T(8,128)(2,1)S(1)} custom-call(bf16[64,2,16,512]{3,2,1,0:T(8,128)(2,1)S(1)} %copy-done.2, f32[16,16,128]{2,1,0:T(8,128)S(1)} %bitcast.35, bf16[512,512]{1,0:T(8,128)(2,1)S(1)} %fusion.score_ref, bf16[512,512]{1,0:T(8,128)(2,1)S(1)} %convolution_convert_fusion.update_ref), custom_call_target="tpu_custom_call" | custom-call | flops 4294967296 | bytes 8388608 | tf_op jit(solution)/shard_map/attend/pallas_call | solution.py:453
  113.8 33.3 %all_to_all.20 = bf16[1,32,64,512]{3,2,0,1:T(8,128)(2,1)S(1)} all-to-all(bf16[1,32,64,512]{3,2,0,1:T(8,128)(2,1)S(1)} %bitcast.33), channel_id=1, replica_groups=mesh['x'=4,'y'=4,'core'=2,'rows'=4] {'x','y','core'}, dimensions={1} | all-to-all | bytes 4194304 | tf_op jit(solution)/shard_map/all_to_all | solution.py:357
  147.1 1.5 %copy.14 = bf16[2,8,16,8,512]{4,3,2,1,0:T(8,128)(2,1)} copy(bf16[2,8,16,8,512]{4,3,1,0,2:T(8,128)(2,1)S(1)} %bitcast.37) | data formatting | bytes 4194304 | tf_op jit(solution)/shard_map/transpose | solution.py:465
  (3 shorter events, 0.0 us)
Async XLA Ops:
  0.0 90.5 %copy-start = (bf16[512,512]{1,0:T(8,128)(2,1)S(1)}, bf16[512,512]{1,0:T(8,128)(2,1)}, u32[]{:S(2)}) copy-start(bf16[512,512]{1,0:T(8,128)(2,1)} %param.8) | copy-start | bytes 1572868
  2.7 8.8 %copy-start.1 = (bf16[1,16,128,512]{3,2,1,0:T(8,128)(2,1)S(1)}, bf16[1,16,128,512]{3,2,1,0:T(8,128)(2,1)}, u32[]{:S(2)}) copy-start(bf16[1,16,128,512]{3,2,1,0:T(8,128)(2,1)} %param.6) | copy-start | bytes 6291460
  2.7 37.1 %all-to-all-start = ((bf16[1,32,64,512]{3,2,0,1:T(8,128)(2,1)}), bf16[1,32,64,512]{3,2,0,1:T(8,128)(2,1)}, u32[]{:S(2)}, u32[]{:S(2)}) async-start(bf16[1,32,64,512]{3,2,0,1:T(8,128)(2,1)} %bitcast.36), calls=%async_computation | async-start | bytes 4194304 | tf_op jit(solution)/shard_map/all_to_all | solution.py:357
  12.8 9.5 %collective-permute-start = (bf16[144,512]{1,0:T(8,128)(2,1)S(1)}, bf16[144,512]{1,0:T(8,128)(2,1)S(1)}, u32[]{:S(2)}, u32[]{:S(2)}) collective-permute-start(bf16[144,512]{1,0:T(8,128)(2,1)S(1)} %get-tuple-element.24), channel_id=1, source_target_pairs={{0,1},{1,2},{2,3},{3,0},{4,5},{5,6},{6,7},{7,4},{8,9},{9,10},{10,1... | collective-permute-start | bytes 442376 | tf_op jit(solution)/shard_map/ppermute | solution.py:395
  14.5 7.8 %collective-permute-start.1 = (bf16[144,512]{1,0:T(8,128)(2,1)S(1)}, bf16[144,512]{1,0:T(8,128)(2,1)S(1)}, u32[]{:S(2)}, u32[]{:S(2)}) collective-permute-start(bf16[144,512]{1,0:T(8,128)(2,1)S(1)} %get-tuple-element.25), channel_id=1, source_target_pairs={{0,3},{1,0},{2,1},{3,2},{4,7},{5,4},{6,5},{7,6},{8,11},{9,8},{10,9... | collective-permute-start | bytes 442376 | tf_op jit(solution)/shard_map/ppermute | solution.py:395
  16.7 5.6 %collective-permute-start.2 = (bf16[16,512]{1,0:T(8,128)(2,1)S(1)}, bf16[16,512]{1,0:T(8,128)(2,1)S(1)}, u32[]{:S(2)}, u32[]{:S(2)}) collective-permute-start(bf16[16,512]{1,0:T(8,128)(2,1)S(1)} %get-tuple-element.21.own_ref), channel_id=1, source_target_pairs={{0,2},{1,3},{2,0},{3,1},{4,6},{5,7},{6,4},{7,5},{8,10},{9,11},{10,... | collective-permute-start | bytes 49160 | tf_op jit(solution)/shard_map/ppermute | solution.py:395
  39.8 18.8 %all-to-all-start.1 = ((bf16[1,32,24,512]{3,2,0,1:T(8,128)(2,1)}), bf16[1,32,24,512]{3,2,0,1:T(8,128)(2,1)S(1)}, u32[]{:S(2)}, u32[]{:S(2)}) async-start(bf16[1,32,24,512]{3,2,0,1:T(8,128)(2,1)} %bitcast.8), calls=%async_computation.1 | async-start | bytes 1572864 | tf_op jit(solution)/shard_map/all_to_all | solution.py:357
  45.3 9.1 %collective-permute-start.3 = (bf16[32,8,512]{2,1,0:T(8,128)(2,1)S(1)}, bf16[32,8,512]{2,1,0:T(8,128)(2,1)S(1)}, u32[]{:S(2)}, u32[]{:S(2)}) collective-permute-start(bf16[32,8,512]{2,1,0:T(8,128)(2,1)S(1)} %get-tuple-element.31), channel_id=1, source_target_pairs={{0,4},{4,0},{1,5},{5,1},{2,6},{6,2},{3,7},{7,3},{8,12},{12,8},{9,1... | collective-permute-start | bytes 786440 | tf_op jit(solution)/shard_map/ppermute | solution.py:417
  45.8 8.6 %collective-permute-start.4 = (bf16[32,8,512]{2,1,0:T(8,128)(2,1)S(1)}, bf16[32,8,512]{2,1,0:T(8,128)(2,1)S(1)}, u32[]{:S(2)}, u32[]{:S(2)}) collective-permute-start(bf16[32,8,512]{2,1,0:T(8,128)(2,1)S(1)} %get-tuple-element.32), channel_id=1, source_target_pairs={{4,1},{5,2},{6,3},{1,4},{2,5},{3,6},{12,9},{13,10},{14,11},{9,12},... | collective-permute-start | bytes 786440 | tf_op jit(solution)/shard_map/ppermute | solution.py:419
  54.4 4.2 %copy-start.7 = (bf16[32,8,512]{2,1,0:T(8,128)(2,1)}, bf16[32,8,512]{2,1,0:T(8,128)(2,1)S(1)}, u32[]{:S(2)}) copy-start(bf16[32,8,512]{2,1,0:T(8,128)(2,1)S(1)} %collective-permute-done.3.core_ref) | copy-start | bytes 786436
  54.4 4.2 %copy-start.8 = (bf16[32,8,512]{2,1,0:T(8,128)(2,1)}, bf16[32,8,512]{2,1,0:T(8,128)(2,1)S(1)}, u32[]{:S(2)}) copy-start(bf16[32,8,512]{2,1,0:T(8,128)(2,1)S(1)} %collective-permute-done.4.band_ref) | copy-start | bytes 786436
  58.6 0.9 copy-start.3
  59.5 31.0 %copy-start.6 = (bf16[512,512]{1,0:T(8,128)(2,1)S(1)}, bf16[512,512]{1,0:T(8,128)(2,1)}, u32[]{:S(2)}) copy-start(bf16[512,512]{1,0:T(8,128)(2,1)} %param.9) | copy-start | bytes 1572868
  84.9 15.0 %copy-start.4 = (bf16[512,512]{1,0:T(8,128)(2,1)S(1)}, bf16[512,512]{1,0:T(8,128)(2,1)}, u32[]{:S(2)}) copy-start(bf16[512,512]{1,0:T(8,128)(2,1)} %param.10) | copy-start | bytes 1572868
  84.9 15.0 %copy-start.5 = (bf16[512,512]{1,0:T(8,128)(2,1)S(1)}, bf16[512,512]{1,0:T(8,128)(2,1)}, u32[]{:S(2)}) copy-start(bf16[512,512]{1,0:T(8,128)(2,1)} %param.11) | copy-start | bytes 1572868
  84.9 10.5 %all-to-all-start.2 = ((f32[1,8,16,128]{3,2,0,1:T(8,128)}), f32[1,8,16,128]{3,2,0,1:T(8,128)S(1)}, u32[]{:S(2)}, u32[]{:S(2)}) async-start(f32[1,8,16,128]{3,2,0,1:T(8,128)} %bitcast.39), calls=%async_computation.2 | async-start | bytes 131072 | tf_op jit(solution)/shard_map/all_to_all | solution.py:357
  96.2 10.2 %all-to-all-start.3 = ((f32[1,16,16,128]{3,2,0,1:T(8,128)}), f32[1,16,16,128]{3,2,0,1:T(8,128)S(1)}, u32[]{:S(2)}, u32[]{:S(2)}) async-start(f32[1,16,16,128]{3,2,0,1:T(8,128)} %bitcast.14), calls=%async_computation.3 | async-start | bytes 262144 | tf_op jit(solution)/shard_map/all_to_all | solution.py:357
  106.4 1.6 %copy-start.2 = (bf16[64,2,16,512]{3,2,1,0:T(8,128)(2,1)S(1)}, bf16[64,2,16,512]{3,2,1,0:T(8,128)(2,1)}, u32[]{:S(2)}) copy-start(bf16[64,2,16,512]{3,2,1,0:T(8,128)(2,1)} %get-tuple-element.35.mid_ref) | copy-start | bytes 6291460
